TPU v7x, 512 devices: a whole 4x4x16 slice. The times are simulated.
512 devices in a mesh: ctx: 32 (over z, y_lo), hid: 16 (over y_hi, x, core).
Axes of the slice: x: 4, y: 4 (y_hi: 2, y_lo: 2; y = y_hi * 2 + y_lo), z: 16, core: 2. Of those that a mesh axis runs over, the one named last changes fastest.
Arguments:
- queries: bfloat16 [16384, 2048], P('ctx', 'hid'), may hold values from -9 to 9
- keys: bfloat16 [16384, 512], P('ctx'), may hold values from -9 to 9
- values: bfloat16 [16384, 512], P('ctx'), may hold values from -7 to 7
- doc_ids: int32 [16384], P('ctx'), may hold values from 0 to 7, never falling along the last dimension, each value on 1 to 12288 neighbouring positions
- hidden: bfloat16 [16384, 3072], P('ctx', 'hid'), may hold values from -6 to 6
- out_weight: bfloat16 [2048, 3072], P(None, 'hid'), may hold values from -0.125 to 0.125
- projector: bfloat16 [3072, 4096], P(None, 'hid'), may hold values from -0.109375 to 0.109375
- teacher: bfloat16 [16384, 4096], P(('ctx', 'hid')), may hold values from -6 to 6
Outputs:
- grad_projector: float32 [3072, 4096], P('ctx', 'hid')
- attended: bfloat16 [16384, 2048], P('ctx', 'hid')
Inputs may be any that keep to these rules, and one draw needn't show every extreme that they name: `doc_ids`: document ids never fall along the sequence; every document spans at most three quarters of 16384 positions.
All inputs are finite; a program needn't handle non-finite values.
Results may differ from a plain program's by a relative error of at most 0.0034.
Values may be sent and summed in bfloat16 or wider, within the bound.
No kernel may reach another device: no remote copies, remote signals or barrier semaphores. Data moves between devices by JAX's collectives and lax.ppermute only.
A program may use at most 64 MiB of HBM per device.

v0:
```python
import functools
import math

import jax
import jax.numpy as jnp
from jax import lax
from jax.sharding import PartitionSpec as P

HEAD = 128
GROUP = 4


NEG_FILL = -1e30


def keep_state(carried):
    return carried


def softmax_update(
    carried, query_rows, query_pos, query_doc, key_block, value_block, key_pos, key_doc
):
    run_max, run_total, run_acc = carried
    row_count = query_rows.shape[0]
    head_count = run_max.shape[0]
    head_size = query_rows.shape[1] // head_count
    query_heads = query_rows.reshape(row_count, head_count, head_size)
    scores = jnp.einsum(
        "qhd,kd->hqk", query_heads, key_block, preferred_element_type=jnp.float32
    ) * head_size ** (-0.5)
    allowed = (key_pos[None, :] <= query_pos[:, None]) & (key_doc[None, :] == query_doc[:, None])
    masked = jnp.where(allowed[None], scores, NEG_FILL)
    new_max = jnp.maximum(run_max, jnp.max(masked, axis=2))
    factor = jnp.exp(run_max - new_max)
    weights = jnp.where(allowed[None], jnp.exp(masked - new_max[:, :, None]), 0.0)
    new_total = run_total * factor + jnp.sum(weights, axis=2)
    blended = jnp.einsum(
        "hqk,kd->qhd", weights.astype(jnp.bfloat16), value_block, preferred_element_type=jnp.float32
    )
    new_acc = run_acc * jnp.transpose(factor)[:, :, None] + blended
    return (new_max, new_total, new_acc)


def attend_all(query_sets, keys, values, doc_wire, head_count):
    initial = []
    for query_rows, query_pos, query_doc in query_sets:
        row_count = query_rows.shape[0]
        head_size = query_rows.shape[1] // head_count
        initial.append(
            (
                jnp.full((head_count, row_count), NEG_FILL, jnp.float32),
                jnp.zeros((head_count, row_count), jnp.float32),
                jnp.zeros((row_count, head_count, head_size), jnp.float32),
            )
        )
    key_all = lax.all_gather(keys, "ctx", axis=0, tiled=True)
    value_all = lax.all_gather(values, "ctx", axis=0, tiled=True)
    doc_all = lax.all_gather(doc_wire, "ctx", axis=0, tiled=True)
    key_total = key_all.shape[0]
    key_width = math.gcd(key_total, 512)

    def one_block(block_index, states):
        offset = block_index * key_width
        key_block = lax.dynamic_slice_in_dim(key_all, offset, key_width, 0)
        value_block = lax.dynamic_slice_in_dim(value_all, offset, key_width, 0)
        key_doc = lax.dynamic_slice_in_dim(doc_all, offset, key_width, 0).astype(jnp.float32)
        key_pos = offset + lax.iota(jnp.int32, key_width)
        query_rows, query_pos, query_doc = query_sets[0]
        active = (offset <= query_pos[-1]) & (key_doc[key_width - 1] >= query_doc[0])
        advance = functools.partial(
            softmax_update,
            query_rows=query_rows,
            query_pos=query_pos,
            query_doc=query_doc,
            key_block=key_block,
            value_block=value_block,
            key_pos=key_pos,
            key_doc=key_doc,
        )
        updated = [lax.cond(active, advance, keep_state, states[0])]
        return tuple(updated)

    finished = lax.fori_loop(0, key_total // key_width, one_block, tuple(initial))
    run_max, run_total, run_acc = finished[0]
    attended = run_acc / jnp.transpose(run_total)[:, :, None]
    outputs = attended.reshape(attended.shape[0], -1).astype(jnp.bfloat16)
    return outputs


def on_device(queries, keys, values, doc_ids, hidden, out_weight, projector, teacher):
    ctx_count = lax.axis_size("ctx")
    ctx_index = lax.axis_index("ctx")
    hid_index = lax.axis_index("hid")
    row_count = queries.shape[0]
    length = row_count * ctx_count
    head_count = queries.shape[1] // HEAD
    shared_column = hid_index * head_count // GROUP * HEAD
    own_keys = lax.dynamic_slice_in_dim(keys, shared_column, HEAD, 1)
    own_values = lax.dynamic_slice_in_dim(values, shared_column, HEAD, 1)
    doc_wire = doc_ids.astype(jnp.bfloat16)
    local_pos = lax.iota(jnp.int32, row_count)
    positions = ctx_index * row_count + local_pos
    query_sets = ((queries, positions, doc_ids.astype(jnp.float32)),)
    attended = attend_all(query_sets, own_keys, own_values, doc_wire, head_count)
    all_heads = lax.all_gather(attended, "hid", axis=1, tiled=True)
    student_cols = (
        hidden.astype(jnp.float32)
        + jnp.dot(all_heads, out_weight, preferred_element_type=jnp.float32)
    ).astype(jnp.bfloat16)
    student_full = lax.all_gather(student_cols, "hid", axis=1, tiled=True)
    teacher_cols = lax.all_to_all(teacher, "hid", split_axis=1, concat_axis=0, tiled=True)
    projected = jnp.dot(student_full, projector, preferred_element_type=jnp.float32)
    mismatch = (projected - teacher_cols.astype(jnp.float32)).astype(jnp.bfloat16)
    summed = lax.psum_scatter(
        lax.dot_general(
            student_full, mismatch, (((0,), (0,)), ((), ())), preferred_element_type=jnp.float32
        ),
        "ctx",
        scatter_dimension=0,
        tiled=True,
    )
    return (summed * length ** (-0.5), attended)


def solution(mesh):
    return jax.shard_map(
        on_device,
        mesh=mesh,
        in_specs=(
            P("ctx", "hid"),
            P("ctx", None),
            P("ctx", None),
            P("ctx"),
            P("ctx", "hid"),
            P(None, "hid"),
            P(None, "hid"),
            P(("ctx", "hid"), None),
        ),
        out_specs=(P("ctx", "hid"), P("ctx", "hid")),
        check_vma=False,
    )
```

profile of v0, /device:TPU:6, one launch (start us, length us, event | category | flops | bytes accessed | tf_op | source)
XLA Modules:
  0.0 775.8 jit_solution(14103764672102937447)
XLA Ops:
  7.2 1.7 constant_dynamic-slice_fusion.1
  9.0 1.6 constant_dynamic-slice_fusion
  10.6 0.8 fusion.29
  11.4 69.3 %all-gather.1 = bf16[32,1,512]{2,1,0:T(2,128)(2,1)S(1)} all-gather(bf16[1,1,512]{2,1,0:T(2,128)(2,1)S(1)} %reshape.138), channel_id=1, replica_groups=mesh['ctx'=32,'hid'=16] {'ctx'}, dimensions={0}, use_global_device_ids=true | all-gather | bytes 33792 | tf_op jit(solution)/shard_map/all_gather | solution.py:58
  80.9 75.6 %all-gather.7.cloned.1.call-done = bf16[16384,128]{1,0:T(8,128)(2,1)} async-done(((bf16[512,128]{1,0:T(8,128)(2,1)}), bf16[16384,128]{1,0:T(8,128)(2,1)}) %all-gather.7.cloned.1.call-update) | async-done | bytes 4194320 | tf_op jit(solution)/shard_map/all_gather | solution.py:56
  156.5 140.1 %all-gather.9.cloned.1.call-done = bf16[16384,128]{1,0:T(8,128)(2,1)} async-done(((bf16[512,128]{1,0:T(8,128)(2,1)}), bf16[16384,128]{1,0:T(8,128)(2,1)}) %all-gather.9.cloned.1.call-update) | async-done | bytes 4194320 | tf_op jit(solution)/shard_map/all_gather | solution.py:57
  296.7 117.6 %while.17 = (s32[]{:T(128)}, f32[1,512]{1,0:T(1,128)S(1)}, f32[1,512]{1,0:T(1,128)S(1)}, f32[512,1,128]{0,2,1:T(8,128)S(1)}, s32[512]{0:T(512)S(1)}, /*index=5*/...) while((s32[]{:T(128)}, f32[1,512]{1,0:T(1,128)S(1)}, ...), condition=%wide.region_5.6_spmd, body=%wide.region_0.5_spmd.sunk | while | flops 139069456 | bytes 4131213 | solution.py:83
  300.2 3.2 conditional.2
  300.2 1.4 fusion.28
  302.0 1.4 fusion.2
  304.6 0.6 slice.25
  308.2 0.6 slice.25
  311.8 0.6 slice.25
  315.4 0.6 slice.25
  329.7 0.6 slice.25
  333.3 0.6 slice.25
  336.8 0.6 slice.25
  340.4 0.6 slice.25
  344.0 0.6 slice.25
  347.6 0.6 slice.25
  365.4 0.6 slice.25
  369.0 0.6 slice.25
  372.6 0.6 slice.25
  414.4 0.8 divide_convert_fusion
  415.3 133.1 %all-gather.13.cloned.1.call-done = bf16[512,1,2048]{2,0,1:T(8,128)(2,1)} async-done(((bf16[512,1,128]{2,0,1:T(8,128)(2,1)}), bf16[512,1,2048]{2,0,1:T(8,128)(2,1)}) %all-gather.13.cloned.1.call-update) | async-done | bytes 2097168 | tf_op jit(solution)/shard_map/all_gather | solution.py:105
  548.5 3.1 fusion.24
  551.7 11.4 %all_to_all.13 = bf16[32,16,256]{2,0,1:T(8,128)(2,1)S(1)} all-to-all(bf16[32,16,256]{2,0,1:T(8,128)(2,1)S(1)} %bitcast.49), channel_id=1, replica_groups=mesh['ctx'=32,'hid'=16] {'hid'}, dimensions={1} | all-to-all | bytes 524288 | tf_op jit(solution)/shard_map/all_to_all | solution.py:111
  563.1 55.2 %all-gather.11.cloned.1.call-done = bf16[512,3072]{0,1:T(8,128)(2,1)} async-done(((bf16[512,192]{0,1:T(8,128)(2,1)}), bf16[512,3072]{0,1:T(8,128)(2,1)}) %all-gather.11.cloned.1.call-update) | async-done | bytes 3145744 | tf_op jit(solution)/shard_map/all_gather | solution.py:110
  618.3 8.0 %fusion.27 = f32[3072,256]{1,0:T(8,128)} fusion(bf16[512,3072]{0,1:T(8,128)(2,1)} %all-gather.11.cloned.1.call-done, f32[512,256]{1,0:T(8,128)S(1)} %bitcast.52, bf16[3072,256]{1,0:T(8,128)(2,1)S(1)} %copy-done), kind=kOutput, calls=%fused_computation.31 | convolution fusion | flops 1610874880 | bytes 8388608 | tf_op jit(solution)/shard_map/dot_general | solution.py:115
  626.4 0.8 fusion.35
  627.2 140.6 %reduce-scatter.2.cloned.1.call-done = f32[96,256]{1,0:T(8,128)} async-done(((f32[3072,256]{1,0:T(8,128)}), f32[96,256]{1,0:T(8,128)}) %reduce-scatter.2.cloned.1.call-update) | async-done | bytes 98320 | tf_op jit(solution)/shard_map/reduce_scatter | solution.py:114
  767.7 1.5 broadcast_multiply_fusion
  (210 shorter events, 50.0 us)
Async XLA Ops:
  7.2 611.2 %copy-start = (bf16[3072,256]{1,0:T(8,128)(2,1)S(1)}, bf16[3072,256]{1,0:T(8,128)(2,1)}, u32[]{:S(2)}) copy-start(bf16[3072,256]{1,0:T(8,128)(2,1)} %param.18) | copy-start | bytes 4718596
  7.2 149.3 %all-gather.7.cloned.1.call-start = ((), (), s32[]{:S(2)}) async-start(), calls=%async_computation.2 | async-start | bytes 4325376 | tf_op jit(solution)/shard_map/all_gather | solution.py:56
  8.9 287.7 %all-gather.9.cloned.1.call-start = ((), (), s32[]{:S(2)}) async-start(), calls=%async_computation.3 | async-start | bytes 4325376 | tf_op jit(solution)/shard_map/all_gather | solution.py:57
  10.6 537.9 %all-gather.13.cloned.1.call-start = ((), (), s32[]{:S(2)}) async-start(), calls=%async_computation.6 | async-start | bytes 2228224 | tf_op jit(solution)/shard_map/all_gather | solution.py:105
  296.6 251.8 %copy-start.2 = (bf16[2048,192]{0,1:T(8,128)(2,1)S(1)}, bf16[2048,192]{0,1:T(8,128)(2,1)}, u32[]{:S(2)}) copy-start(bf16[2048,192]{0,1:T(8,128)(2,1)} %param.17) | copy-start | bytes 2359300
  296.6 251.8 %copy-start.3 = (bf16[512,192]{0,1:T(8,128)(2,1)S(1)}, bf16[512,192]{0,1:T(8,128)(2,1)}, u32[]{:S(2)}) copy-start(bf16[512,192]{0,1:T(8,128)(2,1)} %param.16) | copy-start | bytes 589828
  414.3 137.4 %copy-start.1 = (bf16[32,4096]{1,0:T(8,128)(2,1)S(1)}, bf16[32,4096]{1,0:T(8,128)(2,1)}, u32[]{:S(2)}) copy-start(bf16[32,4096]{1,0:T(8,128)(2,1)} %param.19) | copy-start | bytes 786436
  415.3 203.1 %all-gather.11.cloned.1.call-start = ((), (), s32[]{:S(2)}) async-start(), calls=%async_computation.4 | async-start | bytes 3342336 | tf_op jit(solution)/shard_map/all_gather | solution.py:110
  551.6 216.1 %reduce-scatter.2.cloned.1.call-start = ((), (), s32[]{:S(2)}) async-start(), calls=%async_computation.5 | async-start | bytes 3244032 | tf_op jit(solution)/shard_map/reduce_scatter | solution.py:114
Sparse Core Ops, SparseCore 0:
  10.7 145.7 all-gather.6
  158.6 137.9 all-gather.8
  415.4 133.0 all-gather.12
  551.7 66.5 all-gather.10
  626.5 141.2 reduce-scatter.1
where the time goes:
time: 778 us; the launch traced here: 776 us
  waiting for transfers between devices  545 us (70%)
  blocking collectives  80.7 us (10%)
  loops' own time  58.2 us (7%)
  local copies, waits for them, and re-layouts  57.2 us (7%)
  matrix products  13.9 us (2%)
  between operations  13.9 us (2%)
    reduce_scatter x1, waiting for transfers between devices, on_device(): lax.psum_scatter(lax.dot_general(student_full, mismatch, (((0,), (0,)), (...  141 us
    all_gather x1, waiting for transfers between devices, attend_all(): value_all = lax.all_gather(values, 'ctx', axis=0, tiled=True)  140 us
    all_gather x1, waiting for transfers between devices, on_device(): all_heads = lax.all_gather(attended, 'hid', axis=1, tiled=True)  133 us
    all_gather x1, waiting for transfers between devices, attend_all(): key_all = lax.all_gather(keys, 'ctx', axis=0, tiled=True)  75.6 us
    all_gather x1, blocking collectives, attend_all(): doc_all = lax.all_gather(doc_wire, 'ctx', axis=0, tiled=True)  69.3 us
    another operation x1, loops' own time, attend_all(): lax.fori_loop(0, key_total // key_width, one_block, tuple(initial))  57.7 us
    all_gather x1, waiting for transfers between devices, on_device(): student_full = lax.all_gather(student_cols, 'hid', axis=1, tiled=True)  55.2 us
    slice x32, local copies, waits for them, and re-layouts, one_block(): key_doc[key_width - 1] >= query_doc[0]  19.2 us
  transfers between devices with their start and end apart: 5, of which 5 were waited for; matrix products, arithmetic and copies ran while one was open for 0% of the time, Pallas kernels for 0%

commit v1 on v0

v1 whole, which is shorter than its diff:
```python
import functools

import jax
import jax.numpy as jnp
from jax import lax
from jax.experimental import pallas as pl
from jax.experimental.pallas import tpu as pltpu
from jax.sharding import Mesh
from jax.sharding import PartitionSpec as P

HEAD = 128
SCALE2 = HEAD ** -0.5 * 1.4426950408889634
EMPTY = -1e30
MASKED = -2e30
BF = jnp.bfloat16
F32 = jnp.float32
CTX = ("z", "yl")
HID = ("yh", "xh", "xl", "c")
GROUP = ("xl", "c")
OCTET = ("yl", "xl", "c")
HEADSETS = ("yh", "xh")
CHIPS = ("xl", "yh", "xh")
BLOCKS = 4


def attend_kernel(sc, kv, q_own, q_other, qdoc, out, v_turned):
    depth = kv.shape[0]
    z, yl, j = sc[144], sc[145], sc[146]
    for block in range(depth):
        v_turned[:, block * 128:(block + 1) * 128] = kv[block, 128:256, :].T
    key_iota = lax.broadcasted_iota(jnp.int32, (128, 512), 0)
    row_iota = lax.broadcasted_iota(jnp.int32, (1, 512), 1) % 128
    for side, q_ref in ((0, q_own), (1, q_other)):
        yl_q = yl if side == 0 else 1 - yl
        block_q = 2 * z + yl_q

        def one_tile(rc, carry, side=side, q_ref=q_ref, yl_q=yl_q, block_q=block_q):
            row0 = pl.multiple_of(rc * 128, 128)
            q = jnp.concatenate([q_ref[pl.ds(h * 512 + row0, 128), :] for h in range(4)], axis=0)
            docs = qdoc[pl.ds(side * 4 + rc, 1), :]
            docs = jnp.concatenate([docs] * 4, axis=1)
            first, last = sc[128 + side * 4 + rc], sc[136 + side * 4 + rc]
            q_min = block_q * 512 + row0
            q_pos = q_min + row_iota

            def step(ch, state, masked):
                run_max, run_sum, acc = state
                keys = kv[pl.ds(ch * BLOCKS, BLOCKS), 0:128, :].reshape(BLOCKS * 128, 128)
                s = lax.dot_general(keys, q, (((1,), (1,)), ((), ())), preferred_element_type=F32) * SCALE2
                if masked:
                    parts = []
                    for i in range(BLOCKS):
                        block = ch * BLOCKS + i
                        low = jnp.zeros((1, 512), jnp.int32)
                        for d in range(8):
                            low = jnp.where(docs == d, sc[block * 8 + d], low)
                        low = low - j * 128
                        high = q_pos - ((2 * block + yl) * 512 + j * 128)
                        ok = (key_iota >= low) & (key_iota <= high)
                        parts.append(jnp.where(ok, s[i * 128:(i + 1) * 128], MASKED))
                    s = jnp.concatenate(parts, axis=0)
                new_max = jnp.maximum(run_max, jnp.max(s, axis=0, keepdims=True))
                factor = jnp.exp2(run_max - new_max)
                w = jnp.exp2(s - new_max)
                new_sum = run_sum * factor + jnp.sum(w, axis=0, keepdims=True)
                cols = pl.ds(pl.multiple_of(ch * (BLOCKS * 128), BLOCKS * 128), BLOCKS * 128)
                new_acc = acc * factor + jnp.dot(v_turned[:, cols], w.astype(BF), preferred_element_type=F32)
                return new_max, new_sum, new_acc

            def any_step(ch, state):
                k_max = (2 * (ch * BLOCKS + BLOCKS - 1) + yl) * 512 + j * 128 + 127
                full = (k_max <= q_min) & (sc[ch * (BLOCKS * 8) + last] <= j * 128)
                return lax.cond(full, functools.partial(step, ch, masked=False), functools.partial(step, ch, masked=True), state)

            begin = jnp.int32(0)
            for ch in range(depth // BLOCKS):
                none = sc[(ch * BLOCKS + BLOCKS - 1) * 8 + first] >= (j + 1) * 128
                begin = begin + none.astype(jnp.int32)
            end = z // BLOCKS + 1
            state = (jnp.full((1, 512), EMPTY, F32), jnp.zeros((1, 512), F32), jnp.zeros((128, 512), F32))
            run_max, run_sum, acc = lax.fori_loop(begin, end, any_step, state)
            seen = run_sum > 0
            o = (acc * (1.0 / jnp.where(seen, run_sum, 1.0))).astype(BF)
            lse = jnp.where(seen, run_max + jnp.log2(jnp.where(seen, run_sum, 1.0)), EMPTY)
            hi = lse.astype(BF).astype(F32)
            mid = (lse - hi).astype(BF).astype(F32)
            lo = lse - hi - mid
            dest = yl_q * 4 + rc
            rows = [part[:, h * 128:(h + 1) * 128] for part in (hi, mid, lo) for h in range(4)]
            rows.append(jnp.zeros((4, 128), F32))
            for h in range(4):
                out[dest, h * 128:(h + 1) * 128, :] = o[:, h * 128:(h + 1) * 128]
            out[dest, 512:528, :] = jnp.concatenate(rows, axis=0).astype(BF)
            return carry

        lax.fori_loop(0, 4, one_tile, 0)


def combine_kernel(parts, out):
    count = parts.shape[0]
    tails = [parts[s, 512:528, :].astype(F32) for s in range(count)]
    for h in range(4):
        lses = [t[h:h + 1] + t[4 + h:5 + h] + t[8 + h:9 + h] for t in tails]
        top = functools.reduce(jnp.maximum, lses)
        weights = [jnp.exp2(v - top) for v in lses]
        inverse = 1.0 / sum(weights)
        total = sum(w * inverse * parts[s, h * 128:(h + 1) * 128, :].astype(F32) for s, w in enumerate(weights))
        out[h * 128:(h + 1) * 128, :] = total.astype(BF)


VMEM = pl.BlockSpec(memory_space=pltpu.VMEM)
SMEM = pl.BlockSpec(memory_space=pltpu.SMEM)


def attend(scalars, kv, q_own, q_other, qdoc):
    return pl.pallas_call(
        attend_kernel,
        out_shape=jax.ShapeDtypeStruct((8, 528, 128), BF),
        in_specs=[SMEM, VMEM, VMEM, VMEM, VMEM],
        out_specs=VMEM,
        scratch_shapes=[pltpu.VMEM((128, 128 * kv.shape[0]), BF)],
        compiler_params=pltpu.CompilerParams(vmem_limit_bytes=40 * 1024 * 1024),
    )(scalars, kv, q_own, q_other, qdoc)


def combine(parts):
    return pl.pallas_call(
        combine_kernel,
        out_shape=jax.ShapeDtypeStruct((512, 128), BF),
        in_specs=[VMEM],
        out_specs=VMEM,
        compiler_params=pltpu.CompilerParams(vmem_limit_bytes=16 * 1024 * 1024),
    )(parts)


def spread(x, axes):
    count = 1
    for axis in axes:
        count *= lax.axis_size(axis)
    return lax.all_to_all(jnp.broadcast_to(x[None], (count,) + x.shape), axes, 0, 0)


def on_device(queries, keys, values, doc_ids, hidden, out_weight, projector, teacher):
    z, yl, c = lax.axis_index("z"), lax.axis_index("yl"), lax.axis_index("c")
    g = lax.axis_index("yh") * 2 + lax.axis_index("xh")
    j = lax.axis_index("xl") * 2 + c
    swap = [(0, 1), (1, 0)]

    doc_rows = jnp.pad(doc_ids.astype(BF).reshape(4, 128), ((0, 12), (0, 0)))
    own_k = lax.dynamic_slice(keys, (j * 128, g * 128), (128, 128))
    own_v = lax.dynamic_slice(values, (j * 128, g * 128), (128, 128))
    kv = spread(jnp.concatenate([own_k, own_v, doc_rows], axis=0), ("z",))
    q_own = lax.all_gather(queries, GROUP, axis=0, tiled=True)
    q_other = lax.ppermute(jnp.concatenate([q_own, doc_rows], axis=0), "yl", swap)

    weight_g = lax.all_gather(out_weight, GROUP, axis=0)
    hidden_g = lax.all_to_all(hidden.reshape(4, 128, 192), GROUP, 0, 0)
    hidden_t = jnp.transpose(hidden_g, (0, 2, 1)).reshape(768, 128)
    teacher_cols = lax.all_to_all(teacher.reshape(32, 16, 256), HID, 1, 0)
    teacher_t = jnp.transpose(teacher_cols.reshape(2, 2, 128, 256), (1, 0, 3, 2))
    teacher_own = lax.dynamic_index_in_dim(teacher_t, c, 0, keepdims=False)
    teacher_other = lax.dynamic_index_in_dim(teacher_t, 1 - c, 0, keepdims=False)

    docs_z = kv[:, 256:260, :].reshape(16, 512).astype(jnp.int32)
    counts = jnp.sum(docs_z[:, None, :] < jnp.arange(8, dtype=jnp.int32)[None, :, None], axis=2, dtype=jnp.int32)
    q_docs = jnp.concatenate([doc_ids.reshape(4, 128), q_other[2048:2052].astype(jnp.int32)], axis=0)
    scalars = jnp.concatenate([counts.reshape(128), q_docs[:, 0], q_docs[:, 127], jnp.stack([z, yl, j]).astype(jnp.int32)])
    partial = attend(scalars, kv, q_own, q_other, q_docs)
    att_rows = combine(lax.all_to_all(partial, OCTET, 0, 0))

    att_head = lax.all_to_all(att_rows.reshape(4, 128, 128), GROUP, 0, 0)
    attended = jnp.transpose(att_head, (0, 2, 1)).reshape(512, 128)

    att_all = spread(att_rows, HEADSETS).reshape(2048, 128)
    mixed = lax.dot_general(weight_g, att_all, (((1,), (0,)), ((), ())), preferred_element_type=F32)
    student = (hidden_t.astype(F32) + mixed.reshape(768, 128)).astype(BF)
    own = spread(student, CHIPS).reshape(2, 3072, 128)
    other = lax.ppermute(own, "c", swap)

    student_t = jnp.concatenate([own[0], own[1], other[0], other[1]], axis=1)
    teacher_all = jnp.concatenate([teacher_own[0], teacher_own[1], teacher_other[0], teacher_other[1]], axis=1)
    projected = lax.dot_general(projector, student_t, (((0,), (0,)), ((), ())), preferred_element_type=F32)
    mismatch = (projected - teacher_all.astype(F32)).astype(BF)
    grad = lax.dot_general(student_t, mismatch, (((1,), (1,)), ((), ())), preferred_element_type=F32)
    grad = grad.reshape(16, 2, 96, 256)
    keep = lax.dynamic_index_in_dim(grad, yl, 1, keepdims=False)
    send = lax.dynamic_index_in_dim(grad, 1 - yl, 1, keepdims=False).astype(BF)
    half = (keep + lax.ppermute(send, "yl", swap).astype(F32)).astype(BF)
    terms = lax.all_to_all(half, "z", 0, 0)
    summed = jnp.sum(terms.astype(F32), axis=0)
    return summed * (16384 ** -0.5), attended


def solution(mesh):
    fine = Mesh(mesh.devices.reshape(16, 2, 2, 2, 2, 2), ("z", "yl", "yh", "xh", "xl", "c"))
    return jax.shard_map(
        on_device,
        mesh=fine,
        in_specs=(
            P(CTX, HID),
            P(CTX, None),
            P(CTX, None),
            P(CTX),
            P(CTX, HID),
            P(None, HID),
            P(None, HID),
            P(CTX + HID, None),
        ),
        out_specs=(P(CTX, HID), P(CTX, HID)),
        check_vma=False,
    )
```

time: 778 us -> 279 us (0.36)
  the two profiles are of different devices: /device:TPU:6 before, /device:TPU:34 now
where the time goes in v1:
time: 279 us; the launch traced here: 278 us
  waiting for transfers between devices  107 us (38%)
  starting transfers between devices  63.6 us (23%)
  blocking collectives  50.9 us (18%)
  local copies, waits for them, and re-layouts  16.9 us (6%)
  between operations  14.2 us (5%)
  matrix products  9.83 us (4%)
  Pallas kernels  9.15 us (3%)
  other arithmetic  6.02 us (2%)
    all_to_all x1, waiting for transfers between devices, on_device(): terms = lax.all_to_all(half, 'z', 0, 0)  38.4 us
    all_to_all x2, waiting for transfers between devices, spread(): lax.all_to_all(jnp.broadcast_to(x[None], (count,) + x.shape), axes, 0, 0)  32.6 us
    all_to_all x1, blocking collectives, spread(): lax.all_to_all(jnp.broadcast_to(x[None], (count,) + x.shape), axes, 0, 0)  25.9 us
    all_to_all x2, starting transfers between devices, spread(): lax.all_to_all(jnp.broadcast_to(x[None], (count,) + x.shape), axes, 0, 0)  20.9 us
    all_to_all x1, starting transfers between devices, on_device(): terms = lax.all_to_all(half, 'z', 0, 0)  19.3 us
    all_to_all x1, blocking collectives, on_device(): att_rows = combine(lax.all_to_all(partial, OCTET, 0, 0))  18.5 us
    ppermute x1, waiting for transfers between devices, on_device(): half = (keep + lax.ppermute(send, 'yl', swap).astype(F32)).astype(BF)  14.3 us
    ppermute x1, waiting for transfers between devices, on_device(): lax.ppermute(jnp.concatenate([q_own, doc_rows], axis=0), 'yl', swap)  13 us
  transfers between devices with their start and end apart: 10, of which 7 were waited for; matrix products, arithmetic and copies ran while one was open for 6% of the time, Pallas kernels for 3%

profile of v1, /device:TPU:34, one launch (start us, length us, event | category | flops | bytes accessed | tf_op | source)
XLA Modules:
  0.0 277.5 jit_solution(5145870534441147647)
XLA Ops:
  7.2 0.8 convert_bitcast_fusion
  9.6 1.1 broadcast_in_dim.6
  10.7 15.2 %all-to-all-start.1 = ((bf16[16,272,128]{2,1,0:T(8,128)(2,1)}), bf16[16,272,128]{2,1,0:T(8,128)(2,1)S(1)}, u32[]{:S(2)}, u32[]{:S(2)}) async-start(bf16[16,272,128]{2,1,0:T(8,128)(2,1)} %broadcast_in_dim.6), calls=%async_computation.1 | async-start | bytes 2228224 | tf_op jit(solution)/shard_map/all_to_all | solution.py:140
  26.7 6.5 %all_gather.9.q_own = bf16[2048,128]{1,0:T(8,128)(2,1)S(1)} all-gather(bf16[512,128]{1,0:T(8,128)(2,1)S(1)} %copy-done.5), channel_id=1, replica_groups=mesh['z'=16,'yl'=2,'yh'=2,'xh'=2,'xl'=2,'c'=2] {'xl','c'}, dimensions={0}, use_global_device_ids=true | all-gather | bytes 655360 | tf_op jit(solution)/shard_map/all_gather | solution.py:153
  33.2 0.8 pad_maximum_fusion.3
  34.0 3.5 %collective-permute-start = (bf16[2064,128]{1,0:T(8,128)(2,1)}, bf16[2064,128]{1,0:T(8,128)(2,1)}, u32[]{:S(2)}, u32[]{:S(2)}) collective-permute-start(bf16[2064,128]{1,0:T(8,128)(2,1)} %pad_maximum_fusion.3), channel_id=1, source_target_pairs={{0,16},{16,0},{1,17},{17,1},{2,18},{18,2},{3,19},{19,3},{4,20},{20... | collective-permute-start | bytes 1585160 | tf_op jit(solution)/shard_map/ppermute | solution.py:154
  37.5 13.0 %collective-permute-done.q_other = bf16[2064,128]{1,0:T(8,128)(2,1)} collective-permute-done((bf16[2064,128]{1,0:T(8,128)(2,1)}, bf16[2064,128]{1,0:T(8,128)(2,1)}, u32[]{:S(2)}, u32[]{:S(2)}) %collective-permute-start) | collective-permute-done | bytes 528416 | tf_op jit(solution)/shard_map/ppermute | solution.py:154
  51.4 26.7 %all-to-all-done.1.kv = bf16[16,272,128]{2,1,0:T(8,128)(2,1)S(1)} async-done(((bf16[16,272,128]{2,1,0:T(8,128)(2,1)}), bf16[16,272,128]{2,1,0:T(8,128)(2,1)S(1)}, u32[]{:S(2)}, u32[]{:S(2)}) %all-to-all-start.1) | async-done | bytes 1114144 | tf_op jit(solution)/shard_map/all_to_all | solution.py:140
  78.7 8.3 %shard_map.95 = bf16[8,528,128]{2,1,0:T(8,128)(2,1)S(1)} custom-call(s32[147]{0:T(256)S(1)} %concatenate.21.sc, bf16[16,272,128]{2,1,0:T(8,128)(2,1)S(1)} %all-to-all-done.1.kv, bf16[2048,128]{1,0:T(8,128)(2,1)S(1)} %all_gather.9.q_own, bf16[2064,128]{1,0:T(8,128)(2,1)} %collective-permute-done.q_other, s32[8,128]{1,0:T(8,128)S(1)} %pad_add_fusion.qdoc), custom_call_target="tpu_custom_call" | custom-call | tf_op jit(solution)/shard_map/pallas_call | solution.py:116
  86.9 18.5 %all_to_all.50.parts = bf16[8,528,128]{2,1,0:T(8,128)(2,1)S(1)} all-to-all(bf16[8,528,128]{2,1,0:T(8,128)(2,1)S(1)} %shard_map.95), channel_id=1, replica_groups=mesh['z'=16,'yl'=2,'yh'=2,'xh'=2,'xl'=2,'c'=2] {'yl','xl','c'}, dimensions={0} | all-to-all | bytes 2162688 | tf_op jit(solution)/shard_map/all_to_all | solution.py:169
  105.4 0.9 shard_map.96
  106.3 1.8 broadcast_in_dim.7
  108.1 5.7 %all-to-all-start.3 = ((bf16[4,512,128]{2,1,0:T(8,128)(2,1)}), bf16[4,512,128]{2,1,0:T(8,128)(2,1)S(1)}, u32[]{:S(2)}, u32[]{:S(2)}) async-start(bf16[4,512,128]{2,1,0:T(8,128)(2,1)} %broadcast_in_dim.7), calls=%async_computation.3 | async-start | bytes 1048576 | tf_op jit(solution)/shard_map/all_to_all | solution.py:140
  114.6 4.0 %copy.43 = bf16[24,4,8,2048]{3,2,0,1:T(8,128)(2,1)} copy(bf16[24,4,8,2048]{3,2,1,0:T(8,128)(2,1)} %bitcast.85) | data formatting | bytes 6291456 | tf_op jit(solution)/shard_map/all_gather | solution.py:156
  118.6 5.8 %all-to-all-done.3 = bf16[4,512,128]{2,1,0:T(8,128)(2,1)S(1)} async-done(((bf16[4,512,128]{2,1,0:T(8,128)(2,1)}), bf16[4,512,128]{2,1,0:T(8,128)(2,1)S(1)}, u32[]{:S(2)}, u32[]{:S(2)}) %all-to-all-start.3) | async-done | bytes 524320 | tf_op jit(solution)/shard_map/all_to_all | solution.py:140
  124.4 5.4 %all-to-all-start = ((bf16[4,128,192]{1,2,0:T(8,128)(2,1)}), bf16[4,128,192]{1,2,0:T(8,128)(2,1)S(1)}, u32[]{:S(2)}, u32[]{:S(2)}) async-start(bf16[4,128,192]{1,2,0:T(8,128)(2,1)} %copy_bitcast_fusion.1), calls=%async_computation | async-start | bytes 393216 | tf_op jit(solution)/shard_map/all_to_all | solution.py:157
  129.8 2.9 %fusion.17 = f32[128,768]{0,1:S(1)} fusion(bf16[2048,768]{0,1:T(8,128)(2,1)} %bitcast.83, bf16[2048,128]{1,0:T(8,128)(2,1)S(1)} %bitcast.87), kind=kOutput, calls=%fused_computation.44 | convolution fusion | flops 402653184 | bytes 4063232
  132.6 0.8 all-to-all-done
  133.7 25.9 %all_to_all.51 = bf16[8,768,128]{2,1,0:T(8,128)(2,1)S(1)} all-to-all(bf16[8,768,128]{2,1,0:T(8,128)(2,1)S(1)} %broadcast_in_dim.8), channel_id=1, replica_groups=mesh['z'=16,'yl'=2,'yh'=2,'xh'=2,'xl'=2,'c'=2] {'xl','yh','xh'}, dimensions={0} | all-to-all | bytes 3145728 | tf_op jit(solution)/shard_map/all_to_all | solution.py:140
  159.6 1.9 collective-permute-start.1
  162.4 4.8 %all-to-all-start.5 = ((bf16[1,32,16,256]{3,1,0,2:T(8,128)(2,1)}), bf16[1,32,16,256]{3,1,0,2:T(8,128)(2,1)S(1)}, u32[]{:S(2)}, u32[]{:S(2)}) async-start(bf16[1,32,16,256]{3,1,0,2:T(8,128)(2,1)} %copy.30), calls=%async_computation.5 | async-start | bytes 524288 | tf_op jit(solution)/shard_map/all_to_all | solution.py:159
  167.2 7.0 %all-to-all-done.5 = bf16[1,32,16,256]{3,1,0,2:T(8,128)(2,1)S(1)} async-done(((bf16[1,32,16,256]{3,1,0,2:T(8,128)(2,1)}), bf16[1,32,16,256]{3,1,0,2:T(8,128)(2,1)S(1)}, u32[]{:S(2)}, u32[]{:S(2)}) %all-to-all-start.5) | async-done | bytes 262176 | tf_op jit(solution)/shard_map/all_to_all | solution.py:159
  174.3 1.3 fusion.16
  175.6 2.8 slice_bitcast_fusion.1
  178.3 7.0 %fusion.3 = f32[3072,256]{1,0:T(8,128)} fusion(bf16[3072,256]{1,0:T(8,128)(2,1)S(1)} %copy-done, bf16[3072,128]{1,0:T(8,128)(2,1)} %get-tuple-element.7, bf16[3072,128]{1,0:T(8,128)(2,1)} %get-tuple-element.6, bf16[3072,128]{1,0:T(8,128)(2,1)S(1)} %bitcast.94, bf16[3072,128]{1,0:T(8,128)(2,1)S(1)} %bitcast.93, bf16[256,128]{0,1:T(8,128)(2,1)S(1)} %get-tuple-element.13, ...), kind=kOutput, calls=%fused_computation.9 | convolution fusion | flops 1637089280 | bytes 8126464 | tf_op jit(solution)/shard_map/dot_general | solution.py:184
  185.3 1.5 fusion.4
  186.8 1.9 collective-permute-start.2
  188.7 5.8 %all-to-all-start.7 = ((bf16[4,128,128]{2,1,0:T(8,128)(2,1)}), bf16[4,128,128]{2,1,0:T(8,128)(2,1)S(1)}, u32[]{:S(2)}, u32[]{:S(2)}) async-start(bf16[4,128,128]{2,1,0:T(8,128)(2,1)} %bitcast.32), calls=%async_computation.7 | async-start | bytes 262144 | tf_op jit(solution)/shard_map/all_to_all | solution.py:171
  194.6 14.3 %collective-permute-done.2 = bf16[16,96,256]{2,1,0:T(8,128)(2,1)S(1)} collective-permute-done((bf16[16,96,256]{2,1,0:T(8,128)(2,1)S(1)}, bf16[16,96,256]{2,1,0:T(8,128)(2,1)S(1)}, u32[]{:S(2)}, u32[]{:S(2)}) %collective-permute-start.2) | collective-permute-done | bytes 786464 | tf_op jit(solution)/shard_map/ppermute | solution.py:188
  208.9 2.5 fusion
  211.4 19.3 %all-to-all-start.6 = ((bf16[16,96,256]{2,1,0:T(8,128)(2,1)}), bf16[16,96,256]{2,1,0:T(8,128)(2,1)S(1)}, u32[]{:S(2)}, u32[]{:S(2)}) async-start(bf16[16,96,256]{2,1,0:T(8,128)(2,1)} %fusion), calls=%async_computation.6 | async-start | bytes 1572864 | tf_op jit(solution)/shard_map/all_to_all | solution.py:189
  231.5 38.4 %all-to-all-done.6 = bf16[16,96,256]{2,1,0:T(8,128)(2,1)S(1)} async-done(((bf16[16,96,256]{2,1,0:T(8,128)(2,1)}), bf16[16,96,256]{2,1,0:T(8,128)(2,1)S(1)}, u32[]{:S(2)}, u32[]{:S(2)}) %all-to-all-start.6) | async-done | bytes 786464 | tf_op jit(solution)/shard_map/all_to_all | solution.py:189
  (41 shorter events, 7.1 us)
Async XLA Ops:
  7.2 171.2 %copy-start = (bf16[3072,256]{1,0:T(8,128)(2,1)S(1)}, bf16[3072,256]{1,0:T(8,128)(2,1)}, u32[]{:S(2)}) copy-start(bf16[3072,256]{1,0:T(8,128)(2,1)} %param.14) | copy-start | bytes 4718596
  7.2 44.0 %copy-start.6 = (s32[512]{0:T(512)S(1)}, s32[512]{0:T(512)}, u32[]{:S(2)}) copy-start(s32[512]{0:T(512)} %param.11) | copy-start | bytes 6148
  7.2 19.5 %copy-start.5 = (bf16[512,128]{1,0:T(8,128)(2,1)S(1)}, bf16[512,128]{1,0:T(8,128)(2,1)}, u32[]{:S(2)}) copy-start(bf16[512,128]{1,0:T(8,128)(2,1)} %param.8) | copy-start | bytes 393220
  10.7 67.4 %all-to-all-start.1 = ((bf16[16,272,128]{2,1,0:T(8,128)(2,1)}), bf16[16,272,128]{2,1,0:T(8,128)(2,1)S(1)}, u32[]{:S(2)}, u32[]{:S(2)}) async-start(bf16[16,272,128]{2,1,0:T(8,128)(2,1)} %broadcast_in_dim.6), calls=%async_computation.1 | async-start | bytes 2228224 | tf_op jit(solution)/shard_map/all_to_all | solution.py:140
  25.9 88.6 %all-gather.3.cloned.1.call-start = ((), (), s32[]{:S(2)}) async-start(), calls=%async_computation.8 | async-start | bytes 3932160 | tf_op jit(solution)/shard_map/all_gather | solution.py:156
  34.0 16.5 %collective-permute-start = (bf16[2064,128]{1,0:T(8,128)(2,1)}, bf16[2064,128]{1,0:T(8,128)(2,1)}, u32[]{:S(2)}, u32[]{:S(2)}) collective-permute-start(bf16[2064,128]{1,0:T(8,128)(2,1)} %pad_maximum_fusion.3), channel_id=1, source_target_pairs={{0,16},{16,0},{1,17},{17,1},{2,18},{18,2},{3,19},{19,3},{4,20},{20... | collective-permute-start | bytes 1585160 | tf_op jit(solution)/shard_map/ppermute | solution.py:154
  86.9 26.9 %copy-start.4 = (bf16[512,192]{0,1:T(8,128)(2,1)S(1)}, bf16[512,192]{0,1:T(8,128)(2,1)}, u32[]{:S(2)}) copy-start(bf16[512,192]{0,1:T(8,128)(2,1)} %param.12) | copy-start | bytes 589828
  108.1 16.3 %all-to-all-start.3 = ((bf16[4,512,128]{2,1,0:T(8,128)(2,1)}), bf16[4,512,128]{2,1,0:T(8,128)(2,1)S(1)}, u32[]{:S(2)}, u32[]{:S(2)}) async-start(bf16[4,512,128]{2,1,0:T(8,128)(2,1)} %broadcast_in_dim.7), calls=%async_computation.3 | async-start | bytes 1048576 | tf_op jit(solution)/shard_map/all_to_all | solution.py:140
  124.4 9.0 %all-to-all-start = ((bf16[4,128,192]{1,2,0:T(8,128)(2,1)}), bf16[4,128,192]{1,2,0:T(8,128)(2,1)S(1)}, u32[]{:S(2)}, u32[]{:S(2)}) async-start(bf16[4,128,192]{1,2,0:T(8,128)(2,1)} %copy_bitcast_fusion.1), calls=%async_computation | async-start | bytes 393216 | tf_op jit(solution)/shard_map/all_to_all | solution.py:157
  132.6 28.9 %copy-start.3 = (bf16[32,4096]{1,0:T(8,128)(2,1)S(1)}, bf16[32,4096]{1,0:T(8,128)(2,1)}, u32[]{:S(2)}) copy-start(bf16[32,4096]{1,0:T(8,128)(2,1)} %param.15) | copy-start | bytes 786436
  159.6 15.9 %collective-permute-start.1 = (bf16[2,3072,128]{2,1,0:T(8,128)(2,1)S(1)}, bf16[2,3072,128]{2,1,0:T(8,128)(2,1)}, u32[]{:S(2)}, u32[]{:S(2)}) collective-permute-start(bf16[2,3072,128]{2,1,0:T(8,128)(2,1)S(1)} %bitcast.84), channel_id=1, source_target_pairs={{0,1},{1,0},{2,3},{3,2},{4,5},{5,4},{6,7},{7,6},{8,9},{9,8},{10,11... | collective-permute-start | bytes 4718600 | tf_op jit(solution)/shard_map/ppermute | solution.py:178
  162.4 11.9 %all-to-all-start.5 = ((bf16[1,32,16,256]{3,1,0,2:T(8,128)(2,1)}), bf16[1,32,16,256]{3,1,0,2:T(8,128)(2,1)S(1)}, u32[]{:S(2)}, u32[]{:S(2)}) async-start(bf16[1,32,16,256]{3,1,0,2:T(8,128)(2,1)} %copy.30), calls=%async_computation.5 | async-start | bytes 524288 | tf_op jit(solution)/shard_map/all_to_all | solution.py:159
  175.6 2.8 copy-start.1
  175.6 2.8 copy-start.2
  186.8 22.1 %collective-permute-start.2 = (bf16[16,96,256]{2,1,0:T(8,128)(2,1)S(1)}, bf16[16,96,256]{2,1,0:T(8,128)(2,1)S(1)}, u32[]{:S(2)}, u32[]{:S(2)}) collective-permute-start(bf16[16,96,256]{2,1,0:T(8,128)(2,1)S(1)} %fusion.4), channel_id=1, source_target_pairs={{0,16},{16,0},{1,17},{17,1},{2,18},{18,2},{3,19},{19,3},{4,20},{20... | collective-permute-start | bytes 2359304 | tf_op jit(solution)/shard_map/ppermute | solution.py:188
  188.7 22.7 %all-to-all-start.7 = ((bf16[4,128,128]{2,1,0:T(8,128)(2,1)}), bf16[4,128,128]{2,1,0:T(8,128)(2,1)S(1)}, u32[]{:S(2)}, u32[]{:S(2)}) async-start(bf16[4,128,128]{2,1,0:T(8,128)(2,1)} %bitcast.32), calls=%async_computation.7 | async-start | bytes 262144 | tf_op jit(solution)/shard_map/all_to_all | solution.py:171
  211.4 58.5 %all-to-all-start.6 = ((bf16[16,96,256]{2,1,0:T(8,128)(2,1)}), bf16[16,96,256]{2,1,0:T(8,128)(2,1)S(1)}, u32[]{:S(2)}, u32[]{:S(2)}) async-start(bf16[16,96,256]{2,1,0:T(8,128)(2,1)} %fusion), calls=%async_computation.6 | async-start | bytes 1572864 | tf_op jit(solution)/shard_map/all_to_all | solution.py:189
Sparse Core Ops, SparseCore 0:
  28.9 45.1 all-gather.2

commit v2 on v1

v2 whole, which is shorter than its diff:
```python
import functools

import jax
import jax.numpy as jnp
from jax import lax
from jax.experimental import pallas as pl
from jax.experimental.pallas import tpu as pltpu
from jax.sharding import Mesh
from jax.sharding import PartitionSpec as P

HEAD = 128
SCALE2 = HEAD ** -0.5 * 1.4426950408889634
EMPTY = -1e30
MASKED = -2e30
BF = jnp.bfloat16
F32 = jnp.float32
CTX = ("zh", "zl", "yl")
HID = ("yh", "xh", "xl", "c")
GROUP = ("xl", "c")
OCTET = ("yl", "xl", "c")
HEADSETS = ("yh", "xh")
CHIPS = ("xl", "yh", "xh")
BLOCKS = 4


def pack_kernel(place, keys, values, docs, out):
    rows = jnp.concatenate([docs[...].astype(F32), jnp.zeros((12, 128), F32)], axis=0).astype(BF)
    for copy in range(out.shape[0]):
        out[copy, 0:128, :] = keys[...]
        out[copy, 128:256, :] = values[...]
        out[copy, 256:272, :] = rows


def attend_kernel(sc, kv0, kv1, kv2, kv3, q_own, q_other, qdoc, early1, early2, early3, out, v_turned):
    z, yl, j = sc[144], sc[145], sc[146]
    pieces = (kv0, kv1, kv2, kv3)
    place = [(z + shift) % 4 for shift in (0, 3, 1, 2)]
    for ch in range(4):
        for i in range(BLOCKS):
            v_turned[:, (ch * BLOCKS + i) * 128:(ch * BLOCKS + i + 1) * 128] = pieces[i][ch, 128:256, :].T
    key_iota = lax.broadcasted_iota(jnp.int32, (128, 512), 0)
    row_iota = lax.broadcasted_iota(jnp.int32, (1, 512), 1) % 128
    for side, q_ref in ((0, q_own), (1, q_other)):
        yl_q = yl if side == 0 else 1 - yl
        block_q = 2 * z + yl_q

        def one_tile(rc, carry, side=side, q_ref=q_ref, yl_q=yl_q, block_q=block_q):
            row0 = pl.multiple_of(rc * 128, 128)
            q = jnp.concatenate([q_ref[pl.ds(pl.multiple_of((h ^ j) * 512, 512) + row0, 128), :] for h in range(4)], axis=0)
            docs = qdoc[pl.ds(side * 4 + rc, 1), :]
            docs = jnp.concatenate([docs] * 4, axis=1)
            first, last = sc[128 + side * 4 + rc], sc[136 + side * 4 + rc]
            q_min = block_q * 512 + row0
            q_pos = q_min + row_iota

            def step(ch, state, masked):
                run_max, run_sum, acc = state
                keys = jnp.concatenate([piece[ch, 0:128, :] for piece in pieces], axis=0)
                s = lax.dot_general(keys, q, (((1,), (1,)), ((), ())), preferred_element_type=F32) * SCALE2
                if masked:
                    parts = []
                    for i in range(BLOCKS):
                        low = jnp.zeros((1, 512), jnp.int32)
                        for d in range(8):
                            low = jnp.where(docs == d, sc[i * 32 + ch * 8 + d], low)
                        low = low - j * 128
                        high = q_pos - ((2 * (ch * 4 + place[i]) + yl) * 512 + j * 128)
                        ok = (key_iota >= low) & (key_iota <= high)
                        parts.append(jnp.where(ok, s[i * 128:(i + 1) * 128], MASKED))
                    s = jnp.concatenate(parts, axis=0)
                new_max = jnp.maximum(run_max, jnp.max(s, axis=0, keepdims=True))
                factor = jnp.exp2(run_max - new_max)
                w = jnp.exp2(s - new_max)
                new_sum = run_sum * factor + jnp.sum(w, axis=0, keepdims=True)
                cols = pl.ds(pl.multiple_of(ch * (BLOCKS * 128), BLOCKS * 128), BLOCKS * 128)
                new_acc = acc * factor + jnp.dot(v_turned[:, cols], w.astype(BF), preferred_element_type=F32)
                return new_max, new_sum, new_acc

            def any_step(ch, state):
                most = functools.reduce(jnp.maximum, [sc[i * 32 + ch * 8 + last] for i in range(BLOCKS)])
                k_max = (2 * (ch * BLOCKS + BLOCKS - 1) + yl) * 512 + j * 128 + 127
                full = (k_max <= q_min) & (most <= j * 128)
                return lax.cond(full, functools.partial(step, ch, masked=False), functools.partial(step, ch, masked=True), state)

            begin = jnp.int32(0)
            for ch in range(4):
                fewest = functools.reduce(jnp.minimum, [sc[i * 32 + ch * 8 + first] for i in range(BLOCKS)])
                begin = begin + (fewest >= (j + 1) * 128).astype(jnp.int32)
            end = z // BLOCKS + 1
            state = (jnp.full((1, 512), EMPTY, F32), jnp.zeros((1, 512), F32), jnp.zeros((128, 512), F32))
            run_max, run_sum, acc = lax.fori_loop(begin, end, any_step, state)
            seen = run_sum > 0
            o = (acc * (1.0 / jnp.where(seen, run_sum, 1.0))).astype(BF)
            lse = jnp.where(seen, run_max + jnp.log2(jnp.where(seen, run_sum, 1.0)), EMPTY)
            hi = lse.astype(BF).astype(F32)
            mid = (lse - hi).astype(BF).astype(F32)
            lo = lse - hi - mid
            dest = yl_q * 4 + rc
            rows = [part[:, h * 128:(h + 1) * 128] for part in (hi, mid, lo) for h in range(4)]
            rows.append(jnp.zeros((4, 128), F32))
            for h in range(4):
                out[dest, h * 128:(h + 1) * 128, :] = o[:, h * 128:(h + 1) * 128]
            out[dest, 512:528, :] = jnp.concatenate(rows, axis=0).astype(BF)
            return carry

        lax.fori_loop(0, 4, one_tile, 0)


def combine_kernel(parts, out, copies):
    count = parts.shape[0]
    tails = [parts[s, 512:528, :].astype(F32) for s in range(count)]
    for h in range(4):
        lses = [t[h:h + 1] + t[4 + h:5 + h] + t[8 + h:9 + h] for t in tails]
        top = functools.reduce(jnp.maximum, lses)
        weights = [jnp.exp2(v - top) for v in lses]
        inverse = 1.0 / sum(weights)
        rows = slice(h * 128, (h + 1) * 128)
        total = sum(w * inverse * parts[s, rows, :].astype(F32) for s, w in enumerate(weights)).astype(BF)
        out[rows, :] = total
        for copy in range(copies.shape[0]):
            copies[copy, rows, :] = total


def student_kernel(weight_t, att, hidden_t, out):
    att_all = att[...].reshape(2048, 128)
    for part in range(4):
        rows = slice(part * 192, (part + 1) * 192)
        mixed = jnp.dot(weight_t[rows, :], att_all, preferred_element_type=F32)
        student = (hidden_t[rows, :].astype(F32) + mixed).astype(BF)
        for copy in range(out.shape[0]):
            out[copy, rows, :] = student


def mismatch_of(student, projector_t, teacher_t, core):
    both = jnp.concatenate([student[0], student[1]], axis=1)
    projected = jnp.dot(projector_t[...], both, preferred_element_type=F32)
    taught = [teacher_t[:, pl.ds(pl.multiple_of((xl * 2 + core) * 128, 128), 128)] for xl in range(2)]
    return (projected - jnp.concatenate(taught, axis=1).astype(F32)).astype(BF)


def gradient_rows(own, other, turned, half, out):
    def one(zl, carry):
        rows = []
        for zh in range(4):
            start = pl.multiple_of((zh * 4 + zl) * 192 + half * 96, 32)
            rows.append(jnp.concatenate([ref[xl, pl.ds(start, 96), :] for ref in (own, other) for xl in range(2)], axis=1))
        grad = jnp.dot(jnp.concatenate(rows, axis=0), turned[...], preferred_element_type=F32)
        for zh in range(4):
            out[zl, zh] = grad[zh * 96:(zh + 1) * 96].astype(out.dtype)
        return carry

    lax.fori_loop(0, 4, one, 0)


def own_mismatch_kernel(place, own, projector_t, teacher_t, out):
    out[...] = mismatch_of(own, projector_t, teacher_t, place[0]).T


def sent_kernel(place, own, other, projector_t, teacher_t, own_mismatch, mismatch, out):
    mismatch[0:256, :] = own_mismatch[...]
    mismatch[256:512, :] = mismatch_of(other, projector_t, teacher_t, 1 - place[0]).T
    gradient_rows(own, other, mismatch, 1 - place[1], out)


def kept_kernel(place, own, other, mismatch, out):
    gradient_rows(own, other, mismatch, place[1], out)


VMEM = pl.BlockSpec(memory_space=pltpu.VMEM)
SMEM = pl.BlockSpec(memory_space=pltpu.SMEM)
ANY = pl.BlockSpec(memory_space=pl.ANY)


def call(kernel, out_shape, specs, operands, limit, flops=0, scratch=()):
    single = not isinstance(out_shape, list)
    return pl.pallas_call(
        kernel,
        out_shape=out_shape,
        in_specs=specs,
        out_specs=VMEM if single else [VMEM] * len(out_shape),
        scratch_shapes=list(scratch),
        compiler_params=pltpu.CompilerParams(vmem_limit_bytes=limit * 1024 * 1024),
        cost_estimate=pl.CostEstimate(flops=flops, bytes_accessed=4 * 1024 * 1024, transcendentals=0),
    )(*operands)


def shape(*dims, dtype=BF):
    return jax.ShapeDtypeStruct(dims, dtype)


def pack(place, keys, values, docs):
    return pl.pallas_call(
        pack_kernel,
        grid_spec=pltpu.PrefetchScalarGridSpec(
            num_scalar_prefetch=1,
            grid=(1,),
            in_specs=[
                pl.BlockSpec((128, 128), lambda i, place: (place[0], place[1])),
                pl.BlockSpec((128, 128), lambda i, place: (place[0], place[1])),
                pl.BlockSpec((4, 128), lambda i, place: (0, 0)),
            ],
            out_specs=pl.BlockSpec((4, 272, 128), lambda i, place: (0, 0, 0)),
        ),
        out_shape=shape(4, 272, 128),
    )(place, keys, values, docs)


def on_device(queries, keys, values, doc_ids, hidden, out_weight, projector, teacher):
    zl, yl, c = lax.axis_index("zl"), lax.axis_index("yl"), lax.axis_index("c")
    z = lax.axis_index("zh") * 4 + zl
    g = lax.axis_index("yh") * 2 + lax.axis_index("xh")
    j = lax.axis_index("xl") * 2 + c
    swap = [(0, 1), (1, 0)]

    def from_z(x, shift):
        return lax.ppermute(x, ("zh", "zl"), [((i + shift) % 16, i) for i in range(16)])

    docs = doc_ids.reshape(4, 128)
    packed = pack(jnp.stack([j, g]).astype(jnp.int32), keys, values, docs)
    kv_own = lax.all_to_all(packed, "zh", 0, 0)
    kv_below, kv_above = from_z(kv_own, -1), from_z(kv_own, 1)
    kv_far = jnp.concatenate([from_z(kv_own[0:2], -2), from_z(kv_own[2:4], 2)], axis=0)

    doc_rows = jnp.pad(docs.astype(BF), ((0, 12), (0, 0)))
    q_two = jnp.concatenate([queries, lax.ppermute(queries, "c", swap)], axis=0)
    q_own = jnp.concatenate([q_two, lax.ppermute(q_two, "xl", swap), doc_rows], axis=0)
    q_other = lax.ppermute(q_own, "yl", swap)

    weight_t = lax.all_gather(out_weight.T, GROUP, axis=0, tiled=True)
    hidden_t = jnp.transpose(hidden.T.reshape(192, 4, 128), (1, 0, 2))
    hidden_t = lax.all_to_all(hidden_t, GROUP, 0, 0).reshape(768, 128)
    teacher_cols = jnp.transpose(teacher.reshape(32, 16, 256), (1, 0, 2))
    teacher_t = lax.all_to_all(teacher_cols, HID, 0, 0).reshape(512, 256).T
    projector_t = projector.T

    pieces = (kv_own, kv_below, kv_above, kv_far)
    docs_z = jnp.stack([piece[:, 256:260, :].reshape(4, 512) for piece in pieces]).astype(jnp.int32)
    counts = jnp.sum(docs_z[:, :, None, :] < jnp.arange(8, dtype=jnp.int32)[None, None, :, None], axis=3, dtype=jnp.int32)
    q_docs = jnp.concatenate([docs, q_other[2048:2052].astype(jnp.int32)], axis=0)
    scalars = jnp.concatenate([counts.reshape(128), q_docs[:, 0], q_docs[:, 127], jnp.stack([z, yl, j]).astype(jnp.int32)])
    partial = call(
        attend_kernel,
        shape(8, 528, 128),
        [SMEM] + [VMEM] * 7 + [ANY] * 3,
        (scalars, *pieces, q_own, q_other, q_docs, hidden_t, teacher_t, projector_t),
        40,
        scratch=[pltpu.VMEM((128, 2048), BF)],
    )
    att_rows, att_copies = call(
        combine_kernel, [shape(512, 128), shape(4, 512, 128)], [VMEM], (lax.all_to_all(partial, OCTET, 0, 0),), 16
    )

    att_head = lax.all_to_all(att_rows.reshape(4, 128, 128), GROUP, 0, 0)
    attended = jnp.transpose(att_head, (0, 2, 1)).reshape(512, 128)

    att_all = lax.all_to_all(att_copies, HEADSETS, 0, 0)
    student = call(student_kernel, shape(8, 768, 128), [VMEM] * 3, (weight_t, att_all, hidden_t), 24)
    own = lax.all_to_all(student, CHIPS, 0, 0).reshape(2, 3072, 128)
    other = lax.ppermute(own, "c", swap)

    place = jnp.stack([c, yl]).astype(jnp.int32)
    own_mismatch = call(own_mismatch_kernel, shape(256, 256), [SMEM] + [VMEM] * 3, (place, own, projector_t, teacher_t), 24, 4 * 10 ** 8)
    mismatch, sent = call(
        sent_kernel,
        [shape(512, 256), shape(4, 4, 96, 256)],
        [SMEM] + [VMEM] * 5,
        (place, own, other, projector_t, teacher_t, own_mismatch),
        32,
        8 * 10 ** 8,
    )
    received = lax.ppermute(sent, "yl", swap)
    kept = call(kept_kernel, shape(4, 4, 96, 256, dtype=F32), [SMEM] + [VMEM] * 3, (place, own, other, mismatch), 32, 4 * 10 ** 8)
    half = (kept + received.astype(F32)).astype(BF)
    near = jnp.sum(lax.all_to_all(half, "zl", 0, 0).astype(F32), axis=0).astype(BF)
    summed = jnp.sum(lax.all_to_all(near, "zh", 0, 0).astype(F32), axis=0)
    return summed * (16384 ** -0.5), attended


def solution(mesh):
    fine = Mesh(mesh.devices.reshape(4, 4, 2, 2, 2, 2, 2), ("zh", "zl", "yl", "yh", "xh", "xl", "c"))
    return jax.shard_map(
        on_device,
        mesh=fine,
        in_specs=(
            P(CTX, HID),
            P(CTX, None),
            P(CTX, None),
            P(CTX),
            P(CTX, HID),
            P(None, HID),
            P(None, HID),
            P(CTX + HID, None),
        ),
        out_specs=(P(CTX, HID), P(CTX, HID)),
        check_vma=False,
    )
```

time: 279 us -> 266 us (0.953)
  the two profiles are of different devices: /device:TPU:34 before, /device:TPU:32 now
where the time goes in v2:
time: 266 us; the launch traced here: 265 us
  blocking collectives  81.7 us (31%)
  starting transfers between devices  72.6 us (27%)
  waiting for transfers between devices  64.2 us (24%)
  Pallas kernels  17.6 us (7%)
  between operations  14.4 us (5%)
  local copies, waits for them, and re-layouts  10.7 us (4%)
  other arithmetic  3.49 us (1%)
    all_to_all x1, blocking collectives, on_device(): own = lax.all_to_all(student, CHIPS, 0, 0).reshape(2, 3072, 128)  24 us
    all_to_all x1, blocking collectives, on_device(): lax.all_to_all(half, 'zl', 0, 0).astype(F32)  23.4 us
    all_to_all x1, starting transfers between devices, on_device(): summed = jnp.sum(lax.all_to_all(near, 'zh', 0, 0).astype(F32), axis=0)  18.6 us
    all_to_all x1, blocking collectives, on_device(): lax.all_to_all(partial, OCTET, 0, 0)  18.6 us
    ppermute x1, waiting for transfers between devices, on_device(): received = lax.ppermute(sent, 'yl', swap)  18 us
    all_to_all x1, waiting for transfers between devices, on_device(): summed = jnp.sum(lax.all_to_all(near, 'zh', 0, 0).astype(F32), axis=0)  17.7 us
    all_to_all x1, waiting for transfers between devices, on_device(): kv_own = lax.all_to_all(packed, 'zh', 0, 0)  16.1 us
    all_to_all x1, blocking collectives, on_device(): att_all = lax.all_to_all(att_copies, HEADSETS, 0, 0)  15.8 us
  transfers between devices with their start and end apart: 15, of which 8 were waited for; matrix products, arithmetic and copies ran while one was open for 4% of the time, Pallas kernels for 5%

profile of v2, /device:TPU:32, one launch (start us, length us, event | category | flops | bytes accessed | tf_op | source)
XLA Modules:
  0.0 264.7 jit_solution(18300538925686924844)
XLA Ops:
  7.9 1.9 collective-permute-start.4
  11.6 7.1 %all-to-all-start.2 = ((bf16[16,32,256]{2,1,0:T(8,128)(2,1)}), bf16[16,32,256]{2,1,0:T(8,128)(2,1)S(1)}, u32[]{:S(2)}, u32[]{:S(2)}) async-start(bf16[16,32,256]{2,1,0:T(8,128)(2,1)} %copy.29), calls=%async_computation.2 | async-start | bytes 524288 | tf_op jit(solution)/shard_map/all_to_all | solution.py:233
  18.9 3.8 %collective-permute-start.5 = (bf16[1024,128]{1,0:T(8,128)(2,1)S(1)}, bf16[1024,128]{1,0:T(8,128)(2,1)S(1)}, u32[]{:S(2)}, u32[]{:S(2)}) collective-permute-start(bf16[1024,128]{1,0:T(8,128)(2,1)S(1)} %pad_maximum_fusion), channel_id=1, source_target_pairs={{0,2},{2,0},{1,3},{3,1},{4,6},{6,4},{5,7},{7,5},{8,10},{10,8},{9,1... | collective-permute-start | bytes 786440 | tf_op jit(solution)/shard_map/ppermute | solution.py:226
  23.3 2.2 shard_map.95
  25.4 2.7 %all-to-all-done.2 = bf16[16,32,256]{2,1,0:T(8,128)(2,1)S(1)} async-done(((bf16[16,32,256]{2,1,0:T(8,128)(2,1)}), bf16[16,32,256]{2,1,0:T(8,128)(2,1)S(1)}, u32[]{:S(2)}, u32[]{:S(2)}) %all-to-all-start.2) | async-done | bytes 262176 | tf_op jit(solution)/shard_map/all_to_all | solution.py:233
  28.2 14.2 %all-to-all-start = ((bf16[4,272,128]{2,1,0:T(8,128)(2,1)}), bf16[4,272,128]{2,1,0:T(8,128)(2,1)S(1)}, u32[]{:S(2)}, u32[]{:S(2)}) async-start(bf16[4,272,128]{2,1,0:T(8,128)(2,1)} %shard_map.95), calls=%async_computation | async-start | bytes 557056 | tf_op jit(solution)/shard_map/all_to_all | solution.py:220
  42.4 2.6 collective-permute-start.6
  45.0 1.7 copy.31
  47.6 16.1 %all-to-all-done.kv0 = bf16[4,272,128]{2,1,0:T(8,128)(2,1)S(1)} async-done(((bf16[4,272,128]{2,1,0:T(8,128)(2,1)}), bf16[4,272,128]{2,1,0:T(8,128)(2,1)S(1)}, u32[]{:S(2)}, u32[]{:S(2)}) %all-to-all-start) | async-done | bytes 278560 | tf_op jit(solution)/shard_map/all_to_all | solution.py:220
  63.8 3.4 %all-to-all-start.1 = ((bf16[4,192,128]{2,1,0:T(8,128)(2,1)}), bf16[4,192,128]{2,1,0:T(8,128)(2,1)S(1)}, u32[]{:S(2)}, u32[]{:S(2)}) async-start(bf16[4,192,128]{2,1,0:T(8,128)(2,1)} %bitcast_bitcast_fusion), calls=%async_computation.1 | async-start | bytes 393216 | tf_op jit(solution)/shard_map/all_to_all | solution.py:231
  67.2 1.9 collective-permute-start.2
  69.1 6.0 %collective-permute-start.3 = (bf16[2,272,128]{2,1,0:T(8,128)(2,1)S(1)}, bf16[2,272,128]{2,1,0:T(8,128)(2,1)}, u32[]{:S(2)}, u32[]{:S(2)}) collective-permute-start(bf16[2,272,128]{2,1,0:T(8,128)(2,1)S(1)} %get-tuple-element.12), channel_id=1, source_target_pairs={{64,0},{96,32},{128,64},{160,96},{192,128},{224,160},{256,192},{28... | collective-permute-start | bytes 417800 | tf_op jit(solution)/shard_map/ppermute | solution.py:216
  75.2 1.9 collective-permute-start
  77.1 3.9 %collective-permute-start.1 = (bf16[4,272,128]{2,1,0:T(8,128)(2,1)S(1)}, bf16[4,272,128]{2,1,0:T(8,128)(2,1)}, u32[]{:S(2)}, u32[]{:S(2)}) collective-permute-start(bf16[4,272,128]{2,1,0:T(8,128)(2,1)S(1)} %all-to-all-done.kv0), channel_id=1, source_target_pairs={{32,0},{64,32},{96,64},{128,96},{160,128},{192,160},{224,192},{256... | collective-permute-start | bytes 835592 | tf_op jit(solution)/shard_map/ppermute | solution.py:216
  83.8 1.8 collective-permute-done.kv1
  86.3 1.2 collective-permute-done.1.kv2
  88.8 8.5 %shard_map.96 = bf16[8,528,128]{2,1,0:T(8,128)(2,1)S(1)} custom-call(s32[147]{0:T(256)S(1)} %concatenate.24.sc, bf16[4,272,128]{2,1,0:T(8,128)(2,1)S(1)} %all-to-all-done.kv0, bf16[4,272,128]{2,1,0:T(8,128)(2,1)} %collective-permute-done.kv1, bf16[4,272,128]{2,1,0:T(8,128)(2,1)} %collective-permute-done.1.kv2, ...), custom_call_target="tpu_custom_call" | custom-call | bytes 4194304 | tf_op jit(solution)/shard_map/pallas_call | solution.py:176
  97.4 18.6 %all_to_all.45.parts = bf16[8,528,128]{2,1,0:T(8,128)(2,1)S(1)} all-to-all(bf16[8,528,128]{2,1,0:T(8,128)(2,1)S(1)} %shard_map.96), channel_id=1, replica_groups=mesh['zh'=4,'zl'=4,'yl'=2,'yh'=2,'xh'=2,'xl'=2,'c'=2] {'yl','xl','c'}, dimensions={0} | all-to-all | bytes 2162688 | tf_op jit(solution)/shard_map/all_to_all | solution.py:250
  116.9 15.8 %all_to_all.46.att = bf16[4,512,128]{2,1,0:T(8,128)(2,1)S(1)} all-to-all(bf16[4,512,128]{2,1,0:T(8,128)(2,1)S(1)} %get-tuple-element.6), channel_id=1, replica_groups=mesh['zh'=4,'zl'=4,'yl'=2,'yh'=2,'xh'=2,'xl'=2,'c'=2] {'yh','xh'}, dimensions={0} | all-to-all | bytes 1048576 | tf_op jit(solution)/shard_map/all_to_all | solution.py:256
  132.7 1.9 copy-done.1
  135.5 24.0 %all_to_all.47 = bf16[8,768,128]{2,1,0:T(8,128)(2,1)S(1)} all-to-all(bf16[8,768,128]{2,1,0:T(8,128)(2,1)S(1)} %shard_map.98), channel_id=1, replica_groups=mesh['zh'=4,'zl'=4,'yl'=2,'yh'=2,'xh'=2,'xl'=2,'c'=2] {'xl','yh','xh'}, dimensions={0} | all-to-all | bytes 3145728 | tf_op jit(solution)/shard_map/all_to_all | solution.py:258
  159.5 1.9 collective-permute-start.7
  162.7 2.1 collective-permute-done.7.other
  164.8 2.2 shard_map.100
  167.1 1.9 collective-permute-start.8
  169.0 1.6 shard_map.101
  170.6 18.0 %collective-permute-done.8 = bf16[4,4,96,256]{3,2,1,0:T(8,128)(2,1)S(1)} collective-permute-done((bf16[4,4,96,256]{3,2,1,0:T(8,128)(2,1)S(1)}, bf16[4,4,96,256]{3,2,1,0:T(8,128)(2,1)S(1)}, u32[]{:S(2)}, u32[]{:S(2)}) %collective-permute-start.8) | collective-permute-done | bytes 786464 | tf_op jit(solution)/shard_map/ppermute | solution.py:271
  188.8 23.4 %all_to_all.48 = bf16[4,4,96,256]{3,2,1,0:T(8,128)(2,1)S(1)} all-to-all(bf16[4,4,96,256]{3,2,1,0:T(8,128)(2,1)S(1)} %add_convert_fusion), channel_id=1, replica_groups=mesh['zh'=4,'zl'=4,'yl'=2,'yh'=2,'xh'=2,'xl'=2,'c'=2] {'zl'}, dimensions={0} | all-to-all | bytes 1572864 | tf_op jit(solution)/shard_map/all_to_all | solution.py:274
  212.1 3.3 %all-to-all-start.8 = ((bf16[4,128,128]{2,1,0:T(8,128)(2,1)}), bf16[4,128,128]{2,1,0:T(8,128)(2,1)S(1)}, u32[]{:S(2)}, u32[]{:S(2)}) async-start(bf16[4,128,128]{2,1,0:T(8,128)(2,1)} %bitcast.15), calls=%async_computation.8 | async-start | bytes 262144 | tf_op jit(solution)/shard_map/all_to_all | solution.py:253
  216.3 3.8 %all-to-all-done.8 = bf16[4,128,128]{2,1,0:T(8,128)(2,1)S(1)} async-done(((bf16[4,128,128]{2,1,0:T(8,128)(2,1)}), bf16[4,128,128]{2,1,0:T(8,128)(2,1)S(1)}, u32[]{:S(2)}, u32[]{:S(2)}) %all-to-all-start.8) | async-done | bytes 131104 | tf_op jit(solution)/shard_map/all_to_all | solution.py:253
  220.1 18.6 %all-to-all-start.7 = ((bf16[4,96,256]{2,1,0:T(8,128)(2,1)}), bf16[4,96,256]{2,1,0:T(8,128)(2,1)S(1)}, u32[]{:S(2)}, u32[]{:S(2)}) async-start(bf16[4,96,256]{2,1,0:T(8,128)(2,1)} %reduce_sum.31), calls=%async_computation.7 | async-start | bytes 393216 | tf_op jit(solution)/shard_map/all_to_all | solution.py:275
  239.4 17.7 %all-to-all-done.7 = bf16[4,96,256]{2,1,0:T(8,128)(2,1)S(1)} async-done(((bf16[4,96,256]{2,1,0:T(8,128)(2,1)}), bf16[4,96,256]{2,1,0:T(8,128)(2,1)S(1)}, u32[]{:S(2)}, u32[]{:S(2)}) %all-to-all-start.7) | async-done | bytes 196640 | tf_op jit(solution)/shard_map/all_to_all | solution.py:275
  (51 shorter events, 14.4 us)
Async XLA Ops:
  7.2 39.6 %copy-start = (bf16[512,192]{0,1:T(8,128)(2,1)S(1)}, bf16[512,192]{0,1:T(8,128)(2,1)}, u32[]{:S(2)}) copy-start(bf16[512,192]{0,1:T(8,128)(2,1)} %param.12) | copy-start | bytes 589828
  7.2 125.5 %all-gather.2.cloned.1.call-start = ((), (), s32[]{:S(2)}) async-start(), calls=%async_computation.9 | async-start | bytes 3932160 | tf_op jit(solution)/shard_map/all_gather | solution.py:229
  7.2 11.6 %copy-start.2 = (bf16[512,128]{1,0:T(8,128)(2,1)S(1)}, bf16[512,128]{1,0:T(8,128)(2,1)}, u32[]{:S(2)}) copy-start(bf16[512,128]{1,0:T(8,128)(2,1)} %param.8) | copy-start | bytes 393220
  7.9 10.9 %collective-permute-start.4 = (bf16[512,128]{1,0:T(8,128)(2,1)}, bf16[512,128]{1,0:T(8,128)(2,1)S(1)}, u32[]{:S(2)}, u32[]{:S(2)}) collective-permute-start(bf16[512,128]{1,0:T(8,128)(2,1)} %param.8), channel_id=1, source_target_pairs={{0,1},{1,0},{2,3},{3,2},{4,5},{5,4},{6,7},{7,6},{8,9},{9,8},{10,11... | collective-permute-start | bytes 393224 | tf_op jit(solution)/shard_map/ppermute | solution.py:225
  11.6 16.5 %all-to-all-start.2 = ((bf16[16,32,256]{2,1,0:T(8,128)(2,1)}), bf16[16,32,256]{2,1,0:T(8,128)(2,1)S(1)}, u32[]{:S(2)}, u32[]{:S(2)}) async-start(bf16[16,32,256]{2,1,0:T(8,128)(2,1)} %copy.29), calls=%async_computation.2 | async-start | bytes 524288 | tf_op jit(solution)/shard_map/all_to_all | solution.py:233
  18.8 23.6 %copy-start.3 = (s32[512]{0:T(512)S(1)}, s32[512]{0:T(512)}, u32[]{:S(2)}) copy-start(s32[512]{0:T(512)} %param.11) | copy-start | bytes 6148
  18.9 23.5 %collective-permute-start.5 = (bf16[1024,128]{1,0:T(8,128)(2,1)S(1)}, bf16[1024,128]{1,0:T(8,128)(2,1)S(1)}, u32[]{:S(2)}, u32[]{:S(2)}) collective-permute-start(bf16[1024,128]{1,0:T(8,128)(2,1)S(1)} %pad_maximum_fusion), channel_id=1, source_target_pairs={{0,2},{2,0},{1,3},{3,1},{4,6},{6,4},{5,7},{7,5},{8,10},{10,8},{9,1... | collective-permute-start | bytes 786440 | tf_op jit(solution)/shard_map/ppermute | solution.py:226
  28.2 35.6 %all-to-all-start = ((bf16[4,272,128]{2,1,0:T(8,128)(2,1)}), bf16[4,272,128]{2,1,0:T(8,128)(2,1)S(1)}, u32[]{:S(2)}, u32[]{:S(2)}) async-start(bf16[4,272,128]{2,1,0:T(8,128)(2,1)} %shard_map.95), calls=%async_computation | async-start | bytes 557056 | tf_op jit(solution)/shard_map/all_to_all | solution.py:220
  42.4 38.6 %collective-permute-start.6 = (bf16[2064,128]{1,0:T(8,128)(2,1)S(1)}, bf16[2064,128]{1,0:T(8,128)(2,1)}, u32[]{:S(2)}, u32[]{:S(2)}) collective-permute-start(bf16[2064,128]{1,0:T(8,128)(2,1)S(1)} %fusion.1.q_own), channel_id=1, source_target_pairs={{0,16},{16,0},{1,17},{17,1},{2,18},{18,2},{3,19},{19,3},{4,20},{20... | collective-permute-start | bytes 1585160 | tf_op jit(solution)/shard_map/ppermute | solution.py:227
  63.8 25.1 %all-to-all-start.1 = ((bf16[4,192,128]{2,1,0:T(8,128)(2,1)}), bf16[4,192,128]{2,1,0:T(8,128)(2,1)S(1)}, u32[]{:S(2)}, u32[]{:S(2)}) async-start(bf16[4,192,128]{2,1,0:T(8,128)(2,1)} %bitcast_bitcast_fusion), calls=%async_computation.1 | async-start | bytes 393216 | tf_op jit(solution)/shard_map/all_to_all | solution.py:231
  67.2 14.7 %collective-permute-start.2 = (bf16[2,272,128]{2,1,0:T(8,128)(2,1)S(1)}, bf16[2,272,128]{2,1,0:T(8,128)(2,1)}, u32[]{:S(2)}, u32[]{:S(2)}) collective-permute-start(bf16[2,272,128]{2,1,0:T(8,128)(2,1)S(1)} %get-tuple-element.13), channel_id=1, source_target_pairs={{448,0},{480,32},{0,64},{32,96},{64,128},{96,160},{128,192},{160,2... | collective-permute-start | bytes 417800 | tf_op jit(solution)/shard_map/ppermute | solution.py:216
  69.1 13.7 %collective-permute-start.3 = (bf16[2,272,128]{2,1,0:T(8,128)(2,1)S(1)}, bf16[2,272,128]{2,1,0:T(8,128)(2,1)}, u32[]{:S(2)}, u32[]{:S(2)}) collective-permute-start(bf16[2,272,128]{2,1,0:T(8,128)(2,1)S(1)} %get-tuple-element.12), channel_id=1, source_target_pairs={{64,0},{96,32},{128,64},{160,96},{192,128},{224,160},{256,192},{28... | collective-permute-start | bytes 417800 | tf_op jit(solution)/shard_map/ppermute | solution.py:216
  75.2 10.5 %collective-permute-start = (bf16[4,272,128]{2,1,0:T(8,128)(2,1)S(1)}, bf16[4,272,128]{2,1,0:T(8,128)(2,1)}, u32[]{:S(2)}, u32[]{:S(2)}) collective-permute-start(bf16[4,272,128]{2,1,0:T(8,128)(2,1)S(1)} %all-to-all-done.kv0), channel_id=1, source_target_pairs={{480,0},{0,32},{32,64},{64,96},{96,128},{128,160},{160,192},{192,2... | collective-permute-start | bytes 835592 | tf_op jit(solution)/shard_map/ppermute | solution.py:216
  77.1 10.5 %collective-permute-start.1 = (bf16[4,272,128]{2,1,0:T(8,128)(2,1)S(1)}, bf16[4,272,128]{2,1,0:T(8,128)(2,1)}, u32[]{:S(2)}, u32[]{:S(2)}) collective-permute-start(bf16[4,272,128]{2,1,0:T(8,128)(2,1)S(1)} %all-to-all-done.kv0), channel_id=1, source_target_pairs={{32,0},{64,32},{96,64},{128,96},{160,128},{192,160},{224,192},{256... | collective-permute-start | bytes 835592 | tf_op jit(solution)/shard_map/ppermute | solution.py:216
  132.7 1.9 copy-start.1
  159.5 5.3 %collective-permute-start.7 = (bf16[2,3072,128]{2,1,0:T(8,128)(2,1)S(1)}, bf16[2,3072,128]{2,1,0:T(8,128)(2,1)S(1)}, u32[]{:S(2)}, u32[]{:S(2)}) collective-permute-start(bf16[2,3072,128]{2,1,0:T(8,128)(2,1)S(1)} %bitcast.28), channel_id=1, source_target_pairs={{0,1},{1,0},{2,3},{3,2},{4,5},{5,4},{6,7},{7,6},{8,9},{9,8},{10,11... | collective-permute-start | bytes 4718600 | tf_op jit(solution)/shard_map/ppermute | solution.py:259
  167.1 21.5 %collective-permute-start.8 = (bf16[4,4,96,256]{3,2,1,0:T(8,128)(2,1)S(1)}, bf16[4,4,96,256]{3,2,1,0:T(8,128)(2,1)S(1)}, u32[]{:S(2)}, u32[]{:S(2)}) collective-permute-start(bf16[4,4,96,256]{3,2,1,0:T(8,128)(2,1)S(1)} %get-tuple-element.8), channel_id=1, source_target_pairs={{0,16},{16,0},{1,17},{17,1},{2,18},{18,2},{3,19},{19,3},{4,20},{20... | collective-permute-start | bytes 2359304 | tf_op jit(solution)/shard_map/ppermute | solution.py:271
  212.1 7.9 %all-to-all-start.8 = ((bf16[4,128,128]{2,1,0:T(8,128)(2,1)}), bf16[4,128,128]{2,1,0:T(8,128)(2,1)S(1)}, u32[]{:S(2)}, u32[]{:S(2)}) async-start(bf16[4,128,128]{2,1,0:T(8,128)(2,1)} %bitcast.15), calls=%async_computation.8 | async-start | bytes 262144 | tf_op jit(solution)/shard_map/all_to_all | solution.py:253
  220.1 37.1 %all-to-all-start.7 = ((bf16[4,96,256]{2,1,0:T(8,128)(2,1)}), bf16[4,96,256]{2,1,0:T(8,128)(2,1)S(1)}, u32[]{:S(2)}, u32[]{:S(2)}) async-start(bf16[4,96,256]{2,1,0:T(8,128)(2,1)} %reduce_sum.31), calls=%async_computation.7 | async-start | bytes 393216 | tf_op jit(solution)/shard_map/all_to_all | solution.py:275
Sparse Core Ops, SparseCore 0:
  10.1 49.2 all-gather.1

commit v3 on v2

--- a/solution.py
+++ b/solution.py
@@ -138,32 +138,46 @@
     return (projected - jnp.concatenate(taught, axis=1).astype(F32)).astype(BF)
 
 
-def gradient_rows(own, other, turned, half, out):
-    def one(zl, carry):
-        rows = []
-        for zh in range(4):
-            start = pl.multiple_of((zh * 4 + zl) * 192 + half * 96, 32)
-            rows.append(jnp.concatenate([ref[xl, pl.ds(start, 96), :] for ref in (own, other) for xl in range(2)], axis=1))
-        grad = jnp.dot(jnp.concatenate(rows, axis=0), turned[...], preferred_element_type=F32)
-        for zh in range(4):
-            out[zl, zh] = grad[zh * 96:(zh + 1) * 96].astype(out.dtype)
-        return carry
-
-    lax.fori_loop(0, 4, one, 0)
+def gradient_rows(own, other, turned, near):
+    rows = []
+    for zh in range(4):
+        start = pl.multiple_of((zh * 4 + near) * 192, 64)
+        rows.append(jnp.concatenate([ref[xl, pl.ds(start, 192), :] for ref in (own, other) for xl in range(2)], axis=1))
+    return jnp.dot(jnp.concatenate(rows, axis=0), turned[...], preferred_element_type=F32).reshape(8, 96, 256)
 
 
 def own_mismatch_kernel(place, own, projector_t, teacher_t, out):
     out[...] = mismatch_of(own, projector_t, teacher_t, place[0]).T
 
 
-def sent_kernel(place, own, other, projector_t, teacher_t, own_mismatch, mismatch, out):
+def second_kernel(place, own, other, projector_t, teacher_t, own_mismatch, mismatch, up, down):
     mismatch[0:256, :] = own_mismatch[...]
     mismatch[256:512, :] = mismatch_of(other, projector_t, teacher_t, 1 - place[0]).T
-    gradient_rows(own, other, mismatch, 1 - place[1], out)
+    grad = gradient_rows(own, other, mismatch, (place[1] + 2) % 4).astype(BF)
+    up[...] = grad[0:4]
+    down[...] = grad[4:8]
+
+
+def first_kernel(place, own, other, mismatch, up, down):
+    up[...] = gradient_rows(own, other, mismatch, (place[1] + 1) % 4).astype(BF)
+    down[...] = gradient_rows(own, other, mismatch, (place[1] + 3) % 4).astype(BF)
 
 
 def kept_kernel(place, own, other, mismatch, out):
-    gradient_rows(own, other, mismatch, place[1], out)
+    out[...] = gradient_rows(own, other, mismatch, place[1])
+
+
+def add_kernel(kept, below, above, far_below, far_above, out):
+    near = kept[...] + below[...].astype(F32) + above[...].astype(F32)
+    out[0:4] = (near[0:4] + far_below[...].astype(F32)).astype(BF)
+    out[4:8] = (near[4:8] + far_above[...].astype(F32)).astype(BF)
+
+
+def side_kernel(teacher, hidden_t, early, teacher_out, hidden_out):
+    for part in range(16):
+        teacher_out[part] = teacher[:, part * 256:(part + 1) * 256]
+    for part in range(4):
+        hidden_out[part] = hidden_t[:, part * 128:(part + 1) * 128]
 
 
 VMEM = pl.BlockSpec(memory_space=pltpu.VMEM)
@@ -227,9 +241,10 @@
     q_other = lax.ppermute(q_own, "yl", swap)
 
     weight_t = lax.all_gather(out_weight.T, GROUP, axis=0, tiled=True)
-    hidden_t = jnp.transpose(hidden.T.reshape(192, 4, 128), (1, 0, 2))
-    hidden_t = lax.all_to_all(hidden_t, GROUP, 0, 0).reshape(768, 128)
-    teacher_cols = jnp.transpose(teacher.reshape(32, 16, 256), (1, 0, 2))
+    teacher_cols, hidden_cut = call(
+        side_kernel, [shape(16, 32, 256), shape(4, 192, 128)], [VMEM, VMEM, ANY], (teacher, hidden.T, kv_own), 8
+    )
+    hidden_t = lax.all_to_all(hidden_cut, GROUP, 0, 0).reshape(768, 128)
     teacher_t = lax.all_to_all(teacher_cols, HID, 0, 0).reshape(512, 256).T
     projector_t = projector.T
 
@@ -258,21 +273,24 @@
     own = lax.all_to_all(student, CHIPS, 0, 0).reshape(2, 3072, 128)
     other = lax.ppermute(own, "c", swap)
 
-    place = jnp.stack([c, yl]).astype(jnp.int32)
+    place = jnp.stack([c, zl]).astype(jnp.int32)
     own_mismatch = call(own_mismatch_kernel, shape(256, 256), [SMEM] + [VMEM] * 3, (place, own, projector_t, teacher_t), 24, 4 * 10 ** 8)
-    mismatch, sent = call(
-        sent_kernel,
-        [shape(512, 256), shape(4, 4, 96, 256)],
+    mismatch, up, down = call(
+        second_kernel,
+        [shape(512, 256), shape(4, 96, 256), shape(4, 96, 256)],
         [SMEM] + [VMEM] * 5,
         (place, own, other, projector_t, teacher_t, own_mismatch),
         32,
         8 * 10 ** 8,
     )
-    received = lax.ppermute(sent, "yl", swap)
-    kept = call(kept_kernel, shape(4, 4, 96, 256, dtype=F32), [SMEM] + [VMEM] * 3, (place, own, other, mismatch), 32, 4 * 10 ** 8)
-    half = (kept + received.astype(F32)).astype(BF)
-    near = jnp.sum(lax.all_to_all(half, "zl", 0, 0).astype(F32), axis=0).astype(BF)
-    summed = jnp.sum(lax.all_to_all(near, "zh", 0, 0).astype(F32), axis=0)
+    far_below, far_above = from_z(up, -2), from_z(down, 2)
+    up, down = call(
+        first_kernel, [shape(8, 96, 256), shape(8, 96, 256)], [SMEM] + [VMEM] * 3, (place, own, other, mismatch), 32, 4 * 10 ** 8
+    )
+    below, above = from_z(up, -1), from_z(down, 1)
+    kept = call(kept_kernel, shape(8, 96, 256, dtype=F32), [SMEM] + [VMEM] * 3, (place, own, other, mismatch), 32, 2 * 10 ** 8)
+    near = call(add_kernel, shape(8, 96, 256), [VMEM] * 5, (kept, below, above, far_below, far_above), 16)
+    summed = jnp.sum(lax.all_to_all(near, ("zh", "yl"), 0, 0).astype(F32), axis=0)
     return summed * (16384 ** -0.5), attended
 
 

time: 266 us -> 254 us (0.955)
  the two profiles are of different devices: /device:TPU:32 before, /device:TPU:73 now
where the time goes in v3:
time: 254 us; the launch traced here: 252 us
  starting transfers between devices  91.7 us (36%)
  blocking collectives  56.4 us (22%)
  waiting for transfers between devices  50.2 us (20%)
  Pallas kernels  19.8 us (8%)
  local copies, waits for them, and re-layouts  16.9 us (7%)
  between operations  14.4 us (6%)
  other arithmetic  2.73 us (1%)
    ppermute x8, starting transfers between devices, from_z(): lax.ppermute(x, ('zh', 'zl'), [((i + shift) % 16, i) for i in range(16)])  31.7 us
    all_to_all x1, blocking collectives, on_device(): own = lax.all_to_all(student, CHIPS, 0, 0).reshape(2, 3072, 128)  23.1 us
    all_to_all x1, waiting for transfers between devices, on_device(): lax.all_to_all(near, ('zh', 'yl'), 0, 0).astype(F32)  22.7 us
    all_to_all x1, blocking collectives, on_device(): lax.all_to_all(partial, OCTET, 0, 0)  18.3 us
    pallas_call x9, Pallas kernels, call(): pl.pallas_call(kernel, out_shape=out_shape, in_specs=specs, out_specs=VME...  17.6 us
    all_to_all x1, starting transfers between devices, on_device(): lax.all_to_all(near, ('zh', 'yl'), 0, 0).astype(F32)  16.5 us
    all_to_all x1, waiting for transfers between devices, on_device(): kv_own = lax.all_to_all(packed, 'zh', 0, 0)  16 us
    all_to_all x1, blocking collectives, on_device(): att_all = lax.all_to_all(att_copies, HEADSETS, 0, 0)  15 us
  transfers between devices with their start and end apart: 18, of which 7 were waited for; matrix products, arithmetic and copies ran while one was open for 4% of the time, Pallas kernels for 6%

profile of v3, /device:TPU:73, one launch (start us, length us, event | category | flops | bytes accessed | tf_op | source)
XLA Modules:
  0.0 252.1 jit_solution(15885104263758238020)
XLA Ops:
  7.9 2.6 %collective-permute-start.4 = (bf16[512,128]{1,0:T(8,128)(2,1)}, bf16[512,128]{1,0:T(8,128)(2,1)S(1)}, u32[]{:S(2)}, u32[]{:S(2)}) collective-permute-start(bf16[512,128]{1,0:T(8,128)(2,1)} %param.8), channel_id=1, source_target_pairs={{0,1},{1,0},{2,3},{3,2},{4,5},{5,4},{6,7},{7,6},{8,9},{9,8},{10,11... | collective-permute-start | bytes 393224 | tf_op jit(solution)/shard_map/ppermute | solution.py:239
  12.6 3.3 %collective-permute-start.5 = (bf16[1024,128]{1,0:T(8,128)(2,1)S(1)}, bf16[1024,128]{1,0:T(8,128)(2,1)S(1)}, u32[]{:S(2)}, u32[]{:S(2)}) collective-permute-start(bf16[1024,128]{1,0:T(8,128)(2,1)S(1)} %pad_maximum_fusion), channel_id=1, source_target_pairs={{0,2},{2,0},{1,3},{3,1},{4,6},{6,4},{5,7},{7,5},{8,10},{10,8},{9,1... | collective-permute-start | bytes 786440 | tf_op jit(solution)/shard_map/ppermute | solution.py:240
  16.5 2.2 shard_map.95
  18.7 13.0 %all-to-all-start = ((bf16[4,272,128]{2,1,0:T(8,128)(2,1)}), bf16[4,272,128]{2,1,0:T(8,128)(2,1)S(1)}, u32[]{:S(2)}, u32[]{:S(2)}) async-start(bf16[4,272,128]{2,1,0:T(8,128)(2,1)} %shard_map.95), calls=%async_computation | async-start | bytes 557056 | tf_op jit(solution)/shard_map/all_to_all | solution.py:234
  31.7 2.1 collective-permute-start.6
  33.9 1.8 copy.17
  35.6 16.0 %all-to-all-done.early.kv0 = bf16[4,272,128]{2,1,0:T(8,128)(2,1)S(1)} async-done(((bf16[4,272,128]{2,1,0:T(8,128)(2,1)}), bf16[4,272,128]{2,1,0:T(8,128)(2,1)S(1)}, u32[]{:S(2)}, u32[]{:S(2)}) %all-to-all-start) | async-done | bytes 278560 | tf_op jit(solution)/shard_map/all_to_all | solution.py:234
  52.3 1.9 collective-permute-start.2
  54.2 4.3 %collective-permute-start.3 = (bf16[2,272,128]{2,1,0:T(8,128)(2,1)S(1)}, bf16[2,272,128]{2,1,0:T(8,128)(2,1)}, u32[]{:S(2)}, u32[]{:S(2)}) collective-permute-start(bf16[2,272,128]{2,1,0:T(8,128)(2,1)S(1)} %get-tuple-element.22), channel_id=1, source_target_pairs={{64,0},{96,32},{128,64},{160,96},{192,128},{224,160},{256,192},{28... | collective-permute-start | bytes 417800 | tf_op jit(solution)/shard_map/ppermute | solution.py:230
  60.2 8.9 %all-to-all-start.2 = ((bf16[16,32,256]{2,1,0:T(8,128)(2,1)}), bf16[16,32,256]{2,1,0:T(8,128)(2,1)S(1)}, u32[]{:S(2)}, u32[]{:S(2)}) async-start(bf16[16,32,256]{2,1,0:T(8,128)(2,1)} %copy-done.12), calls=%async_computation.2 | async-start | bytes 524288 | tf_op jit(solution)/shard_map/all_to_all | solution.py:248
  69.1 1.9 collective-permute-start
  71.0 3.8 %collective-permute-start.1 = (bf16[4,272,128]{2,1,0:T(8,128)(2,1)S(1)}, bf16[4,272,128]{2,1,0:T(8,128)(2,1)}, u32[]{:S(2)}, u32[]{:S(2)}) collective-permute-start(bf16[4,272,128]{2,1,0:T(8,128)(2,1)S(1)} %all-to-all-done.early.kv0), channel_id=1, source_target_pairs={{32,0},{64,32},{96,64},{128,96},{160,128},{192,160},{224,192},{256... | collective-permute-start | bytes 835592 | tf_op jit(solution)/shard_map/ppermute | solution.py:230
  77.8 4.1 %all-to-all-start.1 = ((bf16[4,192,128]{2,1,0:T(8,128)(2,1)}), bf16[4,192,128]{2,1,0:T(8,128)(2,1)S(1)}, u32[]{:S(2)}, u32[]{:S(2)}) async-start(bf16[4,192,128]{2,1,0:T(8,128)(2,1)} %copy-done.13), calls=%async_computation.1 | async-start | bytes 393216 | tf_op jit(solution)/shard_map/all_to_all | solution.py:247
  85.1 1.3 all-to-all-done.1
  89.5 8.4 %shard_map.97 = bf16[8,528,128]{2,1,0:T(8,128)(2,1)S(1)} custom-call(s32[147]{0:T(256)S(1)} %concatenate.24.sc, bf16[4,272,128]{2,1,0:T(8,128)(2,1)S(1)} %all-to-all-done.early.kv0, bf16[4,272,128]{2,1,0:T(8,128)(2,1)} %collective-permute-done.kv1, bf16[4,272,128]{2,1,0:T(8,128)(2,1)} %collective-permute-done.1.kv2, bf16[4,272,128]{2,1,0:T(8,128)(2,1)S(1)} %copy-done.8, ...), custom_call_target="tpu_custom_call" | custom-call | bytes 4194304 | tf_op jit(solution)/shard_map/pallas_call | solution.py:190
  97.8 18.3 %all_to_all.40.parts = bf16[8,528,128]{2,1,0:T(8,128)(2,1)S(1)} all-to-all(bf16[8,528,128]{2,1,0:T(8,128)(2,1)S(1)} %shard_map.97), channel_id=1, replica_groups=mesh['zh'=4,'zl'=4,'yl'=2,'yh'=2,'xh'=2,'xl'=2,'c'=2] {'yl','xl','c'}, dimensions={0} | all-to-all | bytes 2162688 | tf_op jit(solution)/shard_map/all_to_all | solution.py:265
  117.1 15.0 %all_to_all.41.att = bf16[4,512,128]{2,1,0:T(8,128)(2,1)S(1)} all-to-all(bf16[4,512,128]{2,1,0:T(8,128)(2,1)S(1)} %get-tuple-element.13), channel_id=1, replica_groups=mesh['zh'=4,'zl'=4,'yl'=2,'yh'=2,'xh'=2,'xl'=2,'c'=2] {'yh','xh'}, dimensions={0} | all-to-all | bytes 1048576 | tf_op jit(solution)/shard_map/all_to_all | solution.py:271
  132.1 1.9 copy-done.2
  134.9 23.1 %all_to_all.42 = bf16[8,768,128]{2,1,0:T(8,128)(2,1)S(1)} all-to-all(bf16[8,768,128]{2,1,0:T(8,128)(2,1)S(1)} %shard_map.99), channel_id=1, replica_groups=mesh['zh'=4,'zl'=4,'yl'=2,'yh'=2,'xh'=2,'xl'=2,'c'=2] {'xl','yh','xh'}, dimensions={0} | all-to-all | bytes 3145728 | tf_op jit(solution)/shard_map/all_to_all | solution.py:273
  158.0 5.0 %collective-permute-start.7 = (bf16[2,3072,128]{2,1,0:T(8,128)(2,1)S(1)}, bf16[2,3072,128]{2,1,0:T(8,128)(2,1)S(1)}, u32[]{:S(2)}, u32[]{:S(2)}) collective-permute-start(bf16[2,3072,128]{2,1,0:T(8,128)(2,1)S(1)} %bitcast.18), channel_id=1, source_target_pairs={{0,1},{1,0},{2,3},{3,2},{4,5},{5,4},{6,7},{7,6},{8,9},{9,8},{10,11... | collective-permute-start | bytes 4718600 | tf_op jit(solution)/shard_map/ppermute | solution.py:274
  164.3 1.8 collective-permute-done.7.other
  166.1 2.4 shard_map.101
  168.4 1.9 shard_map.103
  170.3 3.1 %collective-permute-start.8 = (bf16[8,96,256]{2,1,0:T(8,128)(2,1)}, bf16[8,96,256]{2,1,0:T(8,128)(2,1)S(1)}, u32[]{:S(2)}, u32[]{:S(2)}) collective-permute-start(bf16[8,96,256]{2,1,0:T(8,128)(2,1)} %get-tuple-element.15), channel_id=1, source_target_pairs={{480,0},{0,32},{32,64},{64,96},{96,128},{128,160},{160,192},{192,2... | collective-permute-start | bytes 1179656 | tf_op jit(solution)/shard_map/ppermute | solution.py:230
  173.4 2.5 collective-permute-start.9
  175.9 12.3 %collective-permute-start.10 = (bf16[4,96,256]{2,1,0:T(8,128)(2,1)}, bf16[4,96,256]{2,1,0:T(8,128)(2,1)S(1)}, u32[]{:S(2)}, u32[]{:S(2)}) collective-permute-start(bf16[4,96,256]{2,1,0:T(8,128)(2,1)} %get-tuple-element.17), channel_id=1, source_target_pairs={{448,0},{480,32},{0,64},{32,96},{64,128},{96,160},{128,192},{160,2... | collective-permute-start | bytes 589832 | tf_op jit(solution)/shard_map/ppermute | solution.py:230
  188.2 1.9 collective-permute-start.11
  190.1 4.5 %all-to-all-start.7 = ((bf16[4,128,128]{2,1,0:T(8,128)(2,1)}), bf16[4,128,128]{2,1,0:T(8,128)(2,1)S(1)}, u32[]{:S(2)}, u32[]{:S(2)}) async-start(bf16[4,128,128]{2,1,0:T(8,128)(2,1)} %bitcast.14), calls=%async_computation.7 | async-start | bytes 262144 | tf_op jit(solution)/shard_map/all_to_all | solution.py:268
  194.6 1.4 copy-done.1
  197.9 5.7 %collective-permute-done.11.far_above = bf16[4,96,256]{2,1,0:T(8,128)(2,1)S(1)} collective-permute-done((bf16[4,96,256]{2,1,0:T(8,128)(2,1)}, bf16[4,96,256]{2,1,0:T(8,128)(2,1)S(1)}, u32[]{:S(2)}, u32[]{:S(2)}) %collective-permute-start.11) | collective-permute-done | bytes 196640 | tf_op jit(solution)/shard_map/ppermute | solution.py:230
  204.6 16.5 %all-to-all-start.6 = ((bf16[8,96,256]{2,1,0:T(8,128)(2,1)}), bf16[8,96,256]{2,1,0:T(8,128)(2,1)S(1)}, u32[]{:S(2)}, u32[]{:S(2)}) async-start(bf16[8,96,256]{2,1,0:T(8,128)(2,1)} %shard_map.104), calls=%async_computation.6 | async-start | bytes 786432 | tf_op jit(solution)/shard_map/all_to_all | solution.py:293
  221.9 22.7 %all-to-all-done.6 = bf16[8,96,256]{2,1,0:T(8,128)(2,1)S(1)} async-done(((bf16[8,96,256]{2,1,0:T(8,128)(2,1)}), bf16[8,96,256]{2,1,0:T(8,128)(2,1)S(1)}, u32[]{:S(2)}, u32[]{:S(2)}) %all-to-all-start.6) | async-done | bytes 393248 | tf_op jit(solution)/shard_map/all_to_all | solution.py:293
  (82 shorter events, 22.3 us)
Async XLA Ops:
  7.2 124.9 %all-gather.2.cloned.1.call-start = ((), (), s32[]{:S(2)}) async-start(), calls=%async_computation.8 | async-start | bytes 3932160 | tf_op jit(solution)/shard_map/all_gather | solution.py:243
  7.9 3.8 %collective-permute-start.4 = (bf16[512,128]{1,0:T(8,128)(2,1)}, bf16[512,128]{1,0:T(8,128)(2,1)S(1)}, u32[]{:S(2)}, u32[]{:S(2)}) collective-permute-start(bf16[512,128]{1,0:T(8,128)(2,1)} %param.8), channel_id=1, source_target_pairs={{0,1},{1,0},{2,3},{3,2},{4,5},{5,4},{6,7},{7,6},{8,9},{9,8},{10,11... | collective-permute-start | bytes 393224 | tf_op jit(solution)/shard_map/ppermute | solution.py:239
  12.6 19.1 %copy-start.17 = (s32[512]{0:T(512)S(1)}, s32[512]{0:T(512)}, u32[]{:S(2)}) copy-start(s32[512]{0:T(512)} %param.11) | copy-start | bytes 6148
  12.6 19.1 %copy-start.16 = (bf16[512,128]{1,0:T(8,128)(2,1)S(1)}, bf16[512,128]{1,0:T(8,128)(2,1)}, u32[]{:S(2)}) copy-start(bf16[512,128]{1,0:T(8,128)(2,1)} %param.8) | copy-start | bytes 393220
  12.6 19.1 %collective-permute-start.5 = (bf16[1024,128]{1,0:T(8,128)(2,1)S(1)}, bf16[1024,128]{1,0:T(8,128)(2,1)S(1)}, u32[]{:S(2)}, u32[]{:S(2)}) collective-permute-start(bf16[1024,128]{1,0:T(8,128)(2,1)S(1)} %pad_maximum_fusion), channel_id=1, source_target_pairs={{0,2},{2,0},{1,3},{3,1},{4,6},{6,4},{5,7},{7,5},{8,10},{10,8},{9,1... | collective-permute-start | bytes 786440 | tf_op jit(solution)/shard_map/ppermute | solution.py:240
  18.7 33.0 %all-to-all-start = ((bf16[4,272,128]{2,1,0:T(8,128)(2,1)}), bf16[4,272,128]{2,1,0:T(8,128)(2,1)S(1)}, u32[]{:S(2)}, u32[]{:S(2)}) async-start(bf16[4,272,128]{2,1,0:T(8,128)(2,1)} %shard_map.95), calls=%async_computation | async-start | bytes 557056 | tf_op jit(solution)/shard_map/all_to_all | solution.py:234
  31.7 3.9 %copy-start.3 = (bf16[2064,128]{1,0:T(8,128)(2,1)}, bf16[2064,128]{1,0:T(8,128)(2,1)S(1)}, u32[]{:S(2)}) copy-start(bf16[2064,128]{1,0:T(8,128)(2,1)S(1)} %fusion.1.q_own) | copy-start | bytes 1585156
  31.7 43.1 %collective-permute-start.6 = (bf16[2064,128]{1,0:T(8,128)(2,1)S(1)}, bf16[2064,128]{1,0:T(8,128)(2,1)S(1)}, u32[]{:S(2)}, u32[]{:S(2)}) collective-permute-start(bf16[2064,128]{1,0:T(8,128)(2,1)S(1)} %fusion.1.q_own), channel_id=1, source_target_pairs={{0,16},{16,0},{1,17},{17,1},{2,18},{18,2},{3,19},{19,3},{4,20},{20... | collective-permute-start | bytes 1585160 | tf_op jit(solution)/shard_map/ppermute | solution.py:241
  33.8 24.7 %copy-start.11 = (bf16[32,4096]{1,0:T(8,128)(2,1)S(1)}, bf16[32,4096]{1,0:T(8,128)(2,1)}, u32[]{:S(2)}) copy-start(bf16[32,4096]{1,0:T(8,128)(2,1)} %teacher.1) | copy-start | bytes 786436
  52.3 22.8 %collective-permute-start.2 = (bf16[2,272,128]{2,1,0:T(8,128)(2,1)}, bf16[2,272,128]{2,1,0:T(8,128)(2,1)}, u32[]{:S(2)}, u32[]{:S(2)}) collective-permute-start(bf16[2,272,128]{2,1,0:T(8,128)(2,1)} %get-tuple-element.23), channel_id=1, source_target_pairs={{448,0},{480,32},{0,64},{32,96},{64,128},{96,160},{128,192},{160,2... | collective-permute-start | bytes 417800 | tf_op jit(solution)/shard_map/ppermute | solution.py:230
  54.2 21.8 %collective-permute-start.3 = (bf16[2,272,128]{2,1,0:T(8,128)(2,1)S(1)}, bf16[2,272,128]{2,1,0:T(8,128)(2,1)}, u32[]{:S(2)}, u32[]{:S(2)}) collective-permute-start(bf16[2,272,128]{2,1,0:T(8,128)(2,1)S(1)} %get-tuple-element.22), channel_id=1, source_target_pairs={{64,0},{96,32},{128,64},{160,96},{192,128},{224,160},{256,192},{28... | collective-permute-start | bytes 417800 | tf_op jit(solution)/shard_map/ppermute | solution.py:230
  60.2 17.6 %copy-start.13 = (bf16[4,192,128]{2,1,0:T(8,128)(2,1)}, bf16[4,192,128]{2,1,0:T(8,128)(2,1)S(1)}, u32[]{:S(2)}) copy-start(bf16[4,192,128]{2,1,0:T(8,128)(2,1)S(1)} %get-tuple-element.11) | copy-start | bytes 589828
  60.2 17.6 %all-to-all-start.2 = ((bf16[16,32,256]{2,1,0:T(8,128)(2,1)}), bf16[16,32,256]{2,1,0:T(8,128)(2,1)S(1)}, u32[]{:S(2)}, u32[]{:S(2)}) async-start(bf16[16,32,256]{2,1,0:T(8,128)(2,1)} %copy-done.12), calls=%async_computation.2 | async-start | bytes 524288 | tf_op jit(solution)/shard_map/all_to_all | solution.py:248
  69.1 13.9 %collective-permute-start = (bf16[4,272,128]{2,1,0:T(8,128)(2,1)S(1)}, bf16[4,272,128]{2,1,0:T(8,128)(2,1)}, u32[]{:S(2)}, u32[]{:S(2)}) collective-permute-start(bf16[4,272,128]{2,1,0:T(8,128)(2,1)S(1)} %all-to-all-done.early.kv0), channel_id=1, source_target_pairs={{480,0},{0,32},{32,64},{64,96},{96,128},{128,160},{160,192},{192,2... | collective-permute-start | bytes 835592 | tf_op jit(solution)/shard_map/ppermute | solution.py:230
  71.0 12.7 %collective-permute-start.1 = (bf16[4,272,128]{2,1,0:T(8,128)(2,1)S(1)}, bf16[4,272,128]{2,1,0:T(8,128)(2,1)}, u32[]{:S(2)}, u32[]{:S(2)}) collective-permute-start(bf16[4,272,128]{2,1,0:T(8,128)(2,1)S(1)} %all-to-all-done.early.kv0), channel_id=1, source_target_pairs={{32,0},{64,32},{96,64},{128,96},{160,128},{192,160},{224,192},{256... | collective-permute-start | bytes 835592 | tf_op jit(solution)/shard_map/ppermute | solution.py:230
  74.9 11.6 %copy-start.9 = (bf16[2064,128]{1,0:T(8,128)(2,1)}, bf16[2064,128]{1,0:T(8,128)(2,1)S(1)}, u32[]{:S(2)}) copy-start(bf16[2064,128]{1,0:T(8,128)(2,1)S(1)} %collective-permute-done.6.q_other) | copy-start | bytes 1585156
  76.9 9.5 %copy-start.7 = (bf16[4,272,128]{2,1,0:T(8,128)(2,1)}, bf16[4,272,128]{2,1,0:T(8,128)(2,1)S(1)}, u32[]{:S(2)}) copy-start(bf16[4,272,128]{2,1,0:T(8,128)(2,1)S(1)} %constant_dynamic-update-slice_fusion.kv3) | copy-start | bytes 835588
  77.8 4.1 %copy-start.15 = (bf16[16,32,256]{2,1,0:T(8,128)(2,1)}, bf16[16,32,256]{2,1,0:T(8,128)(2,1)S(1)}, u32[]{:S(2)}) copy-start(bf16[16,32,256]{2,1,0:T(8,128)(2,1)S(1)} %all-to-all-done.2) | copy-start | bytes 786436
  77.8 8.6 %all-to-all-start.1 = ((bf16[4,192,128]{2,1,0:T(8,128)(2,1)}), bf16[4,192,128]{2,1,0:T(8,128)(2,1)S(1)}, u32[]{:S(2)}, u32[]{:S(2)}) async-start(bf16[4,192,128]{2,1,0:T(8,128)(2,1)} %copy-done.13), calls=%async_computation.1 | async-start | bytes 393216 | tf_op jit(solution)/shard_map/all_to_all | solution.py:247
  86.4 1.0 copy-start.4
  88.4 1.0 copy-start.10
  132.1 1.9 copy-start.2
  158.0 8.1 %collective-permute-start.7 = (bf16[2,3072,128]{2,1,0:T(8,128)(2,1)S(1)}, bf16[2,3072,128]{2,1,0:T(8,128)(2,1)S(1)}, u32[]{:S(2)}, u32[]{:S(2)}) collective-permute-start(bf16[2,3072,128]{2,1,0:T(8,128)(2,1)S(1)} %bitcast.18), channel_id=1, source_target_pairs={{0,1},{1,0},{2,3},{3,2},{4,5},{5,4},{6,7},{7,6},{8,9},{9,8},{10,11... | collective-permute-start | bytes 4718600 | tf_op jit(solution)/shard_map/ppermute | solution.py:274
  166.1 2.4 copy-start
  168.4 1.9 copy-start.5
  170.3 33.3 %collective-permute-start.8 = (bf16[8,96,256]{2,1,0:T(8,128)(2,1)}, bf16[8,96,256]{2,1,0:T(8,128)(2,1)S(1)}, u32[]{:S(2)}, u32[]{:S(2)}) collective-permute-start(bf16[8,96,256]{2,1,0:T(8,128)(2,1)} %get-tuple-element.15), channel_id=1, source_target_pairs={{480,0},{0,32},{32,64},{64,96},{96,128},{128,160},{160,192},{192,2... | collective-permute-start | bytes 1179656 | tf_op jit(solution)/shard_map/ppermute | solution.py:230
  173.4 30.2 %collective-permute-start.9 = (bf16[8,96,256]{2,1,0:T(8,128)(2,1)S(1)}, bf16[8,96,256]{2,1,0:T(8,128)(2,1)S(1)}, u32[]{:S(2)}, u32[]{:S(2)}) collective-permute-start(bf16[8,96,256]{2,1,0:T(8,128)(2,1)S(1)} %get-tuple-element.16), channel_id=1, source_target_pairs={{32,0},{64,32},{96,64},{128,96},{160,128},{192,160},{224,192},{256... | collective-permute-start | bytes 1179656 | tf_op jit(solution)/shard_map/ppermute | solution.py:230
  175.9 22.0 %collective-permute-start.10 = (bf16[4,96,256]{2,1,0:T(8,128)(2,1)}, bf16[4,96,256]{2,1,0:T(8,128)(2,1)S(1)}, u32[]{:S(2)}, u32[]{:S(2)}) collective-permute-start(bf16[4,96,256]{2,1,0:T(8,128)(2,1)} %get-tuple-element.17), channel_id=1, source_target_pairs={{448,0},{480,32},{0,64},{32,96},{64,128},{96,160},{128,192},{160,2... | collective-permute-start | bytes 589832 | tf_op jit(solution)/shard_map/ppermute | solution.py:230
  188.2 15.4 %collective-permute-start.11 = (bf16[4,96,256]{2,1,0:T(8,128)(2,1)}, bf16[4,96,256]{2,1,0:T(8,128)(2,1)S(1)}, u32[]{:S(2)}, u32[]{:S(2)}) collective-permute-start(bf16[4,96,256]{2,1,0:T(8,128)(2,1)} %get-tuple-element.18), channel_id=1, source_target_pairs={{64,0},{96,32},{128,64},{160,96},{192,128},{224,160},{256,192},{28... | collective-permute-start | bytes 589832 | tf_op jit(solution)/shard_map/ppermute | solution.py:230
  190.1 14.4 %all-to-all-start.7 = ((bf16[4,128,128]{2,1,0:T(8,128)(2,1)}), bf16[4,128,128]{2,1,0:T(8,128)(2,1)S(1)}, u32[]{:S(2)}, u32[]{:S(2)}) async-start(bf16[4,128,128]{2,1,0:T(8,128)(2,1)} %bitcast.14), calls=%async_computation.7 | async-start | bytes 262144 | tf_op jit(solution)/shard_map/all_to_all | solution.py:268
  194.6 1.4 copy-start.1
  204.6 40.0 %all-to-all-start.6 = ((bf16[8,96,256]{2,1,0:T(8,128)(2,1)}), bf16[8,96,256]{2,1,0:T(8,128)(2,1)S(1)}, u32[]{:S(2)}, u32[]{:S(2)}) async-start(bf16[8,96,256]{2,1,0:T(8,128)(2,1)} %shard_map.104), calls=%async_computation.6 | async-start | bytes 786432 | tf_op jit(solution)/shard_map/all_to_all | solution.py:293
  (4 other events, 3.5 us)
Sparse Core Ops, SparseCore 0:
  10.1 49.5 all-gather.1

commit v4 on v3

v4 whole, which is shorter than its diff:
```python
import functools

import jax
import jax.numpy as jnp
from jax import lax
from jax.experimental import pallas as pl
from jax.experimental.pallas import tpu as pltpu
from jax.sharding import Mesh
from jax.sharding import PartitionSpec as P

HEAD = 128
SCALE2 = HEAD ** -0.5 * 1.4426950408889634
EMPTY = -1e30
MASKED = -2e30
BF = jnp.bfloat16
F32 = jnp.float32
CTX = ("zh", "zl", "yl")
HID = ("yh", "xh", "xl", "c")
GROUP = ("xl", "c")
OCTET = ("yl", "xl", "c")
HEADSETS = ("yh", "xh")
CHIPS = ("xl", "yh", "xh")
BLOCKS = 4


def start_kernel(place, keys, values, docs, hidden_t, queries, packed, doc_rows, kept, sent, q_out):
    rows = jnp.concatenate([docs[...].astype(F32), jnp.zeros((12, 128), F32)], axis=0).astype(BF)
    doc_rows[...] = rows
    for copy in range(4):
        packed[copy, 0:128, :] = keys[...]
        packed[copy, 128:256, :] = values[...]
        packed[copy, 256:272, :] = rows
    q_out[...] = queries[...]
    core = place[2]
    for xl in range(2):
        kept[xl] = hidden_t[:, pl.ds(pl.multiple_of((xl * 2 + core) * 128, 128), 128)]
        sent[xl] = hidden_t[:, pl.ds(pl.multiple_of((xl * 2 + 1 - core) * 128, 128), 128)]


def turn_kernel(place, kept, received, kept_out, sent_out):
    xl = place[3]
    for i, ref in enumerate((kept, received)):
        kept_out[i] = ref[xl]
        sent_out[i] = ref[1 - xl]


def attend_kernel(place, kv0, kv1, kv2, kv3_low, kv3_high, q_own, q_other, docs, early1, early2, early3, out, kv, q_all, v_turned, s_buf, info_v, info, sem):
    j, yl, z = place[0], place[4], place[5]
    copies = [
        pltpu.make_async_copy(src, dst, sem.at[i])
        for i, (src, dst) in enumerate((
            (kv0, kv.at[0]), (kv1, kv.at[1]), (kv2, kv.at[2]), (kv3_low, kv.at[3, pl.ds(0, 2)]), (kv3_high, kv.at[3, pl.ds(2, 2)]),
            (q_own, q_all.at[0]), (q_other, q_all.at[1]),
        ))
    ]
    for copy in copies:
        copy.start()
    for copy in copies:
        copy.wait()
    info_v[16:20, :] = docs[...]
    info_v[20:24, :] = q_all[1, 2048:2064, :].astype(F32)[0:4].astype(jnp.int32)
    block_docs = []
    for ch in range(4):
        for i in range(BLOCKS):
            rows = kv[i, ch, 256:272, :].astype(F32)
            block_docs.append(jnp.concatenate([rows[r:r + 1] for r in range(4)], axis=1))
    block_docs = jnp.concatenate(block_docs, axis=0)
    lane = lax.broadcasted_iota(jnp.int32, (16, 128), 1)
    counts = jnp.zeros((16, 128), F32)
    for d in range(8):
        below = jnp.sum((block_docs < d).astype(F32), axis=1, keepdims=True)
        counts = jnp.where(lane == d, below, counts)
    info_v[0:16, :] = counts.astype(jnp.int32)
    to_scalars = pltpu.make_async_copy(info_v, info, sem.at[7])
    to_scalars.start()
    for ch in range(4):
        for i in range(BLOCKS):
            v_turned[:, (ch * BLOCKS + i) * 128:(ch * BLOCKS + i + 1) * 128] = kv[i, ch, 128:256, :].T
    to_scalars.wait()
    where = [(z + shift) % 4 for shift in (0, 3, 1, 2)]
    key_iota = lax.broadcasted_iota(jnp.int32, (128, 512), 0)
    row_iota = lax.broadcasted_iota(jnp.int32, (1, 512), 1) % 128

    def one_tile(tile, carry):
        side, rc = tile // 4, tile % 4
        yl_q = jnp.where(side == 0, yl, 1 - yl)
        row0 = pl.multiple_of(rc * 128, 128)
        q = jnp.concatenate([q_all[side, pl.ds(pl.multiple_of((h ^ j) * 512, 512) + row0, 128), :] for h in range(4)], axis=0)
        row_docs = jnp.concatenate([info_v[pl.ds(16 + tile, 1), :]] * 4, axis=1)
        first, last = info[16 + tile, 0], info[16 + tile, 127]
        q_min = (2 * z + yl_q) * 512 + row0
        q_pos = q_min + row_iota

        def scores(ch):
            keys = jnp.concatenate([kv[i, ch, 0:128, :] for i in range(BLOCKS)], axis=0)
            return lax.dot_general(keys, q, (((1,), (1,)), ((), ())), preferred_element_type=F32) * SCALE2

        def mask(ch, s):
            parts = []
            for i in range(BLOCKS):
                low = jnp.zeros((1, 512), jnp.int32)
                for d in range(8):
                    low = jnp.where(row_docs == d, info[ch * BLOCKS + i, d], low)
                low = low - j * 128
                high = q_pos - ((2 * (ch * 4 + where[i]) + yl) * 512 + j * 128)
                ok = (key_iota >= low) & (key_iota <= high)
                parts.append(jnp.where(ok, s[i * 128:(i + 1) * 128], MASKED))
            return jnp.concatenate(parts, axis=0)

        def find_max(ch, run_max):
            most = functools.reduce(jnp.maximum, [info[ch * BLOCKS + i, last] for i in range(BLOCKS)])
            k_max = (2 * (ch * BLOCKS + BLOCKS - 1) + yl) * 512 + j * 128 + 127
            full = (k_max <= q_min) & (most <= j * 128)

            def keep(s):
                s_buf[ch] = s
                return jnp.max(s, axis=0, keepdims=True)

            return jnp.maximum(run_max, lax.cond(full, lambda: keep(scores(ch)), lambda: keep(mask(ch, scores(ch)))))

        def add_up(ch, state):
            run_sum, acc = state
            w = jnp.exp2(s_buf[ch] - run_max)
            cols = pl.ds(pl.multiple_of(ch * (BLOCKS * 128), BLOCKS * 128), BLOCKS * 128)
            blended = jnp.dot(v_turned[:, cols], w.astype(BF), preferred_element_type=F32)
            return run_sum + jnp.sum(w, axis=0, keepdims=True), acc + blended

        begin = jnp.int32(0)
        for ch in range(4):
            fewest = functools.reduce(jnp.minimum, [info[ch * BLOCKS + i, first] for i in range(BLOCKS)])
            begin = begin + (fewest >= (j + 1) * 128).astype(jnp.int32)
        end = z // BLOCKS + 1
        run_max = lax.fori_loop(begin, end, find_max, jnp.full((1, 512), EMPTY, F32))
        run_sum, acc = lax.fori_loop(begin, end, add_up, (jnp.zeros((1, 512), F32), jnp.zeros((128, 512), F32)))
        seen = run_sum > 0
        o = (acc * (1.0 / jnp.where(seen, run_sum, 1.0))).astype(BF)
        lse = jnp.where(seen, run_max + jnp.log2(jnp.where(seen, run_sum, 1.0)), EMPTY)
        hi = lse.astype(BF).astype(F32)
        mid = (lse - hi).astype(BF).astype(F32)
        lo = lse - hi - mid
        dest = yl_q * 4 + rc
        rows = [part[:, h * 128:(h + 1) * 128] for part in (hi, mid, lo) for h in range(4)]
        rows.append(jnp.zeros((4, 128), F32))
        for h in range(4):
            out[dest, h * 128:(h + 1) * 128, :] = o[:, h * 128:(h + 1) * 128]
        out[dest, 512:528, :] = jnp.concatenate(rows, axis=0).astype(BF)
        return carry

    lax.fori_loop(0, 8, one_tile, 0)


def combine_kernel(parts, out, copies):
    count = parts.shape[0]
    tails = [parts[s, 512:528, :].astype(F32) for s in range(count)]
    for h in range(4):
        lses = [t[h:h + 1] + t[4 + h:5 + h] + t[8 + h:9 + h] for t in tails]
        top = functools.reduce(jnp.maximum, lses)
        weights = [jnp.exp2(v - top) for v in lses]
        inverse = 1.0 / sum(weights)
        rows = slice(h * 128, (h + 1) * 128)
        total = sum(w * inverse * parts[s, rows, :].astype(F32) for s, w in enumerate(weights)).astype(BF)
        out[rows, :] = total
        for copy in range(copies.shape[0]):
            copies[copy, rows, :] = total


def student_kernel(place, weight_t, att, kept, received, teacher, out):
    part = pl.program_id(0)

    @pl.when(part == 0)
    def _():
        for chip in range(8):
            first = (chip % 4 * 4 + chip // 4 * 2) * 256
            for i in range(4):
                out[chip, 768 + i * 32:800 + i * 32, :] = teacher[:, first + i * 128:first + (i + 1) * 128]

    source = part ^ place[0]
    hidden = jnp.where(source < 2, kept[source % 2].astype(F32), received[source % 2].astype(F32))
    mixed = jnp.dot(weight_t[...], att[...].reshape(2048, 128), preferred_element_type=F32)
    student = (hidden + mixed).astype(BF)
    for copy in range(out.shape[0]):
        out[copy, pl.ds(pl.multiple_of(part * 192, 64), 192), :] = student


def projected(student, projector_t):
    total = 0.0
    for g in range(4):
        both = jnp.concatenate([student[g, 0:768, :], student[4 + g, 0:768, :]], axis=1)
        total = total + jnp.dot(projector_t[:, g * 768:(g + 1) * 768], both, preferred_element_type=F32)
    return total


def teacher_rows(own, other, core, chunk_core):
    pieces = []
    for xl in range(2):
        for t in range(4):
            source = t // 2 * 4 + xl * 2 + chunk_core
            halves = []
            for i in range(2):
                rows = pl.ds(pl.multiple_of(768 + core * 64 + i * 32, 32), 32)
                halves.append(jnp.where(core == t % 2, own[source, rows, :].astype(F32), other[source, rows, :].astype(F32)))
            pieces.append(jnp.concatenate(halves, axis=1))
    return jnp.concatenate(pieces, axis=0)


def gradient_rows(own, other, mismatch, near):
    rows = []
    for zh in range(4):
        cut = pl.ds(pl.multiple_of(near * 192, 64), 192)
        rows.append(jnp.concatenate([ref[xl * 4 + zh, cut, :] for ref in (own, other) for xl in range(2)], axis=1))
    return jnp.dot(jnp.concatenate(rows, axis=0), mismatch[...], preferred_element_type=F32).reshape(8, 96, 256)


def own_projected_kernel(own, projector_t, out):
    out[...] = projected(own, projector_t).T


def second_kernel(place, own, other, projector_t, own_projected, mismatch, up, down):
    core = place[2]
    mismatch[0:256, :] = (own_projected[...] - teacher_rows(own, other, core, core)).astype(BF)
    mismatch[256:512, :] = (projected(other, projector_t).T - teacher_rows(own, other, core, 1 - core)).astype(BF)
    grad = gradient_rows(own, other, mismatch, (place[6] + 2) % 4).astype(BF)
    up[...] = grad[0:4]
    down[...] = grad[4:8]


def first_kernel(place, own, other, mismatch, up, down):
    up[...] = gradient_rows(own, other, mismatch, (place[6] + 1) % 4).astype(BF)
    down[...] = gradient_rows(own, other, mismatch, (place[6] + 3) % 4).astype(BF)


def kept_kernel(place, own, other, mismatch, out):
    out[...] = gradient_rows(own, other, mismatch, place[6])


def add_kernel(kept, below, above, far_below, far_above, out):
    near = kept[...] + below[...].astype(F32) + above[...].astype(F32)
    out[0:4] = (near[0:4] + far_below[...].astype(F32)).astype(BF)
    out[4:8] = (near[4:8] + far_above[...].astype(F32)).astype(BF)


def final_kernel(terms, out):
    out[...] = sum(terms[i].astype(F32) for i in range(terms.shape[0])) * (16384 ** -0.5)


VMEM = pl.BlockSpec(memory_space=pltpu.VMEM)
SMEM = pl.BlockSpec(memory_space=pltpu.SMEM)
ANY = pl.BlockSpec(memory_space=pl.ANY)


def call(kernel, out_shape, specs, operands, limit, flops=0, scratch=()):
    single = not isinstance(out_shape, list)
    return pl.pallas_call(
        kernel,
        out_shape=out_shape,
        in_specs=specs,
        out_specs=VMEM if single else [VMEM] * len(out_shape),
        scratch_shapes=list(scratch),
        compiler_params=pltpu.CompilerParams(vmem_limit_bytes=limit * 1024 * 1024),
        cost_estimate=pl.CostEstimate(flops=flops, bytes_accessed=4 * 1024 * 1024, transcendentals=0),
    )(*operands)


def shape(*dims, dtype=BF):
    return jax.ShapeDtypeStruct(dims, dtype)


def start(place, keys, values, docs, hidden_t, queries):
    def block(*dims):
        return pl.BlockSpec(dims, lambda i, place: (0,) * len(dims))

    picked = pl.BlockSpec((128, 128), lambda i, place: (place[0], place[1]))
    outs = [(4, 272, 128), (16, 128), (2, 192, 128), (2, 192, 128), (512, 128)]
    return pl.pallas_call(
        start_kernel,
        grid_spec=pltpu.PrefetchScalarGridSpec(
            num_scalar_prefetch=1,
            grid=(1,),
            in_specs=[picked, picked, block(4, 128), block(192, 512), block(512, 128)],
            out_specs=[block(*dims) for dims in outs],
        ),
        out_shape=[shape(*dims) for dims in outs],
    )(place, keys, values, docs, hidden_t, queries)


def student_of(place, weight_t, att, kept, received, teacher):
    def block(*dims):
        return pl.BlockSpec(dims, lambda i: (0,) * len(dims))

    return pl.pallas_call(
        student_kernel,
        grid=(4,),
        out_shape=shape(8, 896, 128),
        in_specs=[
            SMEM, pl.BlockSpec((192, 2048), lambda i: (i, 0)), block(4, 512, 128), block(2, 192, 128), block(2, 192, 128), block(32, 4096),
        ],
        out_specs=block(8, 896, 128),
        compiler_params=pltpu.CompilerParams(vmem_limit_bytes=24 * 1024 * 1024),
    )(place, weight_t, att, kept, received, teacher)


def on_device(queries, keys, values, doc_ids, hidden, out_weight, projector, teacher):
    zl, yl, xl, c = lax.axis_index("zl"), lax.axis_index("yl"), lax.axis_index("xl"), lax.axis_index("c")
    z = lax.axis_index("zh") * 4 + zl
    g = lax.axis_index("yh") * 2 + lax.axis_index("xh")
    swap = [(0, 1), (1, 0)]
    place = jnp.stack([xl * 2 + c, g, c, xl, yl, z, zl]).astype(jnp.int32)

    def from_z(x, shift):
        return lax.ppermute(x, ("zh", "zl"), [((i + shift) % 16, i) for i in range(16)])

    docs = doc_ids.reshape(4, 128)
    packed, doc_rows, hidden_kept, hidden_sent, q_first = start(place, keys, values, docs, hidden.T, queries)
    kv_own = lax.all_to_all(packed, "zh", 0, 0)
    kv_below, kv_above = from_z(kv_own, -1), from_z(kv_own, 1)
    kv_low, kv_high = from_z(kv_own[0:2], -2), from_z(kv_own[2:4], 2)

    q_two = jnp.concatenate([q_first, lax.ppermute(q_first, "c", swap)], axis=0)
    q_own = jnp.concatenate([q_two, lax.ppermute(q_two, "xl", swap), doc_rows], axis=0)
    q_other = lax.ppermute(q_own, "yl", swap)
    half = shape(2, 192, 128)
    hidden_kept, hidden_sent = call(
        turn_kernel, [half, half], [SMEM, VMEM, VMEM], (place, hidden_kept, lax.ppermute(hidden_sent, "c", swap)), 8
    )
    hidden_received = lax.ppermute(hidden_sent, "xl", swap)

    weight_t = lax.all_gather(out_weight.T, GROUP, axis=0, tiled=True)
    projector_t = projector.T

    partial = call(
        attend_kernel,
        shape(8, 528, 128),
        [SMEM] + [ANY] * 7 + [VMEM] + [ANY] * 3,
        (place, kv_own, kv_below, kv_above, kv_low, kv_high, q_own, q_other, docs, hidden_kept, hidden_received, projector_t),
        40,
        2 * 10 ** 10,
        scratch=[
            pltpu.VMEM((4, 4, 272, 128), BF),
            pltpu.VMEM((2, 2064, 128), BF),
            pltpu.VMEM((128, 2048), BF),
            pltpu.VMEM((4, 512, 512), F32),
            pltpu.VMEM((24, 128), jnp.int32),
            pltpu.SMEM((24, 128), jnp.int32),
            pltpu.SemaphoreType.DMA((8,)),
        ],
    )
    att_rows, att_copies = call(
        combine_kernel, [shape(512, 128), shape(4, 512, 128)], [VMEM], (lax.all_to_all(partial, OCTET, 0, 0),), 16
    )

    att_head = lax.all_to_all(att_rows.reshape(4, 128, 128), GROUP, 0, 0)
    attended = jnp.transpose(att_head, (0, 2, 1)).reshape(512, 128)

    att_all = lax.all_to_all(att_copies, HEADSETS, 0, 0)
    student = student_of(place, weight_t, att_all, hidden_kept, hidden_received, teacher)
    own = lax.all_to_all(student, CHIPS, 0, 0)
    other = lax.ppermute(own, "c", swap)

    own_projected = call(own_projected_kernel, shape(256, 256, dtype=F32), [VMEM] * 2, (own, projector_t), 24, 4 * 10 ** 8)
    mismatch, up, down = call(
        second_kernel,
        [shape(512, 256), shape(4, 96, 256), shape(4, 96, 256)],
        [SMEM] + [VMEM] * 4,
        (place, own, other, projector_t, own_projected),
        32,
        8 * 10 ** 8,
    )
    far_below, far_above = from_z(up, -2), from_z(down, 2)
    up, down = call(
        first_kernel, [shape(8, 96, 256), shape(8, 96, 256)], [SMEM] + [VMEM] * 3, (place, own, other, mismatch), 32, 4 * 10 ** 8
    )
    below, above = from_z(up, -1), from_z(down, 1)
    kept = call(kept_kernel, shape(8, 96, 256, dtype=F32), [SMEM] + [VMEM] * 3, (place, own, other, mismatch), 32, 2 * 10 ** 8)
    near = call(add_kernel, shape(8, 96, 256), [VMEM] * 5, (kept, below, above, far_below, far_above), 16)
    grad = call(final_kernel, shape(96, 256, dtype=F32), [VMEM], (lax.all_to_all(near, ("zh", "yl"), 0, 0),), 8)
    return grad, attended


def solution(mesh):
    fine = Mesh(mesh.devices.reshape(4, 4, 2, 2, 2, 2, 2), ("zh", "zl", "yl", "yh", "xh", "xl", "c"))
    return jax.shard_map(
        on_device,
        mesh=fine,
        in_specs=(
            P(CTX, HID),
            P(CTX, None),
            P(CTX, None),
            P(CTX),
            P(CTX, HID),
            P(None, HID),
            P(None, HID),
            P(CTX + HID, None),
        ),
        out_specs=(P(CTX, HID), P(CTX, HID)),
        check_vma=False,
    )
```

time: 254 us -> 249 us (0.980)
  local copies, waits for them, and re-layouts: 16.9 us -> 12.1 us
  blocking collectives: 56.4 us -> 60 us
  Pallas kernels: 19.8 us -> 23.3 us
    all_to_all x1, waiting for transfers between devices: 16 us -> 0.01 us  [on_device(): kv_own = lax.all_to_all(packed, 'zh', 0, 0)]
    all_to_all x3 -> x1, starting transfers between devices: 29.6 us -> 17 us  [on_device(): lax.all_to_all(near, ('zh', 'yl'), 0, 0)]
    ppermute x1 -> x3, starting transfers between devices: 2.59 us -> 11.4 us  [the longest x1 4.63 us: on_device(): lax.ppermute(hidden_sent, 'c', swap)]
    ppermute x1, waiting for transfers between devices: 0.01 us -> 8.42 us  [on_device(): lax.ppermute(q_two, 'xl', swap)]
    ppermute x8, waiting for transfers between devices: 5.69 us -> 12.1 us  [from_z(): lax.ppermute(x, ('zh', 'zl'), [((i + shift) % 16, i) for i in range(16)])]
    all_to_all x1, blocking collectives: 23.1 us -> 25.9 us  [on_device(): own = lax.all_to_all(student, CHIPS, 0, 0)]
    pallas_call x1 -> x2, Pallas kernels: 2.19 us -> 4.83 us  [the longest x1 2.7 us: start(): pl.pallas_call(start_kernel, grid_spec=pltpu.PrefetchScalarGridSpec(num_s...]
    all_to_all x3 -> x1, waiting for transfers between devices: 24.9 us -> 22.9 us  [on_device(): lax.all_to_all(near, ('zh', 'yl'), 0, 0)]
  transfers between devices with their start and end apart: 18 -> 18, of which waited for: 7 -> 7; matrix products, arithmetic and copies ran while one was open for 4% -> 2% of each run, Pallas kernels for 6% -> 7%
where the time goes in v4:
time: 249 us; the launch traced here: 248 us
  starting transfers between devices  89.6 us (36%)
  blocking collectives  60 us (24%)
  waiting for transfers between devices  47.8 us (19%)
  Pallas kernels  23.3 us (9%)
  between operations  14.3 us (6%)
  local copies, waits for them, and re-layouts  12.1 us (5%)
    ppermute x8, starting transfers between devices, from_z(): lax.ppermute(x, ('zh', 'zl'), [((i + shift) % 16, i) for i in range(16)])  33.5 us
    all_to_all x1, blocking collectives, on_device(): own = lax.all_to_all(student, CHIPS, 0, 0)  25.9 us
    all_to_all x1, waiting for transfers between devices, on_device(): lax.all_to_all(near, ('zh', 'yl'), 0, 0)  22.9 us
    all_to_all x1, blocking collectives, on_device(): lax.all_to_all(partial, OCTET, 0, 0)  18.7 us
    pallas_call x9, Pallas kernels, call(): pl.pallas_call(kernel, out_shape=out_shape, in_specs=specs, out_specs=VME...  18.4 us
    all_to_all x1, starting transfers between devices, on_device(): lax.all_to_all(near, ('zh', 'yl'), 0, 0)  17 us
    all_to_all x1, blocking collectives, on_device(): att_all = lax.all_to_all(att_copies, HEADSETS, 0, 0)  15.4 us
    all_to_all x1, starting transfers between devices, on_device(): kv_own = lax.all_to_all(packed, 'zh', 0, 0)  13 us
  transfers between devices with their start and end apart: 18, of which 7 were waited for; matrix products, arithmetic and copies ran while one was open for 2% of the time, Pallas kernels for 7%

profile of v4, /device:TPU:73, one launch (start us, length us, event | category | flops | bytes accessed | tf_op | source)
XLA Modules:
  0.0 248.1 jit_solution(573652666089681282)
XLA Ops:
  8.6 2.7 %shard_map.95 = (bf16[4,272,128]{2,1,0:T(8,128)(2,1)}, bf16[16,128]{1,0:T(8,128)(2,1)}, bf16[2,192,128]{2,1,0:T(8,128)(2,1)}, bf16[2,192,128]{2,1,0:T(8,128)(2,1)}, bf16[512,128]{1,0:T(8,128)(2,1)}) custom-call(s32[7]{0:T(128)} %stack.31.place, bf16[512,512]{1,0:T(8,128)(2,1)} %keys.1, bf16[512,512]{1,0:T(8,128)(2,1)} %values.1, s32[4,128]{1,0:T(4,128)} %bitcast.17, ...), custom_call_target="tpu_custom_call" | custom-call | tf_op jit(solution)/shard_map/pallas_call | solution.py:274
  11.3 2.7 %collective-permute-start.4 = (bf16[512,128]{1,0:T(8,128)(2,1)}, bf16[512,128]{1,0:T(8,128)(2,1)S(1)}, u32[]{:S(2)}, u32[]{:S(2)}) collective-permute-start(bf16[512,128]{1,0:T(8,128)(2,1)} %get-tuple-element.17), channel_id=1, source_target_pairs={{0,1},{1,0},{2,3},{3,2},{4,5},{5,4},{6,7},{7,6},{8,9},{9,8},{10,11... | collective-permute-start | bytes 393224 | tf_op jit(solution)/shard_map/ppermute | solution.py:318
  14.0 13.0 %all-to-all-start = ((bf16[4,272,128]{2,1,0:T(8,128)(2,1)}), bf16[4,272,128]{2,1,0:T(8,128)(2,1)S(1)}, u32[]{:S(2)}, u32[]{:S(2)}) async-start(bf16[4,272,128]{2,1,0:T(8,128)(2,1)} %get-tuple-element.16), calls=%async_computation | async-start | bytes 557056 | tf_op jit(solution)/shard_map/all_to_all | solution.py:314
  28.0 3.1 %collective-permute-start.5 = (bf16[1024,128]{1,0:T(8,128)(2,1)S(1)}, bf16[1024,128]{1,0:T(8,128)(2,1)S(1)}, u32[]{:S(2)}, u32[]{:S(2)}) collective-permute-start(bf16[1024,128]{1,0:T(8,128)(2,1)S(1)} %pad_maximum_fusion), channel_id=1, source_target_pairs={{0,2},{2,0},{1,3},{3,1},{4,6},{6,4},{5,7},{7,5},{8,10},{10,8},{9,1... | collective-permute-start | bytes 786440 | tf_op jit(solution)/shard_map/ppermute | solution.py:319
  32.0 8.4 %collective-permute-done.5 = bf16[1024,128]{1,0:T(8,128)(2,1)S(1)} collective-permute-done((bf16[1024,128]{1,0:T(8,128)(2,1)S(1)}, bf16[1024,128]{1,0:T(8,128)(2,1)S(1)}, u32[]{:S(2)}, u32[]{:S(2)}) %collective-permute-start.5) | collective-permute-done | bytes 262176 | tf_op jit(solution)/shard_map/ppermute | solution.py:319
  40.5 2.0 collective-permute-start.6
  42.5 4.6 %collective-permute-start.7 = (bf16[2,192,128]{2,1,0:T(8,128)(2,1)S(1)}, bf16[2,192,128]{2,1,0:T(8,128)(2,1)S(1)}, u32[]{:S(2)}, u32[]{:S(2)}) collective-permute-start(bf16[2,192,128]{2,1,0:T(8,128)(2,1)S(1)} %copy-done.14), channel_id=1, source_target_pairs={{0,1},{1,0},{2,3},{3,2},{4,5},{5,4},{6,7},{7,6},{8,9},{9,8},{10,11... | collective-permute-start | bytes 294920 | tf_op jit(solution)/shard_map/ppermute | solution.py:323
  48.7 4.0 %collective-permute-start.8 = (bf16[2,192,128]{2,1,0:T(8,128)(2,1)S(1)}, bf16[2,192,128]{2,1,0:T(8,128)(2,1)S(1)}, u32[]{:S(2)}, u32[]{:S(2)}) collective-permute-start(bf16[2,192,128]{2,1,0:T(8,128)(2,1)S(1)} %get-tuple-element.22), channel_id=1, source_target_pairs={{0,2},{2,0},{1,3},{3,1},{4,6},{6,4},{5,7},{7,5},{8,10},{10,8},{9,1... | collective-permute-start | bytes 294920 | tf_op jit(solution)/shard_map/ppermute | solution.py:325
  52.8 2.2 collective-permute-start
  54.9 3.1 %collective-permute-start.1 = (bf16[4,272,128]{2,1,0:T(8,128)(2,1)S(1)}, bf16[4,272,128]{2,1,0:T(8,128)(2,1)}, u32[]{:S(2)}, u32[]{:S(2)}) collective-permute-start(bf16[4,272,128]{2,1,0:T(8,128)(2,1)S(1)} %all-to-all-done.kv0), channel_id=1, source_target_pairs={{32,0},{64,32},{96,64},{128,96},{160,128},{192,160},{224,192},{256... | collective-permute-start | bytes 835592 | tf_op jit(solution)/shard_map/ppermute | solution.py:310
  58.8 8.3 %collective-permute-start.2 = (bf16[2,272,128]{2,1,0:T(8,128)(2,1)}, bf16[2,272,128]{2,1,0:T(8,128)(2,1)S(1)}, u32[]{:S(2)}, u32[]{:S(2)}) collective-permute-start(bf16[2,272,128]{2,1,0:T(8,128)(2,1)} %get-tuple-element.31), channel_id=1, source_target_pairs={{448,0},{480,32},{0,64},{32,96},{64,128},{96,160},{128,192},{160,2... | collective-permute-start | bytes 417800 | tf_op jit(solution)/shard_map/ppermute | solution.py:310
  67.1 1.9 collective-permute-start.3
  69.0 1.7 copy.10
  72.7 5.6 %collective-permute-done.3.kv3_high = bf16[2,272,128]{2,1,0:T(8,128)(2,1)S(1)} collective-permute-done((bf16[2,272,128]{2,1,0:T(8,128)(2,1)S(1)}, bf16[2,272,128]{2,1,0:T(8,128)(2,1)S(1)}, u32[]{:S(2)}, u32[]{:S(2)}) %collective-permute-start.3) | collective-permute-done | bytes 139296 | tf_op jit(solution)/shard_map/ppermute | solution.py:310
  80.5 9.5 %shard_map.97 = bf16[8,528,128]{2,1,0:T(8,128)(2,1)S(1)} custom-call(s32[7]{0:T(128)S(1)} %copy-done.9, bf16[4,272,128]{2,1,0:T(8,128)(2,1)S(1)} %all-to-all-done.kv0, bf16[4,272,128]{2,1,0:T(8,128)(2,1)} %collective-permute-done.kv1, bf16[4,272,128]{2,1,0:T(8,128)(2,1)} %collective-permute-done.1.kv2, ...), custom_call_target="tpu_custom_call" | custom-call | flops 20000000000 | bytes 4194304 | tf_op jit(solution)/shard_map/pallas_call | solution.py:253
  90.0 18.7 %all_to_all.30.parts = bf16[8,528,128]{2,1,0:T(8,128)(2,1)S(1)} all-to-all(bf16[8,528,128]{2,1,0:T(8,128)(2,1)S(1)} %shard_map.97), channel_id=1, replica_groups=mesh['zh'=4,'zl'=4,'yl'=2,'yh'=2,'xh'=2,'xl'=2,'c'=2] {'yl','xl','c'}, dimensions={0} | all-to-all | bytes 2162688 | tf_op jit(solution)/shard_map/all_to_all | solution.py:348
  109.6 15.4 %all_to_all.31.att = bf16[4,512,128]{2,1,0:T(8,128)(2,1)S(1)} all-to-all(bf16[4,512,128]{2,1,0:T(8,128)(2,1)S(1)} %get-tuple-element.23), channel_id=1, replica_groups=mesh['zh'=4,'zl'=4,'yl'=2,'yh'=2,'xh'=2,'xl'=2,'c'=2] {'yh','xh'}, dimensions={0} | all-to-all | bytes 1048576 | tf_op jit(solution)/shard_map/all_to_all | solution.py:354
  125.0 1.9 copy-done.2
  126.9 2.1 shard_map.99
  129.0 25.9 %all_to_all.32.own = bf16[8,896,128]{2,1,0:T(8,128)(2,1)S(1)} all-to-all(bf16[8,896,128]{2,1,0:T(8,128)(2,1)S(1)} %shard_map.99), channel_id=1, replica_groups=mesh['zh'=4,'zl'=4,'yl'=2,'yh'=2,'xh'=2,'xl'=2,'c'=2] {'xl','yh','xh'}, dimensions={0} | all-to-all | bytes 3670016 | tf_op jit(solution)/shard_map/all_to_all | solution.py:356
  154.9 5.0 %collective-permute-start.9 = (bf16[8,896,128]{2,1,0:T(8,128)(2,1)S(1)}, bf16[8,896,128]{2,1,0:T(8,128)(2,1)S(1)}, u32[]{:S(2)}, u32[]{:S(2)}) collective-permute-start(bf16[8,896,128]{2,1,0:T(8,128)(2,1)S(1)} %all_to_all.32.own), channel_id=1, source_target_pairs={{0,1},{1,0},{2,3},{3,2},{4,5},{5,4},{6,7},{7,6},{8,9},{9,8},{10,11... | collective-permute-start | bytes 5505032 | tf_op jit(solution)/shard_map/ppermute | solution.py:357
  160.6 2.7 %collective-permute-done.9.other = bf16[8,896,128]{2,1,0:T(8,128)(2,1)S(1)} collective-permute-done((bf16[8,896,128]{2,1,0:T(8,128)(2,1)S(1)}, bf16[8,896,128]{2,1,0:T(8,128)(2,1)S(1)}, u32[]{:S(2)}, u32[]{:S(2)}) %collective-permute-start.9) | collective-permute-done | bytes 1835040 | tf_op jit(solution)/shard_map/ppermute | solution.py:357
  163.4 2.4 shard_map.101
  165.8 1.9 shard_map.103
  167.7 1.9 collective-permute-start.10
  169.6 3.4 %collective-permute-start.11 = (bf16[8,96,256]{2,1,0:T(8,128)(2,1)S(1)}, bf16[8,96,256]{2,1,0:T(8,128)(2,1)S(1)}, u32[]{:S(2)}, u32[]{:S(2)}) collective-permute-start(bf16[8,96,256]{2,1,0:T(8,128)(2,1)S(1)} %get-tuple-element.26), channel_id=1, source_target_pairs={{32,0},{64,32},{96,64},{128,96},{160,128},{192,160},{224,192},{256... | collective-permute-start | bytes 1179656 | tf_op jit(solution)/shard_map/ppermute | solution.py:310
  172.9 10.8 %collective-permute-start.12 = (bf16[4,96,256]{2,1,0:T(8,128)(2,1)}, bf16[4,96,256]{2,1,0:T(8,128)(2,1)S(1)}, u32[]{:S(2)}, u32[]{:S(2)}) collective-permute-start(bf16[4,96,256]{2,1,0:T(8,128)(2,1)} %get-tuple-element.27), channel_id=1, source_target_pairs={{448,0},{480,32},{0,64},{32,96},{64,128},{96,160},{128,192},{160,2... | collective-permute-start | bytes 589832 | tf_op jit(solution)/shard_map/ppermute | solution.py:310
  183.8 1.9 collective-permute-start.13
  185.7 4.5 %all-to-all-start.5 = ((bf16[4,128,128]{2,1,0:T(8,128)(2,1)}), bf16[4,128,128]{2,1,0:T(8,128)(2,1)S(1)}, u32[]{:S(2)}, u32[]{:S(2)}) async-start(bf16[4,128,128]{2,1,0:T(8,128)(2,1)} %bitcast.11), calls=%async_computation.5 | async-start | bytes 262144 | tf_op jit(solution)/shard_map/all_to_all | solution.py:351
  193.6 5.3 %collective-permute-done.13.far_above = bf16[4,96,256]{2,1,0:T(8,128)(2,1)S(1)} collective-permute-done((bf16[4,96,256]{2,1,0:T(8,128)(2,1)}, bf16[4,96,256]{2,1,0:T(8,128)(2,1)S(1)}, u32[]{:S(2)}, u32[]{:S(2)}) %collective-permute-start.13) | collective-permute-done | bytes 196640 | tf_op jit(solution)/shard_map/ppermute | solution.py:310
  199.9 17.0 %all-to-all-start.4 = ((bf16[8,96,256]{2,1,0:T(8,128)(2,1)}), bf16[8,96,256]{2,1,0:T(8,128)(2,1)S(1)}, u32[]{:S(2)}, u32[]{:S(2)}) async-start(bf16[8,96,256]{2,1,0:T(8,128)(2,1)} %shard_map.104), calls=%async_computation.4 | async-start | bytes 786432 | tf_op jit(solution)/shard_map/all_to_all | solution.py:375
  217.7 22.9 %all-to-all-done.4.terms = bf16[8,96,256]{2,1,0:T(8,128)(2,1)S(1)} async-done(((bf16[8,96,256]{2,1,0:T(8,128)(2,1)}), bf16[8,96,256]{2,1,0:T(8,128)(2,1)S(1)}, u32[]{:S(2)}, u32[]{:S(2)}) %all-to-all-start.4) | async-done | bytes 393248 | tf_op jit(solution)/shard_map/all_to_all | solution.py:375
  (58 shorter events, 17.0 us)
Async XLA Ops:
  7.2 117.8 %all-gather.2.cloned.1.call-start = ((), (), s32[]{:S(2)}) async-start(), calls=%async_computation.6 | async-start | bytes 3932160 | tf_op jit(solution)/shard_map/all_gather | solution.py:327
  8.6 39.6 %copy-start.9 = (s32[7]{0:T(128)S(1)}, s32[7]{0:T(128)}, u32[]{:S(2)}) copy-start(s32[7]{0:T(128)} %stack.31.place) | copy-start | bytes 88
  11.3 29.2 %copy-start.13 = (bf16[16,128]{1,0:T(8,128)(2,1)S(1)}, bf16[16,128]{1,0:T(8,128)(2,1)}, u32[]{:S(2)}) copy-start(bf16[16,128]{1,0:T(8,128)(2,1)} %get-tuple-element.18) | copy-start | bytes 12292
  11.3 31.2 %copy-start.14 = (bf16[2,192,128]{2,1,0:T(8,128)(2,1)S(1)}, bf16[2,192,128]{2,1,0:T(8,128)(2,1)}, u32[]{:S(2)}) copy-start(bf16[2,192,128]{2,1,0:T(8,128)(2,1)} %get-tuple-element.20) | copy-start | bytes 294916
  11.3 36.9 %copy-start.6 = (bf16[2,192,128]{2,1,0:T(8,128)(2,1)S(1)}, bf16[2,192,128]{2,1,0:T(8,128)(2,1)}, u32[]{:S(2)}) copy-start(bf16[2,192,128]{2,1,0:T(8,128)(2,1)} %get-tuple-element.19.kept) | copy-start | bytes 294916
  11.3 15.7 %collective-permute-start.4 = (bf16[512,128]{1,0:T(8,128)(2,1)}, bf16[512,128]{1,0:T(8,128)(2,1)S(1)}, u32[]{:S(2)}, u32[]{:S(2)}) collective-permute-start(bf16[512,128]{1,0:T(8,128)(2,1)} %get-tuple-element.17), channel_id=1, source_target_pairs={{0,1},{1,0},{2,3},{3,2},{4,5},{5,4},{6,7},{7,6},{8,9},{9,8},{10,11... | collective-permute-start | bytes 393224 | tf_op jit(solution)/shard_map/ppermute | solution.py:318
  14.0 38.8 %all-to-all-start = ((bf16[4,272,128]{2,1,0:T(8,128)(2,1)}), bf16[4,272,128]{2,1,0:T(8,128)(2,1)S(1)}, u32[]{:S(2)}, u32[]{:S(2)}) async-start(bf16[4,272,128]{2,1,0:T(8,128)(2,1)} %get-tuple-element.16), calls=%async_computation | async-start | bytes 557056 | tf_op jit(solution)/shard_map/all_to_all | solution.py:314
  28.0 12.5 %collective-permute-start.5 = (bf16[1024,128]{1,0:T(8,128)(2,1)S(1)}, bf16[1024,128]{1,0:T(8,128)(2,1)S(1)}, u32[]{:S(2)}, u32[]{:S(2)}) collective-permute-start(bf16[1024,128]{1,0:T(8,128)(2,1)S(1)} %pad_maximum_fusion), channel_id=1, source_target_pairs={{0,2},{2,0},{1,3},{3,1},{4,6},{6,4},{5,7},{7,5},{8,10},{10,8},{9,1... | collective-permute-start | bytes 786440 | tf_op jit(solution)/shard_map/ppermute | solution.py:319
  40.5 30.2 %copy-start.7 = (bf16[2064,128]{1,0:T(8,128)(2,1)}, bf16[2064,128]{1,0:T(8,128)(2,1)S(1)}, u32[]{:S(2)}) copy-start(bf16[2064,128]{1,0:T(8,128)(2,1)S(1)} %constant_dynamic-update-slice_fusion.q_own) | copy-start | bytes 1585156
  40.5 30.2 %collective-permute-start.6 = (bf16[2064,128]{1,0:T(8,128)(2,1)S(1)}, bf16[2064,128]{1,0:T(8,128)(2,1)S(1)}, u32[]{:S(2)}, u32[]{:S(2)}) collective-permute-start(bf16[2064,128]{1,0:T(8,128)(2,1)S(1)} %constant_dynamic-update-slice_fusion.q_own), channel_id=1, source_target_pairs={{0,16},{16,0},{1,17},{17,1},{2,18},{18,2},{3,19},{19,3},{4,20},{20... | collective-permute-start | bytes 1585160 | tf_op jit(solution)/shard_map/ppermute | solution.py:320
  42.5 5.6 %collective-permute-start.7 = (bf16[2,192,128]{2,1,0:T(8,128)(2,1)S(1)}, bf16[2,192,128]{2,1,0:T(8,128)(2,1)S(1)}, u32[]{:S(2)}, u32[]{:S(2)}) collective-permute-start(bf16[2,192,128]{2,1,0:T(8,128)(2,1)S(1)} %copy-done.14), channel_id=1, source_target_pairs={{0,1},{1,0},{2,3},{3,2},{4,5},{5,4},{6,7},{7,6},{8,9},{9,8},{10,11... | collective-permute-start | bytes 294920 | tf_op jit(solution)/shard_map/ppermute | solution.py:323
  48.7 29.6 %copy-start.10 = (s32[512]{0:T(512)S(1)}, s32[512]{0:T(512)}, u32[]{:S(2)}) copy-start(s32[512]{0:T(512)} %param.11) | copy-start | bytes 6148
  48.7 18.3 %collective-permute-start.8 = (bf16[2,192,128]{2,1,0:T(8,128)(2,1)S(1)}, bf16[2,192,128]{2,1,0:T(8,128)(2,1)S(1)}, u32[]{:S(2)}, u32[]{:S(2)}) collective-permute-start(bf16[2,192,128]{2,1,0:T(8,128)(2,1)S(1)} %get-tuple-element.22), channel_id=1, source_target_pairs={{0,2},{2,0},{1,3},{3,1},{4,6},{6,4},{5,7},{7,5},{8,10},{10,8},{9,1... | collective-permute-start | bytes 294920 | tf_op jit(solution)/shard_map/ppermute | solution.py:325
  52.8 25.6 %collective-permute-start = (bf16[4,272,128]{2,1,0:T(8,128)(2,1)S(1)}, bf16[4,272,128]{2,1,0:T(8,128)(2,1)}, u32[]{:S(2)}, u32[]{:S(2)}) collective-permute-start(bf16[4,272,128]{2,1,0:T(8,128)(2,1)S(1)} %all-to-all-done.kv0), channel_id=1, source_target_pairs={{480,0},{0,32},{32,64},{64,96},{96,128},{128,160},{160,192},{192,2... | collective-permute-start | bytes 835592 | tf_op jit(solution)/shard_map/ppermute | solution.py:310
  54.9 23.4 %collective-permute-start.1 = (bf16[4,272,128]{2,1,0:T(8,128)(2,1)S(1)}, bf16[4,272,128]{2,1,0:T(8,128)(2,1)}, u32[]{:S(2)}, u32[]{:S(2)}) collective-permute-start(bf16[4,272,128]{2,1,0:T(8,128)(2,1)S(1)} %all-to-all-done.kv0), channel_id=1, source_target_pairs={{32,0},{64,32},{96,64},{128,96},{160,128},{192,160},{224,192},{256... | collective-permute-start | bytes 835592 | tf_op jit(solution)/shard_map/ppermute | solution.py:310
  58.8 14.0 %collective-permute-start.2 = (bf16[2,272,128]{2,1,0:T(8,128)(2,1)}, bf16[2,272,128]{2,1,0:T(8,128)(2,1)S(1)}, u32[]{:S(2)}, u32[]{:S(2)}) collective-permute-start(bf16[2,272,128]{2,1,0:T(8,128)(2,1)} %get-tuple-element.31), channel_id=1, source_target_pairs={{448,0},{480,32},{0,64},{32,96},{64,128},{96,160},{128,192},{160,2... | collective-permute-start | bytes 417800 | tf_op jit(solution)/shard_map/ppermute | solution.py:310
  67.1 11.3 %collective-permute-start.3 = (bf16[2,272,128]{2,1,0:T(8,128)(2,1)S(1)}, bf16[2,272,128]{2,1,0:T(8,128)(2,1)S(1)}, u32[]{:S(2)}, u32[]{:S(2)}) collective-permute-start(bf16[2,272,128]{2,1,0:T(8,128)(2,1)S(1)} %get-tuple-element.30), channel_id=1, source_target_pairs={{64,0},{96,32},{128,64},{160,96},{192,128},{224,160},{256,192},{28... | collective-permute-start | bytes 417800 | tf_op jit(solution)/shard_map/ppermute | solution.py:310
  78.4 1.0 copy-start.8
  79.4 1.0 copy-start.12
  90.0 35.0 %copy-start.5 = (bf16[32,4096]{1,0:T(8,128)(2,1)S(1)}, bf16[32,4096]{1,0:T(8,128)(2,1)}, u32[]{:S(2)}) copy-start(bf16[32,4096]{1,0:T(8,128)(2,1)} %teacher.1) | copy-start | bytes 786436
  125.0 1.9 copy-start.2
  154.9 8.4 %collective-permute-start.9 = (bf16[8,896,128]{2,1,0:T(8,128)(2,1)S(1)}, bf16[8,896,128]{2,1,0:T(8,128)(2,1)S(1)}, u32[]{:S(2)}, u32[]{:S(2)}) collective-permute-start(bf16[8,896,128]{2,1,0:T(8,128)(2,1)S(1)} %all_to_all.32.own), channel_id=1, source_target_pairs={{0,1},{1,0},{2,3},{3,2},{4,5},{5,4},{6,7},{7,6},{8,9},{9,8},{10,11... | collective-permute-start | bytes 5505032 | tf_op jit(solution)/shard_map/ppermute | solution.py:357
  163.4 2.4 copy-start
  165.8 1.9 copy-start.3
  167.7 31.3 %collective-permute-start.10 = (bf16[8,96,256]{2,1,0:T(8,128)(2,1)}, bf16[8,96,256]{2,1,0:T(8,128)(2,1)S(1)}, u32[]{:S(2)}, u32[]{:S(2)}) collective-permute-start(bf16[8,96,256]{2,1,0:T(8,128)(2,1)} %get-tuple-element.25), channel_id=1, source_target_pairs={{480,0},{0,32},{32,64},{64,96},{96,128},{128,160},{160,192},{192,2... | collective-permute-start | bytes 1179656 | tf_op jit(solution)/shard_map/ppermute | solution.py:310
  169.6 29.4 %collective-permute-start.11 = (bf16[8,96,256]{2,1,0:T(8,128)(2,1)S(1)}, bf16[8,96,256]{2,1,0:T(8,128)(2,1)S(1)}, u32[]{:S(2)}, u32[]{:S(2)}) collective-permute-start(bf16[8,96,256]{2,1,0:T(8,128)(2,1)S(1)} %get-tuple-element.26), channel_id=1, source_target_pairs={{32,0},{64,32},{96,64},{128,96},{160,128},{192,160},{224,192},{256... | collective-permute-start | bytes 1179656 | tf_op jit(solution)/shard_map/ppermute | solution.py:310
  172.9 20.7 %collective-permute-start.12 = (bf16[4,96,256]{2,1,0:T(8,128)(2,1)}, bf16[4,96,256]{2,1,0:T(8,128)(2,1)S(1)}, u32[]{:S(2)}, u32[]{:S(2)}) collective-permute-start(bf16[4,96,256]{2,1,0:T(8,128)(2,1)} %get-tuple-element.27), channel_id=1, source_target_pairs={{448,0},{480,32},{0,64},{32,96},{64,128},{96,160},{128,192},{160,2... | collective-permute-start | bytes 589832 | tf_op jit(solution)/shard_map/ppermute | solution.py:310
  183.8 15.1 %collective-permute-start.13 = (bf16[4,96,256]{2,1,0:T(8,128)(2,1)}, bf16[4,96,256]{2,1,0:T(8,128)(2,1)S(1)}, u32[]{:S(2)}, u32[]{:S(2)}) collective-permute-start(bf16[4,96,256]{2,1,0:T(8,128)(2,1)} %get-tuple-element.28), channel_id=1, source_target_pairs={{64,0},{96,32},{128,64},{160,96},{192,128},{224,160},{256,192},{28... | collective-permute-start | bytes 589832 | tf_op jit(solution)/shard_map/ppermute | solution.py:310
  185.7 14.2 %all-to-all-start.5 = ((bf16[4,128,128]{2,1,0:T(8,128)(2,1)}), bf16[4,128,128]{2,1,0:T(8,128)(2,1)S(1)}, u32[]{:S(2)}, u32[]{:S(2)}) async-start(bf16[4,128,128]{2,1,0:T(8,128)(2,1)} %bitcast.11), calls=%async_computation.5 | async-start | bytes 262144 | tf_op jit(solution)/shard_map/all_to_all | solution.py:351
  190.3 1.5 copy-start.1
  191.8 0.9 copy-start.4
  199.9 40.7 %all-to-all-start.4 = ((bf16[8,96,256]{2,1,0:T(8,128)(2,1)}), bf16[8,96,256]{2,1,0:T(8,128)(2,1)S(1)}, u32[]{:S(2)}, u32[]{:S(2)}) async-start(bf16[8,96,256]{2,1,0:T(8,128)(2,1)} %shard_map.104), calls=%async_computation.4 | async-start | bytes 786432 | tf_op jit(solution)/shard_map/all_to_all | solution.py:375
  (1 other events, 0.8 us)
Sparse Core Ops, SparseCore 0:
  10.1 55.7 all-gather.1

commit v5 on v4

--- a/solution.py
+++ b/solution.py
@@ -23,42 +23,31 @@
 BLOCKS = 4
 
 
-def start_kernel(place, keys, values, docs, hidden_t, queries, packed, doc_rows, kept, sent, q_out):
+def start_kernel(place, keys, values, docs, queries, packed, q_rows):
     rows = jnp.concatenate([docs[...].astype(F32), jnp.zeros((12, 128), F32)], axis=0).astype(BF)
-    doc_rows[...] = rows
     for copy in range(4):
         packed[copy, 0:128, :] = keys[...]
         packed[copy, 128:256, :] = values[...]
         packed[copy, 256:272, :] = rows
-    q_out[...] = queries[...]
-    core = place[2]
-    for xl in range(2):
-        kept[xl] = hidden_t[:, pl.ds(pl.multiple_of((xl * 2 + core) * 128, 128), 128)]
-        sent[xl] = hidden_t[:, pl.ds(pl.multiple_of((xl * 2 + 1 - core) * 128, 128), 128)]
-
-
-def turn_kernel(place, kept, received, kept_out, sent_out):
-    xl = place[3]
-    for i, ref in enumerate((kept, received)):
-        kept_out[i] = ref[xl]
-        sent_out[i] = ref[1 - xl]
-
-
-def attend_kernel(place, kv0, kv1, kv2, kv3_low, kv3_high, q_own, q_other, docs, early1, early2, early3, out, kv, q_all, v_turned, s_buf, info_v, info, sem):
+    q_rows[0:512, :] = queries[...]
+    q_rows[512:528, :] = rows
+
+
+def attend_kernel(place, kv0, kv1, kv2, kv3_low, kv3_high, queries, early, out, kv, q_all, v_turned, s_buf, info_v, info, sem):
     j, yl, z = place[0], place[4], place[5]
     copies = [
         pltpu.make_async_copy(src, dst, sem.at[i])
         for i, (src, dst) in enumerate((
             (kv0, kv.at[0]), (kv1, kv.at[1]), (kv2, kv.at[2]), (kv3_low, kv.at[3, pl.ds(0, 2)]), (kv3_high, kv.at[3, pl.ds(2, 2)]),
-            (q_own, q_all.at[0]), (q_other, q_all.at[1]),
+            (queries, q_all),
         ))
     ]
     for copy in copies:
         copy.start()
     for copy in copies:
         copy.wait()
-    info_v[16:20, :] = docs[...]
-    info_v[20:24, :] = q_all[1, 2048:2064, :].astype(F32)[0:4].astype(jnp.int32)
+    for side in range(2):
+        info_v[16 + 4 * side:20 + 4 * side, :] = q_all[4 * side, 512:528, :].astype(F32)[0:4].astype(jnp.int32)
     block_docs = []
     for ch in range(4):
         for i in range(BLOCKS):
@@ -71,7 +60,7 @@
         below = jnp.sum((block_docs < d).astype(F32), axis=1, keepdims=True)
         counts = jnp.where(lane == d, below, counts)
     info_v[0:16, :] = counts.astype(jnp.int32)
-    to_scalars = pltpu.make_async_copy(info_v, info, sem.at[7])
+    to_scalars = pltpu.make_async_copy(info_v, info, sem.at[6])
     to_scalars.start()
     for ch in range(4):
         for i in range(BLOCKS):
@@ -82,10 +71,9 @@
     row_iota = lax.broadcasted_iota(jnp.int32, (1, 512), 1) % 128
 
     def one_tile(tile, carry):
-        side, rc = tile // 4, tile % 4
-        yl_q = jnp.where(side == 0, yl, 1 - yl)
+        yl_q, rc = tile // 4, tile % 4
         row0 = pl.multiple_of(rc * 128, 128)
-        q = jnp.concatenate([q_all[side, pl.ds(pl.multiple_of((h ^ j) * 512, 512) + row0, 128), :] for h in range(4)], axis=0)
+        q = jnp.concatenate([q_all[yl_q * 4 + h, pl.ds(row0, 128), :] for h in range(4)], axis=0)
         row_docs = jnp.concatenate([info_v[pl.ds(16 + tile, 1), :]] * 4, axis=1)
         first, last = info[16 + tile, 0], info[16 + tile, 127]
         q_min = (2 * z + yl_q) * 512 + row0
@@ -138,12 +126,11 @@
         hi = lse.astype(BF).astype(F32)
         mid = (lse - hi).astype(BF).astype(F32)
         lo = lse - hi - mid
-        dest = yl_q * 4 + rc
         rows = [part[:, h * 128:(h + 1) * 128] for part in (hi, mid, lo) for h in range(4)]
         rows.append(jnp.zeros((4, 128), F32))
         for h in range(4):
-            out[dest, h * 128:(h + 1) * 128, :] = o[:, h * 128:(h + 1) * 128]
-        out[dest, 512:528, :] = jnp.concatenate(rows, axis=0).astype(BF)
+            out[tile, h * 128:(h + 1) * 128, :] = o[:, h * 128:(h + 1) * 128]
+        out[tile, 512:528, :] = jnp.concatenate(rows, axis=0).astype(BF)
         return carry
 
     lax.fori_loop(0, 8, one_tile, 0)
@@ -164,22 +151,30 @@
             copies[copy, rows, :] = total
 
 
-def student_kernel(place, weight_t, att, kept, received, teacher, out):
-    part = pl.program_id(0)
-
-    @pl.when(part == 0)
-    def _():
-        for chip in range(8):
-            first = (chip % 4 * 4 + chip // 4 * 2) * 256
-            for i in range(4):
-                out[chip, 768 + i * 32:800 + i * 32, :] = teacher[:, first + i * 128:first + (i + 1) * 128]
-
-    source = part ^ place[0]
-    hidden = jnp.where(source < 2, kept[source % 2].astype(F32), received[source % 2].astype(F32))
-    mixed = jnp.dot(weight_t[...], att[...].reshape(2048, 128), preferred_element_type=F32)
-    student = (hidden + mixed).astype(BF)
-    for copy in range(out.shape[0]):
-        out[copy, pl.ds(pl.multiple_of(part * 192, 64), 192), :] = student
+def student_kernel(place, gathered, att, teacher, out, weights, hidden, sem):
+    copies = []
+    own_rows = pl.ds(pl.multiple_of(2048 + place[0] * 128, 128), 128)
+    hidden_copy = pltpu.make_async_copy(gathered.at[:, own_rows], hidden, sem.at[4])
+    for part in range(4):
+        rows = pl.ds(part * 192, 192)
+        copies.append(pltpu.make_async_copy(gathered.at[rows, pl.ds(0, 2048)], weights.at[rows], sem.at[part]))
+    copies[0].start()
+    hidden_copy.start()
+    for copy in copies[1:]:
+        copy.start()
+    for chip in range(8):
+        first = (chip % 4 * 4 + chip // 4 * 2) * 256
+        for i in range(4):
+            out[chip, 768 + i * 32:800 + i * 32, :] = teacher[:, first + i * 128:first + (i + 1) * 128]
+    att_all = att[...].reshape(2048, 128)
+    hidden_copy.wait()
+    for part in range(4):
+        copies[part].wait()
+        rows = slice(part * 192, (part + 1) * 192)
+        mixed = jnp.dot(weights[rows, :], att_all, preferred_element_type=F32)
+        student = (hidden[rows, :].astype(F32) + mixed).astype(BF)
+        for copy in range(8):
+            out[copy, rows, :] = student
 
 
 def projected(student, projector_t):
@@ -246,6 +241,7 @@
 VMEM = pl.BlockSpec(memory_space=pltpu.VMEM)
 SMEM = pl.BlockSpec(memory_space=pltpu.SMEM)
 ANY = pl.BlockSpec(memory_space=pl.ANY)
+HBM = pl.BlockSpec(memory_space=pltpu.HBM)
 
 
 def call(kernel, out_shape, specs, operands, limit, flops=0, scratch=()):
@@ -265,83 +261,60 @@
     return jax.ShapeDtypeStruct(dims, dtype)
 
 
-def start(place, keys, values, docs, hidden_t, queries):
+def start(place, keys, values, docs, queries):
     def block(*dims):
         return pl.BlockSpec(dims, lambda i, place: (0,) * len(dims))
 
     picked = pl.BlockSpec((128, 128), lambda i, place: (place[0], place[1]))
-    outs = [(4, 272, 128), (16, 128), (2, 192, 128), (2, 192, 128), (512, 128)]
+    outs = [(4, 272, 128), (528, 128)]
     return pl.pallas_call(
         start_kernel,
         grid_spec=pltpu.PrefetchScalarGridSpec(
             num_scalar_prefetch=1,
             grid=(1,),
-            in_specs=[picked, picked, block(4, 128), block(192, 512), block(512, 128)],
+            in_specs=[picked, picked, block(4, 128), block(512, 128)],
             out_specs=[block(*dims) for dims in outs],
         ),
         out_shape=[shape(*dims) for dims in outs],
-    )(place, keys, values, docs, hidden_t, queries)
-
-
-def student_of(place, weight_t, att, kept, received, teacher):
-    def block(*dims):
-        return pl.BlockSpec(dims, lambda i: (0,) * len(dims))
-
-    return pl.pallas_call(
-        student_kernel,
-        grid=(4,),
-        out_shape=shape(8, 896, 128),
-        in_specs=[
-            SMEM, pl.BlockSpec((192, 2048), lambda i: (i, 0)), block(4, 512, 128), block(2, 192, 128), block(2, 192, 128), block(32, 4096),
-        ],
-        out_specs=block(8, 896, 128),
-        compiler_params=pltpu.CompilerParams(vmem_limit_bytes=24 * 1024 * 1024),
-    )(place, weight_t, att, kept, received, teacher)
+    )(place, keys, values, docs, queries)
 
 
 def on_device(queries, keys, values, doc_ids, hidden, out_weight, projector, teacher):
-    zl, yl, xl, c = lax.axis_index("zl"), lax.axis_index("yl"), lax.axis_index("xl"), lax.axis_index("c")
+    zl, yl, c = lax.axis_index("zl"), lax.axis_index("yl"), lax.axis_index("c")
+    j = lax.axis_index("xl") * 2 + c
     z = lax.axis_index("zh") * 4 + zl
     g = lax.axis_index("yh") * 2 + lax.axis_index("xh")
     swap = [(0, 1), (1, 0)]
-    place = jnp.stack([xl * 2 + c, g, c, xl, yl, z, zl]).astype(jnp.int32)
+    place = jnp.stack([j, g, c, c, yl, z, zl]).astype(jnp.int32)
 
     def from_z(x, shift):
         return lax.ppermute(x, ("zh", "zl"), [((i + shift) % 16, i) for i in range(16)])
 
     docs = doc_ids.reshape(4, 128)
-    packed, doc_rows, hidden_kept, hidden_sent, q_first = start(place, keys, values, docs, hidden.T, queries)
+    packed, q_rows = start(place, keys, values, docs, queries)
     kv_own = lax.all_to_all(packed, "zh", 0, 0)
     kv_below, kv_above = from_z(kv_own, -1), from_z(kv_own, 1)
     kv_low, kv_high = from_z(kv_own[0:2], -2), from_z(kv_own[2:4], 2)
 
-    q_two = jnp.concatenate([q_first, lax.ppermute(q_first, "c", swap)], axis=0)
-    q_own = jnp.concatenate([q_two, lax.ppermute(q_two, "xl", swap), doc_rows], axis=0)
-    q_other = lax.ppermute(q_own, "yl", swap)
-    half = shape(2, 192, 128)
-    hidden_kept, hidden_sent = call(
-        turn_kernel, [half, half], [SMEM, VMEM, VMEM], (place, hidden_kept, lax.ppermute(hidden_sent, "c", swap)), 8
-    )
-    hidden_received = lax.ppermute(hidden_sent, "xl", swap)
-
-    weight_t = lax.all_gather(out_weight.T, GROUP, axis=0, tiled=True)
+    q_all = lax.all_gather(q_rows, OCTET, axis=0)
+    gathered = lax.all_gather(jnp.concatenate([out_weight.T, hidden.T], axis=1), GROUP, axis=0, tiled=True)
     projector_t = projector.T
 
     partial = call(
         attend_kernel,
         shape(8, 528, 128),
-        [SMEM] + [ANY] * 7 + [VMEM] + [ANY] * 3,
-        (place, kv_own, kv_below, kv_above, kv_low, kv_high, q_own, q_other, docs, hidden_kept, hidden_received, projector_t),
+        [SMEM] + [ANY] * 5 + [HBM, ANY],
+        (place, kv_own, kv_below, kv_above, kv_low, kv_high, q_all, projector_t),
         40,
         2 * 10 ** 10,
         scratch=[
             pltpu.VMEM((4, 4, 272, 128), BF),
-            pltpu.VMEM((2, 2064, 128), BF),
+            pltpu.VMEM((8, 528, 128), BF),
             pltpu.VMEM((128, 2048), BF),
             pltpu.VMEM((4, 512, 512), F32),
             pltpu.VMEM((24, 128), jnp.int32),
             pltpu.SMEM((24, 128), jnp.int32),
-            pltpu.SemaphoreType.DMA((8,)),
+            pltpu.SemaphoreType.DMA((7,)),
         ],
     )
     att_rows, att_copies = call(
@@ -352,7 +325,14 @@
     attended = jnp.transpose(att_head, (0, 2, 1)).reshape(512, 128)
 
     att_all = lax.all_to_all(att_copies, HEADSETS, 0, 0)
-    student = student_of(place, weight_t, att_all, hidden_kept, hidden_received, teacher)
+    student = call(
+        student_kernel,
+        shape(8, 896, 128),
+        [SMEM, HBM, VMEM, VMEM],
+        (place, gathered, att_all, teacher),
+        24,
+        scratch=[pltpu.VMEM((768, 2048), BF), pltpu.VMEM((768, 128), BF), pltpu.SemaphoreType.DMA((5,))],
+    )
     own = lax.all_to_all(student, CHIPS, 0, 0)
     other = lax.ppermute(own, "c", swap)
 

time: 249 us -> 241 us (0.968)
  blocking collectives: 60 us -> 111 us
  starting transfers between devices: 89.6 us -> 44.4 us
  waiting for transfers between devices: 47.8 us -> 35.6 us
    all_to_all x0 -> x1, blocking collectives: none -> 34.2 us  [on_device(): kv_own = lax.all_to_all(packed, 'zh', 0, 0)]
    all_to_all x1, blocking collectives: 18.7 us -> 35.5 us  [on_device(): lax.all_to_all(partial, OCTET, 0, 0)]
    ppermute x5 -> x0, starting transfers between devices: 16.4 us -> none  [the longest x1 4.63 us: on_device(): lax.ppermute(hidden_sent, 'c', swap)]
    all_to_all x1 -> x0, starting transfers between devices: 13 us -> none  [on_device(): kv_own = lax.all_to_all(packed, 'zh', 0, 0)]
    ppermute x5 -> x0, waiting for transfers between devices: 9.42 us -> none  [the longest x1 8.42 us: on_device(): lax.ppermute(q_two, 'xl', swap)]
    all_to_all x1, starting transfers between devices: 17 us -> 9.04 us  [on_device(): lax.all_to_all(near, ('zh', 'yl'), 0, 0)]
    ppermute x8, starting transfers between devices: 33.5 us -> 25.8 us  [from_z(): lax.ppermute(x, ('zh', 'zl'), [((i + shift) % 16, i) for i in range(16)])]
    ppermute x8, waiting for transfers between devices: 12.1 us -> 7.57 us  [from_z(): lax.ppermute(x, ('zh', 'zl'), [((i + shift) % 16, i) for i in range(16)])]
  transfers between devices with their start and end apart: 18 -> 13, of which waited for: 7 -> 4; matrix products, arithmetic and copies ran while one was open for 2% -> 2% of each run, Pallas kernels for 7% -> 5%
where the time goes in v5:
time: 241 us; the launch traced here: 240 us
  blocking collectives  111 us (46%)
  starting transfers between devices  44.4 us (18%)
  waiting for transfers between devices  35.6 us (15%)
  Pallas kernels  22.2 us (9%)
  between operations  14.2 us (6%)
  local copies, waits for them, and re-layouts  10.7 us (4%)
    all_to_all x1, blocking collectives, on_device(): lax.all_to_all(partial, OCTET, 0, 0)  35.5 us
    all_to_all x1, blocking collectives, on_device(): kv_own = lax.all_to_all(packed, 'zh', 0, 0)  34.2 us
    all_to_all x1, blocking collectives, on_device(): own = lax.all_to_all(student, CHIPS, 0, 0)  25.9 us
    ppermute x8, starting transfers between devices, from_z(): lax.ppermute(x, ('zh', 'zl'), [((i + shift) % 16, i) for i in range(16)])  25.8 us
    all_to_all x1, waiting for transfers between devices, on_device(): lax.all_to_all(near, ('zh', 'yl'), 0, 0)  25.3 us
    pallas_call x9, Pallas kernels, call(): pl.pallas_call(kernel, out_shape=out_shape, in_specs=specs, out_specs=VME...  19.7 us
    all_to_all x1, blocking collectives, on_device(): att_all = lax.all_to_all(att_copies, HEADSETS, 0, 0)  15.5 us
    unnamed x25, local copies, waits for them, and re-layouts  9.34 us
  transfers between devices with their start and end apart: 13, of which 4 were waited for; matrix products, arithmetic and copies ran while one was open for 2% of the time, Pallas kernels for 5%

profile of v5, /device:TPU:73, one launch (start us, length us, event | category | flops | bytes accessed | tf_op | source)
XLA Modules:
  0.0 240.2 jit_solution(5689169634346291317)
XLA Ops:
  7.8 2.4 %shard_map.95 = (bf16[4,272,128]{2,1,0:T(8,128)(2,1)}, bf16[528,128]{1,0:T(8,128)(2,1)}) custom-call(s32[7]{0:T(128)} %stack.28.place, bf16[512,512]{1,0:T(8,128)(2,1)} %keys.1, bf16[512,512]{1,0:T(8,128)(2,1)} %values.1, s32[4,128]{1,0:T(4,128)} %bitcast.22, bf16[512,128]{1,0:T(8,128)(2,1)} %queries.1), custom_call_target="tpu_custom_call" | custom-call | tf_op jit(solution)/shard_map/pallas_call | solution.py:270
  10.3 2.0 pad_maximum_fusion
  12.3 34.2 %all_to_all.30.kv0 = bf16[4,272,128]{2,1,0:T(8,128)(2,1)S(1)} all-to-all(bf16[4,272,128]{2,1,0:T(8,128)(2,1)S(1)} %copy-done.11), channel_id=1, replica_groups=mesh['zh'=4,'zl'=4,'yl'=2,'yh'=2,'xh'=2,'xl'=2,'c'=2] {'zh'}, dimensions={0} | all-to-all | bytes 557056 | tf_op jit(solution)/shard_map/all_to_all | solution.py:295
  46.5 2.0 collective-permute-start
  48.6 3.4 %collective-permute-start.1 = (bf16[4,272,128]{2,1,0:T(8,128)(2,1)S(1)}, bf16[4,272,128]{2,1,0:T(8,128)(2,1)S(1)}, u32[]{:S(2)}, u32[]{:S(2)}) collective-permute-start(bf16[4,272,128]{2,1,0:T(8,128)(2,1)S(1)} %all_to_all.30.kv0), channel_id=1, source_target_pairs={{32,0},{64,32},{96,64},{128,96},{160,128},{192,160},{224,192},{256... | collective-permute-start | bytes 835592 | tf_op jit(solution)/shard_map/ppermute | solution.py:291
  52.0 2.0 collective-permute-start.2
  54.0 4.2 %collective-permute-start.3 = (bf16[2,272,128]{2,1,0:T(8,128)(2,1)S(1)}, bf16[2,272,128]{2,1,0:T(8,128)(2,1)S(1)}, u32[]{:S(2)}, u32[]{:S(2)}) collective-permute-start(bf16[2,272,128]{2,1,0:T(8,128)(2,1)S(1)} %get-tuple-element.20), channel_id=1, source_target_pairs={{64,0},{96,32},{128,64},{160,96},{192,128},{224,160},{256,192},{28... | collective-permute-start | bytes 417800 | tf_op jit(solution)/shard_map/ppermute | solution.py:291
  58.2 1.7 copy.10
  59.9 2.0 collective-permute-done.3.kv3_high
  62.7 1.3 copy-done.7
  64.0 1.0 copy-done.9
  65.0 9.0 %shard_map.96 = bf16[8,528,128]{2,1,0:T(8,128)(2,1)S(1)} custom-call(s32[7]{0:T(128)S(1)} %copy-done.6, bf16[4,272,128]{2,1,0:T(8,128)(2,1)S(1)} %all_to_all.30.kv0, bf16[4,272,128]{2,1,0:T(8,128)(2,1)S(1)} %collective-permute-done.kv1, bf16[4,272,128]{2,1,0:T(8,128)(2,1)S(1)} %copy-done.9, bf16[2,272,128]{2,1,0:T(8,128)(2,1)S(1)} %collective-permute-done.2.kv3_low, ...), custom_call_target="tpu_custom_call" | custom-call | flops 20000000000 | bytes 4194304 | tf_op jit(solution)/shard_map/pallas_call | solution.py:249
  74.0 35.5 %all_to_all.31.parts = bf16[8,528,128]{2,1,0:T(8,128)(2,1)S(1)} all-to-all(bf16[8,528,128]{2,1,0:T(8,128)(2,1)S(1)} %shard_map.96), channel_id=1, replica_groups=mesh['zh'=4,'zl'=4,'yl'=2,'yh'=2,'xh'=2,'xl'=2,'c'=2] {'yl','xl','c'}, dimensions={0} | all-to-all | bytes 2162688 | tf_op jit(solution)/shard_map/all_to_all | solution.py:321
  110.4 15.5 %all_to_all.32.att = bf16[4,512,128]{2,1,0:T(8,128)(2,1)S(1)} all-to-all(bf16[4,512,128]{2,1,0:T(8,128)(2,1)S(1)} %get-tuple-element.13), channel_id=1, replica_groups=mesh['zh'=4,'zl'=4,'yl'=2,'yh'=2,'xh'=2,'xl'=2,'c'=2] {'yh','xh'}, dimensions={0} | all-to-all | bytes 1048576 | tf_op jit(solution)/shard_map/all_to_all | solution.py:327
  126.0 2.1 copy-done.2
  128.1 2.4 %shard_map.98 = bf16[8,896,128]{2,1,0:T(8,128)(2,1)S(1)} custom-call(s32[7]{0:T(128)S(1)} %copy-done.6, bf16[768,2560]{1,0:T(8,128)(2,1)S(1)} %copy-done.2, bf16[4,512,128]{2,1,0:T(8,128)(2,1)S(1)} %all_to_all.32.att, bf16[32,4096]{1,0:T(8,128)(2,1)S(1)} %copy-done.5), custom_call_target="tpu_custom_call" | custom-call | bytes 4194304 | tf_op jit(solution)/shard_map/pallas_call | solution.py:249
  130.5 25.9 %all_to_all.33.own = bf16[8,896,128]{2,1,0:T(8,128)(2,1)S(1)} all-to-all(bf16[8,896,128]{2,1,0:T(8,128)(2,1)S(1)} %shard_map.98), channel_id=1, replica_groups=mesh['zh'=4,'zl'=4,'yl'=2,'yh'=2,'xh'=2,'xl'=2,'c'=2] {'xl','yh','xh'}, dimensions={0} | all-to-all | bytes 3670016 | tf_op jit(solution)/shard_map/all_to_all | solution.py:336
  156.4 5.0 %collective-permute-start.4 = (bf16[8,896,128]{2,1,0:T(8,128)(2,1)S(1)}, bf16[8,896,128]{2,1,0:T(8,128)(2,1)S(1)}, u32[]{:S(2)}, u32[]{:S(2)}) collective-permute-start(bf16[8,896,128]{2,1,0:T(8,128)(2,1)S(1)} %all_to_all.33.own), channel_id=1, source_target_pairs={{0,1},{1,0},{2,3},{3,2},{4,5},{5,4},{6,7},{7,6},{8,9},{9,8},{10,11... | collective-permute-start | bytes 5505032 | tf_op jit(solution)/shard_map/ppermute | solution.py:337
  162.1 2.7 %collective-permute-done.4.other = bf16[8,896,128]{2,1,0:T(8,128)(2,1)S(1)} collective-permute-done((bf16[8,896,128]{2,1,0:T(8,128)(2,1)S(1)}, bf16[8,896,128]{2,1,0:T(8,128)(2,1)S(1)}, u32[]{:S(2)}, u32[]{:S(2)}) %collective-permute-start.4) | collective-permute-done | bytes 1835040 | tf_op jit(solution)/shard_map/ppermute | solution.py:337
  164.8 2.4 %shard_map.100 = (bf16[512,256]{1,0:T(8,128)(2,1)S(1)}, bf16[4,96,256]{2,1,0:T(8,128)(2,1)}, bf16[4,96,256]{2,1,0:T(8,128)(2,1)}) custom-call(s32[7]{0:T(128)S(1)} %copy-done.6, bf16[8,896,128]{2,1,0:T(8,128)(2,1)S(1)} %all_to_all.33.own, bf16[8,896,128]{2,1,0:T(8,128)(2,1)S(1)} %collective-permute-done.4.other, bf16[256,3072]{1,0:T(8,128)(2,1)S(1)} %bitcast.16, ...), custom_call_target="tpu_custom_call" | custom-call | flops 800000000 | bytes 4194304 | tf_op jit(solution)/shard_map/pallas_call | solution.py:249
  167.2 1.9 shard_map.102
  169.1 1.9 collective-permute-start.5
  171.0 3.3 %collective-permute-start.6 = (bf16[8,96,256]{2,1,0:T(8,128)(2,1)S(1)}, bf16[8,96,256]{2,1,0:T(8,128)(2,1)S(1)}, u32[]{:S(2)}, u32[]{:S(2)}) collective-permute-start(bf16[8,96,256]{2,1,0:T(8,128)(2,1)S(1)} %get-tuple-element.16), channel_id=1, source_target_pairs={{32,0},{64,32},{96,64},{128,96},{160,128},{192,160},{224,192},{256... | collective-permute-start | bytes 1179656 | tf_op jit(solution)/shard_map/ppermute | solution.py:291
  174.4 7.0 %collective-permute-start.7 = (bf16[4,96,256]{2,1,0:T(8,128)(2,1)}, bf16[4,96,256]{2,1,0:T(8,128)(2,1)S(1)}, u32[]{:S(2)}, u32[]{:S(2)}) collective-permute-start(bf16[4,96,256]{2,1,0:T(8,128)(2,1)} %get-tuple-element.17), channel_id=1, source_target_pairs={{448,0},{480,32},{0,64},{32,96},{64,128},{96,160},{128,192},{160,2... | collective-permute-start | bytes 589832 | tf_op jit(solution)/shard_map/ppermute | solution.py:291
  181.4 1.9 collective-permute-start.8
  183.3 4.5 %all-to-all-start.5 = ((bf16[4,128,128]{2,1,0:T(8,128)(2,1)}), bf16[4,128,128]{2,1,0:T(8,128)(2,1)S(1)}, u32[]{:S(2)}, u32[]{:S(2)}) async-start(bf16[4,128,128]{2,1,0:T(8,128)(2,1)} %bitcast.11), calls=%async_computation.5 | async-start | bytes 262144 | tf_op jit(solution)/shard_map/all_to_all | solution.py:324
  187.8 1.5 copy-done.1
  189.3 0.9 copy-done.4
  191.2 5.5 %collective-permute-done.8.far_above = bf16[4,96,256]{2,1,0:T(8,128)(2,1)S(1)} collective-permute-done((bf16[4,96,256]{2,1,0:T(8,128)(2,1)}, bf16[4,96,256]{2,1,0:T(8,128)(2,1)S(1)}, u32[]{:S(2)}, u32[]{:S(2)}) %collective-permute-start.8) | collective-permute-done | bytes 196640 | tf_op jit(solution)/shard_map/ppermute | solution.py:291
  196.7 1.0 shard_map.103
  197.6 9.0 %all-to-all-start.4 = ((bf16[8,96,256]{2,1,0:T(8,128)(2,1)}), bf16[8,96,256]{2,1,0:T(8,128)(2,1)S(1)}, u32[]{:S(2)}, u32[]{:S(2)}) async-start(bf16[8,96,256]{2,1,0:T(8,128)(2,1)} %shard_map.103), calls=%async_computation.4 | async-start | bytes 786432 | tf_op jit(solution)/shard_map/all_to_all | solution.py:355
  207.5 25.3 %all-to-all-done.4.terms = bf16[8,96,256]{2,1,0:T(8,128)(2,1)S(1)} async-done(((bf16[8,96,256]{2,1,0:T(8,128)(2,1)}), bf16[8,96,256]{2,1,0:T(8,128)(2,1)S(1)}, u32[]{:S(2)}, u32[]{:S(2)}) %all-to-all-start.4) | async-done | bytes 393248 | tf_op jit(solution)/shard_map/all_to_all | solution.py:355
  (39 shorter events, 5.4 us)
Async XLA Ops:
  7.2 3.2 %copy-start.10 = (bf16[2048,192]{0,1:T(8,128)(2,1)S(1)}, bf16[2048,192]{0,1:T(8,128)(2,1)}, u32[]{:S(2)}) copy-start(bf16[2048,192]{0,1:T(8,128)(2,1)} %param.13) | copy-start | bytes 2359300
  7.2 55.5 %all-gather.6.cloned.1.call-start = ((), (), s32[]{:S(2)}) async-start(), calls=%async_computation.7 | async-start | bytes 1216512 | tf_op jit(solution)/shard_map/all_gather | solution.py:299
  10.2 2.1 copy-start.11
  10.3 115.7 %all-gather.4.cloned.1.call-start = ((), (), s32[]{:S(2)}) async-start(), calls=%async_computation.6 | async-start | bytes 4915200 | tf_op jit(solution)/shard_map/all_gather | solution.py:300
  46.5 16.2 %copy-start.6 = (s32[7]{0:T(128)S(1)}, s32[7]{0:T(128)}, u32[]{:S(2)}) copy-start(s32[7]{0:T(128)} %stack.28.place) | copy-start | bytes 88
  46.5 15.4 %collective-permute-start = (bf16[4,272,128]{2,1,0:T(8,128)(2,1)S(1)}, bf16[4,272,128]{2,1,0:T(8,128)(2,1)S(1)}, u32[]{:S(2)}, u32[]{:S(2)}) collective-permute-start(bf16[4,272,128]{2,1,0:T(8,128)(2,1)S(1)} %all_to_all.30.kv0), channel_id=1, source_target_pairs={{480,0},{0,32},{32,64},{64,96},{96,128},{128,160},{160,192},{192,2... | collective-permute-start | bytes 835592 | tf_op jit(solution)/shard_map/ppermute | solution.py:291
  48.6 13.4 %collective-permute-start.1 = (bf16[4,272,128]{2,1,0:T(8,128)(2,1)S(1)}, bf16[4,272,128]{2,1,0:T(8,128)(2,1)S(1)}, u32[]{:S(2)}, u32[]{:S(2)}) collective-permute-start(bf16[4,272,128]{2,1,0:T(8,128)(2,1)S(1)} %all_to_all.30.kv0), channel_id=1, source_target_pairs={{32,0},{64,32},{96,64},{128,96},{160,128},{192,160},{224,192},{256... | collective-permute-start | bytes 835592 | tf_op jit(solution)/shard_map/ppermute | solution.py:291
  52.0 7.9 %collective-permute-start.2 = (bf16[2,272,128]{2,1,0:T(8,128)(2,1)S(1)}, bf16[2,272,128]{2,1,0:T(8,128)(2,1)S(1)}, u32[]{:S(2)}, u32[]{:S(2)}) collective-permute-start(bf16[2,272,128]{2,1,0:T(8,128)(2,1)S(1)} %get-tuple-element.21), channel_id=1, source_target_pairs={{448,0},{480,32},{0,64},{32,96},{64,128},{96,160},{128,192},{160,2... | collective-permute-start | bytes 417800 | tf_op jit(solution)/shard_map/ppermute | solution.py:291
  54.0 8.0 %collective-permute-start.3 = (bf16[2,272,128]{2,1,0:T(8,128)(2,1)S(1)}, bf16[2,272,128]{2,1,0:T(8,128)(2,1)S(1)}, u32[]{:S(2)}, u32[]{:S(2)}) collective-permute-start(bf16[2,272,128]{2,1,0:T(8,128)(2,1)S(1)} %get-tuple-element.20), channel_id=1, source_target_pairs={{64,0},{96,32},{128,64},{160,96},{192,128},{224,160},{256,192},{28... | collective-permute-start | bytes 417800 | tf_op jit(solution)/shard_map/ppermute | solution.py:291
  62.0 0.7 copy-start.8
  62.7 1.3 copy-start.7
  64.0 1.0 copy-start.9
  74.0 52.0 %copy-start.5 = (bf16[32,4096]{1,0:T(8,128)(2,1)S(1)}, bf16[32,4096]{1,0:T(8,128)(2,1)}, u32[]{:S(2)}) copy-start(bf16[32,4096]{1,0:T(8,128)(2,1)} %teacher.1) | copy-start | bytes 786436
  126.0 2.1 copy-start.2
  156.4 8.4 %collective-permute-start.4 = (bf16[8,896,128]{2,1,0:T(8,128)(2,1)S(1)}, bf16[8,896,128]{2,1,0:T(8,128)(2,1)S(1)}, u32[]{:S(2)}, u32[]{:S(2)}) collective-permute-start(bf16[8,896,128]{2,1,0:T(8,128)(2,1)S(1)} %all_to_all.33.own), channel_id=1, source_target_pairs={{0,1},{1,0},{2,3},{3,2},{4,5},{5,4},{6,7},{7,6},{8,9},{9,8},{10,11... | collective-permute-start | bytes 5505032 | tf_op jit(solution)/shard_map/ppermute | solution.py:337
  164.8 2.4 %copy-start = (bf16[8,896,128]{2,1,0:T(8,128)(2,1)}, bf16[8,896,128]{2,1,0:T(8,128)(2,1)S(1)}, u32[]{:S(2)}) copy-start(bf16[8,896,128]{2,1,0:T(8,128)(2,1)S(1)} %collective-permute-done.4.other) | copy-start | bytes 5505028
  167.2 1.9 copy-start.3
  169.1 27.6 %collective-permute-start.5 = (bf16[8,96,256]{2,1,0:T(8,128)(2,1)}, bf16[8,96,256]{2,1,0:T(8,128)(2,1)S(1)}, u32[]{:S(2)}, u32[]{:S(2)}) collective-permute-start(bf16[8,96,256]{2,1,0:T(8,128)(2,1)} %get-tuple-element.15), channel_id=1, source_target_pairs={{480,0},{0,32},{32,64},{64,96},{96,128},{128,160},{160,192},{192,2... | collective-permute-start | bytes 1179656 | tf_op jit(solution)/shard_map/ppermute | solution.py:291
  171.0 25.7 %collective-permute-start.6 = (bf16[8,96,256]{2,1,0:T(8,128)(2,1)S(1)}, bf16[8,96,256]{2,1,0:T(8,128)(2,1)S(1)}, u32[]{:S(2)}, u32[]{:S(2)}) collective-permute-start(bf16[8,96,256]{2,1,0:T(8,128)(2,1)S(1)} %get-tuple-element.16), channel_id=1, source_target_pairs={{32,0},{64,32},{96,64},{128,96},{160,128},{192,160},{224,192},{256... | collective-permute-start | bytes 1179656 | tf_op jit(solution)/shard_map/ppermute | solution.py:291
  174.4 16.8 %collective-permute-start.7 = (bf16[4,96,256]{2,1,0:T(8,128)(2,1)}, bf16[4,96,256]{2,1,0:T(8,128)(2,1)S(1)}, u32[]{:S(2)}, u32[]{:S(2)}) collective-permute-start(bf16[4,96,256]{2,1,0:T(8,128)(2,1)} %get-tuple-element.17), channel_id=1, source_target_pairs={{448,0},{480,32},{0,64},{32,96},{64,128},{96,160},{128,192},{160,2... | collective-permute-start | bytes 589832 | tf_op jit(solution)/shard_map/ppermute | solution.py:291
  181.4 15.3 %collective-permute-start.8 = (bf16[4,96,256]{2,1,0:T(8,128)(2,1)}, bf16[4,96,256]{2,1,0:T(8,128)(2,1)S(1)}, u32[]{:S(2)}, u32[]{:S(2)}) collective-permute-start(bf16[4,96,256]{2,1,0:T(8,128)(2,1)} %get-tuple-element.18), channel_id=1, source_target_pairs={{64,0},{96,32},{128,64},{160,96},{192,128},{224,160},{256,192},{28... | collective-permute-start | bytes 589832 | tf_op jit(solution)/shard_map/ppermute | solution.py:291
  183.3 14.3 %all-to-all-start.5 = ((bf16[4,128,128]{2,1,0:T(8,128)(2,1)}), bf16[4,128,128]{2,1,0:T(8,128)(2,1)S(1)}, u32[]{:S(2)}, u32[]{:S(2)}) async-start(bf16[4,128,128]{2,1,0:T(8,128)(2,1)} %bitcast.11), calls=%async_computation.5 | async-start | bytes 262144 | tf_op jit(solution)/shard_map/all_to_all | solution.py:324
  187.8 1.5 copy-start.1
  189.3 0.9 copy-start.4
  197.6 35.1 %all-to-all-start.4 = ((bf16[8,96,256]{2,1,0:T(8,128)(2,1)}), bf16[8,96,256]{2,1,0:T(8,128)(2,1)S(1)}, u32[]{:S(2)}, u32[]{:S(2)}) async-start(bf16[8,96,256]{2,1,0:T(8,128)(2,1)} %shard_map.103), calls=%async_computation.4 | async-start | bytes 786432 | tf_op jit(solution)/shard_map/all_to_all | solution.py:355
Sparse Core Ops, SparseCore 0:
  10.4 33.8 all-gather.5
  46.4 64.3 all-gather.3

commit v6 on v5

--- a/solution.py
+++ b/solution.py
@@ -23,23 +23,22 @@
 BLOCKS = 4
 
 
-def start_kernel(place, keys, values, docs, queries, packed, q_rows):
+def start_kernel(place, keys, values, docs, packed, doc_rows):
     rows = jnp.concatenate([docs[...].astype(F32), jnp.zeros((12, 128), F32)], axis=0).astype(BF)
     for copy in range(4):
         packed[copy, 0:128, :] = keys[...]
         packed[copy, 128:256, :] = values[...]
         packed[copy, 256:272, :] = rows
-    q_rows[0:512, :] = queries[...]
-    q_rows[512:528, :] = rows
-
-
-def attend_kernel(place, kv0, kv1, kv2, kv3_low, kv3_high, queries, early, out, kv, q_all, v_turned, s_buf, info_v, info, sem):
+    doc_rows[...] = rows
+
+
+def attend_kernel(place, kv0, kv1, kv2, kv3_low, kv3_high, q_own, q_other, early, out, kv, q_all, v_turned, s_buf, info_v, info, sem):
     j, yl, z = place[0], place[4], place[5]
     copies = [
         pltpu.make_async_copy(src, dst, sem.at[i])
         for i, (src, dst) in enumerate((
             (kv0, kv.at[0]), (kv1, kv.at[1]), (kv2, kv.at[2]), (kv3_low, kv.at[3, pl.ds(0, 2)]), (kv3_high, kv.at[3, pl.ds(2, 2)]),
-            (queries, q_all),
+            (q_own, q_all.at[0]), (q_other, q_all.at[1]),
         ))
     ]
     for copy in copies:
@@ -47,7 +46,7 @@
     for copy in copies:
         copy.wait()
     for side in range(2):
-        info_v[16 + 4 * side:20 + 4 * side, :] = q_all[4 * side, 512:528, :].astype(F32)[0:4].astype(jnp.int32)
+        info_v[16 + 4 * side:20 + 4 * side, :] = q_all[side, 2048:2064, :].astype(F32)[0:4].astype(jnp.int32)
     block_docs = []
     for ch in range(4):
         for i in range(BLOCKS):
@@ -60,7 +59,7 @@
         below = jnp.sum((block_docs < d).astype(F32), axis=1, keepdims=True)
         counts = jnp.where(lane == d, below, counts)
     info_v[0:16, :] = counts.astype(jnp.int32)
-    to_scalars = pltpu.make_async_copy(info_v, info, sem.at[6])
+    to_scalars = pltpu.make_async_copy(info_v, info, sem.at[7])
     to_scalars.start()
     for ch in range(4):
         for i in range(BLOCKS):
@@ -71,9 +70,11 @@
     row_iota = lax.broadcasted_iota(jnp.int32, (1, 512), 1) % 128
 
     def one_tile(tile, carry):
-        yl_q, rc = tile // 4, tile % 4
+        side, rc = tile // 4, tile % 4
+        yl_q = jnp.where(side == 0, yl, 1 - yl)
+        dest = yl_q * 4 + rc
         row0 = pl.multiple_of(rc * 128, 128)
-        q = jnp.concatenate([q_all[yl_q * 4 + h, pl.ds(row0, 128), :] for h in range(4)], axis=0)
+        q = jnp.concatenate([q_all[side, pl.ds(pl.multiple_of((h ^ j) * 512, 512) + row0, 128), :] for h in range(4)], axis=0)
         row_docs = jnp.concatenate([info_v[pl.ds(16 + tile, 1), :]] * 4, axis=1)
         first, last = info[16 + tile, 0], info[16 + tile, 127]
         q_min = (2 * z + yl_q) * 512 + row0
@@ -129,8 +130,8 @@
         rows = [part[:, h * 128:(h + 1) * 128] for part in (hi, mid, lo) for h in range(4)]
         rows.append(jnp.zeros((4, 128), F32))
         for h in range(4):
-            out[tile, h * 128:(h + 1) * 128, :] = o[:, h * 128:(h + 1) * 128]
-        out[tile, 512:528, :] = jnp.concatenate(rows, axis=0).astype(BF)
+            out[dest, h * 128:(h + 1) * 128, :] = o[:, h * 128:(h + 1) * 128]
+        out[dest, 512:528, :] = jnp.concatenate(rows, axis=0).astype(BF)
         return carry
 
     lax.fori_loop(0, 8, one_tile, 0)
@@ -261,22 +262,22 @@
     return jax.ShapeDtypeStruct(dims, dtype)
 
 
-def start(place, keys, values, docs, queries):
+def start(place, keys, values, docs):
     def block(*dims):
         return pl.BlockSpec(dims, lambda i, place: (0,) * len(dims))
 
     picked = pl.BlockSpec((128, 128), lambda i, place: (place[0], place[1]))
-    outs = [(4, 272, 128), (528, 128)]
+    outs = [(4, 272, 128), (16, 128)]
     return pl.pallas_call(
         start_kernel,
         grid_spec=pltpu.PrefetchScalarGridSpec(
             num_scalar_prefetch=1,
             grid=(1,),
-            in_specs=[picked, picked, block(4, 128), block(512, 128)],
+            in_specs=[picked, picked, block(4, 128)],
             out_specs=[block(*dims) for dims in outs],
         ),
         out_shape=[shape(*dims) for dims in outs],
-    )(place, keys, values, docs, queries)
+    )(place, keys, values, docs)
 
 
 def on_device(queries, keys, values, doc_ids, hidden, out_weight, projector, teacher):
@@ -291,30 +292,32 @@
         return lax.ppermute(x, ("zh", "zl"), [((i + shift) % 16, i) for i in range(16)])
 
     docs = doc_ids.reshape(4, 128)
-    packed, q_rows = start(place, keys, values, docs, queries)
+    packed, doc_rows = start(place, keys, values, docs)
     kv_own = lax.all_to_all(packed, "zh", 0, 0)
     kv_below, kv_above = from_z(kv_own, -1), from_z(kv_own, 1)
     kv_low, kv_high = from_z(kv_own[0:2], -2), from_z(kv_own[2:4], 2)
 
-    q_all = lax.all_gather(q_rows, OCTET, axis=0)
+    q_two = jnp.concatenate([queries, lax.ppermute(queries, "c", swap)], axis=0)
+    q_own = jnp.concatenate([q_two, lax.ppermute(q_two, "xl", swap), doc_rows], axis=0)
+    q_other = lax.ppermute(q_own, "yl", swap)
     gathered = lax.all_gather(jnp.concatenate([out_weight.T, hidden.T], axis=1), GROUP, axis=0, tiled=True)
     projector_t = projector.T
 
     partial = call(
         attend_kernel,
         shape(8, 528, 128),
-        [SMEM] + [ANY] * 5 + [HBM, ANY],
-        (place, kv_own, kv_below, kv_above, kv_low, kv_high, q_all, projector_t),
+        [SMEM] + [ANY] * 8,
+        (place, kv_own, kv_below, kv_above, kv_low, kv_high, q_own, q_other, projector_t),
         40,
         2 * 10 ** 10,
         scratch=[
             pltpu.VMEM((4, 4, 272, 128), BF),
-            pltpu.VMEM((8, 528, 128), BF),
+            pltpu.VMEM((2, 2064, 128), BF),
             pltpu.VMEM((128, 2048), BF),
             pltpu.VMEM((4, 512, 512), F32),
             pltpu.VMEM((24, 128), jnp.int32),
             pltpu.SMEM((24, 128), jnp.int32),
-            pltpu.SemaphoreType.DMA((7,)),
+            pltpu.SemaphoreType.DMA((8,)),
         ],
     )
     att_rows, att_copies = call(

time: 241 us -> 243 us (level); the launches traced: 240 us -> 239 us
  blocking collectives: 111 us -> 64 us
  starting transfers between devices: 44.4 us -> 78.9 us
  waiting for transfers between devices: 35.6 us -> 46.1 us
    all_to_all x1 -> x0, blocking collectives: 34.2 us -> none  [on_device(): kv_own = lax.all_to_all(packed, 'zh', 0, 0)]
    all_to_all x0 -> x1, starting transfers between devices: none -> 13.1 us  [on_device(): kv_own = lax.all_to_all(packed, 'zh', 0, 0)]
    all_to_all x1, blocking collectives: 35.5 us -> 22.4 us  [on_device(): lax.all_to_all(partial, OCTET, 0, 0)]
    all_to_all x1, starting transfers between devices: 9.04 us -> 19.3 us  [on_device(): lax.all_to_all(near, ('zh', 'yl'), 0, 0)]
    ppermute x0 -> x3, waiting for transfers between devices: none -> 9.22 us  [the longest x1 9.22 us: on_device(): lax.ppermute(q_two, 'xl', swap)]
    ppermute x0 -> x3, starting transfers between devices: none -> 7.65 us  [the longest x1 3.11 us: on_device(): lax.ppermute(q_two, 'xl', swap)]
    all_to_all x1, waiting for transfers between devices: 25.3 us -> 19.7 us  [on_device(): lax.all_to_all(near, ('zh', 'yl'), 0, 0)]
    all_to_all x0 -> x1, waiting for transfers between devices: none -> 5.42 us  [on_device(): kv_own = lax.all_to_all(packed, 'zh', 0, 0)]
  transfers between devices with their start and end apart: 13 -> 16, of which waited for: 4 -> 6; matrix products, arithmetic and copies ran while one was open for 2% -> 2% of each run, Pallas kernels for 5% -> 6%
where the time goes in v6:
time: 243 us; the launch traced here: 239 us
  starting transfers between devices  78.9 us (32%)
  blocking collectives  64 us (26%)
  waiting for transfers between devices  46.1 us (19%)
  Pallas kernels  22.5 us (9%)
  between operations  14.3 us (6%)
  local copies, waits for them, and re-layouts  11.3 us (5%)
    ppermute x8, starting transfers between devices, from_z(): lax.ppermute(x, ('zh', 'zl'), [((i + shift) % 16, i) for i in range(16)])  29.1 us
    all_to_all x1, blocking collectives, on_device(): own = lax.all_to_all(student, CHIPS, 0, 0)  25.9 us
    all_to_all x1, blocking collectives, on_device(): lax.all_to_all(partial, OCTET, 0, 0)  22.4 us
    pallas_call x9, Pallas kernels, call(): pl.pallas_call(kernel, out_shape=out_shape, in_specs=specs, out_specs=VME...  20.2 us
    all_to_all x1, waiting for transfers between devices, on_device(): lax.all_to_all(near, ('zh', 'yl'), 0, 0)  19.7 us
    all_to_all x1, starting transfers between devices, on_device(): lax.all_to_all(near, ('zh', 'yl'), 0, 0)  19.3 us
    all_to_all x1, blocking collectives, on_device(): att_all = lax.all_to_all(att_copies, HEADSETS, 0, 0)  15.8 us
    all_to_all x1, starting transfers between devices, on_device(): kv_own = lax.all_to_all(packed, 'zh', 0, 0)  13.1 us
  transfers between devices with their start and end apart: 16, of which 6 were waited for; matrix products, arithmetic and copies ran while one was open for 2% of the time, Pallas kernels for 6%

profile of v6, /device:TPU:73, one launch (start us, length us, event | category | flops | bytes accessed | tf_op | source)
XLA Modules:
  0.0 239.4 jit_solution(9545758189712753910)
XLA Ops:
  7.2 2.3 pad_maximum_fusion
  9.5 2.6 %collective-permute-start.4 = (bf16[512,128]{1,0:T(8,128)(2,1)S(1)}, bf16[512,128]{1,0:T(8,128)(2,1)S(1)}, u32[]{:S(2)}, u32[]{:S(2)}) collective-permute-start(bf16[512,128]{1,0:T(8,128)(2,1)S(1)} %copy-done.11), channel_id=1, source_target_pairs={{0,1},{1,0},{2,3},{3,2},{4,5},{5,4},{6,7},{7,6},{8,9},{9,8},{10,11... | collective-permute-start | bytes 393224 | tf_op jit(solution)/shard_map/ppermute | solution.py:300
  12.7 2.2 shard_map.95
  14.9 13.1 %all-to-all-start = ((bf16[4,272,128]{2,1,0:T(8,128)(2,1)}), bf16[4,272,128]{2,1,0:T(8,128)(2,1)S(1)}, u32[]{:S(2)}, u32[]{:S(2)}) async-start(bf16[4,272,128]{2,1,0:T(8,128)(2,1)} %get-tuple-element.11), calls=%async_computation | async-start | bytes 557056 | tf_op jit(solution)/shard_map/all_to_all | solution.py:296
  28.1 3.1 %collective-permute-start.5 = (bf16[1024,128]{1,0:T(8,128)(2,1)S(1)}, bf16[1024,128]{1,0:T(8,128)(2,1)S(1)}, u32[]{:S(2)}, u32[]{:S(2)}) collective-permute-start(bf16[1024,128]{1,0:T(8,128)(2,1)S(1)} %pad_maximum_fusion.1), channel_id=1, source_target_pairs={{0,2},{2,0},{1,3},{3,1},{4,6},{6,4},{5,7},{7,5},{8,10},{10,8},{9,1... | collective-permute-start | bytes 786440 | tf_op jit(solution)/shard_map/ppermute | solution.py:301
  31.3 9.2 %collective-permute-done.5 = bf16[1024,128]{1,0:T(8,128)(2,1)S(1)} collective-permute-done((bf16[1024,128]{1,0:T(8,128)(2,1)S(1)}, bf16[1024,128]{1,0:T(8,128)(2,1)S(1)}, u32[]{:S(2)}, u32[]{:S(2)}) %collective-permute-start.5) | collective-permute-done | bytes 262176 | tf_op jit(solution)/shard_map/ppermute | solution.py:301
  40.6 2.0 collective-permute-start.6
  42.5 5.4 %all-to-all-done.kv0 = bf16[4,272,128]{2,1,0:T(8,128)(2,1)S(1)} async-done(((bf16[4,272,128]{2,1,0:T(8,128)(2,1)}), bf16[4,272,128]{2,1,0:T(8,128)(2,1)S(1)}, u32[]{:S(2)}, u32[]{:S(2)}) %all-to-all-start) | async-done | bytes 278560 | tf_op jit(solution)/shard_map/all_to_all | solution.py:296
  47.9 1.9 collective-permute-start
  49.9 3.4 %collective-permute-start.1 = (bf16[4,272,128]{2,1,0:T(8,128)(2,1)S(1)}, bf16[4,272,128]{2,1,0:T(8,128)(2,1)}, u32[]{:S(2)}, u32[]{:S(2)}) collective-permute-start(bf16[4,272,128]{2,1,0:T(8,128)(2,1)S(1)} %all-to-all-done.kv0), channel_id=1, source_target_pairs={{32,0},{64,32},{96,64},{128,96},{160,128},{192,160},{224,192},{256... | collective-permute-start | bytes 835592 | tf_op jit(solution)/shard_map/ppermute | solution.py:292
  54.0 3.8 %collective-permute-start.2 = (bf16[2,272,128]{2,1,0:T(8,128)(2,1)}, bf16[2,272,128]{2,1,0:T(8,128)(2,1)S(1)}, u32[]{:S(2)}, u32[]{:S(2)}) collective-permute-start(bf16[2,272,128]{2,1,0:T(8,128)(2,1)} %get-tuple-element.21), channel_id=1, source_target_pairs={{448,0},{480,32},{0,64},{32,96},{64,128},{96,160},{128,192},{160,2... | collective-permute-start | bytes 417800 | tf_op jit(solution)/shard_map/ppermute | solution.py:292
  57.7 2.4 collective-permute-start.3
  60.1 1.7 copy.10
  62.7 4.7 %collective-permute-done.3.kv3_high = bf16[2,272,128]{2,1,0:T(8,128)(2,1)S(1)} collective-permute-done((bf16[2,272,128]{2,1,0:T(8,128)(2,1)}, bf16[2,272,128]{2,1,0:T(8,128)(2,1)S(1)}, u32[]{:S(2)}, u32[]{:S(2)}) %collective-permute-start.3) | collective-permute-done | bytes 139296 | tf_op jit(solution)/shard_map/ppermute | solution.py:292
  69.5 9.5 %shard_map.96 = bf16[8,528,128]{2,1,0:T(8,128)(2,1)S(1)} custom-call(s32[7]{0:T(128)S(1)} %copy-done.8, bf16[4,272,128]{2,1,0:T(8,128)(2,1)S(1)} %all-to-all-done.kv0, bf16[4,272,128]{2,1,0:T(8,128)(2,1)S(1)} %collective-permute-done.kv1, bf16[4,272,128]{2,1,0:T(8,128)(2,1)} %collective-permute-done.1.kv2, ...), custom_call_target="tpu_custom_call" | custom-call | flops 20000000000 | bytes 4194304 | tf_op jit(solution)/shard_map/pallas_call | solution.py:250
  78.9 22.4 %all_to_all.30.parts = bf16[8,528,128]{2,1,0:T(8,128)(2,1)S(1)} all-to-all(bf16[8,528,128]{2,1,0:T(8,128)(2,1)S(1)} %shard_map.96), channel_id=1, replica_groups=mesh['zh'=4,'zl'=4,'yl'=2,'yh'=2,'xh'=2,'xl'=2,'c'=2] {'yl','xl','c'}, dimensions={0} | all-to-all | bytes 2162688 | tf_op jit(solution)/shard_map/all_to_all | solution.py:324
  102.2 15.8 %all_to_all.31.att = bf16[4,512,128]{2,1,0:T(8,128)(2,1)S(1)} all-to-all(bf16[4,512,128]{2,1,0:T(8,128)(2,1)S(1)} %get-tuple-element.13), channel_id=1, replica_groups=mesh['zh'=4,'zl'=4,'yl'=2,'yh'=2,'xh'=2,'xl'=2,'c'=2] {'yh','xh'}, dimensions={0} | all-to-all | bytes 1048576 | tf_op jit(solution)/shard_map/all_to_all | solution.py:330
  118.0 2.1 copy-done.2
  120.1 2.4 %shard_map.98 = bf16[8,896,128]{2,1,0:T(8,128)(2,1)S(1)} custom-call(s32[7]{0:T(128)S(1)} %copy-done.8, bf16[768,2560]{1,0:T(8,128)(2,1)S(1)} %copy-done.2, bf16[4,512,128]{2,1,0:T(8,128)(2,1)S(1)} %all_to_all.31.att, bf16[32,4096]{1,0:T(8,128)(2,1)S(1)} %copy-done.5), custom_call_target="tpu_custom_call" | custom-call | bytes 4194304 | tf_op jit(solution)/shard_map/pallas_call | solution.py:250
  122.5 25.9 %all_to_all.32.own = bf16[8,896,128]{2,1,0:T(8,128)(2,1)S(1)} all-to-all(bf16[8,896,128]{2,1,0:T(8,128)(2,1)S(1)} %shard_map.98), channel_id=1, replica_groups=mesh['zh'=4,'zl'=4,'yl'=2,'yh'=2,'xh'=2,'xl'=2,'c'=2] {'xl','yh','xh'}, dimensions={0} | all-to-all | bytes 3670016 | tf_op jit(solution)/shard_map/all_to_all | solution.py:339
  148.4 5.0 %collective-permute-start.7 = (bf16[8,896,128]{2,1,0:T(8,128)(2,1)S(1)}, bf16[8,896,128]{2,1,0:T(8,128)(2,1)S(1)}, u32[]{:S(2)}, u32[]{:S(2)}) collective-permute-start(bf16[8,896,128]{2,1,0:T(8,128)(2,1)S(1)} %all_to_all.32.own), channel_id=1, source_target_pairs={{0,1},{1,0},{2,3},{3,2},{4,5},{5,4},{6,7},{7,6},{8,9},{9,8},{10,11... | collective-permute-start | bytes 5505032 | tf_op jit(solution)/shard_map/ppermute | solution.py:340
  154.1 2.7 %collective-permute-done.7.other = bf16[8,896,128]{2,1,0:T(8,128)(2,1)S(1)} collective-permute-done((bf16[8,896,128]{2,1,0:T(8,128)(2,1)S(1)}, bf16[8,896,128]{2,1,0:T(8,128)(2,1)S(1)}, u32[]{:S(2)}, u32[]{:S(2)}) %collective-permute-start.7) | collective-permute-done | bytes 1835040 | tf_op jit(solution)/shard_map/ppermute | solution.py:340
  156.9 2.4 %shard_map.100 = (bf16[512,256]{1,0:T(8,128)(2,1)S(1)}, bf16[4,96,256]{2,1,0:T(8,128)(2,1)}, bf16[4,96,256]{2,1,0:T(8,128)(2,1)}) custom-call(s32[7]{0:T(128)S(1)} %copy-done.8, bf16[8,896,128]{2,1,0:T(8,128)(2,1)S(1)} %all_to_all.32.own, bf16[8,896,128]{2,1,0:T(8,128)(2,1)S(1)} %collective-permute-done.7.other, bf16[256,3072]{1,0:T(8,128)(2,1)S(1)} %bitcast.15, ...), custom_call_target="tpu_custom_call" | custom-call | flops 800000000 | bytes 4194304 | tf_op jit(solution)/shard_map/pallas_call | solution.py:250
  159.3 1.9 shard_map.102
  161.2 1.9 collective-permute-start.8
  163.1 3.4 %collective-permute-start.9 = (bf16[8,96,256]{2,1,0:T(8,128)(2,1)S(1)}, bf16[8,96,256]{2,1,0:T(8,128)(2,1)S(1)}, u32[]{:S(2)}, u32[]{:S(2)}) collective-permute-start(bf16[8,96,256]{2,1,0:T(8,128)(2,1)S(1)} %get-tuple-element.16), channel_id=1, source_target_pairs={{32,0},{64,32},{96,64},{128,96},{160,128},{192,160},{224,192},{256... | collective-permute-start | bytes 1179656 | tf_op jit(solution)/shard_map/ppermute | solution.py:292
  166.4 10.5 %collective-permute-start.10 = (bf16[4,96,256]{2,1,0:T(8,128)(2,1)}, bf16[4,96,256]{2,1,0:T(8,128)(2,1)S(1)}, u32[]{:S(2)}, u32[]{:S(2)}) collective-permute-start(bf16[4,96,256]{2,1,0:T(8,128)(2,1)} %get-tuple-element.17), channel_id=1, source_target_pairs={{448,0},{480,32},{0,64},{32,96},{64,128},{96,160},{128,192},{160,2... | collective-permute-start | bytes 589832 | tf_op jit(solution)/shard_map/ppermute | solution.py:292
  176.9 1.9 collective-permute-start.11
  178.9 4.5 %all-to-all-start.5 = ((bf16[4,128,128]{2,1,0:T(8,128)(2,1)}), bf16[4,128,128]{2,1,0:T(8,128)(2,1)S(1)}, u32[]{:S(2)}, u32[]{:S(2)}) async-start(bf16[4,128,128]{2,1,0:T(8,128)(2,1)} %bitcast.10), calls=%async_computation.5 | async-start | bytes 262144 | tf_op jit(solution)/shard_map/all_to_all | solution.py:327
  186.8 4.3 %collective-permute-done.11.far_above = bf16[4,96,256]{2,1,0:T(8,128)(2,1)S(1)} collective-permute-done((bf16[4,96,256]{2,1,0:T(8,128)(2,1)}, bf16[4,96,256]{2,1,0:T(8,128)(2,1)S(1)}, u32[]{:S(2)}, u32[]{:S(2)}) %collective-permute-start.11) | collective-permute-done | bytes 196640 | tf_op jit(solution)/shard_map/ppermute | solution.py:292
  192.1 19.3 %all-to-all-start.4 = ((bf16[8,96,256]{2,1,0:T(8,128)(2,1)}), bf16[8,96,256]{2,1,0:T(8,128)(2,1)S(1)}, u32[]{:S(2)}, u32[]{:S(2)}) async-start(bf16[8,96,256]{2,1,0:T(8,128)(2,1)} %shard_map.103), calls=%async_computation.4 | async-start | bytes 786432 | tf_op jit(solution)/shard_map/all_to_all | solution.py:358
  212.2 19.7 %all-to-all-done.4.terms = bf16[8,96,256]{2,1,0:T(8,128)(2,1)S(1)} async-done(((bf16[8,96,256]{2,1,0:T(8,128)(2,1)}), bf16[8,96,256]{2,1,0:T(8,128)(2,1)S(1)}, u32[]{:S(2)}, u32[]{:S(2)}) %all-to-all-start.4) | async-done | bytes 393248 | tf_op jit(solution)/shard_map/all_to_all | solution.py:358
  (50 shorter events, 11.7 us)
Async XLA Ops:
  7.2 2.4 copy-start.11
  7.2 110.8 %all-gather.2.cloned.1.call-start = ((), (), s32[]{:S(2)}) async-start(), calls=%async_computation.6 | async-start | bytes 4915200 | tf_op jit(solution)/shard_map/all_gather | solution.py:303
  9.5 18.5 %collective-permute-start.4 = (bf16[512,128]{1,0:T(8,128)(2,1)S(1)}, bf16[512,128]{1,0:T(8,128)(2,1)S(1)}, u32[]{:S(2)}, u32[]{:S(2)}) collective-permute-start(bf16[512,128]{1,0:T(8,128)(2,1)S(1)} %copy-done.11), channel_id=1, source_target_pairs={{0,1},{1,0},{2,3},{3,2},{4,5},{5,4},{6,7},{7,6},{8,9},{9,8},{10,11... | collective-permute-start | bytes 393224 | tf_op jit(solution)/shard_map/ppermute | solution.py:300
  14.9 25.6 %copy-start.12 = (bf16[16,128]{1,0:T(8,128)(2,1)S(1)}, bf16[16,128]{1,0:T(8,128)(2,1)}, u32[]{:S(2)}) copy-start(bf16[16,128]{1,0:T(8,128)(2,1)} %get-tuple-element.12) | copy-start | bytes 12292
  14.9 33.0 %all-to-all-start = ((bf16[4,272,128]{2,1,0:T(8,128)(2,1)}), bf16[4,272,128]{2,1,0:T(8,128)(2,1)S(1)}, u32[]{:S(2)}, u32[]{:S(2)}) async-start(bf16[4,272,128]{2,1,0:T(8,128)(2,1)} %get-tuple-element.11), calls=%async_computation | async-start | bytes 557056 | tf_op jit(solution)/shard_map/all_to_all | solution.py:296
  28.1 12.4 %collective-permute-start.5 = (bf16[1024,128]{1,0:T(8,128)(2,1)S(1)}, bf16[1024,128]{1,0:T(8,128)(2,1)S(1)}, u32[]{:S(2)}, u32[]{:S(2)}) collective-permute-start(bf16[1024,128]{1,0:T(8,128)(2,1)S(1)} %pad_maximum_fusion.1), channel_id=1, source_target_pairs={{0,2},{2,0},{1,3},{3,1},{4,6},{6,4},{5,7},{7,5},{8,10},{10,8},{9,1... | collective-permute-start | bytes 786440 | tf_op jit(solution)/shard_map/ppermute | solution.py:301
  40.5 21.3 %copy-start.6 = (bf16[2064,128]{1,0:T(8,128)(2,1)}, bf16[2064,128]{1,0:T(8,128)(2,1)S(1)}, u32[]{:S(2)}) copy-start(bf16[2064,128]{1,0:T(8,128)(2,1)S(1)} %constant_dynamic-update-slice_fusion.q_own) | copy-start | bytes 1585156
  40.5 26.8 %copy-start.8 = (s32[7]{0:T(128)S(1)}, s32[7]{0:T(128)}, u32[]{:S(2)}) copy-start(s32[7]{0:T(128)} %stack.28.place) | copy-start | bytes 88
  40.6 21.3 %collective-permute-start.6 = (bf16[2064,128]{1,0:T(8,128)(2,1)S(1)}, bf16[2064,128]{1,0:T(8,128)(2,1)S(1)}, u32[]{:S(2)}, u32[]{:S(2)}) collective-permute-start(bf16[2064,128]{1,0:T(8,128)(2,1)S(1)} %constant_dynamic-update-slice_fusion.q_own), channel_id=1, source_target_pairs={{0,16},{16,0},{1,17},{17,1},{2,18},{18,2},{3,19},{19,3},{4,20},{20... | collective-permute-start | bytes 1585160 | tf_op jit(solution)/shard_map/ppermute | solution.py:302
  47.9 19.4 %collective-permute-start = (bf16[4,272,128]{2,1,0:T(8,128)(2,1)S(1)}, bf16[4,272,128]{2,1,0:T(8,128)(2,1)S(1)}, u32[]{:S(2)}, u32[]{:S(2)}) collective-permute-start(bf16[4,272,128]{2,1,0:T(8,128)(2,1)S(1)} %all-to-all-done.kv0), channel_id=1, source_target_pairs={{480,0},{0,32},{32,64},{64,96},{96,128},{128,160},{160,192},{192,2... | collective-permute-start | bytes 835592 | tf_op jit(solution)/shard_map/ppermute | solution.py:292
  49.9 17.5 %collective-permute-start.1 = (bf16[4,272,128]{2,1,0:T(8,128)(2,1)S(1)}, bf16[4,272,128]{2,1,0:T(8,128)(2,1)}, u32[]{:S(2)}, u32[]{:S(2)}) collective-permute-start(bf16[4,272,128]{2,1,0:T(8,128)(2,1)S(1)} %all-to-all-done.kv0), channel_id=1, source_target_pairs={{32,0},{64,32},{96,64},{128,96},{160,128},{192,160},{224,192},{256... | collective-permute-start | bytes 835592 | tf_op jit(solution)/shard_map/ppermute | solution.py:292
  54.0 8.7 %collective-permute-start.2 = (bf16[2,272,128]{2,1,0:T(8,128)(2,1)}, bf16[2,272,128]{2,1,0:T(8,128)(2,1)S(1)}, u32[]{:S(2)}, u32[]{:S(2)}) collective-permute-start(bf16[2,272,128]{2,1,0:T(8,128)(2,1)} %get-tuple-element.21), channel_id=1, source_target_pairs={{448,0},{480,32},{0,64},{32,96},{64,128},{96,160},{128,192},{160,2... | collective-permute-start | bytes 417800 | tf_op jit(solution)/shard_map/ppermute | solution.py:292
  57.7 9.6 %collective-permute-start.3 = (bf16[2,272,128]{2,1,0:T(8,128)(2,1)}, bf16[2,272,128]{2,1,0:T(8,128)(2,1)S(1)}, u32[]{:S(2)}, u32[]{:S(2)}) collective-permute-start(bf16[2,272,128]{2,1,0:T(8,128)(2,1)} %get-tuple-element.20), channel_id=1, source_target_pairs={{64,0},{96,32},{128,64},{160,96},{192,128},{224,160},{256,192},{28... | collective-permute-start | bytes 417800 | tf_op jit(solution)/shard_map/ppermute | solution.py:292
  61.9 0.8 copy-start.9
  67.4 1.0 copy-start.7
  68.4 1.0 copy-start.10
  78.9 39.1 %copy-start.5 = (bf16[32,4096]{1,0:T(8,128)(2,1)S(1)}, bf16[32,4096]{1,0:T(8,128)(2,1)}, u32[]{:S(2)}) copy-start(bf16[32,4096]{1,0:T(8,128)(2,1)} %teacher.1) | copy-start | bytes 786436
  118.0 2.1 copy-start.2
  148.4 8.4 %collective-permute-start.7 = (bf16[8,896,128]{2,1,0:T(8,128)(2,1)S(1)}, bf16[8,896,128]{2,1,0:T(8,128)(2,1)S(1)}, u32[]{:S(2)}, u32[]{:S(2)}) collective-permute-start(bf16[8,896,128]{2,1,0:T(8,128)(2,1)S(1)} %all_to_all.32.own), channel_id=1, source_target_pairs={{0,1},{1,0},{2,3},{3,2},{4,5},{5,4},{6,7},{7,6},{8,9},{9,8},{10,11... | collective-permute-start | bytes 5505032 | tf_op jit(solution)/shard_map/ppermute | solution.py:340
  156.9 2.4 %copy-start = (bf16[8,896,128]{2,1,0:T(8,128)(2,1)}, bf16[8,896,128]{2,1,0:T(8,128)(2,1)S(1)}, u32[]{:S(2)}) copy-start(bf16[8,896,128]{2,1,0:T(8,128)(2,1)S(1)} %collective-permute-done.7.other) | copy-start | bytes 5505028
  159.3 1.9 copy-start.3
  161.2 29.9 %collective-permute-start.8 = (bf16[8,96,256]{2,1,0:T(8,128)(2,1)}, bf16[8,96,256]{2,1,0:T(8,128)(2,1)S(1)}, u32[]{:S(2)}, u32[]{:S(2)}) collective-permute-start(bf16[8,96,256]{2,1,0:T(8,128)(2,1)} %get-tuple-element.15), channel_id=1, source_target_pairs={{480,0},{0,32},{32,64},{64,96},{96,128},{128,160},{160,192},{192,2... | collective-permute-start | bytes 1179656 | tf_op jit(solution)/shard_map/ppermute | solution.py:292
  163.1 28.0 %collective-permute-start.9 = (bf16[8,96,256]{2,1,0:T(8,128)(2,1)S(1)}, bf16[8,96,256]{2,1,0:T(8,128)(2,1)S(1)}, u32[]{:S(2)}, u32[]{:S(2)}) collective-permute-start(bf16[8,96,256]{2,1,0:T(8,128)(2,1)S(1)} %get-tuple-element.16), channel_id=1, source_target_pairs={{32,0},{64,32},{96,64},{128,96},{160,128},{192,160},{224,192},{256... | collective-permute-start | bytes 1179656 | tf_op jit(solution)/shard_map/ppermute | solution.py:292
  166.4 20.3 %collective-permute-start.10 = (bf16[4,96,256]{2,1,0:T(8,128)(2,1)}, bf16[4,96,256]{2,1,0:T(8,128)(2,1)S(1)}, u32[]{:S(2)}, u32[]{:S(2)}) collective-permute-start(bf16[4,96,256]{2,1,0:T(8,128)(2,1)} %get-tuple-element.17), channel_id=1, source_target_pairs={{448,0},{480,32},{0,64},{32,96},{64,128},{96,160},{128,192},{160,2... | collective-permute-start | bytes 589832 | tf_op jit(solution)/shard_map/ppermute | solution.py:292
  176.9 14.1 %collective-permute-start.11 = (bf16[4,96,256]{2,1,0:T(8,128)(2,1)}, bf16[4,96,256]{2,1,0:T(8,128)(2,1)S(1)}, u32[]{:S(2)}, u32[]{:S(2)}) collective-permute-start(bf16[4,96,256]{2,1,0:T(8,128)(2,1)} %get-tuple-element.18), channel_id=1, source_target_pairs={{64,0},{96,32},{128,64},{160,96},{192,128},{224,160},{256,192},{28... | collective-permute-start | bytes 589832 | tf_op jit(solution)/shard_map/ppermute | solution.py:292
  178.9 13.2 %all-to-all-start.5 = ((bf16[4,128,128]{2,1,0:T(8,128)(2,1)}), bf16[4,128,128]{2,1,0:T(8,128)(2,1)S(1)}, u32[]{:S(2)}, u32[]{:S(2)}) async-start(bf16[4,128,128]{2,1,0:T(8,128)(2,1)} %bitcast.10), calls=%async_computation.5 | async-start | bytes 262144 | tf_op jit(solution)/shard_map/all_to_all | solution.py:327
  183.4 1.5 copy-start.1
  184.9 0.9 copy-start.4
  192.1 39.8 %all-to-all-start.4 = ((bf16[8,96,256]{2,1,0:T(8,128)(2,1)}), bf16[8,96,256]{2,1,0:T(8,128)(2,1)S(1)}, u32[]{:S(2)}, u32[]{:S(2)}) async-start(bf16[8,96,256]{2,1,0:T(8,128)(2,1)} %shard_map.103), calls=%async_computation.4 | async-start | bytes 786432 | tf_op jit(solution)/shard_map/all_to_all | solution.py:358
Sparse Core Ops, SparseCore 0:
  10.1 59.9 all-gather.1

commit v7 on v6

--- a/solution.py
+++ b/solution.py
@@ -32,15 +32,9 @@
     doc_rows[...] = rows
 
 
-def attend_kernel(place, kv0, kv1, kv2, kv3_low, kv3_high, q_own, q_other, early, out, kv, q_all, v_turned, s_buf, info_v, info, sem):
+def attend_kernel(place, kv, q_own, q_other, early, out, q_all, v_turned, s_buf, info_v, info, sem):
     j, yl, z = place[0], place[4], place[5]
-    copies = [
-        pltpu.make_async_copy(src, dst, sem.at[i])
-        for i, (src, dst) in enumerate((
-            (kv0, kv.at[0]), (kv1, kv.at[1]), (kv2, kv.at[2]), (kv3_low, kv.at[3, pl.ds(0, 2)]), (kv3_high, kv.at[3, pl.ds(2, 2)]),
-            (q_own, q_all.at[0]), (q_other, q_all.at[1]),
-        ))
-    ]
+    copies = [pltpu.make_async_copy(src, q_all.at[i], sem.at[i]) for i, src in enumerate((q_own, q_other))]
     for copy in copies:
         copy.start()
     for copy in copies:
@@ -59,13 +53,12 @@
         below = jnp.sum((block_docs < d).astype(F32), axis=1, keepdims=True)
         counts = jnp.where(lane == d, below, counts)
     info_v[0:16, :] = counts.astype(jnp.int32)
-    to_scalars = pltpu.make_async_copy(info_v, info, sem.at[7])
+    to_scalars = pltpu.make_async_copy(info_v, info, sem.at[2])
     to_scalars.start()
     for ch in range(4):
         for i in range(BLOCKS):
             v_turned[:, (ch * BLOCKS + i) * 128:(ch * BLOCKS + i + 1) * 128] = kv[i, ch, 128:256, :].T
     to_scalars.wait()
-    where = [(z + shift) % 4 for shift in (0, 3, 1, 2)]
     key_iota = lax.broadcasted_iota(jnp.int32, (128, 512), 0)
     row_iota = lax.broadcasted_iota(jnp.int32, (1, 512), 1) % 128
 
@@ -91,13 +84,13 @@
                 for d in range(8):
                     low = jnp.where(row_docs == d, info[ch * BLOCKS + i, d], low)
                 low = low - j * 128
-                high = q_pos - ((2 * (ch * 4 + where[i]) + yl) * 512 + j * 128)
+                high = q_pos - ((2 * (ch * 4 + i) + yl) * 512 + j * 128)
                 ok = (key_iota >= low) & (key_iota <= high)
                 parts.append(jnp.where(ok, s[i * 128:(i + 1) * 128], MASKED))
             return jnp.concatenate(parts, axis=0)
 
         def find_max(ch, run_max):
-            most = functools.reduce(jnp.maximum, [info[ch * BLOCKS + i, last] for i in range(BLOCKS)])
+            most = info[ch * BLOCKS, last]
             k_max = (2 * (ch * BLOCKS + BLOCKS - 1) + yl) * 512 + j * 128 + 127
             full = (k_max <= q_min) & (most <= j * 128)
 
@@ -116,7 +109,7 @@
 
         begin = jnp.int32(0)
         for ch in range(4):
-            fewest = functools.reduce(jnp.minimum, [info[ch * BLOCKS + i, first] for i in range(BLOCKS)])
+            fewest = info[ch * BLOCKS + BLOCKS - 1, first]
             begin = begin + (fewest >= (j + 1) * 128).astype(jnp.int32)
         end = z // BLOCKS + 1
         run_max = lax.fori_loop(begin, end, find_max, jnp.full((1, 512), EMPTY, F32))
@@ -152,13 +145,13 @@
             copies[copy, rows, :] = total
 
 
-def student_kernel(place, gathered, att, teacher, out, weights, hidden, sem):
+def student_kernel(place, weight_t, hidden_t, att, teacher, out, weights, hidden, sem):
     copies = []
-    own_rows = pl.ds(pl.multiple_of(2048 + place[0] * 128, 128), 128)
-    hidden_copy = pltpu.make_async_copy(gathered.at[:, own_rows], hidden, sem.at[4])
+    own_rows = pl.ds(pl.multiple_of(place[0] * 128, 128), 128)
+    hidden_copy = pltpu.make_async_copy(hidden_t.at[:, own_rows], hidden, sem.at[4])
     for part in range(4):
         rows = pl.ds(part * 192, 192)
-        copies.append(pltpu.make_async_copy(gathered.at[rows, pl.ds(0, 2048)], weights.at[rows], sem.at[part]))
+        copies.append(pltpu.make_async_copy(weight_t.at[rows], weights.at[rows], sem.at[part]))
     copies[0].start()
     hidden_copy.start()
     for copy in copies[1:]:
@@ -202,7 +195,7 @@
 def gradient_rows(own, other, mismatch, near):
     rows = []
     for zh in range(4):
-        cut = pl.ds(pl.multiple_of(near * 192, 64), 192)
+        cut = slice(near * 192, (near + 1) * 192)
         rows.append(jnp.concatenate([ref[xl * 4 + zh, cut, :] for ref in (own, other) for xl in range(2)], axis=1))
     return jnp.dot(jnp.concatenate(rows, axis=0), mismatch[...], preferred_element_type=F32).reshape(8, 96, 256)
 
@@ -211,28 +204,16 @@
     out[...] = projected(own, projector_t).T
 
 
-def second_kernel(place, own, other, projector_t, own_projected, mismatch, up, down):
+def gradient_kernel(place, own, other, projector_t, own_projected, out, mismatch):
     core = place[2]
     mismatch[0:256, :] = (own_projected[...] - teacher_rows(own, other, core, core)).astype(BF)
     mismatch[256:512, :] = (projected(other, projector_t).T - teacher_rows(own, other, core, 1 - core)).astype(BF)
-    grad = gradient_rows(own, other, mismatch, (place[6] + 2) % 4).astype(BF)
-    up[...] = grad[0:4]
-    down[...] = grad[4:8]
-
-
-def first_kernel(place, own, other, mismatch, up, down):
-    up[...] = gradient_rows(own, other, mismatch, (place[6] + 1) % 4).astype(BF)
-    down[...] = gradient_rows(own, other, mismatch, (place[6] + 3) % 4).astype(BF)
-
-
-def kept_kernel(place, own, other, mismatch, out):
-    out[...] = gradient_rows(own, other, mismatch, place[6])
-
-
-def add_kernel(kept, below, above, far_below, far_above, out):
-    near = kept[...] + below[...].astype(F32) + above[...].astype(F32)
-    out[0:4] = (near[0:4] + far_below[...].astype(F32)).astype(BF)
-    out[4:8] = (near[4:8] + far_above[...].astype(F32)).astype(BF)
+    for near in range(4):
+        out[near] = gradient_rows(own, other, mismatch, near).astype(BF)
+
+
+def add_kernel(terms, out):
+    out[...] = sum(terms[i].astype(F32) for i in range(terms.shape[0])).astype(BF)
 
 
 def final_kernel(terms, out):
@@ -281,43 +262,39 @@
 
 
 def on_device(queries, keys, values, doc_ids, hidden, out_weight, projector, teacher):
-    zl, yl, c = lax.axis_index("zl"), lax.axis_index("yl"), lax.axis_index("c")
+    yl, c = lax.axis_index("yl"), lax.axis_index("c")
     j = lax.axis_index("xl") * 2 + c
-    z = lax.axis_index("zh") * 4 + zl
+    z = lax.axis_index("zh") * 4 + lax.axis_index("zl")
     g = lax.axis_index("yh") * 2 + lax.axis_index("xh")
     swap = [(0, 1), (1, 0)]
-    place = jnp.stack([j, g, c, c, yl, z, zl]).astype(jnp.int32)
-
-    def from_z(x, shift):
-        return lax.ppermute(x, ("zh", "zl"), [((i + shift) % 16, i) for i in range(16)])
+    place = jnp.stack([j, g, c, c, yl, z]).astype(jnp.int32)
 
     docs = doc_ids.reshape(4, 128)
     packed, doc_rows = start(place, keys, values, docs)
     kv_own = lax.all_to_all(packed, "zh", 0, 0)
-    kv_below, kv_above = from_z(kv_own, -1), from_z(kv_own, 1)
-    kv_low, kv_high = from_z(kv_own[0:2], -2), from_z(kv_own[2:4], 2)
+    kv = lax.all_to_all(jnp.broadcast_to(kv_own[None], (4, 4, 272, 128)), "zl", 0, 0)
 
     q_two = jnp.concatenate([queries, lax.ppermute(queries, "c", swap)], axis=0)
     q_own = jnp.concatenate([q_two, lax.ppermute(q_two, "xl", swap), doc_rows], axis=0)
     q_other = lax.ppermute(q_own, "yl", swap)
-    gathered = lax.all_gather(jnp.concatenate([out_weight.T, hidden.T], axis=1), GROUP, axis=0, tiled=True)
+    weight_t = lax.all_gather(out_weight.T, GROUP, axis=0, tiled=True)
+    hidden_t = lax.all_gather(hidden.T, GROUP, axis=0, tiled=True)
     projector_t = projector.T
 
     partial = call(
         attend_kernel,
         shape(8, 528, 128),
-        [SMEM] + [ANY] * 8,
-        (place, kv_own, kv_below, kv_above, kv_low, kv_high, q_own, q_other, projector_t),
-        40,
+        [SMEM, VMEM] + [ANY] * 3,
+        (place, kv, q_own, q_other, projector_t),
+        58,
         2 * 10 ** 10,
         scratch=[
-            pltpu.VMEM((4, 4, 272, 128), BF),
             pltpu.VMEM((2, 2064, 128), BF),
             pltpu.VMEM((128, 2048), BF),
             pltpu.VMEM((4, 512, 512), F32),
             pltpu.VMEM((24, 128), jnp.int32),
             pltpu.SMEM((24, 128), jnp.int32),
-            pltpu.SemaphoreType.DMA((8,)),
+            pltpu.SemaphoreType.DMA((3,)),
         ],
     )
     att_rows, att_copies = call(
@@ -331,30 +308,25 @@
     student = call(
         student_kernel,
         shape(8, 896, 128),
-        [SMEM, HBM, VMEM, VMEM],
-        (place, gathered, att_all, teacher),
-        24,
+        [SMEM, HBM, HBM, VMEM, VMEM],
+        (place, weight_t, hidden_t, att_all, teacher),
+        58,
         scratch=[pltpu.VMEM((768, 2048), BF), pltpu.VMEM((768, 128), BF), pltpu.SemaphoreType.DMA((5,))],
     )
     own = lax.all_to_all(student, CHIPS, 0, 0)
     other = lax.ppermute(own, "c", swap)
 
     own_projected = call(own_projected_kernel, shape(256, 256, dtype=F32), [VMEM] * 2, (own, projector_t), 24, 4 * 10 ** 8)
-    mismatch, up, down = call(
-        second_kernel,
-        [shape(512, 256), shape(4, 96, 256), shape(4, 96, 256)],
+    share = call(
+        gradient_kernel,
+        shape(4, 8, 96, 256),
         [SMEM] + [VMEM] * 4,
         (place, own, other, projector_t, own_projected),
         32,
         8 * 10 ** 8,
-    )
-    far_below, far_above = from_z(up, -2), from_z(down, 2)
-    up, down = call(
-        first_kernel, [shape(8, 96, 256), shape(8, 96, 256)], [SMEM] + [VMEM] * 3, (place, own, other, mismatch), 32, 4 * 10 ** 8
-    )
-    below, above = from_z(up, -1), from_z(down, 1)
-    kept = call(kept_kernel, shape(8, 96, 256, dtype=F32), [SMEM] + [VMEM] * 3, (place, own, other, mismatch), 32, 2 * 10 ** 8)
-    near = call(add_kernel, shape(8, 96, 256), [VMEM] * 5, (kept, below, above, far_below, far_above), 16)
+        scratch=[pltpu.VMEM((512, 256), BF)],
+    )
+    near = call(add_kernel, shape(8, 96, 256), [VMEM], (lax.all_to_all(share, "zl", 0, 0),), 16)
     grad = call(final_kernel, shape(96, 256, dtype=F32), [VMEM], (lax.all_to_all(near, ("zh", "yl"), 0, 0),), 8)
     return grad, attended
 

time: 243 us -> 277 us (1.14)
  blocking collectives: 64 us -> 138 us
  starting transfers between devices: 78.9 us -> 42.7 us
  local copies, waits for them, and re-layouts: 11.3 us -> 6.34 us
    all_to_all x1 -> x2, blocking collectives: 15.8 us -> 72.7 us  [the longest x1 38.3 us: on_device(): lax.all_to_all(share, 'zl', 0, 0)]
    ppermute x8 -> x0, starting transfers between devices: 29.1 us -> none  [from_z(): lax.ppermute(x, ('zh', 'zl'), [((i + shift) % 16, i) for i in range(16)])]
    all_gather x0 -> x1, blocking collectives: none -> 12.5 us  [on_device(): hidden_t = lax.all_gather(hidden.T, GROUP, axis=0, tiled=True)]
    ppermute x1, waiting for transfers between devices: 0.01 us -> 10.4 us  [on_device(): q_other = lax.ppermute(q_own, 'yl', swap)]
    ppermute x8 -> x0, waiting for transfers between devices: 9.01 us -> none  [from_z(): lax.ppermute(x, ('zh', 'zl'), [((i + shift) % 16, i) for i in range(16)])]
    all_to_all x1, blocking collectives: 25.9 us -> 32.5 us  [on_device(): own = lax.all_to_all(student, CHIPS, 0, 0)]
    unnamed x30 -> x22, local copies, waits for them, and re-layouts: 9.25 us -> 3.72 us
    all_to_all x1 -> x2, waiting for transfers between devices: 5.42 us -> 0.01 us  [the longest x1 0.01 us: on_device(): lax.all_to_all(jnp.broadcast_to(kv_own[None], (4, 4, 272, 128)), 'zl', 0, 0)]
  transfers between devices with their start and end apart: 16 -> 9, of which waited for: 6 -> 6; matrix products, arithmetic and copies ran while one was open for 2% -> 1% of each run, Pallas kernels for 6% -> 5%
where the time goes in v7:
time: 277 us; the launch traced here: 272 us
  blocking collectives  138 us (50%)
  waiting for transfers between devices  46.9 us (17%)
  starting transfers between devices  42.7 us (15%)
  Pallas kernels  24.4 us (9%)
  between operations  14.2 us (5%)
  local copies, waits for them, and re-layouts  6.34 us (2%)
    all_to_all x1, blocking collectives, on_device(): lax.all_to_all(share, 'zl', 0, 0)  38.3 us
    all_to_all x1, blocking collectives, on_device(): kv_own = lax.all_to_all(packed, 'zh', 0, 0)  34.4 us
    all_to_all x1, blocking collectives, on_device(): own = lax.all_to_all(student, CHIPS, 0, 0)  32.5 us
    all_to_all x1, waiting for transfers between devices, on_device(): lax.all_to_all(near, ('zh', 'yl'), 0, 0)  23.2 us
    pallas_call x7, Pallas kernels, call(): pl.pallas_call(kernel, out_shape=out_shape, in_specs=specs, out_specs=VME...  22.3 us
    all_to_all x1, blocking collectives, on_device(): lax.all_to_all(partial, OCTET, 0, 0)  20.1 us
    all_to_all x1, starting transfers between devices, on_device(): lax.all_to_all(near, ('zh', 'yl'), 0, 0)  15.2 us
    all_gather x1, blocking collectives, on_device(): hidden_t = lax.all_gather(hidden.T, GROUP, axis=0, tiled=True)  12.5 us
  transfers between devices with their start and end apart: 9, of which 6 were waited for; matrix products, arithmetic and copies ran while one was open for 1% of the time, Pallas kernels for 5%

profile of v7, /device:TPU:73, one launch (start us, length us, event | category | flops | bytes accessed | tf_op | source)
XLA Modules:
  0.0 272.4 jit_solution(3728831651909438958)
XLA Ops:
  7.9 2.2 shard_map.95
  10.0 34.4 %all_to_all.40 = bf16[4,272,128]{2,1,0:T(8,128)(2,1)S(1)} all-to-all(bf16[4,272,128]{2,1,0:T(8,128)(2,1)} %get-tuple-element.6), channel_id=1, replica_groups=mesh['zh'=4,'zl'=4,'yl'=2,'yh'=2,'xh'=2,'xl'=2,'c'=2] {'zh'}, dimensions={0} | all-to-all | bytes 557056 | tf_op jit(solution)/shard_map/all_to_all | solution.py:274
  44.4 1.2 broadcast_in_dim.2
  45.6 3.8 %all-to-all-start.1 = ((bf16[4,4,272,128]{3,2,1,0:T(8,128)(2,1)}), bf16[4,4,272,128]{3,2,1,0:T(8,128)(2,1)S(1)}, u32[]{:S(2)}, u32[]{:S(2)}) async-start(bf16[4,4,272,128]{3,2,1,0:T(8,128)(2,1)} %broadcast_in_dim.2), calls=%async_computation.1 | async-start | bytes 2228224 | tf_op jit(solution)/shard_map/all_to_all | solution.py:275
  49.4 0.7 all-gather.2.cloned.1.call-update
  50.1 4.5 %collective-permute-start = (bf16[512,128]{1,0:T(8,128)(2,1)S(1)}, bf16[512,128]{1,0:T(8,128)(2,1)S(1)}, u32[]{:S(2)}, u32[]{:S(2)}) collective-permute-start(bf16[512,128]{1,0:T(8,128)(2,1)S(1)} %copy-done.5), channel_id=1, source_target_pairs={{0,1},{1,0},{2,3},{3,2},{4,5},{5,4},{6,7},{7,6},{8,9},{9,8},{10,11... | collective-permute-start | bytes 393224 | tf_op jit(solution)/shard_map/ppermute | solution.py:277
  54.6 1.0 collective-permute-done
  55.6 3.1 %collective-permute-start.1 = (bf16[1024,128]{1,0:T(8,128)(2,1)S(1)}, bf16[1024,128]{1,0:T(8,128)(2,1)S(1)}, u32[]{:S(2)}, u32[]{:S(2)}) collective-permute-start(bf16[1024,128]{1,0:T(8,128)(2,1)S(1)} %pad_maximum_fusion), channel_id=1, source_target_pairs={{0,2},{2,0},{1,3},{3,1},{4,6},{6,4},{5,7},{7,5},{8,10},{10,8},{9,1... | collective-permute-start | bytes 786440 | tf_op jit(solution)/shard_map/ppermute | solution.py:278
  58.8 6.3 %collective-permute-done.1 = bf16[1024,128]{1,0:T(8,128)(2,1)S(1)} collective-permute-done((bf16[1024,128]{1,0:T(8,128)(2,1)S(1)}, bf16[1024,128]{1,0:T(8,128)(2,1)S(1)}, u32[]{:S(2)}, u32[]{:S(2)}) %collective-permute-start.1) | collective-permute-done | bytes 262176 | tf_op jit(solution)/shard_map/ppermute | solution.py:278
  65.1 2.1 collective-permute-start.2
  67.2 1.8 copy.10
  69.0 10.4 %collective-permute-done.2.q_other = bf16[2064,128]{1,0:T(8,128)(2,1)} collective-permute-done((bf16[2064,128]{1,0:T(8,128)(2,1)S(1)}, bf16[2064,128]{1,0:T(8,128)(2,1)}, u32[]{:S(2)}, u32[]{:S(2)}) %collective-permute-start.2) | collective-permute-done | bytes 528416 | tf_op jit(solution)/shard_map/ppermute | solution.py:279
  79.4 1.0 copy-done.4
  80.4 11.2 %shard_map.96 = bf16[8,528,128]{2,1,0:T(8,128)(2,1)} custom-call(s32[6]{0:T(128)} %stack.24.place, bf16[4,4,272,128]{3,2,1,0:T(8,128)(2,1)} %copy-done.4, bf16[2064,128]{1,0:T(8,128)(2,1)} %copy-done.7, bf16[2064,128]{1,0:T(8,128)(2,1)} %collective-permute-done.2.q_other, bf16[256,3072]{1,0:T(8,128)(2,1)} %bitcast.12), custom_call_target="tpu_custom_call" | custom-call | flops 20000000000 | bytes 4194304 | tf_op jit(solution)/shard_map/pallas_call | solution.py:231
  91.6 20.1 %all_to_all.41.parts = bf16[8,528,128]{2,1,0:T(8,128)(2,1)S(1)} all-to-all(bf16[8,528,128]{2,1,0:T(8,128)(2,1)} %shard_map.96), channel_id=1, replica_groups=mesh['zh'=4,'zl'=4,'yl'=2,'yh'=2,'xh'=2,'xl'=2,'c'=2] {'yl','xl','c'}, dimensions={0} | all-to-all | bytes 2162688 | tf_op jit(solution)/shard_map/all_to_all | solution.py:301
  111.7 1.1 shard_map.97
  112.8 5.7 %all-to-all-start.3 = ((bf16[4,512,128]{2,1,0:T(8,128)(2,1)}), bf16[4,512,128]{2,1,0:T(8,128)(2,1)S(1)}, u32[]{:S(2)}, u32[]{:S(2)}) async-start(bf16[4,512,128]{2,1,0:T(8,128)(2,1)} %get-tuple-element.8), calls=%async_computation.3 | async-start | bytes 1048576 | tf_op jit(solution)/shard_map/all_to_all | solution.py:307
  118.5 12.5 %all_gather.7.hidden_t = bf16[768,512]{1,0:T(8,128)(2,1)} all-gather(bf16[192,512]{1,0:T(8,128)(2,1)S(1)} %bitcast.17), channel_id=1, replica_groups=mesh['zh'=4,'zl'=4,'yl'=2,'yh'=2,'xh'=2,'xl'=2,'c'=2] {'xl','c'}, dimensions={0}, use_global_device_ids=true | all-gather | bytes 983040 | tf_op jit(solution)/shard_map/all_gather | solution.py:281
  131.0 0.8 copy-done.2
  131.8 5.0 %shard_map.98 = bf16[8,896,128]{2,1,0:T(8,128)(2,1)} custom-call(s32[6]{0:T(128)} %stack.24.place, bf16[768,2048]{1,0:T(8,128)(2,1)} %all-gather.2.cloned.1.call-done.weight_t, bf16[768,512]{1,0:T(8,128)(2,1)} %all_gather.7.hidden_t, bf16[4,512,128]{2,1,0:T(8,128)(2,1)} %copy-done.2, bf16[32,4096]{1,0:T(8,128)(2,1)} %teacher.1), custom_call_target="tpu_custom_call" | custom-call | bytes 4194304 | tf_op jit(solution)/shard_map/pallas_call | solution.py:231
  136.8 32.5 %all_to_all.42.own = bf16[8,896,128]{2,1,0:T(8,128)(2,1)S(1)} all-to-all(bf16[8,896,128]{2,1,0:T(8,128)(2,1)} %shard_map.98), channel_id=1, replica_groups=mesh['zh'=4,'zl'=4,'yl'=2,'yh'=2,'xh'=2,'xl'=2,'c'=2] {'xl','yh','xh'}, dimensions={0} | all-to-all | bytes 3670016 | tf_op jit(solution)/shard_map/all_to_all | solution.py:316
  169.2 3.6 %collective-permute-start.3 = (bf16[8,896,128]{2,1,0:T(8,128)(2,1)S(1)}, bf16[8,896,128]{2,1,0:T(8,128)(2,1)S(1)}, u32[]{:S(2)}, u32[]{:S(2)}) collective-permute-start(bf16[8,896,128]{2,1,0:T(8,128)(2,1)S(1)} %all_to_all.42.own), channel_id=1, source_target_pairs={{0,1},{1,0},{2,3},{3,2},{4,5},{5,4},{6,7},{7,6},{8,9},{9,8},{10,11... | collective-permute-start | bytes 5505032 | tf_op jit(solution)/shard_map/ppermute | solution.py:317
  173.5 2.7 %collective-permute-done.3.other = bf16[8,896,128]{2,1,0:T(8,128)(2,1)S(1)} collective-permute-done((bf16[8,896,128]{2,1,0:T(8,128)(2,1)S(1)}, bf16[8,896,128]{2,1,0:T(8,128)(2,1)S(1)}, u32[]{:S(2)}, u32[]{:S(2)}) %collective-permute-start.3) | collective-permute-done | bytes 1835040 | tf_op jit(solution)/shard_map/ppermute | solution.py:317
  176.2 2.7 %shard_map.100 = bf16[4,8,96,256]{3,2,1,0:T(8,128)(2,1)S(1)} custom-call(s32[6]{0:T(128)S(1)} %copy-done.1, bf16[8,896,128]{2,1,0:T(8,128)(2,1)S(1)} %all_to_all.42.own, bf16[8,896,128]{2,1,0:T(8,128)(2,1)S(1)} %collective-permute-done.3.other, bf16[256,3072]{1,0:T(8,128)(2,1)S(1)} %bitcast.14, f32[256,256]{1,0:T(8,128)S(1)} %shard_map.99.own_projected), custom_call_target="tpu_custom_call" | custom-call | flops 800000000 | bytes 4194304 | tf_op jit(solution)/shard_map/pallas_call | solution.py:231
  179.0 38.3 %all_to_all.43.terms = bf16[4,8,96,256]{3,2,1,0:T(8,128)(2,1)S(1)} all-to-all(bf16[4,8,96,256]{3,2,1,0:T(8,128)(2,1)S(1)} %shard_map.100), channel_id=1, replica_groups=mesh['zh'=4,'zl'=4,'yl'=2,'yh'=2,'xh'=2,'xl'=2,'c'=2] {'zl'}, dimensions={0} | all-to-all | bytes 3145728 | tf_op jit(solution)/shard_map/all_to_all | solution.py:329
  217.3 4.8 %all-to-all-start.7 = ((bf16[4,128,128]{2,1,0:T(8,128)(2,1)}), bf16[4,128,128]{2,1,0:T(8,128)(2,1)S(1)}, u32[]{:S(2)}, u32[]{:S(2)}) async-start(bf16[4,128,128]{2,1,0:T(8,128)(2,1)} %bitcast.9), calls=%async_computation.7 | async-start | bytes 262144 | tf_op jit(solution)/shard_map/all_to_all | solution.py:304
  222.1 0.9 shard_map.101
  223.0 2.7 all-to-all-done.7
  225.7 15.2 %all-to-all-start.6 = ((bf16[8,96,256]{2,1,0:T(8,128)(2,1)}), bf16[8,96,256]{2,1,0:T(8,128)(2,1)S(1)}, u32[]{:S(2)}, u32[]{:S(2)}) async-start(bf16[8,96,256]{2,1,0:T(8,128)(2,1)} %shard_map.101), calls=%async_computation.6 | async-start | bytes 786432 | tf_op jit(solution)/shard_map/all_to_all | solution.py:330
  240.9 0.8 copy.11
  241.6 23.2 %all-to-all-done.6.terms = bf16[8,96,256]{2,1,0:T(8,128)(2,1)S(1)} async-done(((bf16[8,96,256]{2,1,0:T(8,128)(2,1)}), bf16[8,96,256]{2,1,0:T(8,128)(2,1)S(1)}, u32[]{:S(2)}, u32[]{:S(2)}) %all-to-all-start.6) | async-done | bytes 393248 | tf_op jit(solution)/shard_map/all_to_all | solution.py:330
  264.8 0.7 shard_map.102
  (27 shorter events, 1.5 us)
Async XLA Ops:
  45.6 4.5 %copy-start.5 = (bf16[512,128]{1,0:T(8,128)(2,1)S(1)}, bf16[512,128]{1,0:T(8,128)(2,1)}, u32[]{:S(2)}) copy-start(bf16[512,128]{1,0:T(8,128)(2,1)} %param.8) | copy-start | bytes 393220
  45.6 33.8 %all-to-all-start.1 = ((bf16[4,4,272,128]{3,2,1,0:T(8,128)(2,1)}), bf16[4,4,272,128]{3,2,1,0:T(8,128)(2,1)S(1)}, u32[]{:S(2)}, u32[]{:S(2)}) async-start(bf16[4,4,272,128]{3,2,1,0:T(8,128)(2,1)} %broadcast_in_dim.2), calls=%async_computation.1 | async-start | bytes 2228224 | tf_op jit(solution)/shard_map/all_to_all | solution.py:275
  49.4 15.7 %copy-start.8 = (bf16[16,128]{1,0:T(8,128)(2,1)S(1)}, bf16[16,128]{1,0:T(8,128)(2,1)}, u32[]{:S(2)}) copy-start(bf16[16,128]{1,0:T(8,128)(2,1)} %get-tuple-element.7) | copy-start | bytes 12292
  49.4 17.8 %copy-start.3 = (bf16[3072,256]{1,0:T(8,128)(2,1)S(1)}, bf16[3072,256]{1,0:T(8,128)(2,1)}, u32[]{:S(2)}) copy-start(bf16[3072,256]{1,0:T(8,128)(2,1)} %param.14) | copy-start | bytes 4718596
  49.4 81.6 %all-gather.2.cloned.1.call-start = ((), (), s32[]{:S(2)}) async-start(), calls=%async_computation.8 | async-start | bytes 3932160 | tf_op jit(solution)/shard_map/all_gather | solution.py:280
  50.1 5.5 %collective-permute-start = (bf16[512,128]{1,0:T(8,128)(2,1)S(1)}, bf16[512,128]{1,0:T(8,128)(2,1)S(1)}, u32[]{:S(2)}, u32[]{:S(2)}) collective-permute-start(bf16[512,128]{1,0:T(8,128)(2,1)S(1)} %copy-done.5), channel_id=1, source_target_pairs={{0,1},{1,0},{2,3},{3,2},{4,5},{5,4},{6,7},{7,6},{8,9},{9,8},{10,11... | collective-permute-start | bytes 393224 | tf_op jit(solution)/shard_map/ppermute | solution.py:277
  55.6 9.4 %collective-permute-start.1 = (bf16[1024,128]{1,0:T(8,128)(2,1)S(1)}, bf16[1024,128]{1,0:T(8,128)(2,1)S(1)}, u32[]{:S(2)}, u32[]{:S(2)}) collective-permute-start(bf16[1024,128]{1,0:T(8,128)(2,1)S(1)} %pad_maximum_fusion), channel_id=1, source_target_pairs={{0,2},{2,0},{1,3},{3,1},{4,6},{6,4},{5,7},{7,5},{8,10},{10,8},{9,1... | collective-permute-start | bytes 786440 | tf_op jit(solution)/shard_map/ppermute | solution.py:278
  65.1 3.9 %copy-start.7 = (bf16[2064,128]{1,0:T(8,128)(2,1)}, bf16[2064,128]{1,0:T(8,128)(2,1)S(1)}, u32[]{:S(2)}) copy-start(bf16[2064,128]{1,0:T(8,128)(2,1)S(1)} %constant_dynamic-update-slice_fusion.q_own) | copy-start | bytes 1585156
  65.1 14.3 %collective-permute-start.2 = (bf16[2064,128]{1,0:T(8,128)(2,1)S(1)}, bf16[2064,128]{1,0:T(8,128)(2,1)}, u32[]{:S(2)}, u32[]{:S(2)}) collective-permute-start(bf16[2064,128]{1,0:T(8,128)(2,1)S(1)} %constant_dynamic-update-slice_fusion.q_own), channel_id=1, source_target_pairs={{0,16},{16,0},{1,17},{17,1},{2,18},{18,2},{3,19},{19,3},{4,20},{20... | collective-permute-start | bytes 1585160 | tf_op jit(solution)/shard_map/ppermute | solution.py:279
  79.4 1.0 copy-start.4
  111.7 6.8 %copy-start.6 = (bf16[512,192]{0,1:T(8,128)(2,1)S(1)}, bf16[512,192]{0,1:T(8,128)(2,1)}, u32[]{:S(2)}) copy-start(bf16[512,192]{0,1:T(8,128)(2,1)} %param.12) | copy-start | bytes 589828
  112.8 18.2 %all-to-all-start.3 = ((bf16[4,512,128]{2,1,0:T(8,128)(2,1)}), bf16[4,512,128]{2,1,0:T(8,128)(2,1)S(1)}, u32[]{:S(2)}, u32[]{:S(2)}) async-start(bf16[4,512,128]{2,1,0:T(8,128)(2,1)} %get-tuple-element.8), calls=%async_computation.3 | async-start | bytes 1048576 | tf_op jit(solution)/shard_map/all_to_all | solution.py:307
  130.9 0.8 copy-start.2
  136.7 36.1 %copy-start = (bf16[3072,256]{0,1:T(8,128)(2,1)S(1)}, bf16[3072,256]{0,1:T(8,128)(2,1)}, u32[]{:S(2)}) copy-start(bf16[3072,256]{0,1:T(8,128)(2,1)} %copy.10) | copy-start | bytes 4718596
  169.2 7.0 %copy-start.1 = (s32[6]{0:T(128)S(1)}, s32[6]{0:T(128)}, u32[]{:S(2)}) copy-start(s32[6]{0:T(128)} %stack.24.place) | copy-start | bytes 76
  169.2 7.0 %collective-permute-start.3 = (bf16[8,896,128]{2,1,0:T(8,128)(2,1)S(1)}, bf16[8,896,128]{2,1,0:T(8,128)(2,1)S(1)}, u32[]{:S(2)}, u32[]{:S(2)}) collective-permute-start(bf16[8,896,128]{2,1,0:T(8,128)(2,1)S(1)} %all_to_all.42.own), channel_id=1, source_target_pairs={{0,1},{1,0},{2,3},{3,2},{4,5},{5,4},{6,7},{7,6},{8,9},{9,8},{10,11... | collective-permute-start | bytes 5505032 | tf_op jit(solution)/shard_map/ppermute | solution.py:317
  217.3 8.4 %all-to-all-start.7 = ((bf16[4,128,128]{2,1,0:T(8,128)(2,1)}), bf16[4,128,128]{2,1,0:T(8,128)(2,1)S(1)}, u32[]{:S(2)}, u32[]{:S(2)}) async-start(bf16[4,128,128]{2,1,0:T(8,128)(2,1)} %bitcast.9), calls=%async_computation.7 | async-start | bytes 262144 | tf_op jit(solution)/shard_map/all_to_all | solution.py:304
  225.7 39.1 %all-to-all-start.6 = ((bf16[8,96,256]{2,1,0:T(8,128)(2,1)}), bf16[8,96,256]{2,1,0:T(8,128)(2,1)S(1)}, u32[]{:S(2)}, u32[]{:S(2)}) async-start(bf16[8,96,256]{2,1,0:T(8,128)(2,1)} %shard_map.101), calls=%async_computation.6 | async-start | bytes 786432 | tf_op jit(solution)/shard_map/all_to_all | solution.py:330
Sparse Core Ops, SparseCore 0:
  52.3 43.1 all-gather.1

commit v8 on v6

--- a/solution.py
+++ b/solution.py
@@ -23,16 +23,44 @@
 BLOCKS = 4
 
 
-def start_kernel(place, keys, values, docs, packed, doc_rows):
+def start_kernel(place, keys, values, docs, queries, hidden_t, packed, doc_rows, sent, kept):
     rows = jnp.concatenate([docs[...].astype(F32), jnp.zeros((12, 128), F32)], axis=0).astype(BF)
     for copy in range(4):
         packed[copy, 0:128, :] = keys[...]
         packed[copy, 128:256, :] = values[...]
         packed[copy, 256:272, :] = rows
     doc_rows[...] = rows
-
-
-def attend_kernel(place, kv0, kv1, kv2, kv3_low, kv3_high, q_own, q_other, early, out, kv, q_all, v_turned, s_buf, info_v, info, sem):
+    sent[0:512, :] = queries[...]
+    for xl in range(2):
+        kept[xl] = hidden_t[:, pl.ds(pl.multiple_of((xl * 2 + place[2]) * 128, 128), 128)]
+        other = pl.ds(pl.multiple_of((xl * 2 + 1 - place[2]) * 128, 128), 128)
+        sent[512 + xl * 192:704 + xl * 192, :] = hidden_t[:, other]
+
+
+def turn_kernel(place, sent, received, kept, two, kept_out):
+    xl = place[3]
+    two[0:512, :] = sent[0:512, :]
+    two[512:1024, :] = received[0:512, :]
+    two[1024:1216, :] = kept[1 - xl]
+    two[1216:1408, :] = received[pl.ds(pl.multiple_of(512 + (1 - xl) * 192, 64), 192), :]
+    kept_out[0] = kept[xl]
+    kept_out[1] = received[pl.ds(pl.multiple_of(512 + xl * 192, 64), 192), :]
+
+
+def join_kernel(two, received, doc_rows, token, q_own, hidden_out):
+    q_own[0:1024, :] = two[0:1024, :]
+    q_own[1024:2048, :] = received[0:1024, :]
+    q_own[2048:2064, :] = doc_rows[...]
+    for i in range(2):
+        hidden_out[i] = received[1024 + i * 192:1216 + i * 192, :]
+
+
+def transpose_kernel(x, out, token):
+    out[...] = x[...].T
+    token[...] = jnp.zeros((8, 128), F32)
+
+
+def attend_kernel(place, kv0, kv1, kv2, kv3_low, kv3_high, q_own, q_other, out, kv, q_all, v_turned, q_even, q_odd, s_even, s_odd, max_even, max_odd, acc, total, info_v, info, sem):
     j, yl, z = place[0], place[4], place[5]
     copies = [
         pltpu.make_async_copy(src, dst, sem.at[i])
@@ -69,22 +97,34 @@
     key_iota = lax.broadcasted_iota(jnp.int32, (128, 512), 0)
     row_iota = lax.broadcasted_iota(jnp.int32, (1, 512), 1) % 128
 
-    def one_tile(tile, carry):
-        side, rc = tile // 4, tile % 4
-        yl_q = jnp.where(side == 0, yl, 1 - yl)
-        dest = yl_q * 4 + rc
-        row0 = pl.multiple_of(rc * 128, 128)
-        q = jnp.concatenate([q_all[side, pl.ds(pl.multiple_of((h ^ j) * 512, 512) + row0, 128), :] for h in range(4)], axis=0)
-        row_docs = jnp.concatenate([info_v[pl.ds(16 + tile, 1), :]] * 4, axis=1)
-        first, last = info[16 + tile, 0], info[16 + tile, 127]
-        q_min = (2 * z + yl_q) * 512 + row0
-        q_pos = q_min + row_iota
-
-        def scores(ch):
-            keys = jnp.concatenate([kv[i, ch, 0:128, :] for i in range(BLOCKS)], axis=0)
-            return lax.dot_general(keys, q, (((1,), (1,)), ((), ())), preferred_element_type=F32) * SCALE2
-
-        def mask(ch, s):
+    first_doc = jnp.minimum(info[16, 0], info[20, 0])
+    begin = jnp.int32(0)
+    for ch in range(4):
+        fewest = functools.reduce(jnp.minimum, [info[ch * BLOCKS + i, first_doc] for i in range(BLOCKS)])
+        begin = begin + (fewest >= (j + 1) * 128).astype(jnp.int32)
+    end = z // BLOCKS + 1
+
+    def begin_scores(tile, q_ref, max_ref):
+        side, row0 = tile // 4, pl.multiple_of(tile % 4 * 128, 128)
+        for h in range(4):
+            q_ref[h * 128:(h + 1) * 128, :] = q_all[side, pl.ds(pl.multiple_of((h ^ j) * 512, 512) + row0, 128), :]
+        max_ref[...] = jnp.full((1, 512), EMPTY, F32)
+
+    def is_full(tile, ch):
+        yl_q = jnp.where(tile // 4 == 0, yl, 1 - yl)
+        q_min = (2 * z + yl_q) * 512 + tile % 4 * 128
+        last = info[16 + tile, 127]
+        most = functools.reduce(jnp.maximum, [info[ch * BLOCKS + i, last] for i in range(BLOCKS)])
+        k_max = (2 * (ch * BLOCKS + BLOCKS - 1) + yl) * 512 + j * 128 + 127
+        return (k_max <= q_min) & (most <= j * 128)
+
+    def put_scores(tile, ch, masked, q_ref, s_ref, max_ref):
+        keys = jnp.concatenate([kv[i, ch, 0:128, :] for i in range(BLOCKS)], axis=0)
+        s = lax.dot_general(keys, q_ref[...], (((1,), (1,)), ((), ())), preferred_element_type=F32) * SCALE2
+        if masked:
+            yl_q = jnp.where(tile // 4 == 0, yl, 1 - yl)
+            q_pos = (2 * z + yl_q) * 512 + tile % 4 * 128 + row_iota
+            row_docs = jnp.concatenate([info_v[pl.ds(16 + tile, 1), :]] * 4, axis=1)
             parts = []
             for i in range(BLOCKS):
                 low = jnp.zeros((1, 512), jnp.int32)
@@ -94,47 +134,69 @@
                 high = q_pos - ((2 * (ch * 4 + where[i]) + yl) * 512 + j * 128)
                 ok = (key_iota >= low) & (key_iota <= high)
                 parts.append(jnp.where(ok, s[i * 128:(i + 1) * 128], MASKED))
-            return jnp.concatenate(parts, axis=0)
-
-        def find_max(ch, run_max):
-            most = functools.reduce(jnp.maximum, [info[ch * BLOCKS + i, last] for i in range(BLOCKS)])
-            k_max = (2 * (ch * BLOCKS + BLOCKS - 1) + yl) * 512 + j * 128 + 127
-            full = (k_max <= q_min) & (most <= j * 128)
-
-            def keep(s):
-                s_buf[ch] = s
-                return jnp.max(s, axis=0, keepdims=True)
-
-            return jnp.maximum(run_max, lax.cond(full, lambda: keep(scores(ch)), lambda: keep(mask(ch, scores(ch)))))
-
-        def add_up(ch, state):
-            run_sum, acc = state
-            w = jnp.exp2(s_buf[ch] - run_max)
-            cols = pl.ds(pl.multiple_of(ch * (BLOCKS * 128), BLOCKS * 128), BLOCKS * 128)
-            blended = jnp.dot(v_turned[:, cols], w.astype(BF), preferred_element_type=F32)
-            return run_sum + jnp.sum(w, axis=0, keepdims=True), acc + blended
-
-        begin = jnp.int32(0)
-        for ch in range(4):
-            fewest = functools.reduce(jnp.minimum, [info[ch * BLOCKS + i, first] for i in range(BLOCKS)])
-            begin = begin + (fewest >= (j + 1) * 128).astype(jnp.int32)
-        end = z // BLOCKS + 1
-        run_max = lax.fori_loop(begin, end, find_max, jnp.full((1, 512), EMPTY, F32))
-        run_sum, acc = lax.fori_loop(begin, end, add_up, (jnp.zeros((1, 512), F32), jnp.zeros((128, 512), F32)))
+            s = jnp.concatenate(parts, axis=0)
+        s_ref[ch] = s
+        max_ref[...] = jnp.maximum(max_ref[...], jnp.max(s, axis=0, keepdims=True))
+
+    def add_up(ch, s_ref, max_ref):
+        w = jnp.exp2(s_ref[ch] - max_ref[...])
+        cols = pl.ds(pl.multiple_of(ch * (BLOCKS * 128), BLOCKS * 128), BLOCKS * 128)
+        acc[...] += jnp.dot(v_turned[:, cols], w.astype(BF), preferred_element_type=F32)
+        total[...] += jnp.sum(w, axis=0, keepdims=True)
+
+    def finish(tile, max_ref):
+        run_sum, run_max = total[...], max_ref[...]
         seen = run_sum > 0
-        o = (acc * (1.0 / jnp.where(seen, run_sum, 1.0))).astype(BF)
+        o = (acc[...] * (1.0 / jnp.where(seen, run_sum, 1.0))).astype(BF)
         lse = jnp.where(seen, run_max + jnp.log2(jnp.where(seen, run_sum, 1.0)), EMPTY)
         hi = lse.astype(BF).astype(F32)
         mid = (lse - hi).astype(BF).astype(F32)
         lo = lse - hi - mid
+        dest = jnp.where(tile // 4 == 0, yl, 1 - yl) * 4 + tile % 4
         rows = [part[:, h * 128:(h + 1) * 128] for part in (hi, mid, lo) for h in range(4)]
         rows.append(jnp.zeros((4, 128), F32))
         for h in range(4):
             out[dest, h * 128:(h + 1) * 128, :] = o[:, h * 128:(h + 1) * 128]
         out[dest, 512:528, :] = jnp.concatenate(rows, axis=0).astype(BF)
+        acc[...] = jnp.zeros((128, 512), F32)
+        total[...] = jnp.zeros((1, 512), F32)
+
+    def sweep(tile, put, use):
+        if put is not None:
+            begin_scores(tile, put[0], put[2])
+
+        def one(ch, carry):
+            def work(masked):
+                if put is not None:
+                    put_scores(tile, ch, masked, *put)
+                if use is not None:
+                    add_up(ch, use[1], use[2])
+
+            if put is None:
+                work(False)
+            else:
+                full = is_full(tile, ch)
+                pl.when(full)(lambda: work(False))
+                pl.when(jnp.logical_not(full))(lambda: work(True))
+            return carry
+
+        lax.fori_loop(begin, end, one, 0)
+        if use is not None:
+            finish(tile - 1, use[2])
+
+    even, odd = (q_even, s_even, max_even), (q_odd, s_odd, max_odd)
+    acc[...] = jnp.zeros((128, 512), F32)
+    total[...] = jnp.zeros((1, 512), F32)
+    sweep(0, even, None)
+
+    def two_tiles(pair, carry):
+        sweep(2 * pair + 1, odd, even)
+        sweep(2 * pair + 2, even, odd)
         return carry
 
-    lax.fori_loop(0, 8, one_tile, 0)
+    lax.fori_loop(0, 3, two_tiles, 0)
+    sweep(7, odd, even)
+    sweep(8, None, odd)
 
 
 def combine_kernel(parts, out, copies):
@@ -152,28 +214,25 @@
             copies[copy, rows, :] = total
 
 
-def student_kernel(place, gathered, att, teacher, out, weights, hidden, sem):
+def student_kernel(place, weight_t, att, kept, received, teacher, out, weights, sem):
     copies = []
-    own_rows = pl.ds(pl.multiple_of(2048 + place[0] * 128, 128), 128)
-    hidden_copy = pltpu.make_async_copy(gathered.at[:, own_rows], hidden, sem.at[4])
     for part in range(4):
         rows = pl.ds(part * 192, 192)
-        copies.append(pltpu.make_async_copy(gathered.at[rows, pl.ds(0, 2048)], weights.at[rows], sem.at[part]))
-    copies[0].start()
-    hidden_copy.start()
-    for copy in copies[1:]:
+        copies.append(pltpu.make_async_copy(weight_t.at[rows], weights.at[rows], sem.at[part]))
+    for copy in copies:
         copy.start()
     for chip in range(8):
         first = (chip % 4 * 4 + chip // 4 * 2) * 256
         for i in range(4):
             out[chip, 768 + i * 32:800 + i * 32, :] = teacher[:, first + i * 128:first + (i + 1) * 128]
     att_all = att[...].reshape(2048, 128)
-    hidden_copy.wait()
     for part in range(4):
+        source = part ^ place[0]
+        hidden = jnp.where(source < 2, kept[source % 2].astype(F32), received[source % 2].astype(F32))
         copies[part].wait()
         rows = slice(part * 192, (part + 1) * 192)
         mixed = jnp.dot(weights[rows, :], att_all, preferred_element_type=F32)
-        student = (hidden[rows, :].astype(F32) + mixed).astype(BF)
+        student = (hidden + mixed).astype(BF)
         for copy in range(8):
             out[copy, rows, :] = student
 
@@ -262,59 +321,82 @@
     return jax.ShapeDtypeStruct(dims, dtype)
 
 
-def start(place, keys, values, docs):
+def start(place, keys, values, docs, queries, hidden_t):
     def block(*dims):
         return pl.BlockSpec(dims, lambda i, place: (0,) * len(dims))
 
     picked = pl.BlockSpec((128, 128), lambda i, place: (place[0], place[1]))
-    outs = [(4, 272, 128), (16, 128)]
+    outs = [(4, 272, 128), (16, 128), (896, 128), (2, 192, 128)]
     return pl.pallas_call(
         start_kernel,
         grid_spec=pltpu.PrefetchScalarGridSpec(
             num_scalar_prefetch=1,
             grid=(1,),
-            in_specs=[picked, picked, block(4, 128)],
+            in_specs=[picked, picked, block(4, 128), block(512, 128), block(192, 512)],
             out_specs=[block(*dims) for dims in outs],
         ),
         out_shape=[shape(*dims) for dims in outs],
-    )(place, keys, values, docs)
+    )(place, keys, values, docs, queries, hidden_t)
+
+
+def transposed(x):
+    rows, columns = x.shape
+    return pl.pallas_call(
+        transpose_kernel,
+        grid=(4,),
+        in_specs=[pl.BlockSpec((rows // 4, columns), lambda i: (i, 0))],
+        out_specs=[pl.BlockSpec((columns, rows // 4), lambda i: (0, i)), pl.BlockSpec((8, 128), lambda i: (0, 0))],
+        out_shape=[shape(columns, rows), shape(8, 128, dtype=F32)],
+        compiler_params=pltpu.CompilerParams(vmem_limit_bytes=58 * 1024 * 1024),
+    )(x)
 
 
 def on_device(queries, keys, values, doc_ids, hidden, out_weight, projector, teacher):
-    zl, yl, c = lax.axis_index("zl"), lax.axis_index("yl"), lax.axis_index("c")
-    j = lax.axis_index("xl") * 2 + c
+    zl, yl, xl, c = lax.axis_index("zl"), lax.axis_index("yl"), lax.axis_index("xl"), lax.axis_index("c")
+    j = xl * 2 + c
     z = lax.axis_index("zh") * 4 + zl
     g = lax.axis_index("yh") * 2 + lax.axis_index("xh")
     swap = [(0, 1), (1, 0)]
-    place = jnp.stack([j, g, c, c, yl, z, zl]).astype(jnp.int32)
+    place = jnp.stack([j, g, c, xl, yl, z, zl]).astype(jnp.int32)
 
     def from_z(x, shift):
         return lax.ppermute(x, ("zh", "zl"), [((i + shift) % 16, i) for i in range(16)])
 
     docs = doc_ids.reshape(4, 128)
-    packed, doc_rows = start(place, keys, values, docs)
+    packed, doc_rows, sent, hidden_kept = start(place, keys, values, docs, queries, hidden.T)
     kv_own = lax.all_to_all(packed, "zh", 0, 0)
     kv_below, kv_above = from_z(kv_own, -1), from_z(kv_own, 1)
     kv_low, kv_high = from_z(kv_own[0:2], -2), from_z(kv_own[2:4], 2)
 
-    q_two = jnp.concatenate([queries, lax.ppermute(queries, "c", swap)], axis=0)
-    q_own = jnp.concatenate([q_two, lax.ppermute(q_two, "xl", swap), doc_rows], axis=0)
+    projector_t, token = transposed(projector)
+    half = shape(2, 192, 128)
+    two, hidden_kept = call(
+        turn_kernel, [shape(1408, 128), half], [SMEM] + [VMEM] * 3, (place, sent, lax.ppermute(sent, "c", swap), hidden_kept), 16
+    )
+    q_own, hidden_received = call(
+        join_kernel, [shape(2064, 128), half], [VMEM] * 4, (two, lax.ppermute(two, "xl", swap), doc_rows, token), 16
+    )
     q_other = lax.ppermute(q_own, "yl", swap)
-    gathered = lax.all_gather(jnp.concatenate([out_weight.T, hidden.T], axis=1), GROUP, axis=0, tiled=True)
-    projector_t = projector.T
-
+    weight_t = lax.all_gather(out_weight.T, GROUP, axis=0, tiled=True)
     partial = call(
         attend_kernel,
         shape(8, 528, 128),
-        [SMEM] + [ANY] * 8,
-        (place, kv_own, kv_below, kv_above, kv_low, kv_high, q_own, q_other, projector_t),
+        [SMEM] + [ANY] * 7,
+        (place, kv_own, kv_below, kv_above, kv_low, kv_high, q_own, q_other),
         40,
         2 * 10 ** 10,
         scratch=[
             pltpu.VMEM((4, 4, 272, 128), BF),
             pltpu.VMEM((2, 2064, 128), BF),
             pltpu.VMEM((128, 2048), BF),
+            pltpu.VMEM((512, 128), BF),
+            pltpu.VMEM((512, 128), BF),
             pltpu.VMEM((4, 512, 512), F32),
+            pltpu.VMEM((4, 512, 512), F32),
+            pltpu.VMEM((1, 512), F32),
+            pltpu.VMEM((1, 512), F32),
+            pltpu.VMEM((128, 512), F32),
+            pltpu.VMEM((1, 512), F32),
             pltpu.VMEM((24, 128), jnp.int32),
             pltpu.SMEM((24, 128), jnp.int32),
             pltpu.SemaphoreType.DMA((8,)),
@@ -331,10 +413,10 @@
     student = call(
         student_kernel,
         shape(8, 896, 128),
-        [SMEM, HBM, VMEM, VMEM],
-        (place, gathered, att_all, teacher),
+        [SMEM, HBM] + [VMEM] * 4,
+        (place, weight_t, att_all, hidden_kept, hidden_received, teacher),
         24,
-        scratch=[pltpu.VMEM((768, 2048), BF), pltpu.VMEM((768, 128), BF), pltpu.SemaphoreType.DMA((5,))],
+        scratch=[pltpu.VMEM((768, 2048), BF), pltpu.SemaphoreType.DMA((4,))],
     )
     own = lax.all_to_all(student, CHIPS, 0, 0)
     other = lax.ppermute(own, "c", swap)

time: 243 us -> 243 us (level)
  waiting for transfers between devices: 46.1 us -> 51.6 us
  local copies, waits for them, and re-layouts: 11.3 us -> 8.28 us
  Pallas kernels: 22.5 us -> 25.1 us
    all_to_all x1, waiting for transfers between devices: 5.42 us -> 0.01 us  [on_device(): kv_own = lax.all_to_all(packed, 'zh', 0, 0)]
    ppermute x2, waiting for transfers between devices: 9.22 us -> 13.7 us  [the longest x1 12.4 us: on_device(): lax.ppermute(two, 'xl', swap)]
    ppermute x8, waiting for transfers between devices: 9.01 us -> 13 us  [from_z(): lax.ppermute(x, ('zh', 'zl'), [((i + shift) % 16, i) for i in range(16)])]
    pallas_call x0 -> x1, Pallas kernels: none -> 3.93 us  [transposed(): pl.pallas_call(transpose_kernel, grid=(4,), in_specs=[pl.BlockSpec((rows...]
    all_to_all x1, starting transfers between devices: 19.3 us -> 15.7 us  [on_device(): lax.all_to_all(near, ('zh', 'yl'), 0, 0)]
    ppermute x8, starting transfers between devices: 29.1 us -> 32.4 us  [from_z(): lax.ppermute(x, ('zh', 'zl'), [((i + shift) % 16, i) for i in range(16)])]
    unnamed x30 -> x20, local copies, waits for them, and re-layouts: 9.25 us -> 5.94 us
    pallas_call x9 -> x11, Pallas kernels: 20.2 us -> 18.5 us  [call(): pl.pallas_call(kernel, out_shape=out_shape, in_specs=specs, out_specs=VME...]
  transfers between devices with their start and end apart: 16 -> 16, of which waited for: 6 -> 7; matrix products, arithmetic and copies ran while one was open for 2% -> 1% of each run, Pallas kernels for 6% -> 7%
where the time goes in v8:
time: 243 us; the launch traced here: 242 us
  starting transfers between devices  79.5 us (33%)
  blocking collectives  62.8 us (26%)
  waiting for transfers between devices  51.6 us (21%)
  Pallas kernels  25.1 us (10%)
  between operations  14.2 us (6%)
  local copies, waits for them, and re-layouts  8.28 us (3%)
    ppermute x8, starting transfers between devices, from_z(): lax.ppermute(x, ('zh', 'zl'), [((i + shift) % 16, i) for i in range(16)])  32.4 us
    all_to_all x1, blocking collectives, on_device(): own = lax.all_to_all(student, CHIPS, 0, 0)  26 us
    all_to_all x1, waiting for transfers between devices, on_device(): lax.all_to_all(near, ('zh', 'yl'), 0, 0)  21.5 us
    all_to_all x1, blocking collectives, on_device(): lax.all_to_all(partial, OCTET, 0, 0)  21.1 us
    pallas_call x11, Pallas kernels, call(): pl.pallas_call(kernel, out_shape=out_shape, in_specs=specs, out_specs=VME...  18.5 us
    all_to_all x1, blocking collectives, on_device(): att_all = lax.all_to_all(att_copies, HEADSETS, 0, 0)  15.7 us
    all_to_all x1, starting transfers between devices, on_device(): lax.all_to_all(near, ('zh', 'yl'), 0, 0)  15.7 us
    all_to_all x1, starting transfers between devices, on_device(): kv_own = lax.all_to_all(packed, 'zh', 0, 0)  13.1 us
  transfers between devices with their start and end apart: 16, of which 7 were waited for; matrix products, arithmetic and copies ran while one was open for 1% of the time, Pallas kernels for 7%

profile of v8, /device:TPU:73, one launch (start us, length us, event | category | flops | bytes accessed | tf_op | source)
XLA Modules:
  0.0 241.5 jit_solution(119475163253875901)
XLA Ops:
  8.6 2.7 %shard_map.95 = (bf16[4,272,128]{2,1,0:T(8,128)(2,1)}, bf16[16,128]{1,0:T(8,128)(2,1)}, bf16[896,128]{1,0:T(8,128)(2,1)}, bf16[2,192,128]{2,1,0:T(8,128)(2,1)}) custom-call(s32[7]{0:T(128)} %stack.31.place, bf16[512,512]{1,0:T(8,128)(2,1)} %keys.1, bf16[512,512]{1,0:T(8,128)(2,1)} %values.1, s32[4,128]{1,0:T(4,128)} %bitcast.16, bf16[512,128]{1,0:T(8,128)(2,1)} %queries.1, ...), custom_call_target="tpu_custom_call" | custom-call | tf_op jit(solution)/shard_map/pallas_call | solution.py:330
  11.3 13.1 %all-to-all-start = ((bf16[4,272,128]{2,1,0:T(8,128)(2,1)}), bf16[4,272,128]{2,1,0:T(8,128)(2,1)S(1)}, u32[]{:S(2)}, u32[]{:S(2)}) async-start(bf16[4,272,128]{2,1,0:T(8,128)(2,1)} %get-tuple-element.19), calls=%async_computation | async-start | bytes 557056 | tf_op jit(solution)/shard_map/all_to_all | solution.py:367
  24.4 2.9 %collective-permute-start.4 = (bf16[896,128]{1,0:T(8,128)(2,1)}, bf16[896,128]{1,0:T(8,128)(2,1)S(1)}, u32[]{:S(2)}, u32[]{:S(2)}) collective-permute-start(bf16[896,128]{1,0:T(8,128)(2,1)} %get-tuple-element.20.sent), channel_id=1, source_target_pairs={{0,1},{1,0},{2,3},{3,2},{4,5},{5,4},{6,7},{7,6},{8,9},{9,8},{10,11... | collective-permute-start | bytes 688136 | tf_op jit(solution)/shard_map/ppermute | solution.py:374
  31.0 3.1 %collective-permute-start.5 = (bf16[1408,128]{1,0:T(8,128)(2,1)S(1)}, bf16[1408,128]{1,0:T(8,128)(2,1)S(1)}, u32[]{:S(2)}, u32[]{:S(2)}) collective-permute-start(bf16[1408,128]{1,0:T(8,128)(2,1)S(1)} %get-tuple-element.22.two), channel_id=1, source_target_pairs={{0,2},{2,0},{1,3},{3,1},{4,6},{6,4},{5,7},{7,5},{8,10},{10,8},{9,1... | collective-permute-start | bytes 1081352 | tf_op jit(solution)/shard_map/ppermute | solution.py:377
  34.1 3.9 %shard_map.97 = (bf16[256,3072]{1,0:T(8,128)(2,1)}, f32[8,128]{1,0:T(8,128)}) custom-call(bf16[3072,256]{1,0:T(8,128)(2,1)} %x.1), custom_call_target="tpu_custom_call" | custom-call | tf_op jit(solution)/shard_map/pallas_call | solution.py:344
  38.1 12.4 %collective-permute-done.5.received = bf16[1408,128]{1,0:T(8,128)(2,1)S(1)} collective-permute-done((bf16[1408,128]{1,0:T(8,128)(2,1)S(1)}, bf16[1408,128]{1,0:T(8,128)(2,1)S(1)}, u32[]{:S(2)}, u32[]{:S(2)}) %collective-permute-start.5) | collective-permute-done | bytes 360480 | tf_op jit(solution)/shard_map/ppermute | solution.py:377
  51.2 2.0 collective-permute-start.6
  53.3 2.9 %collective-permute-start = (bf16[4,272,128]{2,1,0:T(8,128)(2,1)S(1)}, bf16[4,272,128]{2,1,0:T(8,128)(2,1)S(1)}, u32[]{:S(2)}, u32[]{:S(2)}) collective-permute-start(bf16[4,272,128]{2,1,0:T(8,128)(2,1)S(1)} %all-to-all-done.kv0), channel_id=1, source_target_pairs={{480,0},{0,32},{32,64},{64,96},{96,128},{128,160},{160,192},{192,2... | collective-permute-start | bytes 835592 | tf_op jit(solution)/shard_map/ppermute | solution.py:363
  56.2 2.3 collective-permute-start.1
  58.6 8.3 %collective-permute-start.2 = (bf16[2,272,128]{2,1,0:T(8,128)(2,1)S(1)}, bf16[2,272,128]{2,1,0:T(8,128)(2,1)S(1)}, u32[]{:S(2)}, u32[]{:S(2)}) collective-permute-start(bf16[2,272,128]{2,1,0:T(8,128)(2,1)S(1)} %get-tuple-element.37), channel_id=1, source_target_pairs={{448,0},{480,32},{0,64},{32,96},{64,128},{96,160},{128,192},{160,2... | collective-permute-start | bytes 417800 | tf_op jit(solution)/shard_map/ppermute | solution.py:363
  66.9 1.9 collective-permute-start.3
  68.8 3.7 %collective-permute-done.2.kv3_low = bf16[2,272,128]{2,1,0:T(8,128)(2,1)S(1)} collective-permute-done((bf16[2,272,128]{2,1,0:T(8,128)(2,1)S(1)}, bf16[2,272,128]{2,1,0:T(8,128)(2,1)S(1)}, u32[]{:S(2)}, u32[]{:S(2)}) %collective-permute-start.2) | collective-permute-done | bytes 139296 | tf_op jit(solution)/shard_map/ppermute | solution.py:363
  72.5 3.6 %collective-permute-done.3.kv3_high = bf16[2,272,128]{2,1,0:T(8,128)(2,1)S(1)} collective-permute-done((bf16[2,272,128]{2,1,0:T(8,128)(2,1)S(1)}, bf16[2,272,128]{2,1,0:T(8,128)(2,1)S(1)}, u32[]{:S(2)}, u32[]{:S(2)}) %collective-permute-start.3) | collective-permute-done | bytes 139296 | tf_op jit(solution)/shard_map/ppermute | solution.py:363
  76.1 7.1 %shard_map.99 = bf16[8,528,128]{2,1,0:T(8,128)(2,1)S(1)} custom-call(s32[7]{0:T(128)S(1)} %copy-done.7, bf16[4,272,128]{2,1,0:T(8,128)(2,1)S(1)} %all-to-all-done.kv0, bf16[4,272,128]{2,1,0:T(8,128)(2,1)S(1)} %collective-permute-done.kv1, bf16[4,272,128]{2,1,0:T(8,128)(2,1)S(1)} %collective-permute-done.1.kv2, ...), custom_call_target="tpu_custom_call" | custom-call | flops 20000000000 | bytes 4194304 | tf_op jit(solution)/shard_map/pallas_call | solution.py:309
  83.2 21.1 %all_to_all.30.parts = bf16[8,528,128]{2,1,0:T(8,128)(2,1)S(1)} all-to-all(bf16[8,528,128]{2,1,0:T(8,128)(2,1)S(1)} %shard_map.99), channel_id=1, replica_groups=mesh['zh'=4,'zl'=4,'yl'=2,'yh'=2,'xh'=2,'xl'=2,'c'=2] {'yl','xl','c'}, dimensions={0} | all-to-all | bytes 2162688 | tf_op jit(solution)/shard_map/all_to_all | solution.py:406
  105.2 15.7 %all_to_all.31.att = bf16[4,512,128]{2,1,0:T(8,128)(2,1)S(1)} all-to-all(bf16[4,512,128]{2,1,0:T(8,128)(2,1)S(1)} %get-tuple-element.26), channel_id=1, replica_groups=mesh['zh'=4,'zl'=4,'yl'=2,'yh'=2,'xh'=2,'xl'=2,'c'=2] {'yh','xh'}, dimensions={0} | all-to-all | bytes 1048576 | tf_op jit(solution)/shard_map/all_to_all | solution.py:412
  120.9 1.9 copy-done.3
  122.8 2.4 shard_map.101
  125.2 26.0 %all_to_all.32.own = bf16[8,896,128]{2,1,0:T(8,128)(2,1)S(1)} all-to-all(bf16[8,896,128]{2,1,0:T(8,128)(2,1)S(1)} %shard_map.101), channel_id=1, replica_groups=mesh['zh'=4,'zl'=4,'yl'=2,'yh'=2,'xh'=2,'xl'=2,'c'=2] {'xl','yh','xh'}, dimensions={0} | all-to-all | bytes 3670016 | tf_op jit(solution)/shard_map/all_to_all | solution.py:421
  151.2 5.0 %collective-permute-start.7 = (bf16[8,896,128]{2,1,0:T(8,128)(2,1)S(1)}, bf16[8,896,128]{2,1,0:T(8,128)(2,1)S(1)}, u32[]{:S(2)}, u32[]{:S(2)}) collective-permute-start(bf16[8,896,128]{2,1,0:T(8,128)(2,1)S(1)} %all_to_all.32.own), channel_id=1, source_target_pairs={{0,1},{1,0},{2,3},{3,2},{4,5},{5,4},{6,7},{7,6},{8,9},{9,8},{10,11... | collective-permute-start | bytes 5505032 | tf_op jit(solution)/shard_map/ppermute | solution.py:422
  156.9 2.7 %collective-permute-done.7.other = bf16[8,896,128]{2,1,0:T(8,128)(2,1)S(1)} collective-permute-done((bf16[8,896,128]{2,1,0:T(8,128)(2,1)S(1)}, bf16[8,896,128]{2,1,0:T(8,128)(2,1)S(1)}, u32[]{:S(2)}, u32[]{:S(2)}) %collective-permute-start.7) | collective-permute-done | bytes 1835040 | tf_op jit(solution)/shard_map/ppermute | solution.py:422
  159.6 2.3 shard_map.103
  161.9 2.0 shard_map.105
  163.9 1.9 collective-permute-start.8
  165.8 3.4 %collective-permute-start.9 = (bf16[8,96,256]{2,1,0:T(8,128)(2,1)}, bf16[8,96,256]{2,1,0:T(8,128)(2,1)S(1)}, u32[]{:S(2)}, u32[]{:S(2)}) collective-permute-start(bf16[8,96,256]{2,1,0:T(8,128)(2,1)} %get-tuple-element.32), channel_id=1, source_target_pairs={{32,0},{64,32},{96,64},{128,96},{160,128},{192,160},{224,192},{256... | collective-permute-start | bytes 1179656 | tf_op jit(solution)/shard_map/ppermute | solution.py:363
  169.2 9.8 %collective-permute-start.10 = (bf16[4,96,256]{2,1,0:T(8,128)(2,1)}, bf16[4,96,256]{2,1,0:T(8,128)(2,1)S(1)}, u32[]{:S(2)}, u32[]{:S(2)}) collective-permute-start(bf16[4,96,256]{2,1,0:T(8,128)(2,1)} %get-tuple-element.33), channel_id=1, source_target_pairs={{448,0},{480,32},{0,64},{32,96},{64,128},{96,160},{128,192},{160,2... | collective-permute-start | bytes 589832 | tf_op jit(solution)/shard_map/ppermute | solution.py:363
  179.0 1.9 collective-permute-start.11
  180.9 5.1 %all-to-all-start.5 = ((bf16[4,128,128]{2,1,0:T(8,128)(2,1)}), bf16[4,128,128]{2,1,0:T(8,128)(2,1)}, u32[]{:S(2)}, u32[]{:S(2)}) async-start(bf16[4,128,128]{2,1,0:T(8,128)(2,1)} %bitcast.10), calls=%async_computation.5 | async-start | bytes 262144 | tf_op jit(solution)/shard_map/all_to_all | solution.py:409
  188.5 5.7 %collective-permute-done.11.far_above = bf16[4,96,256]{2,1,0:T(8,128)(2,1)S(1)} collective-permute-done((bf16[4,96,256]{2,1,0:T(8,128)(2,1)S(1)}, bf16[4,96,256]{2,1,0:T(8,128)(2,1)S(1)}, u32[]{:S(2)}, u32[]{:S(2)}) %collective-permute-start.11) | collective-permute-done | bytes 196640 | tf_op jit(solution)/shard_map/ppermute | solution.py:363
  195.2 15.7 %all-to-all-start.4 = ((bf16[8,96,256]{2,1,0:T(8,128)(2,1)}), bf16[8,96,256]{2,1,0:T(8,128)(2,1)S(1)}, u32[]{:S(2)}, u32[]{:S(2)}) async-start(bf16[8,96,256]{2,1,0:T(8,128)(2,1)} %shard_map.106), calls=%async_computation.4 | async-start | bytes 786432 | tf_op jit(solution)/shard_map/all_to_all | solution.py:440
  210.8 1.7 copy.10
  212.5 21.5 %all-to-all-done.4.terms = bf16[8,96,256]{2,1,0:T(8,128)(2,1)S(1)} async-done(((bf16[8,96,256]{2,1,0:T(8,128)(2,1)}), bf16[8,96,256]{2,1,0:T(8,128)(2,1)S(1)}, u32[]{:S(2)}, u32[]{:S(2)}) %all-to-all-start.4) | async-done | bytes 393248 | tf_op jit(solution)/shard_map/all_to_all | solution.py:440
  (40 shorter events, 11.5 us)
Async XLA Ops:
  7.2 113.7 %all-gather.2.cloned.1.call-start = ((), (), s32[]{:S(2)}) async-start(), calls=%async_computation.6 | async-start | bytes 3932160 | tf_op jit(solution)/shard_map/all_gather | solution.py:380
  8.6 20.0 %copy-start.7 = (s32[7]{0:T(128)S(1)}, s32[7]{0:T(128)}, u32[]{:S(2)}) copy-start(s32[7]{0:T(128)} %stack.31.place) | copy-start | bytes 88
  11.3 39.2 %copy-start.8 = (bf16[16,128]{1,0:T(8,128)(2,1)S(1)}, bf16[16,128]{1,0:T(8,128)(2,1)}, u32[]{:S(2)}) copy-start(bf16[16,128]{1,0:T(8,128)(2,1)} %get-tuple-element.23.doc_rows) | copy-start | bytes 12292
  11.3 42.0 %all-to-all-start = ((bf16[4,272,128]{2,1,0:T(8,128)(2,1)}), bf16[4,272,128]{2,1,0:T(8,128)(2,1)S(1)}, u32[]{:S(2)}, u32[]{:S(2)}) async-start(bf16[4,272,128]{2,1,0:T(8,128)(2,1)} %get-tuple-element.19), calls=%async_computation | async-start | bytes 557056 | tf_op jit(solution)/shard_map/all_to_all | solution.py:367
  24.4 4.2 %collective-permute-start.4 = (bf16[896,128]{1,0:T(8,128)(2,1)}, bf16[896,128]{1,0:T(8,128)(2,1)S(1)}, u32[]{:S(2)}, u32[]{:S(2)}) collective-permute-start(bf16[896,128]{1,0:T(8,128)(2,1)} %get-tuple-element.20.sent), channel_id=1, source_target_pairs={{0,1},{1,0},{2,3},{3,2},{4,5},{5,4},{6,7},{7,6},{8,9},{9,8},{10,11... | collective-permute-start | bytes 688136 | tf_op jit(solution)/shard_map/ppermute | solution.py:374
  28.6 0.9 copy-start.5
  29.5 0.9 copy-start.6
  31.0 19.4 %collective-permute-start.5 = (bf16[1408,128]{1,0:T(8,128)(2,1)S(1)}, bf16[1408,128]{1,0:T(8,128)(2,1)S(1)}, u32[]{:S(2)}, u32[]{:S(2)}) collective-permute-start(bf16[1408,128]{1,0:T(8,128)(2,1)S(1)} %get-tuple-element.22.two), channel_id=1, source_target_pairs={{0,2},{2,0},{1,3},{3,1},{4,6},{6,4},{5,7},{7,5},{8,10},{10,8},{9,1... | collective-permute-start | bytes 1081352 | tf_op jit(solution)/shard_map/ppermute | solution.py:377
  50.5 0.7 copy-start.9
  51.2 24.9 %collective-permute-start.6 = (bf16[2064,128]{1,0:T(8,128)(2,1)S(1)}, bf16[2064,128]{1,0:T(8,128)(2,1)S(1)}, u32[]{:S(2)}, u32[]{:S(2)}) collective-permute-start(bf16[2064,128]{1,0:T(8,128)(2,1)S(1)} %get-tuple-element.25.q_own), channel_id=1, source_target_pairs={{0,16},{16,0},{1,17},{17,1},{2,18},{18,2},{3,19},{19,3},{4,20},{20... | collective-permute-start | bytes 1585160 | tf_op jit(solution)/shard_map/ppermute | solution.py:379
  53.3 22.9 %collective-permute-start = (bf16[4,272,128]{2,1,0:T(8,128)(2,1)S(1)}, bf16[4,272,128]{2,1,0:T(8,128)(2,1)S(1)}, u32[]{:S(2)}, u32[]{:S(2)}) collective-permute-start(bf16[4,272,128]{2,1,0:T(8,128)(2,1)S(1)} %all-to-all-done.kv0), channel_id=1, source_target_pairs={{480,0},{0,32},{32,64},{64,96},{96,128},{128,160},{160,192},{192,2... | collective-permute-start | bytes 835592 | tf_op jit(solution)/shard_map/ppermute | solution.py:363
  56.2 19.9 %collective-permute-start.1 = (bf16[4,272,128]{2,1,0:T(8,128)(2,1)S(1)}, bf16[4,272,128]{2,1,0:T(8,128)(2,1)S(1)}, u32[]{:S(2)}, u32[]{:S(2)}) collective-permute-start(bf16[4,272,128]{2,1,0:T(8,128)(2,1)S(1)} %all-to-all-done.kv0), channel_id=1, source_target_pairs={{32,0},{64,32},{96,64},{128,96},{160,128},{192,160},{224,192},{256... | collective-permute-start | bytes 835592 | tf_op jit(solution)/shard_map/ppermute | solution.py:363
  58.6 13.9 %collective-permute-start.2 = (bf16[2,272,128]{2,1,0:T(8,128)(2,1)S(1)}, bf16[2,272,128]{2,1,0:T(8,128)(2,1)S(1)}, u32[]{:S(2)}, u32[]{:S(2)}) collective-permute-start(bf16[2,272,128]{2,1,0:T(8,128)(2,1)S(1)} %get-tuple-element.37), channel_id=1, source_target_pairs={{448,0},{480,32},{0,64},{32,96},{64,128},{96,160},{128,192},{160,2... | collective-permute-start | bytes 417800 | tf_op jit(solution)/shard_map/ppermute | solution.py:363
  66.9 9.2 %collective-permute-start.3 = (bf16[2,272,128]{2,1,0:T(8,128)(2,1)S(1)}, bf16[2,272,128]{2,1,0:T(8,128)(2,1)S(1)}, u32[]{:S(2)}, u32[]{:S(2)}) collective-permute-start(bf16[2,272,128]{2,1,0:T(8,128)(2,1)S(1)} %get-tuple-element.36), channel_id=1, source_target_pairs={{64,0},{96,32},{128,64},{160,96},{192,128},{224,160},{256,192},{28... | collective-permute-start | bytes 417800 | tf_op jit(solution)/shard_map/ppermute | solution.py:363
  83.2 37.7 %copy-start.4 = (bf16[32,4096]{1,0:T(8,128)(2,1)S(1)}, bf16[32,4096]{1,0:T(8,128)(2,1)}, u32[]{:S(2)}) copy-start(bf16[32,4096]{1,0:T(8,128)(2,1)} %teacher.1) | copy-start | bytes 786436
  120.9 1.9 copy-start.3
  125.2 31.1 %copy-start.2 = (bf16[256,3072]{1,0:T(8,128)(2,1)S(1)}, bf16[256,3072]{1,0:T(8,128)(2,1)}, u32[]{:S(2)}) copy-start(bf16[256,3072]{1,0:T(8,128)(2,1)} %get-tuple-element.29.projector_t) | copy-start | bytes 4718596
  151.2 8.4 %collective-permute-start.7 = (bf16[8,896,128]{2,1,0:T(8,128)(2,1)S(1)}, bf16[8,896,128]{2,1,0:T(8,128)(2,1)S(1)}, u32[]{:S(2)}, u32[]{:S(2)}) collective-permute-start(bf16[8,896,128]{2,1,0:T(8,128)(2,1)S(1)} %all_to_all.32.own), channel_id=1, source_target_pairs={{0,1},{1,0},{2,3},{3,2},{4,5},{5,4},{6,7},{7,6},{8,9},{9,8},{10,11... | collective-permute-start | bytes 5505032 | tf_op jit(solution)/shard_map/ppermute | solution.py:422
  159.6 2.3 copy-start
  163.9 30.3 %collective-permute-start.8 = (bf16[8,96,256]{2,1,0:T(8,128)(2,1)}, bf16[8,96,256]{2,1,0:T(8,128)(2,1)S(1)}, u32[]{:S(2)}, u32[]{:S(2)}) collective-permute-start(bf16[8,96,256]{2,1,0:T(8,128)(2,1)} %get-tuple-element.31), channel_id=1, source_target_pairs={{480,0},{0,32},{32,64},{64,96},{96,128},{128,160},{160,192},{192,2... | collective-permute-start | bytes 1179656 | tf_op jit(solution)/shard_map/ppermute | solution.py:363
  165.8 28.4 %collective-permute-start.9 = (bf16[8,96,256]{2,1,0:T(8,128)(2,1)}, bf16[8,96,256]{2,1,0:T(8,128)(2,1)S(1)}, u32[]{:S(2)}, u32[]{:S(2)}) collective-permute-start(bf16[8,96,256]{2,1,0:T(8,128)(2,1)} %get-tuple-element.32), channel_id=1, source_target_pairs={{32,0},{64,32},{96,64},{128,96},{160,128},{192,160},{224,192},{256... | collective-permute-start | bytes 1179656 | tf_op jit(solution)/shard_map/ppermute | solution.py:363
  169.2 19.2 %collective-permute-start.10 = (bf16[4,96,256]{2,1,0:T(8,128)(2,1)}, bf16[4,96,256]{2,1,0:T(8,128)(2,1)S(1)}, u32[]{:S(2)}, u32[]{:S(2)}) collective-permute-start(bf16[4,96,256]{2,1,0:T(8,128)(2,1)} %get-tuple-element.33), channel_id=1, source_target_pairs={{448,0},{480,32},{0,64},{32,96},{64,128},{96,160},{128,192},{160,2... | collective-permute-start | bytes 589832 | tf_op jit(solution)/shard_map/ppermute | solution.py:363
  179.0 15.2 %collective-permute-start.11 = (bf16[4,96,256]{2,1,0:T(8,128)(2,1)S(1)}, bf16[4,96,256]{2,1,0:T(8,128)(2,1)S(1)}, u32[]{:S(2)}, u32[]{:S(2)}) collective-permute-start(bf16[4,96,256]{2,1,0:T(8,128)(2,1)S(1)} %get-tuple-element.34), channel_id=1, source_target_pairs={{64,0},{96,32},{128,64},{160,96},{192,128},{224,160},{256,192},{28... | collective-permute-start | bytes 589832 | tf_op jit(solution)/shard_map/ppermute | solution.py:363
  180.9 14.3 %all-to-all-start.5 = ((bf16[4,128,128]{2,1,0:T(8,128)(2,1)}), bf16[4,128,128]{2,1,0:T(8,128)(2,1)}, u32[]{:S(2)}, u32[]{:S(2)}) async-start(bf16[4,128,128]{2,1,0:T(8,128)(2,1)} %bitcast.10), calls=%async_computation.5 | async-start | bytes 262144 | tf_op jit(solution)/shard_map/all_to_all | solution.py:409
  186.0 1.5 copy-start.1
  195.2 38.8 %all-to-all-start.4 = ((bf16[8,96,256]{2,1,0:T(8,128)(2,1)}), bf16[8,96,256]{2,1,0:T(8,128)(2,1)S(1)}, u32[]{:S(2)}, u32[]{:S(2)}) async-start(bf16[8,96,256]{2,1,0:T(8,128)(2,1)} %shard_map.106), calls=%async_computation.4 | async-start | bytes 786432 | tf_op jit(solution)/shard_map/all_to_all | solution.py:440
Sparse Core Ops, SparseCore 0:
  10.1 57.4 all-gather.1

commit v9 on v8

--- a/solution.py
+++ b/solution.py
@@ -23,41 +23,21 @@
 BLOCKS = 4
 
 
-def start_kernel(place, keys, values, docs, queries, hidden_t, packed, doc_rows, sent, kept):
+def start_kernel(place, keys, values, docs, weight_t, hidden_t, packed, doc_rows, both, sem):
+    copies = [
+        pltpu.make_async_copy(weight_t, both.at[:, pl.ds(0, 2048)], sem.at[0]),
+        pltpu.make_async_copy(hidden_t, both.at[:, pl.ds(2048, 512)], sem.at[1]),
+    ]
+    for copy in copies:
+        copy.start()
     rows = jnp.concatenate([docs[...].astype(F32), jnp.zeros((12, 128), F32)], axis=0).astype(BF)
-    for copy in range(4):
-        packed[copy, 0:128, :] = keys[...]
-        packed[copy, 128:256, :] = values[...]
-        packed[copy, 256:272, :] = rows
+    for i in range(4):
+        packed[i, 0:128, :] = keys[...]
+        packed[i, 128:256, :] = values[...]
+        packed[i, 256:272, :] = rows
     doc_rows[...] = rows
-    sent[0:512, :] = queries[...]
-    for xl in range(2):
-        kept[xl] = hidden_t[:, pl.ds(pl.multiple_of((xl * 2 + place[2]) * 128, 128), 128)]
-        other = pl.ds(pl.multiple_of((xl * 2 + 1 - place[2]) * 128, 128), 128)
-        sent[512 + xl * 192:704 + xl * 192, :] = hidden_t[:, other]
-
-
-def turn_kernel(place, sent, received, kept, two, kept_out):
-    xl = place[3]
-    two[0:512, :] = sent[0:512, :]
-    two[512:1024, :] = received[0:512, :]
-    two[1024:1216, :] = kept[1 - xl]
-    two[1216:1408, :] = received[pl.ds(pl.multiple_of(512 + (1 - xl) * 192, 64), 192), :]
-    kept_out[0] = kept[xl]
-    kept_out[1] = received[pl.ds(pl.multiple_of(512 + xl * 192, 64), 192), :]
-
-
-def join_kernel(two, received, doc_rows, token, q_own, hidden_out):
-    q_own[0:1024, :] = two[0:1024, :]
-    q_own[1024:2048, :] = received[0:1024, :]
-    q_own[2048:2064, :] = doc_rows[...]
-    for i in range(2):
-        hidden_out[i] = received[1024 + i * 192:1216 + i * 192, :]
-
-
-def transpose_kernel(x, out, token):
-    out[...] = x[...].T
-    token[...] = jnp.zeros((8, 128), F32)
+    for copy in copies:
+        copy.wait()
 
 
 def attend_kernel(place, kv0, kv1, kv2, kv3_low, kv3_high, q_own, q_other, out, kv, q_all, v_turned, q_even, q_odd, s_even, s_odd, max_even, max_odd, acc, total, info_v, info, sem):
@@ -107,7 +87,7 @@
     def begin_scores(tile, q_ref, max_ref):
         side, row0 = tile // 4, pl.multiple_of(tile % 4 * 128, 128)
         for h in range(4):
-            q_ref[h * 128:(h + 1) * 128, :] = q_all[side, pl.ds(pl.multiple_of((h ^ j) * 512, 512) + row0, 128), :]
+            q_ref[h * 128:(h + 1) * 128, :] = q_all[side, pl.ds(h * 512 + row0, 128), :]
         max_ref[...] = jnp.full((1, 512), EMPTY, F32)
 
     def is_full(tile, ch):
@@ -214,25 +194,28 @@
             copies[copy, rows, :] = total
 
 
-def student_kernel(place, weight_t, att, kept, received, teacher, out, weights, sem):
+def student_kernel(place, gathered, att, teacher, out, weights, hidden, sem):
     copies = []
+    own_rows = pl.ds(pl.multiple_of(2048 + place[0] * 128, 128), 128)
+    hidden_copy = pltpu.make_async_copy(gathered.at[:, own_rows], hidden, sem.at[4])
     for part in range(4):
         rows = pl.ds(part * 192, 192)
-        copies.append(pltpu.make_async_copy(weight_t.at[rows], weights.at[rows], sem.at[part]))
-    for copy in copies:
+        copies.append(pltpu.make_async_copy(gathered.at[rows, pl.ds(0, 2048)], weights.at[rows], sem.at[part]))
+    copies[0].start()
+    hidden_copy.start()
+    for copy in copies[1:]:
         copy.start()
     for chip in range(8):
         first = (chip % 4 * 4 + chip // 4 * 2) * 256
         for i in range(4):
             out[chip, 768 + i * 32:800 + i * 32, :] = teacher[:, first + i * 128:first + (i + 1) * 128]
     att_all = att[...].reshape(2048, 128)
+    hidden_copy.wait()
     for part in range(4):
-        source = part ^ place[0]
-        hidden = jnp.where(source < 2, kept[source % 2].astype(F32), received[source % 2].astype(F32))
         copies[part].wait()
         rows = slice(part * 192, (part + 1) * 192)
         mixed = jnp.dot(weights[rows, :], att_all, preferred_element_type=F32)
-        student = (hidden + mixed).astype(BF)
+        student = (hidden[rows, :].astype(F32) + mixed).astype(BF)
         for copy in range(8):
             out[copy, rows, :] = student
 
@@ -266,7 +249,9 @@
     return jnp.dot(jnp.concatenate(rows, axis=0), mismatch[...], preferred_element_type=F32).reshape(8, 96, 256)
 
 
-def own_projected_kernel(own, projector_t, out):
+def own_projected_kernel(own, projector, projector_t, out):
+    for g in range(4):
+        projector_t[:, g * 768:(g + 1) * 768] = projector[g * 768:(g + 1) * 768, :].T
     out[...] = projected(own, projector_t).T
 
 
@@ -321,34 +306,22 @@
     return jax.ShapeDtypeStruct(dims, dtype)
 
 
-def start(place, keys, values, docs, queries, hidden_t):
+def start(place, keys, values, docs, weight_t, hidden_t):
     def block(*dims):
         return pl.BlockSpec(dims, lambda i, place: (0,) * len(dims))
 
     picked = pl.BlockSpec((128, 128), lambda i, place: (place[0], place[1]))
-    outs = [(4, 272, 128), (16, 128), (896, 128), (2, 192, 128)]
     return pl.pallas_call(
         start_kernel,
         grid_spec=pltpu.PrefetchScalarGridSpec(
             num_scalar_prefetch=1,
             grid=(1,),
-            in_specs=[picked, picked, block(4, 128), block(512, 128), block(192, 512)],
-            out_specs=[block(*dims) for dims in outs],
+            in_specs=[picked, picked, block(4, 128), ANY, ANY],
+            out_specs=[block(4, 272, 128), block(16, 128), ANY],
+            scratch_shapes=[pltpu.SemaphoreType.DMA((2,))],
         ),
-        out_shape=[shape(*dims) for dims in outs],
-    )(place, keys, values, docs, queries, hidden_t)
-
-
-def transposed(x):
-    rows, columns = x.shape
-    return pl.pallas_call(
-        transpose_kernel,
-        grid=(4,),
-        in_specs=[pl.BlockSpec((rows // 4, columns), lambda i: (i, 0))],
-        out_specs=[pl.BlockSpec((columns, rows // 4), lambda i: (0, i)), pl.BlockSpec((8, 128), lambda i: (0, 0))],
-        out_shape=[shape(columns, rows), shape(8, 128, dtype=F32)],
-        compiler_params=pltpu.CompilerParams(vmem_limit_bytes=58 * 1024 * 1024),
-    )(x)
+        out_shape=[shape(4, 272, 128), shape(16, 128), shape(192, 2560)],
+    )(place, keys, values, docs, weight_t, hidden_t)
 
 
 def on_device(queries, keys, values, doc_ids, hidden, out_weight, projector, teacher):
@@ -363,21 +336,15 @@
         return lax.ppermute(x, ("zh", "zl"), [((i + shift) % 16, i) for i in range(16)])
 
     docs = doc_ids.reshape(4, 128)
-    packed, doc_rows, sent, hidden_kept = start(place, keys, values, docs, queries, hidden.T)
+    packed, doc_rows, both = start(place, keys, values, docs, out_weight.T, hidden.T)
     kv_own = lax.all_to_all(packed, "zh", 0, 0)
     kv_below, kv_above = from_z(kv_own, -1), from_z(kv_own, 1)
     kv_low, kv_high = from_z(kv_own[0:2], -2), from_z(kv_own[2:4], 2)
 
-    projector_t, token = transposed(projector)
-    half = shape(2, 192, 128)
-    two, hidden_kept = call(
-        turn_kernel, [shape(1408, 128), half], [SMEM] + [VMEM] * 3, (place, sent, lax.ppermute(sent, "c", swap), hidden_kept), 16
-    )
-    q_own, hidden_received = call(
-        join_kernel, [shape(2064, 128), half], [VMEM] * 4, (two, lax.ppermute(two, "xl", swap), doc_rows, token), 16
-    )
+    q_own = jnp.concatenate([lax.all_gather(queries, GROUP, axis=0, tiled=True), doc_rows], axis=0)
     q_other = lax.ppermute(q_own, "yl", swap)
-    weight_t = lax.all_gather(out_weight.T, GROUP, axis=0, tiled=True)
+    gathered = lax.all_gather(both, GROUP, axis=0, tiled=True)
+
     partial = call(
         attend_kernel,
         shape(8, 528, 128),
@@ -413,15 +380,17 @@
     student = call(
         student_kernel,
         shape(8, 896, 128),
-        [SMEM, HBM] + [VMEM] * 4,
-        (place, weight_t, att_all, hidden_kept, hidden_received, teacher),
+        [SMEM, HBM, VMEM, VMEM],
+        (place, gathered, att_all, teacher),
         24,
-        scratch=[pltpu.VMEM((768, 2048), BF), pltpu.SemaphoreType.DMA((4,))],
+        scratch=[pltpu.VMEM((768, 2048), BF), pltpu.VMEM((768, 128), BF), pltpu.SemaphoreType.DMA((5,))],
     )
     own = lax.all_to_all(student, CHIPS, 0, 0)
     other = lax.ppermute(own, "c", swap)
 
-    own_projected = call(own_projected_kernel, shape(256, 256, dtype=F32), [VMEM] * 2, (own, projector_t), 24, 4 * 10 ** 8)
+    projector_t, own_projected = call(
+        own_projected_kernel, [shape(256, 3072), shape(256, 256, dtype=F32)], [VMEM] * 2, (own, projector), 24, 4 * 10 ** 8
+    )
     mismatch, up, down = call(
         second_kernel,
         [shape(512, 256), shape(4, 96, 256), shape(4, 96, 256)],

time: 243 us -> 257 us (1.058); the launches traced: 242 us -> 253 us
  Pallas kernels: 25.1 us -> 51 us
  starting transfers between devices: 79.5 us -> 66.3 us
  blocking collectives: 62.8 us -> 73.4 us
  waiting for transfers between devices: 51.6 us -> 41.9 us
    pallas_call x1, Pallas kernels: 2.72 us -> 33.1 us  [start(): pl.pallas_call(start_kernel, grid_spec=pltpu.PrefetchScalarGridSpec(num_s...]
    ppermute x2 -> x0, waiting for transfers between devices: 13.7 us -> none  [the longest x1 12.4 us: on_device(): lax.ppermute(two, 'xl', swap)]
    all_to_all x1, waiting for transfers between devices: 0.01 us -> 9.87 us  [on_device(): kv_own = lax.all_to_all(packed, 'zh', 0, 0)]
    all_gather x0 -> x1, blocking collectives: none -> 7.95 us  [on_device(): lax.all_gather(queries, GROUP, axis=0, tiled=True)]
    ppermute x8, starting transfers between devices: 32.4 us -> 25.5 us  [from_z(): lax.ppermute(x, ('zh', 'zl'), [((i + shift) % 16, i) for i in range(16)])]
    ppermute x2 -> x0, starting transfers between devices: 5.97 us -> none  [the longest x1 3.12 us: on_device(): lax.ppermute(two, 'xl', swap)]
    pallas_call x1 -> x0, Pallas kernels: 3.93 us -> none  [transposed(): pl.pallas_call(transpose_kernel, grid=(4,), in_specs=[pl.BlockSpec((rows...]
    all_to_all x1, waiting for transfers between devices: 21.5 us -> 18.4 us  [on_device(): lax.all_to_all(near, ('zh', 'yl'), 0, 0)]
  transfers between devices with their start and end apart: 16 -> 14, of which waited for: 7 -> 6; matrix products, arithmetic and copies ran while one was open for 1% -> 1% of each run, Pallas kernels for 7% -> 4%
where the time goes in v9:
time: 257 us; the launch traced here: 253 us
  blocking collectives  73.4 us (29%)
  starting transfers between devices  66.3 us (26%)
  Pallas kernels  51 us (20%)
  waiting for transfers between devices  41.9 us (16%)
  between operations  14.3 us (6%)
  local copies, waits for them, and re-layouts  5.98 us (2%)
    pallas_call x1, Pallas kernels, start(): pl.pallas_call(start_kernel, grid_spec=pltpu.PrefetchScalarGridSpec(num_s...  33.1 us
    all_to_all x1, blocking collectives, on_device(): own = lax.all_to_all(student, CHIPS, 0, 0)  26 us
    ppermute x8, starting transfers between devices, from_z(): lax.ppermute(x, ('zh', 'zl'), [((i + shift) % 16, i) for i in range(16)])  25.5 us
    all_to_all x1, blocking collectives, on_device(): lax.all_to_all(partial, OCTET, 0, 0)  24.1 us
    all_to_all x1, waiting for transfers between devices, on_device(): lax.all_to_all(near, ('zh', 'yl'), 0, 0)  18.4 us
    pallas_call x9, Pallas kernels, call(): pl.pallas_call(kernel, out_shape=out_shape, in_specs=specs, out_specs=VME...  17.9 us
    all_to_all x1, starting transfers between devices, on_device(): lax.all_to_all(near, ('zh', 'yl'), 0, 0)  15.5 us
    all_to_all x1, blocking collectives, on_device(): att_all = lax.all_to_all(att_copies, HEADSETS, 0, 0)  15.4 us
  transfers between devices with their start and end apart: 14, of which 6 were waited for; matrix products, arithmetic and copies ran while one was open for 1% of the time, Pallas kernels for 4%

profile of v9, /device:TPU:73, one launch (start us, length us, event | category | flops | bytes accessed | tf_op | source)
XLA Modules:
  0.0 252.9 jit_solution(2697927531020996325)
XLA Ops:
  7.8 33.1 %shard_map.95 = (bf16[4,272,128]{2,1,0:T(8,128)(2,1)}, bf16[16,128]{1,0:T(8,128)(2,1)}, bf16[192,2560]{1,0:T(8,128)(2,1)}) custom-call(s32[7]{0:T(128)} %stack.31.place, bf16[512,512]{1,0:T(8,128)(2,1)} %keys.1, bf16[512,512]{1,0:T(8,128)(2,1)} %values.1, s32[4,128]{1,0:T(4,128)} %bitcast.16, bf16[192,2048]{1,0:T(8,128)(2,1)} %bitcast.13, ...), custom_call_target="tpu_custom_call" | custom-call | tf_op jit(solution)/shard_map/pallas_call | solution.py:314
  41.0 13.0 %all-to-all-start = ((bf16[4,272,128]{2,1,0:T(8,128)(2,1)}), bf16[4,272,128]{2,1,0:T(8,128)(2,1)S(1)}, u32[]{:S(2)}, u32[]{:S(2)}) async-start(bf16[4,272,128]{2,1,0:T(8,128)(2,1)} %get-tuple-element.15), calls=%async_computation | async-start | bytes 557056 | tf_op jit(solution)/shard_map/all_to_all | solution.py:340
  54.0 7.9 %all_gather.7 = bf16[2048,128]{1,0:T(8,128)(2,1)S(1)} all-gather(bf16[512,128]{1,0:T(8,128)(2,1)S(1)} %copy-done.6), channel_id=1, replica_groups=mesh['zh'=4,'zl'=4,'yl'=2,'yh'=2,'xh'=2,'xl'=2,'c'=2] {'xl','c'}, dimensions={0}, use_global_device_ids=true | all-gather | bytes 655360 | tf_op jit(solution)/shard_map/all_gather | solution.py:344
  62.0 2.1 collective-permute-start.4
  64.1 9.9 %all-to-all-done.kv0 = bf16[4,272,128]{2,1,0:T(8,128)(2,1)S(1)} async-done(((bf16[4,272,128]{2,1,0:T(8,128)(2,1)}), bf16[4,272,128]{2,1,0:T(8,128)(2,1)S(1)}, u32[]{:S(2)}, u32[]{:S(2)}) %all-to-all-start) | async-done | bytes 278560 | tf_op jit(solution)/shard_map/all_to_all | solution.py:340
  73.9 1.9 collective-permute-start
  75.9 3.4 %collective-permute-start.1 = (bf16[4,272,128]{2,1,0:T(8,128)(2,1)S(1)}, bf16[4,272,128]{2,1,0:T(8,128)(2,1)S(1)}, u32[]{:S(2)}, u32[]{:S(2)}) collective-permute-start(bf16[4,272,128]{2,1,0:T(8,128)(2,1)S(1)} %all-to-all-done.kv0), channel_id=1, source_target_pairs={{32,0},{64,32},{96,64},{128,96},{160,128},{192,160},{224,192},{256... | collective-permute-start | bytes 835592 | tf_op jit(solution)/shard_map/ppermute | solution.py:336
  79.3 3.0 %collective-permute-start.2 = (bf16[2,272,128]{2,1,0:T(8,128)(2,1)S(1)}, bf16[2,272,128]{2,1,0:T(8,128)(2,1)S(1)}, u32[]{:S(2)}, u32[]{:S(2)}) collective-permute-start(bf16[2,272,128]{2,1,0:T(8,128)(2,1)S(1)} %get-tuple-element.27), channel_id=1, source_target_pairs={{448,0},{480,32},{0,64},{32,96},{64,128},{96,160},{128,192},{160,2... | collective-permute-start | bytes 417800 | tf_op jit(solution)/shard_map/ppermute | solution.py:336
  82.3 3.1 %collective-permute-start.3 = (bf16[2,272,128]{2,1,0:T(8,128)(2,1)S(1)}, bf16[2,272,128]{2,1,0:T(8,128)(2,1)S(1)}, u32[]{:S(2)}, u32[]{:S(2)}) collective-permute-start(bf16[2,272,128]{2,1,0:T(8,128)(2,1)S(1)} %get-tuple-element.26), channel_id=1, source_target_pairs={{64,0},{96,32},{128,64},{160,96},{192,128},{224,160},{256,192},{28... | collective-permute-start | bytes 417800 | tf_op jit(solution)/shard_map/ppermute | solution.py:336
  86.3 4.3 %collective-permute-done.3.kv3_high = bf16[2,272,128]{2,1,0:T(8,128)(2,1)S(1)} collective-permute-done((bf16[2,272,128]{2,1,0:T(8,128)(2,1)S(1)}, bf16[2,272,128]{2,1,0:T(8,128)(2,1)S(1)}, u32[]{:S(2)}, u32[]{:S(2)}) %collective-permute-start.3) | collective-permute-done | bytes 139296 | tf_op jit(solution)/shard_map/ppermute | solution.py:336
  90.6 7.1 %shard_map.96 = bf16[8,528,128]{2,1,0:T(8,128)(2,1)S(1)} custom-call(s32[7]{0:T(128)S(1)} %copy-done.5, bf16[4,272,128]{2,1,0:T(8,128)(2,1)S(1)} %all-to-all-done.kv0, bf16[4,272,128]{2,1,0:T(8,128)(2,1)S(1)} %collective-permute-done.kv1, bf16[4,272,128]{2,1,0:T(8,128)(2,1)S(1)} %collective-permute-done.1.kv2, ...), custom_call_target="tpu_custom_call" | custom-call | flops 20000000000 | bytes 4194304 | tf_op jit(solution)/shard_map/pallas_call | solution.py:294
  97.7 24.1 %all_to_all.30.parts = bf16[8,528,128]{2,1,0:T(8,128)(2,1)S(1)} all-to-all(bf16[8,528,128]{2,1,0:T(8,128)(2,1)S(1)} %shard_map.96), channel_id=1, replica_groups=mesh['zh'=4,'zl'=4,'yl'=2,'yh'=2,'xh'=2,'xl'=2,'c'=2] {'yl','xl','c'}, dimensions={0} | all-to-all | bytes 2162688 | tf_op jit(solution)/shard_map/all_to_all | solution.py:373
  122.6 15.4 %all_to_all.31.att = bf16[4,512,128]{2,1,0:T(8,128)(2,1)S(1)} all-to-all(bf16[4,512,128]{2,1,0:T(8,128)(2,1)S(1)} %get-tuple-element.17), channel_id=1, replica_groups=mesh['zh'=4,'zl'=4,'yl'=2,'yh'=2,'xh'=2,'xl'=2,'c'=2] {'yh','xh'}, dimensions={0} | all-to-all | bytes 1048576 | tf_op jit(solution)/shard_map/all_to_all | solution.py:379
  138.1 2.1 copy-done.2
  140.2 2.4 shard_map.98
  142.6 26.0 %all_to_all.32.own = bf16[8,896,128]{2,1,0:T(8,128)(2,1)S(1)} all-to-all(bf16[8,896,128]{2,1,0:T(8,128)(2,1)S(1)} %shard_map.98), channel_id=1, replica_groups=mesh['zh'=4,'zl'=4,'yl'=2,'yh'=2,'xh'=2,'xl'=2,'c'=2] {'xl','yh','xh'}, dimensions={0} | all-to-all | bytes 3670016 | tf_op jit(solution)/shard_map/all_to_all | solution.py:388
  168.6 5.1 %collective-permute-start.5 = (bf16[8,896,128]{2,1,0:T(8,128)(2,1)S(1)}, bf16[8,896,128]{2,1,0:T(8,128)(2,1)S(1)}, u32[]{:S(2)}, u32[]{:S(2)}) collective-permute-start(bf16[8,896,128]{2,1,0:T(8,128)(2,1)S(1)} %all_to_all.32.own), channel_id=1, source_target_pairs={{0,1},{1,0},{2,3},{3,2},{4,5},{5,4},{6,7},{7,6},{8,9},{9,8},{10,11... | collective-permute-start | bytes 5505032 | tf_op jit(solution)/shard_map/ppermute | solution.py:389
  174.4 2.7 %collective-permute-done.5.other = bf16[8,896,128]{2,1,0:T(8,128)(2,1)S(1)} collective-permute-done((bf16[8,896,128]{2,1,0:T(8,128)(2,1)S(1)}, bf16[8,896,128]{2,1,0:T(8,128)(2,1)S(1)}, u32[]{:S(2)}, u32[]{:S(2)}) %collective-permute-start.5) | collective-permute-done | bytes 1835040 | tf_op jit(solution)/shard_map/ppermute | solution.py:389
  177.0 2.3 shard_map.100
  179.4 2.0 shard_map.102
  181.4 2.0 collective-permute-start.6
  183.4 3.3 %collective-permute-start.7 = (bf16[8,96,256]{2,1,0:T(8,128)(2,1)}, bf16[8,96,256]{2,1,0:T(8,128)(2,1)S(1)}, u32[]{:S(2)}, u32[]{:S(2)}) collective-permute-start(bf16[8,96,256]{2,1,0:T(8,128)(2,1)} %get-tuple-element.22), channel_id=1, source_target_pairs={{32,0},{64,32},{96,64},{128,96},{160,128},{192,160},{224,192},{256... | collective-permute-start | bytes 1179656 | tf_op jit(solution)/shard_map/ppermute | solution.py:336
  186.7 6.9 %collective-permute-start.8 = (bf16[4,96,256]{2,1,0:T(8,128)(2,1)}, bf16[4,96,256]{2,1,0:T(8,128)(2,1)S(1)}, u32[]{:S(2)}, u32[]{:S(2)}) collective-permute-start(bf16[4,96,256]{2,1,0:T(8,128)(2,1)} %get-tuple-element.23), channel_id=1, source_target_pairs={{448,0},{480,32},{0,64},{32,96},{64,128},{96,160},{128,192},{160,2... | collective-permute-start | bytes 589832 | tf_op jit(solution)/shard_map/ppermute | solution.py:336
  193.5 1.9 collective-permute-start.9
  195.5 5.1 %all-to-all-start.5 = ((bf16[4,128,128]{2,1,0:T(8,128)(2,1)}), bf16[4,128,128]{2,1,0:T(8,128)(2,1)}, u32[]{:S(2)}, u32[]{:S(2)}) async-start(bf16[4,128,128]{2,1,0:T(8,128)(2,1)} %bitcast.10), calls=%async_computation.5 | async-start | bytes 262144 | tf_op jit(solution)/shard_map/all_to_all | solution.py:376
  200.6 1.5 copy-done.1
  202.1 0.9 shard_map.101.kept
  203.0 5.8 %collective-permute-done.9.far_above = bf16[4,96,256]{2,1,0:T(8,128)(2,1)S(1)} collective-permute-done((bf16[4,96,256]{2,1,0:T(8,128)(2,1)S(1)}, bf16[4,96,256]{2,1,0:T(8,128)(2,1)S(1)}, u32[]{:S(2)}, u32[]{:S(2)}) %collective-permute-start.9) | collective-permute-done | bytes 196640 | tf_op jit(solution)/shard_map/ppermute | solution.py:336
  208.8 1.0 shard_map.103
  209.7 15.5 %all-to-all-start.4 = ((bf16[8,96,256]{2,1,0:T(8,128)(2,1)}), bf16[8,96,256]{2,1,0:T(8,128)(2,1)S(1)}, u32[]{:S(2)}, u32[]{:S(2)}) async-start(bf16[8,96,256]{2,1,0:T(8,128)(2,1)} %shard_map.103), calls=%async_computation.4 | async-start | bytes 786432 | tf_op jit(solution)/shard_map/all_to_all | solution.py:409
  225.3 1.7 copy.10
  226.9 18.4 %all-to-all-done.4.terms = bf16[8,96,256]{2,1,0:T(8,128)(2,1)S(1)} async-done(((bf16[8,96,256]{2,1,0:T(8,128)(2,1)}), bf16[8,96,256]{2,1,0:T(8,128)(2,1)S(1)}, u32[]{:S(2)}, u32[]{:S(2)}) %all-to-all-start.4) | async-done | bytes 393248 | tf_op jit(solution)/shard_map/all_to_all | solution.py:409
  (32 shorter events, 3.9 us)
Async XLA Ops:
  7.2 46.8 %copy-start.6 = (bf16[512,128]{1,0:T(8,128)(2,1)S(1)}, bf16[512,128]{1,0:T(8,128)(2,1)}, u32[]{:S(2)}) copy-start(bf16[512,128]{1,0:T(8,128)(2,1)} %param.8) | copy-start | bytes 393220
  7.2 130.9 %all-gather.2.cloned.1.call-start = ((), (), s32[]{:S(2)}) async-start(), calls=%async_computation.6 | async-start | bytes 4915200 | tf_op jit(solution)/shard_map/all_gather | solution.py:346
  40.9 21.1 %copy-start.7 = (bf16[16,128]{1,0:T(8,128)(2,1)S(1)}, bf16[16,128]{1,0:T(8,128)(2,1)}, u32[]{:S(2)}) copy-start(bf16[16,128]{1,0:T(8,128)(2,1)} %get-tuple-element.16) | copy-start | bytes 12292
  40.9 49.7 %copy-start.5 = (s32[7]{0:T(128)S(1)}, s32[7]{0:T(128)}, u32[]{:S(2)}) copy-start(s32[7]{0:T(128)} %stack.31.place) | copy-start | bytes 88
  41.0 33.0 %all-to-all-start = ((bf16[4,272,128]{2,1,0:T(8,128)(2,1)}), bf16[4,272,128]{2,1,0:T(8,128)(2,1)S(1)}, u32[]{:S(2)}, u32[]{:S(2)}) async-start(bf16[4,272,128]{2,1,0:T(8,128)(2,1)} %get-tuple-element.15), calls=%async_computation | async-start | bytes 557056 | tf_op jit(solution)/shard_map/all_to_all | solution.py:340
  62.0 23.5 %collective-permute-start.4 = (bf16[2064,128]{1,0:T(8,128)(2,1)S(1)}, bf16[2064,128]{1,0:T(8,128)(2,1)S(1)}, u32[]{:S(2)}, u32[]{:S(2)}) collective-permute-start(bf16[2064,128]{1,0:T(8,128)(2,1)S(1)} %constant_dynamic-update-slice_fusion.q_own), channel_id=1, source_target_pairs={{0,16},{16,0},{1,17},{17,1},{2,18},{18,2},{3,19},{19,3},{4,20},{20... | collective-permute-start | bytes 1585160 | tf_op jit(solution)/shard_map/ppermute | solution.py:345
  73.9 16.6 %collective-permute-start = (bf16[4,272,128]{2,1,0:T(8,128)(2,1)S(1)}, bf16[4,272,128]{2,1,0:T(8,128)(2,1)S(1)}, u32[]{:S(2)}, u32[]{:S(2)}) collective-permute-start(bf16[4,272,128]{2,1,0:T(8,128)(2,1)S(1)} %all-to-all-done.kv0), channel_id=1, source_target_pairs={{480,0},{0,32},{32,64},{64,96},{96,128},{128,160},{160,192},{192,2... | collective-permute-start | bytes 835592 | tf_op jit(solution)/shard_map/ppermute | solution.py:336
  75.9 14.7 %collective-permute-start.1 = (bf16[4,272,128]{2,1,0:T(8,128)(2,1)S(1)}, bf16[4,272,128]{2,1,0:T(8,128)(2,1)S(1)}, u32[]{:S(2)}, u32[]{:S(2)}) collective-permute-start(bf16[4,272,128]{2,1,0:T(8,128)(2,1)S(1)} %all-to-all-done.kv0), channel_id=1, source_target_pairs={{32,0},{64,32},{96,64},{128,96},{160,128},{192,160},{224,192},{256... | collective-permute-start | bytes 835592 | tf_op jit(solution)/shard_map/ppermute | solution.py:336
  79.3 7.0 %collective-permute-start.2 = (bf16[2,272,128]{2,1,0:T(8,128)(2,1)S(1)}, bf16[2,272,128]{2,1,0:T(8,128)(2,1)S(1)}, u32[]{:S(2)}, u32[]{:S(2)}) collective-permute-start(bf16[2,272,128]{2,1,0:T(8,128)(2,1)S(1)} %get-tuple-element.27), channel_id=1, source_target_pairs={{448,0},{480,32},{0,64},{32,96},{64,128},{96,160},{128,192},{160,2... | collective-permute-start | bytes 417800 | tf_op jit(solution)/shard_map/ppermute | solution.py:336
  82.3 8.3 %collective-permute-start.3 = (bf16[2,272,128]{2,1,0:T(8,128)(2,1)S(1)}, bf16[2,272,128]{2,1,0:T(8,128)(2,1)S(1)}, u32[]{:S(2)}, u32[]{:S(2)}) collective-permute-start(bf16[2,272,128]{2,1,0:T(8,128)(2,1)S(1)} %get-tuple-element.26), channel_id=1, source_target_pairs={{64,0},{96,32},{128,64},{160,96},{192,128},{224,160},{256,192},{28... | collective-permute-start | bytes 417800 | tf_op jit(solution)/shard_map/ppermute | solution.py:336
  97.7 40.4 %copy-start.4 = (bf16[32,4096]{1,0:T(8,128)(2,1)S(1)}, bf16[32,4096]{1,0:T(8,128)(2,1)}, u32[]{:S(2)}) copy-start(bf16[32,4096]{1,0:T(8,128)(2,1)} %teacher.1) | copy-start | bytes 786436
  138.1 2.1 copy-start.2
  142.6 31.1 %copy-start.3 = (bf16[3072,256]{1,0:T(8,128)(2,1)S(1)}, bf16[3072,256]{1,0:T(8,128)(2,1)}, u32[]{:S(2)}) copy-start(bf16[3072,256]{1,0:T(8,128)(2,1)} %projector.1) | copy-start | bytes 4718596
  168.6 8.5 %collective-permute-start.5 = (bf16[8,896,128]{2,1,0:T(8,128)(2,1)S(1)}, bf16[8,896,128]{2,1,0:T(8,128)(2,1)S(1)}, u32[]{:S(2)}, u32[]{:S(2)}) collective-permute-start(bf16[8,896,128]{2,1,0:T(8,128)(2,1)S(1)} %all_to_all.32.own), channel_id=1, source_target_pairs={{0,1},{1,0},{2,3},{3,2},{4,5},{5,4},{6,7},{7,6},{8,9},{9,8},{10,11... | collective-permute-start | bytes 5505032 | tf_op jit(solution)/shard_map/ppermute | solution.py:389
  177.0 2.3 copy-start
  181.4 27.4 %collective-permute-start.6 = (bf16[8,96,256]{2,1,0:T(8,128)(2,1)}, bf16[8,96,256]{2,1,0:T(8,128)(2,1)S(1)}, u32[]{:S(2)}, u32[]{:S(2)}) collective-permute-start(bf16[8,96,256]{2,1,0:T(8,128)(2,1)} %get-tuple-element.21), channel_id=1, source_target_pairs={{480,0},{0,32},{32,64},{64,96},{96,128},{128,160},{160,192},{192,2... | collective-permute-start | bytes 1179656 | tf_op jit(solution)/shard_map/ppermute | solution.py:336
  183.4 25.4 %collective-permute-start.7 = (bf16[8,96,256]{2,1,0:T(8,128)(2,1)}, bf16[8,96,256]{2,1,0:T(8,128)(2,1)S(1)}, u32[]{:S(2)}, u32[]{:S(2)}) collective-permute-start(bf16[8,96,256]{2,1,0:T(8,128)(2,1)} %get-tuple-element.22), channel_id=1, source_target_pairs={{32,0},{64,32},{96,64},{128,96},{160,128},{192,160},{224,192},{256... | collective-permute-start | bytes 1179656 | tf_op jit(solution)/shard_map/ppermute | solution.py:336
  186.7 16.3 %collective-permute-start.8 = (bf16[4,96,256]{2,1,0:T(8,128)(2,1)}, bf16[4,96,256]{2,1,0:T(8,128)(2,1)S(1)}, u32[]{:S(2)}, u32[]{:S(2)}) collective-permute-start(bf16[4,96,256]{2,1,0:T(8,128)(2,1)} %get-tuple-element.23), channel_id=1, source_target_pairs={{448,0},{480,32},{0,64},{32,96},{64,128},{96,160},{128,192},{160,2... | collective-permute-start | bytes 589832 | tf_op jit(solution)/shard_map/ppermute | solution.py:336
  193.5 15.2 %collective-permute-start.9 = (bf16[4,96,256]{2,1,0:T(8,128)(2,1)S(1)}, bf16[4,96,256]{2,1,0:T(8,128)(2,1)S(1)}, u32[]{:S(2)}, u32[]{:S(2)}) collective-permute-start(bf16[4,96,256]{2,1,0:T(8,128)(2,1)S(1)} %get-tuple-element.24), channel_id=1, source_target_pairs={{64,0},{96,32},{128,64},{160,96},{192,128},{224,160},{256,192},{28... | collective-permute-start | bytes 589832 | tf_op jit(solution)/shard_map/ppermute | solution.py:336
  195.5 14.3 %all-to-all-start.5 = ((bf16[4,128,128]{2,1,0:T(8,128)(2,1)}), bf16[4,128,128]{2,1,0:T(8,128)(2,1)}, u32[]{:S(2)}, u32[]{:S(2)}) async-start(bf16[4,128,128]{2,1,0:T(8,128)(2,1)} %bitcast.10), calls=%async_computation.5 | async-start | bytes 262144 | tf_op jit(solution)/shard_map/all_to_all | solution.py:376
  200.6 1.5 copy-start.1
  209.7 35.6 %all-to-all-start.4 = ((bf16[8,96,256]{2,1,0:T(8,128)(2,1)}), bf16[8,96,256]{2,1,0:T(8,128)(2,1)S(1)}, u32[]{:S(2)}, u32[]{:S(2)}) async-start(bf16[8,96,256]{2,1,0:T(8,128)(2,1)} %shard_map.103), calls=%async_computation.4 | async-start | bytes 786432 | tf_op jit(solution)/shard_map/all_to_all | solution.py:409
Sparse Core Ops, SparseCore 0:
  41.1 56.0 all-gather.1

commit v10 on v9

--- a/solution.py
+++ b/solution.py
@@ -23,10 +23,10 @@
 BLOCKS = 4
 
 
-def start_kernel(place, keys, values, docs, weight_t, hidden_t, packed, doc_rows, both, sem):
+def start_kernel(place, keys, values, docs, weight_t, hidden_t, packed, doc_rows, both, joined, sem):
     copies = [
-        pltpu.make_async_copy(weight_t, both.at[:, pl.ds(0, 2048)], sem.at[0]),
-        pltpu.make_async_copy(hidden_t, both.at[:, pl.ds(2048, 512)], sem.at[1]),
+        pltpu.make_async_copy(weight_t, joined.at[:, pl.ds(0, 2048)], sem.at[0]),
+        pltpu.make_async_copy(hidden_t, joined.at[:, pl.ds(2048, 512)], sem.at[1]),
     ]
     for copy in copies:
         copy.start()
@@ -38,6 +38,9 @@
     doc_rows[...] = rows
     for copy in copies:
         copy.wait()
+    last = pltpu.make_async_copy(joined, both, sem.at[2])
+    last.start()
+    last.wait()
 
 
 def attend_kernel(place, kv0, kv1, kv2, kv3_low, kv3_high, q_own, q_other, out, kv, q_all, v_turned, q_even, q_odd, s_even, s_odd, max_even, max_odd, acc, total, info_v, info, sem):
@@ -318,7 +321,7 @@
             grid=(1,),
             in_specs=[picked, picked, block(4, 128), ANY, ANY],
             out_specs=[block(4, 272, 128), block(16, 128), ANY],
-            scratch_shapes=[pltpu.SemaphoreType.DMA((2,))],
+            scratch_shapes=[pltpu.VMEM((192, 2560), BF), pltpu.SemaphoreType.DMA((3,))],
         ),
         out_shape=[shape(4, 272, 128), shape(16, 128), shape(192, 2560)],
     )(place, keys, values, docs, weight_t, hidden_t)

time: 257 us -> 230 us (0.89); the launches traced: 253 us -> 229 us
  Pallas kernels: 51 us -> 22.2 us
  starting transfers between devices: 66.3 us -> 71.9 us
    pallas_call x1, Pallas kernels: 33.1 us -> 4.29 us  [start(): pl.pallas_call(start_kernel, grid_spec=pltpu.PrefetchScalarGridSpec(num_s...]
    ppermute x8, starting transfers between devices: 25.5 us -> 34.4 us  [from_z(): lax.ppermute(x, ('zh', 'zl'), [((i + shift) % 16, i) for i in range(16)])]
    ppermute x8, waiting for transfers between devices: 10.9 us -> 5.13 us  [from_z(): lax.ppermute(x, ('zh', 'zl'), [((i + shift) % 16, i) for i in range(16)])]
    all_to_all x1, waiting for transfers between devices: 18.4 us -> 23.6 us  [on_device(): lax.all_to_all(near, ('zh', 'yl'), 0, 0)]
    all_to_all x1, starting transfers between devices: 15.5 us -> 12.4 us  [on_device(): lax.all_to_all(near, ('zh', 'yl'), 0, 0)]
  transfers between devices with their start and end apart: 14 -> 14, of which waited for: 6 -> 6; matrix products, arithmetic and copies ran while one was open for 1% -> 1% of each run, Pallas kernels for 4% -> 5%
where the time goes in v10:
time: 230 us; the launch traced here: 229 us
  blocking collectives  73.4 us (32%)
  starting transfers between devices  71.9 us (31%)
  waiting for transfers between devices  41.5 us (18%)
  Pallas kernels  22.2 us (10%)
  between operations  14.3 us (6%)
  local copies, waits for them, and re-layouts  5.98 us (3%)
    ppermute x8, starting transfers between devices, from_z(): lax.ppermute(x, ('zh', 'zl'), [((i + shift) % 16, i) for i in range(16)])  34.4 us
    all_to_all x1, blocking collectives, on_device(): own = lax.all_to_all(student, CHIPS, 0, 0)  26 us
    all_to_all x1, blocking collectives, on_device(): lax.all_to_all(partial, OCTET, 0, 0)  24.1 us
    all_to_all x1, waiting for transfers between devices, on_device(): lax.all_to_all(near, ('zh', 'yl'), 0, 0)  23.6 us
    pallas_call x9, Pallas kernels, call(): pl.pallas_call(kernel, out_shape=out_shape, in_specs=specs, out_specs=VME...  18 us
    all_to_all x1, blocking collectives, on_device(): att_all = lax.all_to_all(att_copies, HEADSETS, 0, 0)  15.4 us
    all_to_all x1, starting transfers between devices, on_device(): kv_own = lax.all_to_all(packed, 'zh', 0, 0)  13 us
    all_to_all x1, starting transfers between devices, on_device(): lax.all_to_all(near, ('zh', 'yl'), 0, 0)  12.4 us
  transfers between devices with their start and end apart: 14, of which 6 were waited for; matrix products, arithmetic and copies ran while one was open for 1% of the time, Pallas kernels for 5%

profile of v10, /device:TPU:73, one launch (start us, length us, event | category | flops | bytes accessed | tf_op | source)
XLA Modules:
  0.0 229.4 jit_solution(6045560758855262068)
XLA Ops:
  7.8 4.3 %shard_map.95 = (bf16[4,272,128]{2,1,0:T(8,128)(2,1)}, bf16[16,128]{1,0:T(8,128)(2,1)}, bf16[192,2560]{1,0:T(8,128)(2,1)}) custom-call(s32[7]{0:T(128)} %stack.31.place, bf16[512,512]{1,0:T(8,128)(2,1)} %keys.1, bf16[512,512]{1,0:T(8,128)(2,1)} %values.1, s32[4,128]{1,0:T(4,128)} %bitcast.16, bf16[192,2048]{1,0:T(8,128)(2,1)} %bitcast.13, ...), custom_call_target="tpu_custom_call" | custom-call | tf_op jit(solution)/shard_map/pallas_call | solution.py:317
  12.2 13.0 %all-to-all-start = ((bf16[4,272,128]{2,1,0:T(8,128)(2,1)}), bf16[4,272,128]{2,1,0:T(8,128)(2,1)S(1)}, u32[]{:S(2)}, u32[]{:S(2)}) async-start(bf16[4,272,128]{2,1,0:T(8,128)(2,1)} %get-tuple-element.15), calls=%async_computation | async-start | bytes 557056 | tf_op jit(solution)/shard_map/all_to_all | solution.py:343
  25.2 7.9 %all_gather.7 = bf16[2048,128]{1,0:T(8,128)(2,1)S(1)} all-gather(bf16[512,128]{1,0:T(8,128)(2,1)S(1)} %copy-done.6), channel_id=1, replica_groups=mesh['zh'=4,'zl'=4,'yl'=2,'yh'=2,'xh'=2,'xl'=2,'c'=2] {'xl','c'}, dimensions={0}, use_global_device_ids=true | all-gather | bytes 655360 | tf_op jit(solution)/shard_map/all_gather | solution.py:347
  33.2 2.1 collective-permute-start.4
  35.3 9.9 %all-to-all-done.kv0 = bf16[4,272,128]{2,1,0:T(8,128)(2,1)S(1)} async-done(((bf16[4,272,128]{2,1,0:T(8,128)(2,1)}), bf16[4,272,128]{2,1,0:T(8,128)(2,1)S(1)}, u32[]{:S(2)}, u32[]{:S(2)}) %all-to-all-start) | async-done | bytes 278560 | tf_op jit(solution)/shard_map/all_to_all | solution.py:343
  45.2 1.9 collective-permute-start
  47.1 3.4 %collective-permute-start.1 = (bf16[4,272,128]{2,1,0:T(8,128)(2,1)S(1)}, bf16[4,272,128]{2,1,0:T(8,128)(2,1)S(1)}, u32[]{:S(2)}, u32[]{:S(2)}) collective-permute-start(bf16[4,272,128]{2,1,0:T(8,128)(2,1)S(1)} %all-to-all-done.kv0), channel_id=1, source_target_pairs={{32,0},{64,32},{96,64},{128,96},{160,128},{192,160},{224,192},{256... | collective-permute-start | bytes 835592 | tf_op jit(solution)/shard_map/ppermute | solution.py:339
  50.5 3.0 %collective-permute-start.2 = (bf16[2,272,128]{2,1,0:T(8,128)(2,1)S(1)}, bf16[2,272,128]{2,1,0:T(8,128)(2,1)S(1)}, u32[]{:S(2)}, u32[]{:S(2)}) collective-permute-start(bf16[2,272,128]{2,1,0:T(8,128)(2,1)S(1)} %get-tuple-element.27), channel_id=1, source_target_pairs={{448,0},{480,32},{0,64},{32,96},{64,128},{96,160},{128,192},{160,2... | collective-permute-start | bytes 417800 | tf_op jit(solution)/shard_map/ppermute | solution.py:339
  53.5 3.1 %collective-permute-start.3 = (bf16[2,272,128]{2,1,0:T(8,128)(2,1)S(1)}, bf16[2,272,128]{2,1,0:T(8,128)(2,1)S(1)}, u32[]{:S(2)}, u32[]{:S(2)}) collective-permute-start(bf16[2,272,128]{2,1,0:T(8,128)(2,1)S(1)} %get-tuple-element.26), channel_id=1, source_target_pairs={{64,0},{96,32},{128,64},{160,96},{192,128},{224,160},{256,192},{28... | collective-permute-start | bytes 417800 | tf_op jit(solution)/shard_map/ppermute | solution.py:339
  57.5 4.3 %collective-permute-done.3.kv3_high = bf16[2,272,128]{2,1,0:T(8,128)(2,1)S(1)} collective-permute-done((bf16[2,272,128]{2,1,0:T(8,128)(2,1)S(1)}, bf16[2,272,128]{2,1,0:T(8,128)(2,1)S(1)}, u32[]{:S(2)}, u32[]{:S(2)}) %collective-permute-start.3) | collective-permute-done | bytes 139296 | tf_op jit(solution)/shard_map/ppermute | solution.py:339
  61.8 7.1 %shard_map.96 = bf16[8,528,128]{2,1,0:T(8,128)(2,1)S(1)} custom-call(s32[7]{0:T(128)S(1)} %copy-done.5, bf16[4,272,128]{2,1,0:T(8,128)(2,1)S(1)} %all-to-all-done.kv0, bf16[4,272,128]{2,1,0:T(8,128)(2,1)S(1)} %collective-permute-done.kv1, bf16[4,272,128]{2,1,0:T(8,128)(2,1)S(1)} %collective-permute-done.1.kv2, ...), custom_call_target="tpu_custom_call" | custom-call | flops 20000000000 | bytes 4194304 | tf_op jit(solution)/shard_map/pallas_call | solution.py:297
  68.9 24.1 %all_to_all.30.parts = bf16[8,528,128]{2,1,0:T(8,128)(2,1)S(1)} all-to-all(bf16[8,528,128]{2,1,0:T(8,128)(2,1)S(1)} %shard_map.96), channel_id=1, replica_groups=mesh['zh'=4,'zl'=4,'yl'=2,'yh'=2,'xh'=2,'xl'=2,'c'=2] {'yl','xl','c'}, dimensions={0} | all-to-all | bytes 2162688 | tf_op jit(solution)/shard_map/all_to_all | solution.py:376
  93.0 0.9 shard_map.97
  93.9 15.4 %all_to_all.31.att = bf16[4,512,128]{2,1,0:T(8,128)(2,1)S(1)} all-to-all(bf16[4,512,128]{2,1,0:T(8,128)(2,1)S(1)} %get-tuple-element.17), channel_id=1, replica_groups=mesh['zh'=4,'zl'=4,'yl'=2,'yh'=2,'xh'=2,'xl'=2,'c'=2] {'yh','xh'}, dimensions={0} | all-to-all | bytes 1048576 | tf_op jit(solution)/shard_map/all_to_all | solution.py:382
  109.3 2.1 copy-done.2
  111.4 2.4 %shard_map.98 = bf16[8,896,128]{2,1,0:T(8,128)(2,1)S(1)} custom-call(s32[7]{0:T(128)S(1)} %copy-done.5, bf16[768,2560]{1,0:T(8,128)(2,1)S(1)} %copy-done.2, bf16[4,512,128]{2,1,0:T(8,128)(2,1)S(1)} %all_to_all.31.att, bf16[32,4096]{1,0:T(8,128)(2,1)S(1)} %copy-done.4), custom_call_target="tpu_custom_call" | custom-call | bytes 4194304 | tf_op jit(solution)/shard_map/pallas_call | solution.py:297
  113.8 26.0 %all_to_all.32.own = bf16[8,896,128]{2,1,0:T(8,128)(2,1)S(1)} all-to-all(bf16[8,896,128]{2,1,0:T(8,128)(2,1)S(1)} %shard_map.98), channel_id=1, replica_groups=mesh['zh'=4,'zl'=4,'yl'=2,'yh'=2,'xh'=2,'xl'=2,'c'=2] {'xl','yh','xh'}, dimensions={0} | all-to-all | bytes 3670016 | tf_op jit(solution)/shard_map/all_to_all | solution.py:391
  139.8 5.1 %collective-permute-start.5 = (bf16[8,896,128]{2,1,0:T(8,128)(2,1)S(1)}, bf16[8,896,128]{2,1,0:T(8,128)(2,1)S(1)}, u32[]{:S(2)}, u32[]{:S(2)}) collective-permute-start(bf16[8,896,128]{2,1,0:T(8,128)(2,1)S(1)} %all_to_all.32.own), channel_id=1, source_target_pairs={{0,1},{1,0},{2,3},{3,2},{4,5},{5,4},{6,7},{7,6},{8,9},{9,8},{10,11... | collective-permute-start | bytes 5505032 | tf_op jit(solution)/shard_map/ppermute | solution.py:392
  145.6 2.7 %collective-permute-done.5.other = bf16[8,896,128]{2,1,0:T(8,128)(2,1)S(1)} collective-permute-done((bf16[8,896,128]{2,1,0:T(8,128)(2,1)S(1)}, bf16[8,896,128]{2,1,0:T(8,128)(2,1)S(1)}, u32[]{:S(2)}, u32[]{:S(2)}) %collective-permute-start.5) | collective-permute-done | bytes 1835040 | tf_op jit(solution)/shard_map/ppermute | solution.py:392
  148.3 2.3 %shard_map.100 = (bf16[512,256]{1,0:T(8,128)(2,1)S(1)}, bf16[4,96,256]{2,1,0:T(8,128)(2,1)}, bf16[4,96,256]{2,1,0:T(8,128)(2,1)S(1)}) custom-call(s32[7]{0:T(128)S(1)} %copy-done.5, bf16[8,896,128]{2,1,0:T(8,128)(2,1)S(1)} %all_to_all.32.own, bf16[8,896,128]{2,1,0:T(8,128)(2,1)S(1)} %collective-permute-done.5.other, ...), custom_call_target="tpu_custom_call" | custom-call | flops 800000000 | bytes 4194304 | tf_op jit(solution)/shard_map/pallas_call | solution.py:297
  150.6 2.0 shard_map.102
  152.6 2.0 collective-permute-start.6
  154.6 3.3 %collective-permute-start.7 = (bf16[8,96,256]{2,1,0:T(8,128)(2,1)}, bf16[8,96,256]{2,1,0:T(8,128)(2,1)S(1)}, u32[]{:S(2)}, u32[]{:S(2)}) collective-permute-start(bf16[8,96,256]{2,1,0:T(8,128)(2,1)} %get-tuple-element.22), channel_id=1, source_target_pairs={{32,0},{64,32},{96,64},{128,96},{160,128},{192,160},{224,192},{256... | collective-permute-start | bytes 1179656 | tf_op jit(solution)/shard_map/ppermute | solution.py:339
  157.9 6.9 %collective-permute-start.8 = (bf16[4,96,256]{2,1,0:T(8,128)(2,1)}, bf16[4,96,256]{2,1,0:T(8,128)(2,1)S(1)}, u32[]{:S(2)}, u32[]{:S(2)}) collective-permute-start(bf16[4,96,256]{2,1,0:T(8,128)(2,1)} %get-tuple-element.23), channel_id=1, source_target_pairs={{448,0},{480,32},{0,64},{32,96},{64,128},{96,160},{128,192},{160,2... | collective-permute-start | bytes 589832 | tf_op jit(solution)/shard_map/ppermute | solution.py:339
  164.8 10.8 %collective-permute-start.9 = (bf16[4,96,256]{2,1,0:T(8,128)(2,1)S(1)}, bf16[4,96,256]{2,1,0:T(8,128)(2,1)S(1)}, u32[]{:S(2)}, u32[]{:S(2)}) collective-permute-start(bf16[4,96,256]{2,1,0:T(8,128)(2,1)S(1)} %get-tuple-element.24), channel_id=1, source_target_pairs={{64,0},{96,32},{128,64},{160,96},{192,128},{224,160},{256,192},{28... | collective-permute-start | bytes 589832 | tf_op jit(solution)/shard_map/ppermute | solution.py:339
  175.6 4.8 %all-to-all-start.5 = ((bf16[4,128,128]{2,1,0:T(8,128)(2,1)}), bf16[4,128,128]{2,1,0:T(8,128)(2,1)}, u32[]{:S(2)}, u32[]{:S(2)}) async-start(bf16[4,128,128]{2,1,0:T(8,128)(2,1)} %bitcast.10), calls=%async_computation.5 | async-start | bytes 262144 | tf_op jit(solution)/shard_map/all_to_all | solution.py:379
  180.5 1.5 copy-done.1
  182.0 0.9 shard_map.101.kept
  182.9 1.0 shard_map.103
  184.2 12.4 %all-to-all-start.4 = ((bf16[8,96,256]{2,1,0:T(8,128)(2,1)}), bf16[8,96,256]{2,1,0:T(8,128)(2,1)S(1)}, u32[]{:S(2)}, u32[]{:S(2)}) async-start(bf16[8,96,256]{2,1,0:T(8,128)(2,1)} %shard_map.103), calls=%async_computation.4 | async-start | bytes 786432 | tf_op jit(solution)/shard_map/all_to_all | solution.py:412
  196.6 1.7 copy.10
  198.3 23.6 %all-to-all-done.4.terms = bf16[8,96,256]{2,1,0:T(8,128)(2,1)S(1)} async-done(((bf16[8,96,256]{2,1,0:T(8,128)(2,1)}), bf16[8,96,256]{2,1,0:T(8,128)(2,1)S(1)}, u32[]{:S(2)}, u32[]{:S(2)}) %all-to-all-start.4) | async-done | bytes 393248 | tf_op jit(solution)/shard_map/all_to_all | solution.py:412
  (32 shorter events, 3.3 us)
Async XLA Ops:
  7.2 18.0 %copy-start.6 = (bf16[512,128]{1,0:T(8,128)(2,1)S(1)}, bf16[512,128]{1,0:T(8,128)(2,1)}, u32[]{:S(2)}) copy-start(bf16[512,128]{1,0:T(8,128)(2,1)} %param.8) | copy-start | bytes 393220
  7.2 102.1 %all-gather.2.cloned.1.call-start = ((), (), s32[]{:S(2)}) async-start(), calls=%async_computation.6 | async-start | bytes 4915200 | tf_op jit(solution)/shard_map/all_gather | solution.py:349
  12.1 21.1 %copy-start.7 = (bf16[16,128]{1,0:T(8,128)(2,1)S(1)}, bf16[16,128]{1,0:T(8,128)(2,1)}, u32[]{:S(2)}) copy-start(bf16[16,128]{1,0:T(8,128)(2,1)} %get-tuple-element.16) | copy-start | bytes 12292
  12.2 49.7 %copy-start.5 = (s32[7]{0:T(128)S(1)}, s32[7]{0:T(128)}, u32[]{:S(2)}) copy-start(s32[7]{0:T(128)} %stack.31.place) | copy-start | bytes 88
  12.2 33.0 %all-to-all-start = ((bf16[4,272,128]{2,1,0:T(8,128)(2,1)}), bf16[4,272,128]{2,1,0:T(8,128)(2,1)S(1)}, u32[]{:S(2)}, u32[]{:S(2)}) async-start(bf16[4,272,128]{2,1,0:T(8,128)(2,1)} %get-tuple-element.15), calls=%async_computation | async-start | bytes 557056 | tf_op jit(solution)/shard_map/all_to_all | solution.py:343
  33.2 23.5 %collective-permute-start.4 = (bf16[2064,128]{1,0:T(8,128)(2,1)S(1)}, bf16[2064,128]{1,0:T(8,128)(2,1)S(1)}, u32[]{:S(2)}, u32[]{:S(2)}) collective-permute-start(bf16[2064,128]{1,0:T(8,128)(2,1)S(1)} %constant_dynamic-update-slice_fusion.q_own), channel_id=1, source_target_pairs={{0,16},{16,0},{1,17},{17,1},{2,18},{18,2},{3,19},{19,3},{4,20},{20... | collective-permute-start | bytes 1585160 | tf_op jit(solution)/shard_map/ppermute | solution.py:348
  45.2 16.6 %collective-permute-start = (bf16[4,272,128]{2,1,0:T(8,128)(2,1)S(1)}, bf16[4,272,128]{2,1,0:T(8,128)(2,1)S(1)}, u32[]{:S(2)}, u32[]{:S(2)}) collective-permute-start(bf16[4,272,128]{2,1,0:T(8,128)(2,1)S(1)} %all-to-all-done.kv0), channel_id=1, source_target_pairs={{480,0},{0,32},{32,64},{64,96},{96,128},{128,160},{160,192},{192,2... | collective-permute-start | bytes 835592 | tf_op jit(solution)/shard_map/ppermute | solution.py:339
  47.1 14.7 %collective-permute-start.1 = (bf16[4,272,128]{2,1,0:T(8,128)(2,1)S(1)}, bf16[4,272,128]{2,1,0:T(8,128)(2,1)S(1)}, u32[]{:S(2)}, u32[]{:S(2)}) collective-permute-start(bf16[4,272,128]{2,1,0:T(8,128)(2,1)S(1)} %all-to-all-done.kv0), channel_id=1, source_target_pairs={{32,0},{64,32},{96,64},{128,96},{160,128},{192,160},{224,192},{256... | collective-permute-start | bytes 835592 | tf_op jit(solution)/shard_map/ppermute | solution.py:339
  50.5 7.0 %collective-permute-start.2 = (bf16[2,272,128]{2,1,0:T(8,128)(2,1)S(1)}, bf16[2,272,128]{2,1,0:T(8,128)(2,1)S(1)}, u32[]{:S(2)}, u32[]{:S(2)}) collective-permute-start(bf16[2,272,128]{2,1,0:T(8,128)(2,1)S(1)} %get-tuple-element.27), channel_id=1, source_target_pairs={{448,0},{480,32},{0,64},{32,96},{64,128},{96,160},{128,192},{160,2... | collective-permute-start | bytes 417800 | tf_op jit(solution)/shard_map/ppermute | solution.py:339
  53.5 8.3 %collective-permute-start.3 = (bf16[2,272,128]{2,1,0:T(8,128)(2,1)S(1)}, bf16[2,272,128]{2,1,0:T(8,128)(2,1)S(1)}, u32[]{:S(2)}, u32[]{:S(2)}) collective-permute-start(bf16[2,272,128]{2,1,0:T(8,128)(2,1)S(1)} %get-tuple-element.26), channel_id=1, source_target_pairs={{64,0},{96,32},{128,64},{160,96},{192,128},{224,160},{256,192},{28... | collective-permute-start | bytes 417800 | tf_op jit(solution)/shard_map/ppermute | solution.py:339
  68.9 40.4 %copy-start.4 = (bf16[32,4096]{1,0:T(8,128)(2,1)S(1)}, bf16[32,4096]{1,0:T(8,128)(2,1)}, u32[]{:S(2)}) copy-start(bf16[32,4096]{1,0:T(8,128)(2,1)} %teacher.1) | copy-start | bytes 786436
  109.3 2.1 copy-start.2
  113.8 31.1 %copy-start.3 = (bf16[3072,256]{1,0:T(8,128)(2,1)S(1)}, bf16[3072,256]{1,0:T(8,128)(2,1)}, u32[]{:S(2)}) copy-start(bf16[3072,256]{1,0:T(8,128)(2,1)} %projector.1) | copy-start | bytes 4718596
  139.8 8.5 %collective-permute-start.5 = (bf16[8,896,128]{2,1,0:T(8,128)(2,1)S(1)}, bf16[8,896,128]{2,1,0:T(8,128)(2,1)S(1)}, u32[]{:S(2)}, u32[]{:S(2)}) collective-permute-start(bf16[8,896,128]{2,1,0:T(8,128)(2,1)S(1)} %all_to_all.32.own), channel_id=1, source_target_pairs={{0,1},{1,0},{2,3},{3,2},{4,5},{5,4},{6,7},{7,6},{8,9},{9,8},{10,11... | collective-permute-start | bytes 5505032 | tf_op jit(solution)/shard_map/ppermute | solution.py:392
  148.3 2.3 %copy-start = (bf16[8,896,128]{2,1,0:T(8,128)(2,1)}, bf16[8,896,128]{2,1,0:T(8,128)(2,1)S(1)}, u32[]{:S(2)}) copy-start(bf16[8,896,128]{2,1,0:T(8,128)(2,1)S(1)} %collective-permute-done.5.other) | copy-start | bytes 5505028
  152.6 30.3 %collective-permute-start.6 = (bf16[8,96,256]{2,1,0:T(8,128)(2,1)}, bf16[8,96,256]{2,1,0:T(8,128)(2,1)S(1)}, u32[]{:S(2)}, u32[]{:S(2)}) collective-permute-start(bf16[8,96,256]{2,1,0:T(8,128)(2,1)} %get-tuple-element.21), channel_id=1, source_target_pairs={{480,0},{0,32},{32,64},{64,96},{96,128},{128,160},{160,192},{192,2... | collective-permute-start | bytes 1179656 | tf_op jit(solution)/shard_map/ppermute | solution.py:339
  154.6 28.3 %collective-permute-start.7 = (bf16[8,96,256]{2,1,0:T(8,128)(2,1)}, bf16[8,96,256]{2,1,0:T(8,128)(2,1)S(1)}, u32[]{:S(2)}, u32[]{:S(2)}) collective-permute-start(bf16[8,96,256]{2,1,0:T(8,128)(2,1)} %get-tuple-element.22), channel_id=1, source_target_pairs={{32,0},{64,32},{96,64},{128,96},{160,128},{192,160},{224,192},{256... | collective-permute-start | bytes 1179656 | tf_op jit(solution)/shard_map/ppermute | solution.py:339
  157.9 25.0 %collective-permute-start.8 = (bf16[4,96,256]{2,1,0:T(8,128)(2,1)}, bf16[4,96,256]{2,1,0:T(8,128)(2,1)S(1)}, u32[]{:S(2)}, u32[]{:S(2)}) collective-permute-start(bf16[4,96,256]{2,1,0:T(8,128)(2,1)} %get-tuple-element.23), channel_id=1, source_target_pairs={{448,0},{480,32},{0,64},{32,96},{64,128},{96,160},{128,192},{160,2... | collective-permute-start | bytes 589832 | tf_op jit(solution)/shard_map/ppermute | solution.py:339
  164.8 18.1 %collective-permute-start.9 = (bf16[4,96,256]{2,1,0:T(8,128)(2,1)S(1)}, bf16[4,96,256]{2,1,0:T(8,128)(2,1)S(1)}, u32[]{:S(2)}, u32[]{:S(2)}) collective-permute-start(bf16[4,96,256]{2,1,0:T(8,128)(2,1)S(1)} %get-tuple-element.24), channel_id=1, source_target_pairs={{64,0},{96,32},{128,64},{160,96},{192,128},{224,160},{256,192},{28... | collective-permute-start | bytes 589832 | tf_op jit(solution)/shard_map/ppermute | solution.py:339
  175.6 8.5 %all-to-all-start.5 = ((bf16[4,128,128]{2,1,0:T(8,128)(2,1)}), bf16[4,128,128]{2,1,0:T(8,128)(2,1)}, u32[]{:S(2)}, u32[]{:S(2)}) async-start(bf16[4,128,128]{2,1,0:T(8,128)(2,1)} %bitcast.10), calls=%async_computation.5 | async-start | bytes 262144 | tf_op jit(solution)/shard_map/all_to_all | solution.py:379
  180.5 1.5 copy-start.1
  184.2 37.6 %all-to-all-start.4 = ((bf16[8,96,256]{2,1,0:T(8,128)(2,1)}), bf16[8,96,256]{2,1,0:T(8,128)(2,1)S(1)}, u32[]{:S(2)}, u32[]{:S(2)}) async-start(bf16[8,96,256]{2,1,0:T(8,128)(2,1)} %shard_map.103), calls=%async_computation.4 | async-start | bytes 786432 | tf_op jit(solution)/shard_map/all_to_all | solution.py:412
Sparse Core Ops, SparseCore 0:
  12.3 56.0 all-gather.1

commit v11 on v9

--- a/solution.py
+++ b/solution.py
@@ -23,20 +23,31 @@
 BLOCKS = 4
 
 
-def start_kernel(place, keys, values, docs, weight_t, hidden_t, packed, doc_rows, both, sem):
-    copies = [
-        pltpu.make_async_copy(weight_t, both.at[:, pl.ds(0, 2048)], sem.at[0]),
-        pltpu.make_async_copy(hidden_t, both.at[:, pl.ds(2048, 512)], sem.at[1]),
+def start_kernel(keys, values, docs, weight_t, hidden_t, packed, doc_rows, both, block, joined, sem):
+    j = lax.axis_index("xl") * 2 + lax.axis_index("c")
+    g = lax.axis_index("yh") * 2 + lax.axis_index("xh")
+    rows, columns = pl.ds(pl.multiple_of(j * 128, 128), 128), pl.ds(pl.multiple_of(g * 128, 128), 128)
+    taken = [
+        pltpu.make_async_copy(keys.at[rows, columns], block.at[pl.ds(0, 128)], sem.at[0]),
+        pltpu.make_async_copy(values.at[rows, columns], block.at[pl.ds(128, 128)], sem.at[1]),
+        pltpu.make_async_copy(weight_t, joined.at[:, pl.ds(0, 2048)], sem.at[2]),
+        pltpu.make_async_copy(hidden_t, joined.at[:, pl.ds(2048, 512)], sem.at[3]),
     ]
-    for copy in copies:
+    for copy in taken:
         copy.start()
-    rows = jnp.concatenate([docs[...].astype(F32), jnp.zeros((12, 128), F32)], axis=0).astype(BF)
-    for i in range(4):
-        packed[i, 0:128, :] = keys[...]
-        packed[i, 128:256, :] = values[...]
-        packed[i, 256:272, :] = rows
-    doc_rows[...] = rows
-    for copy in copies:
+    row_docs = jnp.concatenate([docs[...].astype(F32), jnp.zeros((12, 128), F32)], axis=0).astype(BF)
+    block[256:272, :] = row_docs
+    doc_rows[...] = row_docs
+    given = [pltpu.make_async_copy(block, packed.at[i], sem.at[4 + i]) for i in range(4)]
+    given.append(pltpu.make_async_copy(joined, both, sem.at[8]))
+    taken[0].wait()
+    taken[1].wait()
+    for copy in given[:4]:
+        copy.start()
+    taken[2].wait()
+    taken[3].wait()
+    given[4].start()
+    for copy in given:
         copy.wait()
 
 
@@ -51,10 +62,8 @@
     ]
     for copy in copies:
         copy.start()
-    for copy in copies:
+    for copy in copies[:5]:
         copy.wait()
-    for side in range(2):
-        info_v[16 + 4 * side:20 + 4 * side, :] = q_all[side, 2048:2064, :].astype(F32)[0:4].astype(jnp.int32)
     block_docs = []
     for ch in range(4):
         for i in range(BLOCKS):
@@ -67,6 +76,10 @@
         below = jnp.sum((block_docs < d).astype(F32), axis=1, keepdims=True)
         counts = jnp.where(lane == d, below, counts)
     info_v[0:16, :] = counts.astype(jnp.int32)
+    for copy in copies[5:]:
+        copy.wait()
+    for side in range(2):
+        info_v[16 + 4 * side:20 + 4 * side, :] = q_all[side, 2048:2064, :].astype(F32)[0:4].astype(jnp.int32)
     to_scalars = pltpu.make_async_copy(info_v, info, sem.at[7])
     to_scalars.start()
     for ch in range(4):
@@ -255,18 +268,15 @@
     out[...] = projected(own, projector_t).T
 
 
-def second_kernel(place, own, other, projector_t, own_projected, mismatch, up, down):
-    core = place[2]
+def sent_kernel(place, own, other, projector_t, own_projected, mismatch, far_up, far_down, up, down):
+    core, near = place[2], place[6]
     mismatch[0:256, :] = (own_projected[...] - teacher_rows(own, other, core, core)).astype(BF)
     mismatch[256:512, :] = (projected(other, projector_t).T - teacher_rows(own, other, core, 1 - core)).astype(BF)
-    grad = gradient_rows(own, other, mismatch, (place[6] + 2) % 4).astype(BF)
-    up[...] = grad[0:4]
-    down[...] = grad[4:8]
-
-
-def first_kernel(place, own, other, mismatch, up, down):
-    up[...] = gradient_rows(own, other, mismatch, (place[6] + 1) % 4).astype(BF)
-    down[...] = gradient_rows(own, other, mismatch, (place[6] + 3) % 4).astype(BF)
+    up[...] = gradient_rows(own, other, mismatch, (near + 1) % 4).astype(BF)
+    down[...] = gradient_rows(own, other, mismatch, (near + 3) % 4).astype(BF)
+    far = gradient_rows(own, other, mismatch, (near + 2) % 4).astype(BF)
+    far_up[...] = far[0:4]
+    far_down[...] = far[4:8]
 
 
 def kept_kernel(place, own, other, mismatch, out):
@@ -306,22 +316,14 @@
     return jax.ShapeDtypeStruct(dims, dtype)
 
 
-def start(place, keys, values, docs, weight_t, hidden_t):
-    def block(*dims):
-        return pl.BlockSpec(dims, lambda i, place: (0,) * len(dims))
-
-    picked = pl.BlockSpec((128, 128), lambda i, place: (place[0], place[1]))
+def start(keys, values, docs, weight_t, hidden_t):
     return pl.pallas_call(
         start_kernel,
-        grid_spec=pltpu.PrefetchScalarGridSpec(
-            num_scalar_prefetch=1,
-            grid=(1,),
-            in_specs=[picked, picked, block(4, 128), ANY, ANY],
-            out_specs=[block(4, 272, 128), block(16, 128), ANY],
-            scratch_shapes=[pltpu.SemaphoreType.DMA((2,))],
-        ),
+        in_specs=[ANY, ANY, VMEM, ANY, ANY],
+        out_specs=[ANY, VMEM, ANY],
+        scratch_shapes=[pltpu.VMEM((272, 128), BF), pltpu.VMEM((192, 2560), BF), pltpu.SemaphoreType.DMA((9,))],
         out_shape=[shape(4, 272, 128), shape(16, 128), shape(192, 2560)],
-    )(place, keys, values, docs, weight_t, hidden_t)
+    )(keys, values, docs, weight_t, hidden_t)
 
 
 def on_device(queries, keys, values, doc_ids, hidden, out_weight, projector, teacher):
@@ -336,7 +338,7 @@
         return lax.ppermute(x, ("zh", "zl"), [((i + shift) % 16, i) for i in range(16)])
 
     docs = doc_ids.reshape(4, 128)
-    packed, doc_rows, both = start(place, keys, values, docs, out_weight.T, hidden.T)
+    packed, doc_rows, both = start(keys, values, docs, out_weight.T, hidden.T)
     kv_own = lax.all_to_all(packed, "zh", 0, 0)
     kv_below, kv_above = from_z(kv_own, -1), from_z(kv_own, 1)
     kv_low, kv_high = from_z(kv_own[0:2], -2), from_z(kv_own[2:4], 2)
@@ -391,19 +393,17 @@
     projector_t, own_projected = call(
         own_projected_kernel, [shape(256, 3072), shape(256, 256, dtype=F32)], [VMEM] * 2, (own, projector), 24, 4 * 10 ** 8
     )
-    mismatch, up, down = call(
-        second_kernel,
-        [shape(512, 256), shape(4, 96, 256), shape(4, 96, 256)],
+    eight = shape(8, 96, 256)
+    mismatch, far_up, far_down, up, down = call(
+        sent_kernel,
+        [shape(512, 256), shape(4, 96, 256), shape(4, 96, 256), eight, eight],
         [SMEM] + [VMEM] * 4,
         (place, own, other, projector_t, own_projected),
         32,
         8 * 10 ** 8,
     )
-    far_below, far_above = from_z(up, -2), from_z(down, 2)
-    up, down = call(
-        first_kernel, [shape(8, 96, 256), shape(8, 96, 256)], [SMEM] + [VMEM] * 3, (place, own, other, mismatch), 32, 4 * 10 ** 8
-    )
     below, above = from_z(up, -1), from_z(down, 1)
+    far_below, far_above = from_z(far_up, -2), from_z(far_down, 2)
     kept = call(kept_kernel, shape(8, 96, 256, dtype=F32), [SMEM] + [VMEM] * 3, (place, own, other, mismatch), 32, 2 * 10 ** 8)
     near = call(add_kernel, shape(8, 96, 256), [VMEM] * 5, (kept, below, above, far_below, far_above), 16)
     grad = call(final_kernel, shape(96, 256, dtype=F32), [VMEM], (lax.all_to_all(near, ("zh", "yl"), 0, 0),), 8)

time: 257 us -> 228 us (0.89)
  the two profiles are of different devices: /device:TPU:73 before, /device:TPU:40 now
where the time goes in v11:
time: 228 us; the launch traced here: 227 us
  starting transfers between devices  73.8 us (32%)
  blocking collectives  69.7 us (31%)
  waiting for transfers between devices  43.8 us (19%)
  Pallas kernels  20.4 us (9%)
  between operations  14.3 us (6%)
  local copies, waits for them, and re-layouts  5.45 us (2%)
    ppermute x8, starting transfers between devices, from_z(): lax.ppermute(x, ('zh', 'zl'), [((i + shift) % 16, i) for i in range(16)])  39.3 us
    all_to_all x1, blocking collectives, on_device(): own = lax.all_to_all(student, CHIPS, 0, 0)  26.9 us
    all_to_all x1, waiting for transfers between devices, on_device(): lax.all_to_all(near, ('zh', 'yl'), 0, 0)  23.7 us
    all_to_all x1, blocking collectives, on_device(): lax.all_to_all(partial, OCTET, 0, 0)  18.4 us
    all_to_all x1, blocking collectives, on_device(): att_all = lax.all_to_all(att_copies, HEADSETS, 0, 0)  17.2 us
    pallas_call x8, Pallas kernels, call(): pl.pallas_call(kernel, out_shape=out_shape, in_specs=specs, out_specs=VME...  16.8 us
    all_to_all x1, starting transfers between devices, on_device(): kv_own = lax.all_to_all(packed, 'zh', 0, 0)  14.2 us
    all_to_all x1, starting transfers between devices, on_device(): lax.all_to_all(near, ('zh', 'yl'), 0, 0)  12 us
  transfers between devices with their start and end apart: 14, of which 6 were waited for; matrix products, arithmetic and copies ran while one was open for 1% of the time, Pallas kernels for 5%

profile of v11, /device:TPU:40, one launch (start us, length us, event | category | flops | bytes accessed | tf_op | source)
XLA Modules:
  0.0 227.3 jit_solution(269232960938907165)
XLA Ops:
  7.2 3.5 %shard_map.95 = (bf16[4,272,128]{2,1,0:T(8,128)(2,1)}, bf16[16,128]{1,0:T(8,128)(2,1)}, bf16[192,2560]{1,0:T(8,128)(2,1)}) custom-call(bf16[512,512]{1,0:T(8,128)(2,1)} %keys.1, bf16[512,512]{1,0:T(8,128)(2,1)} %values.1, s32[4,128]{1,0:T(4,128)} %bitcast.16, bf16[192,2048]{1,0:T(8,128)(2,1)} %bitcast.13, bf16[192,512]{1,0:T(8,128)(2,1)} %bitcast.14), custom_call_target="tpu_custom_call" | custom-call | tf_op jit(solution)/shard_map/pallas_call | solution.py:320
  10.8 14.2 %all-to-all-start = ((bf16[4,272,128]{2,1,0:T(8,128)(2,1)}), bf16[4,272,128]{2,1,0:T(8,128)(2,1)S(1)}, u32[]{:S(2)}, u32[]{:S(2)}) async-start(bf16[4,272,128]{2,1,0:T(8,128)(2,1)} %get-tuple-element.15), calls=%async_computation | async-start | bytes 557056 | tf_op jit(solution)/shard_map/all_to_all | solution.py:342
  25.0 7.2 %all_gather.7 = bf16[2048,128]{1,0:T(8,128)(2,1)S(1)} all-gather(bf16[512,128]{1,0:T(8,128)(2,1)S(1)} %copy-done.5), channel_id=1, replica_groups=mesh['zh'=4,'zl'=4,'yl'=2,'yh'=2,'xh'=2,'xl'=2,'c'=2] {'xl','c'}, dimensions={0}, use_global_device_ids=true | all-gather | bytes 655360 | tf_op jit(solution)/shard_map/all_gather | solution.py:346
  32.2 2.4 %collective-permute-start.4 = (bf16[2064,128]{1,0:T(8,128)(2,1)S(1)}, bf16[2064,128]{1,0:T(8,128)(2,1)S(1)}, u32[]{:S(2)}, u32[]{:S(2)}) collective-permute-start(bf16[2064,128]{1,0:T(8,128)(2,1)S(1)} %constant_dynamic-update-slice_fusion.q_own), channel_id=1, source_target_pairs={{0,16},{16,0},{1,17},{17,1},{2,18},{18,2},{3,19},{19,3},{4,20},{20... | collective-permute-start | bytes 1585160 | tf_op jit(solution)/shard_map/ppermute | solution.py:347
  34.6 11.9 %all-to-all-done.kv0 = bf16[4,272,128]{2,1,0:T(8,128)(2,1)S(1)} async-done(((bf16[4,272,128]{2,1,0:T(8,128)(2,1)}), bf16[4,272,128]{2,1,0:T(8,128)(2,1)S(1)}, u32[]{:S(2)}, u32[]{:S(2)}) %all-to-all-start) | async-done | bytes 278560 | tf_op jit(solution)/shard_map/all_to_all | solution.py:342
  46.5 3.0 %collective-permute-start = (bf16[4,272,128]{2,1,0:T(8,128)(2,1)S(1)}, bf16[4,272,128]{2,1,0:T(8,128)(2,1)S(1)}, u32[]{:S(2)}, u32[]{:S(2)}) collective-permute-start(bf16[4,272,128]{2,1,0:T(8,128)(2,1)S(1)} %all-to-all-done.kv0), channel_id=1, source_target_pairs={{480,0},{0,32},{32,64},{64,96},{96,128},{128,160},{160,192},{192,2... | collective-permute-start | bytes 835592 | tf_op jit(solution)/shard_map/ppermute | solution.py:338
  49.5 2.8 %collective-permute-start.1 = (bf16[4,272,128]{2,1,0:T(8,128)(2,1)S(1)}, bf16[4,272,128]{2,1,0:T(8,128)(2,1)S(1)}, u32[]{:S(2)}, u32[]{:S(2)}) collective-permute-start(bf16[4,272,128]{2,1,0:T(8,128)(2,1)S(1)} %all-to-all-done.kv0), channel_id=1, source_target_pairs={{32,0},{64,32},{96,64},{128,96},{160,128},{192,160},{224,192},{256... | collective-permute-start | bytes 835592 | tf_op jit(solution)/shard_map/ppermute | solution.py:338
  52.4 2.5 %collective-permute-start.2 = (bf16[2,272,128]{2,1,0:T(8,128)(2,1)S(1)}, bf16[2,272,128]{2,1,0:T(8,128)(2,1)S(1)}, u32[]{:S(2)}, u32[]{:S(2)}) collective-permute-start(bf16[2,272,128]{2,1,0:T(8,128)(2,1)S(1)} %get-tuple-element.27), channel_id=1, source_target_pairs={{448,0},{480,32},{0,64},{32,96},{64,128},{96,160},{128,192},{160,2... | collective-permute-start | bytes 417800 | tf_op jit(solution)/shard_map/ppermute | solution.py:338
  54.9 5.5 %collective-permute-start.3 = (bf16[2,272,128]{2,1,0:T(8,128)(2,1)S(1)}, bf16[2,272,128]{2,1,0:T(8,128)(2,1)S(1)}, u32[]{:S(2)}, u32[]{:S(2)}) collective-permute-start(bf16[2,272,128]{2,1,0:T(8,128)(2,1)S(1)} %get-tuple-element.26), channel_id=1, source_target_pairs={{64,0},{96,32},{128,64},{160,96},{192,128},{224,160},{256,192},{28... | collective-permute-start | bytes 417800 | tf_op jit(solution)/shard_map/ppermute | solution.py:338
  60.5 2.4 %collective-permute-done.2.kv3_low = bf16[2,272,128]{2,1,0:T(8,128)(2,1)S(1)} collective-permute-done((bf16[2,272,128]{2,1,0:T(8,128)(2,1)S(1)}, bf16[2,272,128]{2,1,0:T(8,128)(2,1)S(1)}, u32[]{:S(2)}, u32[]{:S(2)}) %collective-permute-start.2) | collective-permute-done | bytes 139296 | tf_op jit(solution)/shard_map/ppermute | solution.py:338
  62.9 1.4 collective-permute-done.3.kv3_high
  64.3 7.1 %shard_map.96 = bf16[8,528,128]{2,1,0:T(8,128)(2,1)S(1)} custom-call(s32[7]{0:T(128)S(1)} %stack.31.place, bf16[4,272,128]{2,1,0:T(8,128)(2,1)S(1)} %all-to-all-done.kv0, bf16[4,272,128]{2,1,0:T(8,128)(2,1)S(1)} %collective-permute-done.kv1, bf16[4,272,128]{2,1,0:T(8,128)(2,1)S(1)} %collective-permute-done.1.kv2, ...), custom_call_target="tpu_custom_call" | custom-call | flops 20000000000 | bytes 4194304 | tf_op jit(solution)/shard_map/pallas_call | solution.py:304
  71.4 18.4 %all_to_all.30.parts = bf16[8,528,128]{2,1,0:T(8,128)(2,1)S(1)} all-to-all(bf16[8,528,128]{2,1,0:T(8,128)(2,1)S(1)} %shard_map.96), channel_id=1, replica_groups=mesh['zh'=4,'zl'=4,'yl'=2,'yh'=2,'xh'=2,'xl'=2,'c'=2] {'yl','xl','c'}, dimensions={0} | all-to-all | bytes 2162688 | tf_op jit(solution)/shard_map/all_to_all | solution.py:375
  90.7 17.2 %all_to_all.31.att = bf16[4,512,128]{2,1,0:T(8,128)(2,1)S(1)} all-to-all(bf16[4,512,128]{2,1,0:T(8,128)(2,1)S(1)} %get-tuple-element.17), channel_id=1, replica_groups=mesh['zh'=4,'zl'=4,'yl'=2,'yh'=2,'xh'=2,'xl'=2,'c'=2] {'yh','xh'}, dimensions={0} | all-to-all | bytes 1048576 | tf_op jit(solution)/shard_map/all_to_all | solution.py:381
  107.9 2.1 copy-done.2
  110.1 2.4 %shard_map.98 = bf16[8,896,128]{2,1,0:T(8,128)(2,1)S(1)} custom-call(s32[7]{0:T(128)S(1)} %stack.31.place, bf16[768,2560]{1,0:T(8,128)(2,1)S(1)} %copy-done.2, bf16[4,512,128]{2,1,0:T(8,128)(2,1)S(1)} %all_to_all.31.att, bf16[32,4096]{1,0:T(8,128)(2,1)S(1)} %copy-done.4), custom_call_target="tpu_custom_call" | custom-call | bytes 4194304 | tf_op jit(solution)/shard_map/pallas_call | solution.py:304
  112.5 26.9 %all_to_all.32.own = bf16[8,896,128]{2,1,0:T(8,128)(2,1)S(1)} all-to-all(bf16[8,896,128]{2,1,0:T(8,128)(2,1)S(1)} %shard_map.98), channel_id=1, replica_groups=mesh['zh'=4,'zl'=4,'yl'=2,'yh'=2,'xh'=2,'xl'=2,'c'=2] {'xl','yh','xh'}, dimensions={0} | all-to-all | bytes 3670016 | tf_op jit(solution)/shard_map/all_to_all | solution.py:390
  139.4 1.9 collective-permute-start.5
  142.0 3.0 %collective-permute-done.5.other = bf16[8,896,128]{2,1,0:T(8,128)(2,1)S(1)} collective-permute-done((bf16[8,896,128]{2,1,0:T(8,128)(2,1)S(1)}, bf16[8,896,128]{2,1,0:T(8,128)(2,1)S(1)}, u32[]{:S(2)}, u32[]{:S(2)}) %collective-permute-start.5) | collective-permute-done | bytes 1835040 | tf_op jit(solution)/shard_map/ppermute | solution.py:391
  145.0 3.2 %shard_map.100 = (bf16[512,256]{1,0:T(8,128)(2,1)S(1)}, bf16[4,96,256]{2,1,0:T(8,128)(2,1)}, bf16[4,96,256]{2,1,0:T(8,128)(2,1)S(1)}, bf16[8,96,256]{2,1,0:T(8,128)(2,1)}, bf16[8,96,256]{2,1,0:T(8,128)(2,1)}) custom-call(s32[7]{0:T(128)S(1)} %stack.31.place, bf16[8,896,128]{2,1,0:T(8,128)(2,1)S(1)} %all_to_all.32.own, ...), custom_call_target="tpu_custom_call" | custom-call | flops 800000000 | bytes 4194304 | tf_op jit(solution)/shard_map/pallas_call | solution.py:304
  148.2 5.4 %collective-permute-start.6 = (bf16[8,96,256]{2,1,0:T(8,128)(2,1)}, bf16[8,96,256]{2,1,0:T(8,128)(2,1)S(1)}, u32[]{:S(2)}, u32[]{:S(2)}) collective-permute-start(bf16[8,96,256]{2,1,0:T(8,128)(2,1)} %get-tuple-element.21), channel_id=1, source_target_pairs={{480,0},{0,32},{32,64},{64,96},{96,128},{128,160},{160,192},{192,2... | collective-permute-start | bytes 1179656 | tf_op jit(solution)/shard_map/ppermute | solution.py:338
  153.6 1.9 collective-permute-start.7
  155.5 6.0 %collective-permute-start.8 = (bf16[4,96,256]{2,1,0:T(8,128)(2,1)}, bf16[4,96,256]{2,1,0:T(8,128)(2,1)S(1)}, u32[]{:S(2)}, u32[]{:S(2)}) collective-permute-start(bf16[4,96,256]{2,1,0:T(8,128)(2,1)} %get-tuple-element.23), channel_id=1, source_target_pairs={{448,0},{480,32},{0,64},{32,96},{64,128},{96,160},{128,192},{160,2... | collective-permute-start | bytes 589832 | tf_op jit(solution)/shard_map/ppermute | solution.py:338
  161.5 12.2 %collective-permute-start.9 = (bf16[4,96,256]{2,1,0:T(8,128)(2,1)S(1)}, bf16[4,96,256]{2,1,0:T(8,128)(2,1)S(1)}, u32[]{:S(2)}, u32[]{:S(2)}) collective-permute-start(bf16[4,96,256]{2,1,0:T(8,128)(2,1)S(1)} %get-tuple-element.24), channel_id=1, source_target_pairs={{64,0},{96,32},{128,64},{160,96},{192,128},{224,160},{256,192},{28... | collective-permute-start | bytes 589832 | tf_op jit(solution)/shard_map/ppermute | solution.py:338
  173.7 4.0 %all-to-all-start.5 = ((bf16[4,128,128]{2,1,0:T(8,128)(2,1)}), bf16[4,128,128]{2,1,0:T(8,128)(2,1)}, u32[]{:S(2)}, u32[]{:S(2)}) async-start(bf16[4,128,128]{2,1,0:T(8,128)(2,1)} %bitcast.10), calls=%async_computation.5 | async-start | bytes 262144 | tf_op jit(solution)/shard_map/all_to_all | solution.py:378
  177.7 1.5 copy-done.1
  179.2 0.9 shard_map.101.kept
  180.2 1.0 shard_map.102
  181.1 1.3 all-to-all-done.5
  182.4 12.0 %all-to-all-start.4 = ((bf16[8,96,256]{2,1,0:T(8,128)(2,1)}), bf16[8,96,256]{2,1,0:T(8,128)(2,1)S(1)}, u32[]{:S(2)}, u32[]{:S(2)}) async-start(bf16[8,96,256]{2,1,0:T(8,128)(2,1)} %shard_map.102), calls=%async_computation.4 | async-start | bytes 786432 | tf_op jit(solution)/shard_map/all_to_all | solution.py:409
  194.4 1.7 copy.10
  196.1 23.7 %all-to-all-done.4.terms = bf16[8,96,256]{2,1,0:T(8,128)(2,1)S(1)} async-done(((bf16[8,96,256]{2,1,0:T(8,128)(2,1)}), bf16[8,96,256]{2,1,0:T(8,128)(2,1)S(1)}, u32[]{:S(2)}, u32[]{:S(2)}) %all-to-all-start.4) | async-done | bytes 393248 | tf_op jit(solution)/shard_map/all_to_all | solution.py:409
  (29 shorter events, 2.5 us)
Async XLA Ops:
  7.2 17.8 %copy-start.5 = (bf16[512,128]{1,0:T(8,128)(2,1)S(1)}, bf16[512,128]{1,0:T(8,128)(2,1)}, u32[]{:S(2)}) copy-start(bf16[512,128]{1,0:T(8,128)(2,1)} %param.8) | copy-start | bytes 393220
  7.2 100.8 %all-gather.2.cloned.1.call-start = ((), (), s32[]{:S(2)}) async-start(), calls=%async_computation.6 | async-start | bytes 4915200 | tf_op jit(solution)/shard_map/all_gather | solution.py:348
  10.8 21.4 %copy-start.6 = (bf16[16,128]{1,0:T(8,128)(2,1)S(1)}, bf16[16,128]{1,0:T(8,128)(2,1)}, u32[]{:S(2)}) copy-start(bf16[16,128]{1,0:T(8,128)(2,1)} %get-tuple-element.16) | copy-start | bytes 12292
  10.8 35.7 %all-to-all-start = ((bf16[4,272,128]{2,1,0:T(8,128)(2,1)}), bf16[4,272,128]{2,1,0:T(8,128)(2,1)S(1)}, u32[]{:S(2)}, u32[]{:S(2)}) async-start(bf16[4,272,128]{2,1,0:T(8,128)(2,1)} %get-tuple-element.15), calls=%async_computation | async-start | bytes 557056 | tf_op jit(solution)/shard_map/all_to_all | solution.py:342
  32.2 28.3 %collective-permute-start.4 = (bf16[2064,128]{1,0:T(8,128)(2,1)S(1)}, bf16[2064,128]{1,0:T(8,128)(2,1)S(1)}, u32[]{:S(2)}, u32[]{:S(2)}) collective-permute-start(bf16[2064,128]{1,0:T(8,128)(2,1)S(1)} %constant_dynamic-update-slice_fusion.q_own), channel_id=1, source_target_pairs={{0,16},{16,0},{1,17},{17,1},{2,18},{18,2},{3,19},{19,3},{4,20},{20... | collective-permute-start | bytes 1585160 | tf_op jit(solution)/shard_map/ppermute | solution.py:347
  46.5 17.8 %collective-permute-start = (bf16[4,272,128]{2,1,0:T(8,128)(2,1)S(1)}, bf16[4,272,128]{2,1,0:T(8,128)(2,1)S(1)}, u32[]{:S(2)}, u32[]{:S(2)}) collective-permute-start(bf16[4,272,128]{2,1,0:T(8,128)(2,1)S(1)} %all-to-all-done.kv0), channel_id=1, source_target_pairs={{480,0},{0,32},{32,64},{64,96},{96,128},{128,160},{160,192},{192,2... | collective-permute-start | bytes 835592 | tf_op jit(solution)/shard_map/ppermute | solution.py:338
  49.5 14.8 %collective-permute-start.1 = (bf16[4,272,128]{2,1,0:T(8,128)(2,1)S(1)}, bf16[4,272,128]{2,1,0:T(8,128)(2,1)S(1)}, u32[]{:S(2)}, u32[]{:S(2)}) collective-permute-start(bf16[4,272,128]{2,1,0:T(8,128)(2,1)S(1)} %all-to-all-done.kv0), channel_id=1, source_target_pairs={{32,0},{64,32},{96,64},{128,96},{160,128},{192,160},{224,192},{256... | collective-permute-start | bytes 835592 | tf_op jit(solution)/shard_map/ppermute | solution.py:338
  52.4 10.5 %collective-permute-start.2 = (bf16[2,272,128]{2,1,0:T(8,128)(2,1)S(1)}, bf16[2,272,128]{2,1,0:T(8,128)(2,1)S(1)}, u32[]{:S(2)}, u32[]{:S(2)}) collective-permute-start(bf16[2,272,128]{2,1,0:T(8,128)(2,1)S(1)} %get-tuple-element.27), channel_id=1, source_target_pairs={{448,0},{480,32},{0,64},{32,96},{64,128},{96,160},{128,192},{160,2... | collective-permute-start | bytes 417800 | tf_op jit(solution)/shard_map/ppermute | solution.py:338
  54.9 9.4 %collective-permute-start.3 = (bf16[2,272,128]{2,1,0:T(8,128)(2,1)S(1)}, bf16[2,272,128]{2,1,0:T(8,128)(2,1)S(1)}, u32[]{:S(2)}, u32[]{:S(2)}) collective-permute-start(bf16[2,272,128]{2,1,0:T(8,128)(2,1)S(1)} %get-tuple-element.26), channel_id=1, source_target_pairs={{64,0},{96,32},{128,64},{160,96},{192,128},{224,160},{256,192},{28... | collective-permute-start | bytes 417800 | tf_op jit(solution)/shard_map/ppermute | solution.py:338
  71.4 36.5 %copy-start.4 = (bf16[32,4096]{1,0:T(8,128)(2,1)S(1)}, bf16[32,4096]{1,0:T(8,128)(2,1)}, u32[]{:S(2)}) copy-start(bf16[32,4096]{1,0:T(8,128)(2,1)} %teacher.1) | copy-start | bytes 786436
  107.9 2.1 copy-start.2
  112.5 28.8 %copy-start.3 = (bf16[3072,256]{1,0:T(8,128)(2,1)S(1)}, bf16[3072,256]{1,0:T(8,128)(2,1)}, u32[]{:S(2)}) copy-start(bf16[3072,256]{1,0:T(8,128)(2,1)} %projector.1) | copy-start | bytes 4718596
  139.4 5.7 %collective-permute-start.5 = (bf16[8,896,128]{2,1,0:T(8,128)(2,1)S(1)}, bf16[8,896,128]{2,1,0:T(8,128)(2,1)S(1)}, u32[]{:S(2)}, u32[]{:S(2)}) collective-permute-start(bf16[8,896,128]{2,1,0:T(8,128)(2,1)S(1)} %all_to_all.32.own), channel_id=1, source_target_pairs={{0,1},{1,0},{2,3},{3,2},{4,5},{5,4},{6,7},{7,6},{8,9},{9,8},{10,11... | collective-permute-start | bytes 5505032 | tf_op jit(solution)/shard_map/ppermute | solution.py:391
  145.0 3.2 %copy-start = (bf16[8,896,128]{2,1,0:T(8,128)(2,1)}, bf16[8,896,128]{2,1,0:T(8,128)(2,1)S(1)}, u32[]{:S(2)}) copy-start(bf16[8,896,128]{2,1,0:T(8,128)(2,1)S(1)} %collective-permute-done.5.other) | copy-start | bytes 5505028
  148.2 31.9 %collective-permute-start.6 = (bf16[8,96,256]{2,1,0:T(8,128)(2,1)}, bf16[8,96,256]{2,1,0:T(8,128)(2,1)S(1)}, u32[]{:S(2)}, u32[]{:S(2)}) collective-permute-start(bf16[8,96,256]{2,1,0:T(8,128)(2,1)} %get-tuple-element.21), channel_id=1, source_target_pairs={{480,0},{0,32},{32,64},{64,96},{96,128},{128,160},{160,192},{192,2... | collective-permute-start | bytes 1179656 | tf_op jit(solution)/shard_map/ppermute | solution.py:338
  153.6 26.5 %collective-permute-start.7 = (bf16[8,96,256]{2,1,0:T(8,128)(2,1)}, bf16[8,96,256]{2,1,0:T(8,128)(2,1)S(1)}, u32[]{:S(2)}, u32[]{:S(2)}) collective-permute-start(bf16[8,96,256]{2,1,0:T(8,128)(2,1)} %get-tuple-element.22), channel_id=1, source_target_pairs={{32,0},{64,32},{96,64},{128,96},{160,128},{192,160},{224,192},{256... | collective-permute-start | bytes 1179656 | tf_op jit(solution)/shard_map/ppermute | solution.py:338
  155.5 24.6 %collective-permute-start.8 = (bf16[4,96,256]{2,1,0:T(8,128)(2,1)}, bf16[4,96,256]{2,1,0:T(8,128)(2,1)S(1)}, u32[]{:S(2)}, u32[]{:S(2)}) collective-permute-start(bf16[4,96,256]{2,1,0:T(8,128)(2,1)} %get-tuple-element.23), channel_id=1, source_target_pairs={{448,0},{480,32},{0,64},{32,96},{64,128},{96,160},{128,192},{160,2... | collective-permute-start | bytes 589832 | tf_op jit(solution)/shard_map/ppermute | solution.py:338
  161.5 18.6 %collective-permute-start.9 = (bf16[4,96,256]{2,1,0:T(8,128)(2,1)S(1)}, bf16[4,96,256]{2,1,0:T(8,128)(2,1)S(1)}, u32[]{:S(2)}, u32[]{:S(2)}) collective-permute-start(bf16[4,96,256]{2,1,0:T(8,128)(2,1)S(1)} %get-tuple-element.24), channel_id=1, source_target_pairs={{64,0},{96,32},{128,64},{160,96},{192,128},{224,160},{256,192},{28... | collective-permute-start | bytes 589832 | tf_op jit(solution)/shard_map/ppermute | solution.py:338
  173.7 8.7 %all-to-all-start.5 = ((bf16[4,128,128]{2,1,0:T(8,128)(2,1)}), bf16[4,128,128]{2,1,0:T(8,128)(2,1)}, u32[]{:S(2)}, u32[]{:S(2)}) async-start(bf16[4,128,128]{2,1,0:T(8,128)(2,1)} %bitcast.10), calls=%async_computation.5 | async-start | bytes 262144 | tf_op jit(solution)/shard_map/all_to_all | solution.py:378
  177.7 1.5 copy-start.1
  182.4 37.4 %all-to-all-start.4 = ((bf16[8,96,256]{2,1,0:T(8,128)(2,1)}), bf16[8,96,256]{2,1,0:T(8,128)(2,1)S(1)}, u32[]{:S(2)}, u32[]{:S(2)}) async-start(bf16[8,96,256]{2,1,0:T(8,128)(2,1)} %shard_map.102), calls=%async_computation.4 | async-start | bytes 786432 | tf_op jit(solution)/shard_map/all_to_all | solution.py:409
Sparse Core Ops, SparseCore 0:
  10.9 55.5 all-gather.1

commit v12 on v11

--- a/solution.py
+++ b/solution.py
@@ -207,10 +207,10 @@
             copies[copy, rows, :] = total
 
 
-def student_kernel(place, gathered, att, teacher, out, weights, hidden, sem):
-    copies = []
+def student_kernel(place, gathered, att, teacher, out, weights, hidden, taught, student, sem):
     own_rows = pl.ds(pl.multiple_of(2048 + place[0] * 128, 128), 128)
     hidden_copy = pltpu.make_async_copy(gathered.at[:, own_rows], hidden, sem.at[4])
+    copies = []
     for part in range(4):
         rows = pl.ds(part * 192, 192)
         copies.append(pltpu.make_async_copy(gathered.at[rows, pl.ds(0, 2048)], weights.at[rows], sem.at[part]))
@@ -218,19 +218,26 @@
     hidden_copy.start()
     for copy in copies[1:]:
         copy.start()
+    given = []
     for chip in range(8):
         first = (chip % 4 * 4 + chip // 4 * 2) * 256
         for i in range(4):
-            out[chip, 768 + i * 32:800 + i * 32, :] = teacher[:, first + i * 128:first + (i + 1) * 128]
+            taught[chip, i * 32:(i + 1) * 32, :] = teacher[:, first + i * 128:first + (i + 1) * 128]
+        given.append(pltpu.make_async_copy(taught.at[chip], out.at[chip, pl.ds(768, 128)], sem.at[5 + chip]))
+        given[-1].start()
     att_all = att[...].reshape(2048, 128)
     hidden_copy.wait()
     for part in range(4):
         copies[part].wait()
         rows = slice(part * 192, (part + 1) * 192)
         mixed = jnp.dot(weights[rows, :], att_all, preferred_element_type=F32)
-        student = (hidden[rows, :].astype(F32) + mixed).astype(BF)
-        for copy in range(8):
-            out[copy, rows, :] = student
+        student[rows, :] = (hidden[rows, :].astype(F32) + mixed).astype(BF)
+        for chip in range(8):
+            cut = pl.ds(part * 192, 192)
+            given.append(pltpu.make_async_copy(student.at[cut], out.at[chip, cut], sem.at[13 + part * 8 + chip]))
+            given[-1].start()
+    for copy in given:
+        copy.wait()
 
 
 def projected(student, projector_t):
@@ -379,14 +386,20 @@
     attended = jnp.transpose(att_head, (0, 2, 1)).reshape(512, 128)
 
     att_all = lax.all_to_all(att_copies, HEADSETS, 0, 0)
-    student = call(
+    student = pl.pallas_call(
         student_kernel,
-        shape(8, 896, 128),
-        [SMEM, HBM, VMEM, VMEM],
-        (place, gathered, att_all, teacher),
-        24,
-        scratch=[pltpu.VMEM((768, 2048), BF), pltpu.VMEM((768, 128), BF), pltpu.SemaphoreType.DMA((5,))],
-    )
+        out_shape=shape(8, 896, 128),
+        in_specs=[SMEM, HBM, VMEM, VMEM],
+        out_specs=ANY,
+        scratch_shapes=[
+            pltpu.VMEM((768, 2048), BF),
+            pltpu.VMEM((768, 128), BF),
+            pltpu.VMEM((8, 128, 128), BF),
+            pltpu.VMEM((768, 128), BF),
+            pltpu.SemaphoreType.DMA((45,)),
+        ],
+        compiler_params=pltpu.CompilerParams(vmem_limit_bytes=59 * 1024 * 1024),
+    )(place, gathered, att_all, teacher)
     own = lax.all_to_all(student, CHIPS, 0, 0)
     other = lax.ppermute(own, "c", swap)
 

time: 228 us -> 224 us (0.982)
  the two profiles are of different devices: /device:TPU:40 before, /device:TPU:73 now
where the time goes in v12:
time: 224 us; the launch traced here: 223 us
  blocking collectives  74.5 us (33%)
  starting transfers between devices  62.1 us (28%)
  waiting for transfers between devices  46.3 us (21%)
  Pallas kernels  22.9 us (10%)
  between operations  14.2 us (6%)
  local copies, waits for them, and re-layouts  3.34 us (1%)
    all_to_all x1, blocking collectives, on_device(): own = lax.all_to_all(student, CHIPS, 0, 0)  27.1 us
    ppermute x8, starting transfers between devices, from_z(): lax.ppermute(x, ('zh', 'zl'), [((i + shift) % 16, i) for i in range(16)])  24.7 us
    all_to_all x1, blocking collectives, on_device(): lax.all_to_all(partial, OCTET, 0, 0)  23.9 us
    all_to_all x1, waiting for transfers between devices, on_device(): lax.all_to_all(near, ('zh', 'yl'), 0, 0)  22.9 us
    all_to_all x1, blocking collectives, on_device(): att_all = lax.all_to_all(att_copies, HEADSETS, 0, 0)  15.5 us
    pallas_call x7, Pallas kernels, call(): pl.pallas_call(kernel, out_shape=out_shape, in_specs=specs, out_specs=VME...  14.4 us
    all_to_all x1, starting transfers between devices, on_device(): kv_own = lax.all_to_all(packed, 'zh', 0, 0)  13 us
    all_to_all x1, starting transfers between devices, on_device(): lax.all_to_all(near, ('zh', 'yl'), 0, 0)  11.9 us
  transfers between devices with their start and end apart: 14, of which 6 were waited for; matrix products, arithmetic and copies ran while one was open for 1% of the time, Pallas kernels for 5%

profile of v12, /device:TPU:73, one launch (start us, length us, event | category | flops | bytes accessed | tf_op | source)
XLA Modules:
  0.0 223.4 jit_solution(17857200065249437925)
XLA Ops:
  7.2 3.5 %shard_map.95 = (bf16[4,272,128]{2,1,0:T(8,128)(2,1)}, bf16[16,128]{1,0:T(8,128)(2,1)}, bf16[192,2560]{1,0:T(8,128)(2,1)}) custom-call(bf16[512,512]{1,0:T(8,128)(2,1)} %keys.1, bf16[512,512]{1,0:T(8,128)(2,1)} %values.1, s32[4,128]{1,0:T(4,128)} %bitcast.16, bf16[192,2048]{1,0:T(8,128)(2,1)} %bitcast.13, bf16[192,512]{1,0:T(8,128)(2,1)} %bitcast.14), custom_call_target="tpu_custom_call" | custom-call | tf_op jit(solution)/shard_map/pallas_call | solution.py:327
  10.8 13.0 %all-to-all-start = ((bf16[4,272,128]{2,1,0:T(8,128)(2,1)}), bf16[4,272,128]{2,1,0:T(8,128)(2,1)S(1)}, u32[]{:S(2)}, u32[]{:S(2)}) async-start(bf16[4,272,128]{2,1,0:T(8,128)(2,1)} %get-tuple-element.15), calls=%async_computation | async-start | bytes 557056 | tf_op jit(solution)/shard_map/all_to_all | solution.py:349
  23.8 7.9 %all_gather.7 = bf16[2048,128]{1,0:T(8,128)(2,1)S(1)} all-gather(bf16[512,128]{1,0:T(8,128)(2,1)S(1)} %copy-done.5), channel_id=1, replica_groups=mesh['zh'=4,'zl'=4,'yl'=2,'yh'=2,'xh'=2,'xl'=2,'c'=2] {'xl','c'}, dimensions={0}, use_global_device_ids=true | all-gather | bytes 655360 | tf_op jit(solution)/shard_map/all_gather | solution.py:353
  31.8 2.1 collective-permute-start.4
  33.9 9.9 %all-to-all-done.kv0 = bf16[4,272,128]{2,1,0:T(8,128)(2,1)S(1)} async-done(((bf16[4,272,128]{2,1,0:T(8,128)(2,1)}), bf16[4,272,128]{2,1,0:T(8,128)(2,1)S(1)}, u32[]{:S(2)}, u32[]{:S(2)}) %all-to-all-start) | async-done | bytes 278560 | tf_op jit(solution)/shard_map/all_to_all | solution.py:349
  43.8 1.9 collective-permute-start
  45.7 3.4 %collective-permute-start.1 = (bf16[4,272,128]{2,1,0:T(8,128)(2,1)S(1)}, bf16[4,272,128]{2,1,0:T(8,128)(2,1)S(1)}, u32[]{:S(2)}, u32[]{:S(2)}) collective-permute-start(bf16[4,272,128]{2,1,0:T(8,128)(2,1)S(1)} %all-to-all-done.kv0), channel_id=1, source_target_pairs={{32,0},{64,32},{96,64},{128,96},{160,128},{192,160},{224,192},{256... | collective-permute-start | bytes 835592 | tf_op jit(solution)/shard_map/ppermute | solution.py:345
  49.1 3.0 %collective-permute-start.2 = (bf16[2,272,128]{2,1,0:T(8,128)(2,1)S(1)}, bf16[2,272,128]{2,1,0:T(8,128)(2,1)S(1)}, u32[]{:S(2)}, u32[]{:S(2)}) collective-permute-start(bf16[2,272,128]{2,1,0:T(8,128)(2,1)S(1)} %get-tuple-element.27), channel_id=1, source_target_pairs={{448,0},{480,32},{0,64},{32,96},{64,128},{96,160},{128,192},{160,2... | collective-permute-start | bytes 417800 | tf_op jit(solution)/shard_map/ppermute | solution.py:345
  52.1 3.1 %collective-permute-start.3 = (bf16[2,272,128]{2,1,0:T(8,128)(2,1)S(1)}, bf16[2,272,128]{2,1,0:T(8,128)(2,1)S(1)}, u32[]{:S(2)}, u32[]{:S(2)}) collective-permute-start(bf16[2,272,128]{2,1,0:T(8,128)(2,1)S(1)} %get-tuple-element.26), channel_id=1, source_target_pairs={{64,0},{96,32},{128,64},{160,96},{192,128},{224,160},{256,192},{28... | collective-permute-start | bytes 417800 | tf_op jit(solution)/shard_map/ppermute | solution.py:345
  55.4 0.7 collective-permute-done.2.kv3_low
  56.1 4.3 %collective-permute-done.3.kv3_high = bf16[2,272,128]{2,1,0:T(8,128)(2,1)S(1)} collective-permute-done((bf16[2,272,128]{2,1,0:T(8,128)(2,1)S(1)}, bf16[2,272,128]{2,1,0:T(8,128)(2,1)S(1)}, u32[]{:S(2)}, u32[]{:S(2)}) %collective-permute-start.3) | collective-permute-done | bytes 139296 | tf_op jit(solution)/shard_map/ppermute | solution.py:345
  60.4 7.1 %shard_map.96 = bf16[8,528,128]{2,1,0:T(8,128)(2,1)S(1)} custom-call(s32[7]{0:T(128)S(1)} %stack.31.place, bf16[4,272,128]{2,1,0:T(8,128)(2,1)S(1)} %all-to-all-done.kv0, bf16[4,272,128]{2,1,0:T(8,128)(2,1)S(1)} %collective-permute-done.kv1, bf16[4,272,128]{2,1,0:T(8,128)(2,1)S(1)} %collective-permute-done.1.kv2, ...), custom_call_target="tpu_custom_call" | custom-call | flops 20000000000 | bytes 4194304 | tf_op jit(solution)/shard_map/pallas_call | solution.py:311
  67.6 23.9 %all_to_all.30.parts = bf16[8,528,128]{2,1,0:T(8,128)(2,1)S(1)} all-to-all(bf16[8,528,128]{2,1,0:T(8,128)(2,1)S(1)} %shard_map.96), channel_id=1, replica_groups=mesh['zh'=4,'zl'=4,'yl'=2,'yh'=2,'xh'=2,'xl'=2,'c'=2] {'yl','xl','c'}, dimensions={0} | all-to-all | bytes 2162688 | tf_op jit(solution)/shard_map/all_to_all | solution.py:382
  91.5 0.9 shard_map.97
  92.4 15.5 %all_to_all.31.att = bf16[4,512,128]{2,1,0:T(8,128)(2,1)} all-to-all(bf16[4,512,128]{2,1,0:T(8,128)(2,1)S(1)} %get-tuple-element.17), channel_id=1, replica_groups=mesh['zh'=4,'zl'=4,'yl'=2,'yh'=2,'xh'=2,'xl'=2,'c'=2] {'yh','xh'}, dimensions={0} | all-to-all | bytes 1048576 | tf_op jit(solution)/shard_map/all_to_all | solution.py:388
  107.9 5.0 %shard_map.98 = bf16[8,896,128]{2,1,0:T(8,128)(2,1)} custom-call(s32[7]{0:T(128)} %copy-done.3, bf16[768,2560]{1,0:T(8,128)(2,1)} %all-gather.2.cloned.1.call-done.gathered, bf16[4,512,128]{2,1,0:T(8,128)(2,1)} %all_to_all.31.att, bf16[32,4096]{1,0:T(8,128)(2,1)} %teacher.1), custom_call_target="tpu_custom_call" | custom-call | tf_op jit(solution)/shard_map/pallas_call | solution.py:389
  112.9 27.1 %all_to_all.32.own = bf16[8,896,128]{2,1,0:T(8,128)(2,1)S(1)} all-to-all(bf16[8,896,128]{2,1,0:T(8,128)(2,1)} %shard_map.98), channel_id=1, replica_groups=mesh['zh'=4,'zl'=4,'yl'=2,'yh'=2,'xh'=2,'xl'=2,'c'=2] {'xl','yh','xh'}, dimensions={0} | all-to-all | bytes 3670016 | tf_op jit(solution)/shard_map/all_to_all | solution.py:403
  140.0 5.2 %collective-permute-start.5 = (bf16[8,896,128]{2,1,0:T(8,128)(2,1)S(1)}, bf16[8,896,128]{2,1,0:T(8,128)(2,1)S(1)}, u32[]{:S(2)}, u32[]{:S(2)}) collective-permute-start(bf16[8,896,128]{2,1,0:T(8,128)(2,1)S(1)} %all_to_all.32.own), channel_id=1, source_target_pairs={{0,1},{1,0},{2,3},{3,2},{4,5},{5,4},{6,7},{7,6},{8,9},{9,8},{10,11... | collective-permute-start | bytes 5505032 | tf_op jit(solution)/shard_map/ppermute | solution.py:404
  145.9 2.7 %collective-permute-done.5.other = bf16[8,896,128]{2,1,0:T(8,128)(2,1)S(1)} collective-permute-done((bf16[8,896,128]{2,1,0:T(8,128)(2,1)S(1)}, bf16[8,896,128]{2,1,0:T(8,128)(2,1)S(1)}, u32[]{:S(2)}, u32[]{:S(2)}) %collective-permute-start.5) | collective-permute-done | bytes 1835040 | tf_op jit(solution)/shard_map/ppermute | solution.py:404
  148.6 3.2 %shard_map.100 = (bf16[512,256]{1,0:T(8,128)(2,1)S(1)}, bf16[4,96,256]{2,1,0:T(8,128)(2,1)}, bf16[4,96,256]{2,1,0:T(8,128)(2,1)S(1)}, bf16[8,96,256]{2,1,0:T(8,128)(2,1)}, bf16[8,96,256]{2,1,0:T(8,128)(2,1)}) custom-call(s32[7]{0:T(128)S(1)} %copy-done.4, bf16[8,896,128]{2,1,0:T(8,128)(2,1)S(1)} %all_to_all.32.own, ...), custom_call_target="tpu_custom_call" | custom-call | flops 800000000 | bytes 4194304 | tf_op jit(solution)/shard_map/pallas_call | solution.py:311
  151.7 1.9 collective-permute-start.6
  153.6 3.4 %collective-permute-start.7 = (bf16[8,96,256]{2,1,0:T(8,128)(2,1)}, bf16[8,96,256]{2,1,0:T(8,128)(2,1)S(1)}, u32[]{:S(2)}, u32[]{:S(2)}) collective-permute-start(bf16[8,96,256]{2,1,0:T(8,128)(2,1)} %get-tuple-element.22), channel_id=1, source_target_pairs={{32,0},{64,32},{96,64},{128,96},{160,128},{192,160},{224,192},{256... | collective-permute-start | bytes 1179656 | tf_op jit(solution)/shard_map/ppermute | solution.py:345
  157.0 6.1 %collective-permute-start.8 = (bf16[4,96,256]{2,1,0:T(8,128)(2,1)}, bf16[4,96,256]{2,1,0:T(8,128)(2,1)S(1)}, u32[]{:S(2)}, u32[]{:S(2)}) collective-permute-start(bf16[4,96,256]{2,1,0:T(8,128)(2,1)} %get-tuple-element.23), channel_id=1, source_target_pairs={{448,0},{480,32},{0,64},{32,96},{64,128},{96,160},{128,192},{160,2... | collective-permute-start | bytes 589832 | tf_op jit(solution)/shard_map/ppermute | solution.py:345
  163.1 1.9 collective-permute-start.9
  165.1 5.1 %all-to-all-start.5 = ((bf16[4,128,128]{2,1,0:T(8,128)(2,1)}), bf16[4,128,128]{2,1,0:T(8,128)(2,1)}, u32[]{:S(2)}, u32[]{:S(2)}) async-start(bf16[4,128,128]{2,1,0:T(8,128)(2,1)} %bitcast.10), calls=%async_computation.5 | async-start | bytes 262144 | tf_op jit(solution)/shard_map/all_to_all | solution.py:385
  170.2 1.5 copy-done.1
  171.7 0.9 shard_map.101.kept
  172.6 5.8 %collective-permute-done.9.far_above = bf16[4,96,256]{2,1,0:T(8,128)(2,1)S(1)} collective-permute-done((bf16[4,96,256]{2,1,0:T(8,128)(2,1)S(1)}, bf16[4,96,256]{2,1,0:T(8,128)(2,1)S(1)}, u32[]{:S(2)}, u32[]{:S(2)}) %collective-permute-start.9) | collective-permute-done | bytes 196640 | tf_op jit(solution)/shard_map/ppermute | solution.py:345
  178.4 1.0 shard_map.102
  179.3 11.9 %all-to-all-start.4 = ((bf16[8,96,256]{2,1,0:T(8,128)(2,1)}), bf16[8,96,256]{2,1,0:T(8,128)(2,1)S(1)}, u32[]{:S(2)}, u32[]{:S(2)}) async-start(bf16[8,96,256]{2,1,0:T(8,128)(2,1)} %shard_map.102), calls=%async_computation.4 | async-start | bytes 786432 | tf_op jit(solution)/shard_map/all_to_all | solution.py:422
  191.3 1.7 copy.10
  192.9 22.9 %all-to-all-done.4.terms = bf16[8,96,256]{2,1,0:T(8,128)(2,1)S(1)} async-done(((bf16[8,96,256]{2,1,0:T(8,128)(2,1)}), bf16[8,96,256]{2,1,0:T(8,128)(2,1)S(1)}, u32[]{:S(2)}, u32[]{:S(2)}) %all-to-all-start.4) | async-done | bytes 393248 | tf_op jit(solution)/shard_map/all_to_all | solution.py:422
  (29 shorter events, 1.6 us)
Async XLA Ops:
  7.2 16.6 %copy-start.5 = (bf16[512,128]{1,0:T(8,128)(2,1)S(1)}, bf16[512,128]{1,0:T(8,128)(2,1)}, u32[]{:S(2)}) copy-start(bf16[512,128]{1,0:T(8,128)(2,1)} %param.8) | copy-start | bytes 393220
  7.2 100.7 %all-gather.2.cloned.1.call-start = ((), (), s32[]{:S(2)}) async-start(), calls=%async_computation.6 | async-start | bytes 4915200 | tf_op jit(solution)/shard_map/all_gather | solution.py:355
  10.8 21.0 %copy-start.6 = (bf16[16,128]{1,0:T(8,128)(2,1)S(1)}, bf16[16,128]{1,0:T(8,128)(2,1)}, u32[]{:S(2)}) copy-start(bf16[16,128]{1,0:T(8,128)(2,1)} %get-tuple-element.16) | copy-start | bytes 12292
  10.8 33.0 %all-to-all-start = ((bf16[4,272,128]{2,1,0:T(8,128)(2,1)}), bf16[4,272,128]{2,1,0:T(8,128)(2,1)S(1)}, u32[]{:S(2)}, u32[]{:S(2)}) async-start(bf16[4,272,128]{2,1,0:T(8,128)(2,1)} %get-tuple-element.15), calls=%async_computation | async-start | bytes 557056 | tf_op jit(solution)/shard_map/all_to_all | solution.py:349
  31.8 23.6 %collective-permute-start.4 = (bf16[2064,128]{1,0:T(8,128)(2,1)S(1)}, bf16[2064,128]{1,0:T(8,128)(2,1)S(1)}, u32[]{:S(2)}, u32[]{:S(2)}) collective-permute-start(bf16[2064,128]{1,0:T(8,128)(2,1)S(1)} %constant_dynamic-update-slice_fusion.q_own), channel_id=1, source_target_pairs={{0,16},{16,0},{1,17},{17,1},{2,18},{18,2},{3,19},{19,3},{4,20},{20... | collective-permute-start | bytes 1585160 | tf_op jit(solution)/shard_map/ppermute | solution.py:354
  43.8 16.6 %collective-permute-start = (bf16[4,272,128]{2,1,0:T(8,128)(2,1)S(1)}, bf16[4,272,128]{2,1,0:T(8,128)(2,1)S(1)}, u32[]{:S(2)}, u32[]{:S(2)}) collective-permute-start(bf16[4,272,128]{2,1,0:T(8,128)(2,1)S(1)} %all-to-all-done.kv0), channel_id=1, source_target_pairs={{480,0},{0,32},{32,64},{64,96},{96,128},{128,160},{160,192},{192,2... | collective-permute-start | bytes 835592 | tf_op jit(solution)/shard_map/ppermute | solution.py:345
  45.7 14.7 %collective-permute-start.1 = (bf16[4,272,128]{2,1,0:T(8,128)(2,1)S(1)}, bf16[4,272,128]{2,1,0:T(8,128)(2,1)S(1)}, u32[]{:S(2)}, u32[]{:S(2)}) collective-permute-start(bf16[4,272,128]{2,1,0:T(8,128)(2,1)S(1)} %all-to-all-done.kv0), channel_id=1, source_target_pairs={{32,0},{64,32},{96,64},{128,96},{160,128},{192,160},{224,192},{256... | collective-permute-start | bytes 835592 | tf_op jit(solution)/shard_map/ppermute | solution.py:345
  49.1 7.0 %collective-permute-start.2 = (bf16[2,272,128]{2,1,0:T(8,128)(2,1)S(1)}, bf16[2,272,128]{2,1,0:T(8,128)(2,1)S(1)}, u32[]{:S(2)}, u32[]{:S(2)}) collective-permute-start(bf16[2,272,128]{2,1,0:T(8,128)(2,1)S(1)} %get-tuple-element.27), channel_id=1, source_target_pairs={{448,0},{480,32},{0,64},{32,96},{64,128},{96,160},{128,192},{160,2... | collective-permute-start | bytes 417800 | tf_op jit(solution)/shard_map/ppermute | solution.py:345
  52.1 8.3 %collective-permute-start.3 = (bf16[2,272,128]{2,1,0:T(8,128)(2,1)S(1)}, bf16[2,272,128]{2,1,0:T(8,128)(2,1)S(1)}, u32[]{:S(2)}, u32[]{:S(2)}) collective-permute-start(bf16[2,272,128]{2,1,0:T(8,128)(2,1)S(1)} %get-tuple-element.26), channel_id=1, source_target_pairs={{64,0},{96,32},{128,64},{160,96},{192,128},{224,160},{256,192},{28... | collective-permute-start | bytes 417800 | tf_op jit(solution)/shard_map/ppermute | solution.py:345
  55.4 12.2 %copy-start.3 = (s32[7]{0:T(128)}, s32[7]{0:T(128)S(1)}, u32[]{:S(2)}) copy-start(s32[7]{0:T(128)S(1)} %stack.31.place) | copy-start | bytes 88
  112.9 32.3 %copy-start.2 = (bf16[3072,256]{1,0:T(8,128)(2,1)S(1)}, bf16[3072,256]{1,0:T(8,128)(2,1)}, u32[]{:S(2)}) copy-start(bf16[3072,256]{1,0:T(8,128)(2,1)} %projector.1) | copy-start | bytes 4718596
  140.0 8.6 %copy-start.4 = (s32[7]{0:T(128)S(1)}, s32[7]{0:T(128)}, u32[]{:S(2)}) copy-start(s32[7]{0:T(128)} %copy-done.3) | copy-start | bytes 88
  140.0 8.6 %collective-permute-start.5 = (bf16[8,896,128]{2,1,0:T(8,128)(2,1)S(1)}, bf16[8,896,128]{2,1,0:T(8,128)(2,1)S(1)}, u32[]{:S(2)}, u32[]{:S(2)}) collective-permute-start(bf16[8,896,128]{2,1,0:T(8,128)(2,1)S(1)} %all_to_all.32.own), channel_id=1, source_target_pairs={{0,1},{1,0},{2,3},{3,2},{4,5},{5,4},{6,7},{7,6},{8,9},{9,8},{10,11... | collective-permute-start | bytes 5505032 | tf_op jit(solution)/shard_map/ppermute | solution.py:404
  148.6 3.2 %copy-start = (bf16[8,896,128]{2,1,0:T(8,128)(2,1)}, bf16[8,896,128]{2,1,0:T(8,128)(2,1)S(1)}, u32[]{:S(2)}) copy-start(bf16[8,896,128]{2,1,0:T(8,128)(2,1)S(1)} %collective-permute-done.5.other) | copy-start | bytes 5505028
  151.7 26.6 %collective-permute-start.6 = (bf16[8,96,256]{2,1,0:T(8,128)(2,1)}, bf16[8,96,256]{2,1,0:T(8,128)(2,1)S(1)}, u32[]{:S(2)}, u32[]{:S(2)}) collective-permute-start(bf16[8,96,256]{2,1,0:T(8,128)(2,1)} %get-tuple-element.21), channel_id=1, source_target_pairs={{480,0},{0,32},{32,64},{64,96},{96,128},{128,160},{160,192},{192,2... | collective-permute-start | bytes 1179656 | tf_op jit(solution)/shard_map/ppermute | solution.py:345
  153.6 24.7 %collective-permute-start.7 = (bf16[8,96,256]{2,1,0:T(8,128)(2,1)}, bf16[8,96,256]{2,1,0:T(8,128)(2,1)S(1)}, u32[]{:S(2)}, u32[]{:S(2)}) collective-permute-start(bf16[8,96,256]{2,1,0:T(8,128)(2,1)} %get-tuple-element.22), channel_id=1, source_target_pairs={{32,0},{64,32},{96,64},{128,96},{160,128},{192,160},{224,192},{256... | collective-permute-start | bytes 1179656 | tf_op jit(solution)/shard_map/ppermute | solution.py:345
  157.0 15.6 %collective-permute-start.8 = (bf16[4,96,256]{2,1,0:T(8,128)(2,1)}, bf16[4,96,256]{2,1,0:T(8,128)(2,1)S(1)}, u32[]{:S(2)}, u32[]{:S(2)}) collective-permute-start(bf16[4,96,256]{2,1,0:T(8,128)(2,1)} %get-tuple-element.23), channel_id=1, source_target_pairs={{448,0},{480,32},{0,64},{32,96},{64,128},{96,160},{128,192},{160,2... | collective-permute-start | bytes 589832 | tf_op jit(solution)/shard_map/ppermute | solution.py:345
  163.1 15.2 %collective-permute-start.9 = (bf16[4,96,256]{2,1,0:T(8,128)(2,1)S(1)}, bf16[4,96,256]{2,1,0:T(8,128)(2,1)S(1)}, u32[]{:S(2)}, u32[]{:S(2)}) collective-permute-start(bf16[4,96,256]{2,1,0:T(8,128)(2,1)S(1)} %get-tuple-element.24), channel_id=1, source_target_pairs={{64,0},{96,32},{128,64},{160,96},{192,128},{224,160},{256,192},{28... | collective-permute-start | bytes 589832 | tf_op jit(solution)/shard_map/ppermute | solution.py:345
  165.1 14.3 %all-to-all-start.5 = ((bf16[4,128,128]{2,1,0:T(8,128)(2,1)}), bf16[4,128,128]{2,1,0:T(8,128)(2,1)}, u32[]{:S(2)}, u32[]{:S(2)}) async-start(bf16[4,128,128]{2,1,0:T(8,128)(2,1)} %bitcast.10), calls=%async_computation.5 | async-start | bytes 262144 | tf_op jit(solution)/shard_map/all_to_all | solution.py:385
  170.2 1.5 copy-start.1
  179.3 36.5 %all-to-all-start.4 = ((bf16[8,96,256]{2,1,0:T(8,128)(2,1)}), bf16[8,96,256]{2,1,0:T(8,128)(2,1)S(1)}, u32[]{:S(2)}, u32[]{:S(2)}) async-start(bf16[8,96,256]{2,1,0:T(8,128)(2,1)} %shard_map.102), calls=%async_computation.4 | async-start | bytes 786432 | tf_op jit(solution)/shard_map/all_to_all | solution.py:422
Sparse Core Ops, SparseCore 0:
  10.9 56.0 all-gather.1

commit v13 on v11

--- a/solution.py
+++ b/solution.py
@@ -207,30 +207,19 @@
             copies[copy, rows, :] = total
 
 
-def student_kernel(place, gathered, att, teacher, out, weights, hidden, sem):
-    copies = []
+def student_kernel(place, gathered, att, teacher, out):
     own_rows = pl.ds(pl.multiple_of(2048 + place[0] * 128, 128), 128)
-    hidden_copy = pltpu.make_async_copy(gathered.at[:, own_rows], hidden, sem.at[4])
+    att_all = att[...].reshape(2048, 128)
     for part in range(4):
-        rows = pl.ds(part * 192, 192)
-        copies.append(pltpu.make_async_copy(gathered.at[rows, pl.ds(0, 2048)], weights.at[rows], sem.at[part]))
-    copies[0].start()
-    hidden_copy.start()
-    for copy in copies[1:]:
-        copy.start()
+        rows = slice(part * 192, (part + 1) * 192)
+        mixed = jnp.dot(gathered[rows, 0:2048], att_all, preferred_element_type=F32)
+        student = (gathered[rows, own_rows].astype(F32) + mixed).astype(BF)
+        for copy in range(8):
+            out[copy, rows, :] = student
     for chip in range(8):
         first = (chip % 4 * 4 + chip // 4 * 2) * 256
         for i in range(4):
             out[chip, 768 + i * 32:800 + i * 32, :] = teacher[:, first + i * 128:first + (i + 1) * 128]
-    att_all = att[...].reshape(2048, 128)
-    hidden_copy.wait()
-    for part in range(4):
-        copies[part].wait()
-        rows = slice(part * 192, (part + 1) * 192)
-        mixed = jnp.dot(weights[rows, :], att_all, preferred_element_type=F32)
-        student = (hidden[rows, :].astype(F32) + mixed).astype(BF)
-        for copy in range(8):
-            out[copy, rows, :] = student
 
 
 def projected(student, projector_t):
@@ -382,10 +371,9 @@
     student = call(
         student_kernel,
         shape(8, 896, 128),
-        [SMEM, HBM, VMEM, VMEM],
+        [SMEM, VMEM, VMEM, VMEM],
         (place, gathered, att_all, teacher),
         24,
-        scratch=[pltpu.VMEM((768, 2048), BF), pltpu.VMEM((768, 128), BF), pltpu.SemaphoreType.DMA((5,))],
     )
     own = lax.all_to_all(student, CHIPS, 0, 0)
     other = lax.ppermute(own, "c", swap)

time: 228 us -> 227 us (level)
  the two profiles are of different devices: /device:TPU:40 before, /device:TPU:73 now
where the time goes in v13:
time: 227 us; the launch traced here: 226 us
  blocking collectives  73.4 us (32%)
  starting transfers between devices  66.4 us (29%)
  waiting for transfers between devices  46.5 us (20%)
  Pallas kernels  19.5 us (9%)
  between operations  14.2 us (6%)
  local copies, waits for them, and re-layouts  5.45 us (2%)
    all_to_all x1, blocking collectives, on_device(): own = lax.all_to_all(student, CHIPS, 0, 0)  26 us
    ppermute x8, starting transfers between devices, from_z(): lax.ppermute(x, ('zh', 'zl'), [((i + shift) % 16, i) for i in range(16)])  25.5 us
    all_to_all x1, blocking collectives, on_device(): lax.all_to_all(partial, OCTET, 0, 0)  24.1 us
    all_to_all x1, waiting for transfers between devices, on_device(): lax.all_to_all(near, ('zh', 'yl'), 0, 0)  23.2 us
    pallas_call x8, Pallas kernels, call(): pl.pallas_call(kernel, out_shape=out_shape, in_specs=specs, out_specs=VME...  16 us
    all_to_all x1, starting transfers between devices, on_device(): lax.all_to_all(near, ('zh', 'yl'), 0, 0)  15.6 us
    all_to_all x1, blocking collectives, on_device(): att_all = lax.all_to_all(att_copies, HEADSETS, 0, 0)  15.4 us
    all_to_all x1, starting transfers between devices, on_device(): kv_own = lax.all_to_all(packed, 'zh', 0, 0)  13 us
  transfers between devices with their start and end apart: 14, of which 6 were waited for; matrix products, arithmetic and copies ran while one was open for 1% of the time, Pallas kernels for 5%

profile of v13, /device:TPU:73, one launch (start us, length us, event | category | flops | bytes accessed | tf_op | source)
XLA Modules:
  0.0 225.6 jit_solution(12002014000150757068)
XLA Ops:
  7.2 3.5 %shard_map.95 = (bf16[4,272,128]{2,1,0:T(8,128)(2,1)}, bf16[16,128]{1,0:T(8,128)(2,1)}, bf16[192,2560]{1,0:T(8,128)(2,1)}) custom-call(bf16[512,512]{1,0:T(8,128)(2,1)} %keys.1, bf16[512,512]{1,0:T(8,128)(2,1)} %values.1, s32[4,128]{1,0:T(4,128)} %bitcast.16, bf16[192,2048]{1,0:T(8,128)(2,1)} %bitcast.13, bf16[192,512]{1,0:T(8,128)(2,1)} %bitcast.14), custom_call_target="tpu_custom_call" | custom-call | tf_op jit(solution)/shard_map/pallas_call | solution.py:309
  10.8 13.0 %all-to-all-start = ((bf16[4,272,128]{2,1,0:T(8,128)(2,1)}), bf16[4,272,128]{2,1,0:T(8,128)(2,1)S(1)}, u32[]{:S(2)}, u32[]{:S(2)}) async-start(bf16[4,272,128]{2,1,0:T(8,128)(2,1)} %get-tuple-element.15), calls=%async_computation | async-start | bytes 557056 | tf_op jit(solution)/shard_map/all_to_all | solution.py:331
  23.8 7.9 %all_gather.7 = bf16[2048,128]{1,0:T(8,128)(2,1)S(1)} all-gather(bf16[512,128]{1,0:T(8,128)(2,1)S(1)} %copy-done.5), channel_id=1, replica_groups=mesh['zh'=4,'zl'=4,'yl'=2,'yh'=2,'xh'=2,'xl'=2,'c'=2] {'xl','c'}, dimensions={0}, use_global_device_ids=true | all-gather | bytes 655360 | tf_op jit(solution)/shard_map/all_gather | solution.py:335
  31.8 2.1 collective-permute-start.4
  33.9 9.9 %all-to-all-done.kv0 = bf16[4,272,128]{2,1,0:T(8,128)(2,1)S(1)} async-done(((bf16[4,272,128]{2,1,0:T(8,128)(2,1)}), bf16[4,272,128]{2,1,0:T(8,128)(2,1)S(1)}, u32[]{:S(2)}, u32[]{:S(2)}) %all-to-all-start) | async-done | bytes 278560 | tf_op jit(solution)/shard_map/all_to_all | solution.py:331
  43.8 1.9 collective-permute-start
  45.7 3.4 %collective-permute-start.1 = (bf16[4,272,128]{2,1,0:T(8,128)(2,1)S(1)}, bf16[4,272,128]{2,1,0:T(8,128)(2,1)S(1)}, u32[]{:S(2)}, u32[]{:S(2)}) collective-permute-start(bf16[4,272,128]{2,1,0:T(8,128)(2,1)S(1)} %all-to-all-done.kv0), channel_id=1, source_target_pairs={{32,0},{64,32},{96,64},{128,96},{160,128},{192,160},{224,192},{256... | collective-permute-start | bytes 835592 | tf_op jit(solution)/shard_map/ppermute | solution.py:327
  49.1 3.0 %collective-permute-start.2 = (bf16[2,272,128]{2,1,0:T(8,128)(2,1)S(1)}, bf16[2,272,128]{2,1,0:T(8,128)(2,1)S(1)}, u32[]{:S(2)}, u32[]{:S(2)}) collective-permute-start(bf16[2,272,128]{2,1,0:T(8,128)(2,1)S(1)} %get-tuple-element.27), channel_id=1, source_target_pairs={{448,0},{480,32},{0,64},{32,96},{64,128},{96,160},{128,192},{160,2... | collective-permute-start | bytes 417800 | tf_op jit(solution)/shard_map/ppermute | solution.py:327
  52.1 3.1 %collective-permute-start.3 = (bf16[2,272,128]{2,1,0:T(8,128)(2,1)S(1)}, bf16[2,272,128]{2,1,0:T(8,128)(2,1)S(1)}, u32[]{:S(2)}, u32[]{:S(2)}) collective-permute-start(bf16[2,272,128]{2,1,0:T(8,128)(2,1)S(1)} %get-tuple-element.26), channel_id=1, source_target_pairs={{64,0},{96,32},{128,64},{160,96},{192,128},{224,160},{256,192},{28... | collective-permute-start | bytes 417800 | tf_op jit(solution)/shard_map/ppermute | solution.py:327
  56.1 4.3 %collective-permute-done.3.kv3_high = bf16[2,272,128]{2,1,0:T(8,128)(2,1)S(1)} collective-permute-done((bf16[2,272,128]{2,1,0:T(8,128)(2,1)S(1)}, bf16[2,272,128]{2,1,0:T(8,128)(2,1)S(1)}, u32[]{:S(2)}, u32[]{:S(2)}) %collective-permute-start.3) | collective-permute-done | bytes 139296 | tf_op jit(solution)/shard_map/ppermute | solution.py:327
  60.4 7.1 %shard_map.96 = bf16[8,528,128]{2,1,0:T(8,128)(2,1)S(1)} custom-call(s32[7]{0:T(128)S(1)} %stack.31.place, bf16[4,272,128]{2,1,0:T(8,128)(2,1)S(1)} %all-to-all-done.kv0, bf16[4,272,128]{2,1,0:T(8,128)(2,1)S(1)} %collective-permute-done.kv1, bf16[4,272,128]{2,1,0:T(8,128)(2,1)S(1)} %collective-permute-done.1.kv2, ...), custom_call_target="tpu_custom_call" | custom-call | flops 20000000000 | bytes 4194304 | tf_op jit(solution)/shard_map/pallas_call | solution.py:293
  67.6 24.1 %all_to_all.30.parts = bf16[8,528,128]{2,1,0:T(8,128)(2,1)S(1)} all-to-all(bf16[8,528,128]{2,1,0:T(8,128)(2,1)S(1)} %shard_map.96), channel_id=1, replica_groups=mesh['zh'=4,'zl'=4,'yl'=2,'yh'=2,'xh'=2,'xl'=2,'c'=2] {'yl','xl','c'}, dimensions={0} | all-to-all | bytes 2162688 | tf_op jit(solution)/shard_map/all_to_all | solution.py:364
  91.6 0.9 shard_map.97
  92.5 15.4 %all_to_all.31.att = bf16[4,512,128]{2,1,0:T(8,128)(2,1)S(1)} all-to-all(bf16[4,512,128]{2,1,0:T(8,128)(2,1)S(1)} %get-tuple-element.17), channel_id=1, replica_groups=mesh['zh'=4,'zl'=4,'yl'=2,'yh'=2,'xh'=2,'xl'=2,'c'=2] {'yh','xh'}, dimensions={0} | all-to-all | bytes 1048576 | tf_op jit(solution)/shard_map/all_to_all | solution.py:370
  107.9 2.1 copy-done.2
  110.1 1.5 shard_map.98
  111.6 26.0 %all_to_all.32.own = bf16[8,896,128]{2,1,0:T(8,128)(2,1)S(1)} all-to-all(bf16[8,896,128]{2,1,0:T(8,128)(2,1)S(1)} %shard_map.98), channel_id=1, replica_groups=mesh['zh'=4,'zl'=4,'yl'=2,'yh'=2,'xh'=2,'xl'=2,'c'=2] {'xl','yh','xh'}, dimensions={0} | all-to-all | bytes 3670016 | tf_op jit(solution)/shard_map/all_to_all | solution.py:378
  137.6 5.0 %collective-permute-start.5 = (bf16[8,896,128]{2,1,0:T(8,128)(2,1)S(1)}, bf16[8,896,128]{2,1,0:T(8,128)(2,1)S(1)}, u32[]{:S(2)}, u32[]{:S(2)}) collective-permute-start(bf16[8,896,128]{2,1,0:T(8,128)(2,1)S(1)} %all_to_all.32.own), channel_id=1, source_target_pairs={{0,1},{1,0},{2,3},{3,2},{4,5},{5,4},{6,7},{7,6},{8,9},{9,8},{10,11... | collective-permute-start | bytes 5505032 | tf_op jit(solution)/shard_map/ppermute | solution.py:379
  143.4 2.7 %collective-permute-done.5.other = bf16[8,896,128]{2,1,0:T(8,128)(2,1)S(1)} collective-permute-done((bf16[8,896,128]{2,1,0:T(8,128)(2,1)S(1)}, bf16[8,896,128]{2,1,0:T(8,128)(2,1)S(1)}, u32[]{:S(2)}, u32[]{:S(2)}) %collective-permute-start.5) | collective-permute-done | bytes 1835040 | tf_op jit(solution)/shard_map/ppermute | solution.py:379
  146.1 3.2 %shard_map.100 = (bf16[512,256]{1,0:T(8,128)(2,1)S(1)}, bf16[4,96,256]{2,1,0:T(8,128)(2,1)}, bf16[4,96,256]{2,1,0:T(8,128)(2,1)S(1)}, bf16[8,96,256]{2,1,0:T(8,128)(2,1)}, bf16[8,96,256]{2,1,0:T(8,128)(2,1)}) custom-call(s32[7]{0:T(128)S(1)} %stack.31.place, bf16[8,896,128]{2,1,0:T(8,128)(2,1)S(1)} %all_to_all.32.own, ...), custom_call_target="tpu_custom_call" | custom-call | flops 800000000 | bytes 4194304 | tf_op jit(solution)/shard_map/pallas_call | solution.py:293
  149.3 2.0 collective-permute-start.6
  151.2 3.3 %collective-permute-start.7 = (bf16[8,96,256]{2,1,0:T(8,128)(2,1)}, bf16[8,96,256]{2,1,0:T(8,128)(2,1)S(1)}, u32[]{:S(2)}, u32[]{:S(2)}) collective-permute-start(bf16[8,96,256]{2,1,0:T(8,128)(2,1)} %get-tuple-element.22), channel_id=1, source_target_pairs={{32,0},{64,32},{96,64},{128,96},{160,128},{192,160},{224,192},{256... | collective-permute-start | bytes 1179656 | tf_op jit(solution)/shard_map/ppermute | solution.py:327
  154.5 6.9 %collective-permute-start.8 = (bf16[4,96,256]{2,1,0:T(8,128)(2,1)}, bf16[4,96,256]{2,1,0:T(8,128)(2,1)S(1)}, u32[]{:S(2)}, u32[]{:S(2)}) collective-permute-start(bf16[4,96,256]{2,1,0:T(8,128)(2,1)} %get-tuple-element.23), channel_id=1, source_target_pairs={{448,0},{480,32},{0,64},{32,96},{64,128},{96,160},{128,192},{160,2... | collective-permute-start | bytes 589832 | tf_op jit(solution)/shard_map/ppermute | solution.py:327
  161.4 1.9 collective-permute-start.9
  163.3 5.1 %all-to-all-start.5 = ((bf16[4,128,128]{2,1,0:T(8,128)(2,1)}), bf16[4,128,128]{2,1,0:T(8,128)(2,1)}, u32[]{:S(2)}, u32[]{:S(2)}) async-start(bf16[4,128,128]{2,1,0:T(8,128)(2,1)} %bitcast.10), calls=%async_computation.5 | async-start | bytes 262144 | tf_op jit(solution)/shard_map/all_to_all | solution.py:367
  168.5 1.5 copy-done.1
  170.0 0.9 shard_map.101.kept
  170.9 5.7 %collective-permute-done.9.far_above = bf16[4,96,256]{2,1,0:T(8,128)(2,1)S(1)} collective-permute-done((bf16[4,96,256]{2,1,0:T(8,128)(2,1)S(1)}, bf16[4,96,256]{2,1,0:T(8,128)(2,1)S(1)}, u32[]{:S(2)}, u32[]{:S(2)}) %collective-permute-start.9) | collective-permute-done | bytes 196640 | tf_op jit(solution)/shard_map/ppermute | solution.py:327
  176.6 1.0 shard_map.102
  177.6 15.6 %all-to-all-start.4 = ((bf16[8,96,256]{2,1,0:T(8,128)(2,1)}), bf16[8,96,256]{2,1,0:T(8,128)(2,1)S(1)}, u32[]{:S(2)}, u32[]{:S(2)}) async-start(bf16[8,96,256]{2,1,0:T(8,128)(2,1)} %shard_map.102), calls=%async_computation.4 | async-start | bytes 786432 | tf_op jit(solution)/shard_map/all_to_all | solution.py:397
  193.2 1.7 copy.10
  194.9 23.2 %all-to-all-done.4.terms = bf16[8,96,256]{2,1,0:T(8,128)(2,1)S(1)} async-done(((bf16[8,96,256]{2,1,0:T(8,128)(2,1)}), bf16[8,96,256]{2,1,0:T(8,128)(2,1)S(1)}, u32[]{:S(2)}, u32[]{:S(2)}) %all-to-all-start.4) | async-done | bytes 393248 | tf_op jit(solution)/shard_map/all_to_all | solution.py:397
  (29 shorter events, 2.4 us)
Async XLA Ops:
  7.2 16.6 %copy-start.5 = (bf16[512,128]{1,0:T(8,128)(2,1)S(1)}, bf16[512,128]{1,0:T(8,128)(2,1)}, u32[]{:S(2)}) copy-start(bf16[512,128]{1,0:T(8,128)(2,1)} %param.8) | copy-start | bytes 393220
  7.2 100.8 %all-gather.2.cloned.1.call-start = ((), (), s32[]{:S(2)}) async-start(), calls=%async_computation.6 | async-start | bytes 4915200 | tf_op jit(solution)/shard_map/all_gather | solution.py:337
  10.8 21.0 %copy-start.6 = (bf16[16,128]{1,0:T(8,128)(2,1)S(1)}, bf16[16,128]{1,0:T(8,128)(2,1)}, u32[]{:S(2)}) copy-start(bf16[16,128]{1,0:T(8,128)(2,1)} %get-tuple-element.16) | copy-start | bytes 12292
  10.8 33.0 %all-to-all-start = ((bf16[4,272,128]{2,1,0:T(8,128)(2,1)}), bf16[4,272,128]{2,1,0:T(8,128)(2,1)S(1)}, u32[]{:S(2)}, u32[]{:S(2)}) async-start(bf16[4,272,128]{2,1,0:T(8,128)(2,1)} %get-tuple-element.15), calls=%async_computation | async-start | bytes 557056 | tf_op jit(solution)/shard_map/all_to_all | solution.py:331
  31.8 23.6 %collective-permute-start.4 = (bf16[2064,128]{1,0:T(8,128)(2,1)S(1)}, bf16[2064,128]{1,0:T(8,128)(2,1)S(1)}, u32[]{:S(2)}, u32[]{:S(2)}) collective-permute-start(bf16[2064,128]{1,0:T(8,128)(2,1)S(1)} %constant_dynamic-update-slice_fusion.q_own), channel_id=1, source_target_pairs={{0,16},{16,0},{1,17},{17,1},{2,18},{18,2},{3,19},{19,3},{4,20},{20... | collective-permute-start | bytes 1585160 | tf_op jit(solution)/shard_map/ppermute | solution.py:336
  43.8 16.6 %collective-permute-start = (bf16[4,272,128]{2,1,0:T(8,128)(2,1)S(1)}, bf16[4,272,128]{2,1,0:T(8,128)(2,1)S(1)}, u32[]{:S(2)}, u32[]{:S(2)}) collective-permute-start(bf16[4,272,128]{2,1,0:T(8,128)(2,1)S(1)} %all-to-all-done.kv0), channel_id=1, source_target_pairs={{480,0},{0,32},{32,64},{64,96},{96,128},{128,160},{160,192},{192,2... | collective-permute-start | bytes 835592 | tf_op jit(solution)/shard_map/ppermute | solution.py:327
  45.7 14.7 %collective-permute-start.1 = (bf16[4,272,128]{2,1,0:T(8,128)(2,1)S(1)}, bf16[4,272,128]{2,1,0:T(8,128)(2,1)S(1)}, u32[]{:S(2)}, u32[]{:S(2)}) collective-permute-start(bf16[4,272,128]{2,1,0:T(8,128)(2,1)S(1)} %all-to-all-done.kv0), channel_id=1, source_target_pairs={{32,0},{64,32},{96,64},{128,96},{160,128},{192,160},{224,192},{256... | collective-permute-start | bytes 835592 | tf_op jit(solution)/shard_map/ppermute | solution.py:327
  49.1 7.0 %collective-permute-start.2 = (bf16[2,272,128]{2,1,0:T(8,128)(2,1)S(1)}, bf16[2,272,128]{2,1,0:T(8,128)(2,1)S(1)}, u32[]{:S(2)}, u32[]{:S(2)}) collective-permute-start(bf16[2,272,128]{2,1,0:T(8,128)(2,1)S(1)} %get-tuple-element.27), channel_id=1, source_target_pairs={{448,0},{480,32},{0,64},{32,96},{64,128},{96,160},{128,192},{160,2... | collective-permute-start | bytes 417800 | tf_op jit(solution)/shard_map/ppermute | solution.py:327
  52.1 8.3 %collective-permute-start.3 = (bf16[2,272,128]{2,1,0:T(8,128)(2,1)S(1)}, bf16[2,272,128]{2,1,0:T(8,128)(2,1)S(1)}, u32[]{:S(2)}, u32[]{:S(2)}) collective-permute-start(bf16[2,272,128]{2,1,0:T(8,128)(2,1)S(1)} %get-tuple-element.26), channel_id=1, source_target_pairs={{64,0},{96,32},{128,64},{160,96},{192,128},{224,160},{256,192},{28... | collective-permute-start | bytes 417800 | tf_op jit(solution)/shard_map/ppermute | solution.py:327
  67.5 40.4 %copy-start.4 = (bf16[32,4096]{1,0:T(8,128)(2,1)S(1)}, bf16[32,4096]{1,0:T(8,128)(2,1)}, u32[]{:S(2)}) copy-start(bf16[32,4096]{1,0:T(8,128)(2,1)} %teacher.1) | copy-start | bytes 786436
  107.9 2.1 copy-start.2
  111.6 31.1 %copy-start.3 = (bf16[3072,256]{1,0:T(8,128)(2,1)S(1)}, bf16[3072,256]{1,0:T(8,128)(2,1)}, u32[]{:S(2)}) copy-start(bf16[3072,256]{1,0:T(8,128)(2,1)} %projector.1) | copy-start | bytes 4718596
  137.6 8.4 %collective-permute-start.5 = (bf16[8,896,128]{2,1,0:T(8,128)(2,1)S(1)}, bf16[8,896,128]{2,1,0:T(8,128)(2,1)S(1)}, u32[]{:S(2)}, u32[]{:S(2)}) collective-permute-start(bf16[8,896,128]{2,1,0:T(8,128)(2,1)S(1)} %all_to_all.32.own), channel_id=1, source_target_pairs={{0,1},{1,0},{2,3},{3,2},{4,5},{5,4},{6,7},{7,6},{8,9},{9,8},{10,11... | collective-permute-start | bytes 5505032 | tf_op jit(solution)/shard_map/ppermute | solution.py:379
  146.1 3.2 %copy-start = (bf16[8,896,128]{2,1,0:T(8,128)(2,1)}, bf16[8,896,128]{2,1,0:T(8,128)(2,1)S(1)}, u32[]{:S(2)}) copy-start(bf16[8,896,128]{2,1,0:T(8,128)(2,1)S(1)} %collective-permute-done.5.other) | copy-start | bytes 5505028
  149.3 27.4 %collective-permute-start.6 = (bf16[8,96,256]{2,1,0:T(8,128)(2,1)}, bf16[8,96,256]{2,1,0:T(8,128)(2,1)S(1)}, u32[]{:S(2)}, u32[]{:S(2)}) collective-permute-start(bf16[8,96,256]{2,1,0:T(8,128)(2,1)} %get-tuple-element.21), channel_id=1, source_target_pairs={{480,0},{0,32},{32,64},{64,96},{96,128},{128,160},{160,192},{192,2... | collective-permute-start | bytes 1179656 | tf_op jit(solution)/shard_map/ppermute | solution.py:327
  151.2 25.4 %collective-permute-start.7 = (bf16[8,96,256]{2,1,0:T(8,128)(2,1)}, bf16[8,96,256]{2,1,0:T(8,128)(2,1)S(1)}, u32[]{:S(2)}, u32[]{:S(2)}) collective-permute-start(bf16[8,96,256]{2,1,0:T(8,128)(2,1)} %get-tuple-element.22), channel_id=1, source_target_pairs={{32,0},{64,32},{96,64},{128,96},{160,128},{192,160},{224,192},{256... | collective-permute-start | bytes 1179656 | tf_op jit(solution)/shard_map/ppermute | solution.py:327
  154.5 16.3 %collective-permute-start.8 = (bf16[4,96,256]{2,1,0:T(8,128)(2,1)}, bf16[4,96,256]{2,1,0:T(8,128)(2,1)S(1)}, u32[]{:S(2)}, u32[]{:S(2)}) collective-permute-start(bf16[4,96,256]{2,1,0:T(8,128)(2,1)} %get-tuple-element.23), channel_id=1, source_target_pairs={{448,0},{480,32},{0,64},{32,96},{64,128},{96,160},{128,192},{160,2... | collective-permute-start | bytes 589832 | tf_op jit(solution)/shard_map/ppermute | solution.py:327
  161.4 15.2 %collective-permute-start.9 = (bf16[4,96,256]{2,1,0:T(8,128)(2,1)S(1)}, bf16[4,96,256]{2,1,0:T(8,128)(2,1)S(1)}, u32[]{:S(2)}, u32[]{:S(2)}) collective-permute-start(bf16[4,96,256]{2,1,0:T(8,128)(2,1)S(1)} %get-tuple-element.24), channel_id=1, source_target_pairs={{64,0},{96,32},{128,64},{160,96},{192,128},{224,160},{256,192},{28... | collective-permute-start | bytes 589832 | tf_op jit(solution)/shard_map/ppermute | solution.py:327
  163.3 14.3 %all-to-all-start.5 = ((bf16[4,128,128]{2,1,0:T(8,128)(2,1)}), bf16[4,128,128]{2,1,0:T(8,128)(2,1)}, u32[]{:S(2)}, u32[]{:S(2)}) async-start(bf16[4,128,128]{2,1,0:T(8,128)(2,1)} %bitcast.10), calls=%async_computation.5 | async-start | bytes 262144 | tf_op jit(solution)/shard_map/all_to_all | solution.py:367
  168.5 1.5 copy-start.1
  177.6 40.5 %all-to-all-start.4 = ((bf16[8,96,256]{2,1,0:T(8,128)(2,1)}), bf16[8,96,256]{2,1,0:T(8,128)(2,1)S(1)}, u32[]{:S(2)}, u32[]{:S(2)}) async-start(bf16[8,96,256]{2,1,0:T(8,128)(2,1)} %shard_map.102), calls=%async_computation.4 | async-start | bytes 786432 | tf_op jit(solution)/shard_map/all_to_all | solution.py:397
Sparse Core Ops, SparseCore 0:
  10.9 56.0 all-gather.1

commit v14 on v13

--- a/solution.py
+++ b/solution.py
@@ -272,7 +272,7 @@
     out[...] = gradient_rows(own, other, mismatch, place[6])
 
 
-def add_kernel(kept, below, above, far_below, far_above, out):
+def add_kernel(kept, far_below, far_above, below, above, out):
     near = kept[...] + below[...].astype(F32) + above[...].astype(F32)
     out[0:4] = (near[0:4] + far_below[...].astype(F32)).astype(BF)
     out[4:8] = (near[4:8] + far_above[...].astype(F32)).astype(BF)
@@ -393,7 +393,7 @@
     below, above = from_z(up, -1), from_z(down, 1)
     far_below, far_above = from_z(far_up, -2), from_z(far_down, 2)
     kept = call(kept_kernel, shape(8, 96, 256, dtype=F32), [SMEM] + [VMEM] * 3, (place, own, other, mismatch), 32, 2 * 10 ** 8)
-    near = call(add_kernel, shape(8, 96, 256), [VMEM] * 5, (kept, below, above, far_below, far_above), 16)
+    near = call(add_kernel, shape(8, 96, 256), [VMEM] * 5, (kept, far_below, far_above, below, above), 16)
     grad = call(final_kernel, shape(96, 256, dtype=F32), [VMEM], (lax.all_to_all(near, ("zh", "yl"), 0, 0),), 8)
     return grad, attended
 

time: 227 us -> 221 us (0.974)
  starting transfers between devices: 66.4 us -> 62 us
    all_to_all x1, starting transfers between devices: 15.6 us -> 11.9 us  [on_device(): lax.all_to_all(near, ('zh', 'yl'), 0, 0)]
where the time goes in v14:
time: 221 us
  blocking collectives  73.4 us (33%)
  starting transfers between devices  62 us (28%)
  waiting for transfers between devices  46.3 us (21%)
  Pallas kernels  19.5 us (9%)
  between operations  14.2 us (6%)
  local copies, waits for them, and re-layouts  5.45 us (2%)
    all_to_all x1, blocking collectives, on_device(): own = lax.all_to_all(student, CHIPS, 0, 0)  26 us
    ppermute x8, starting transfers between devices, from_z(): lax.ppermute(x, ('zh', 'zl'), [((i + shift) % 16, i) for i in range(16)])  24.7 us
    all_to_all x1, blocking collectives, on_device(): lax.all_to_all(partial, OCTET, 0, 0)  24.1 us
    all_to_all x1, waiting for transfers between devices, on_device(): lax.all_to_all(near, ('zh', 'yl'), 0, 0)  23 us
    pallas_call x8, Pallas kernels, call(): pl.pallas_call(kernel, out_shape=out_shape, in_specs=specs, out_specs=VME...  16 us
    all_to_all x1, blocking collectives, on_device(): att_all = lax.all_to_all(att_copies, HEADSETS, 0, 0)  15.4 us
    all_to_all x1, starting transfers between devices, on_device(): kv_own = lax.all_to_all(packed, 'zh', 0, 0)  13 us
    all_to_all x1, starting transfers between devices, on_device(): lax.all_to_all(near, ('zh', 'yl'), 0, 0)  11.9 us
  transfers between devices with their start and end apart: 14, of which 6 were waited for; matrix products, arithmetic and copies ran while one was open for 1% of the time, Pallas kernels for 5%

profile of v14, /device:TPU:73, one launch (start us, length us, event | category | flops | bytes accessed | tf_op | source)
XLA Modules:
  0.0 221.0 jit_solution(8119772423090944637)
XLA Ops:
  7.2 3.5 %shard_map.95 = (bf16[4,272,128]{2,1,0:T(8,128)(2,1)}, bf16[16,128]{1,0:T(8,128)(2,1)}, bf16[192,2560]{1,0:T(8,128)(2,1)}) custom-call(bf16[512,512]{1,0:T(8,128)(2,1)} %keys.1, bf16[512,512]{1,0:T(8,128)(2,1)} %values.1, s32[4,128]{1,0:T(4,128)} %bitcast.16, bf16[192,2048]{1,0:T(8,128)(2,1)} %bitcast.13, bf16[192,512]{1,0:T(8,128)(2,1)} %bitcast.14), custom_call_target="tpu_custom_call" | custom-call | tf_op jit(solution)/shard_map/pallas_call | solution.py:309
  10.8 13.0 %all-to-all-start = ((bf16[4,272,128]{2,1,0:T(8,128)(2,1)}), bf16[4,272,128]{2,1,0:T(8,128)(2,1)S(1)}, u32[]{:S(2)}, u32[]{:S(2)}) async-start(bf16[4,272,128]{2,1,0:T(8,128)(2,1)} %get-tuple-element.15), calls=%async_computation | async-start | bytes 557056 | tf_op jit(solution)/shard_map/all_to_all | solution.py:331
  23.8 7.9 %all_gather.7 = bf16[2048,128]{1,0:T(8,128)(2,1)S(1)} all-gather(bf16[512,128]{1,0:T(8,128)(2,1)S(1)} %copy-done.5), channel_id=1, replica_groups=mesh['zh'=4,'zl'=4,'yl'=2,'yh'=2,'xh'=2,'xl'=2,'c'=2] {'xl','c'}, dimensions={0}, use_global_device_ids=true | all-gather | bytes 655360 | tf_op jit(solution)/shard_map/all_gather | solution.py:335
  31.8 2.1 collective-permute-start.4
  33.9 9.9 %all-to-all-done.kv0 = bf16[4,272,128]{2,1,0:T(8,128)(2,1)S(1)} async-done(((bf16[4,272,128]{2,1,0:T(8,128)(2,1)}), bf16[4,272,128]{2,1,0:T(8,128)(2,1)S(1)}, u32[]{:S(2)}, u32[]{:S(2)}) %all-to-all-start) | async-done | bytes 278560 | tf_op jit(solution)/shard_map/all_to_all | solution.py:331
  43.8 1.9 collective-permute-start
  45.7 3.4 %collective-permute-start.1 = (bf16[4,272,128]{2,1,0:T(8,128)(2,1)S(1)}, bf16[4,272,128]{2,1,0:T(8,128)(2,1)S(1)}, u32[]{:S(2)}, u32[]{:S(2)}) collective-permute-start(bf16[4,272,128]{2,1,0:T(8,128)(2,1)S(1)} %all-to-all-done.kv0), channel_id=1, source_target_pairs={{32,0},{64,32},{96,64},{128,96},{160,128},{192,160},{224,192},{256... | collective-permute-start | bytes 835592 | tf_op jit(solution)/shard_map/ppermute | solution.py:327
  49.1 3.0 %collective-permute-start.2 = (bf16[2,272,128]{2,1,0:T(8,128)(2,1)S(1)}, bf16[2,272,128]{2,1,0:T(8,128)(2,1)S(1)}, u32[]{:S(2)}, u32[]{:S(2)}) collective-permute-start(bf16[2,272,128]{2,1,0:T(8,128)(2,1)S(1)} %get-tuple-element.27), channel_id=1, source_target_pairs={{448,0},{480,32},{0,64},{32,96},{64,128},{96,160},{128,192},{160,2... | collective-permute-start | bytes 417800 | tf_op jit(solution)/shard_map/ppermute | solution.py:327
  52.1 3.1 %collective-permute-start.3 = (bf16[2,272,128]{2,1,0:T(8,128)(2,1)S(1)}, bf16[2,272,128]{2,1,0:T(8,128)(2,1)S(1)}, u32[]{:S(2)}, u32[]{:S(2)}) collective-permute-start(bf16[2,272,128]{2,1,0:T(8,128)(2,1)S(1)} %get-tuple-element.26), channel_id=1, source_target_pairs={{64,0},{96,32},{128,64},{160,96},{192,128},{224,160},{256,192},{28... | collective-permute-start | bytes 417800 | tf_op jit(solution)/shard_map/ppermute | solution.py:327
  56.1 4.3 %collective-permute-done.3.kv3_high = bf16[2,272,128]{2,1,0:T(8,128)(2,1)S(1)} collective-permute-done((bf16[2,272,128]{2,1,0:T(8,128)(2,1)S(1)}, bf16[2,272,128]{2,1,0:T(8,128)(2,1)S(1)}, u32[]{:S(2)}, u32[]{:S(2)}) %collective-permute-start.3) | collective-permute-done | bytes 139296 | tf_op jit(solution)/shard_map/ppermute | solution.py:327
  60.4 7.1 %shard_map.96 = bf16[8,528,128]{2,1,0:T(8,128)(2,1)S(1)} custom-call(s32[7]{0:T(128)S(1)} %stack.31.place, bf16[4,272,128]{2,1,0:T(8,128)(2,1)S(1)} %all-to-all-done.kv0, bf16[4,272,128]{2,1,0:T(8,128)(2,1)S(1)} %collective-permute-done.kv1, bf16[4,272,128]{2,1,0:T(8,128)(2,1)S(1)} %collective-permute-done.1.kv2, ...), custom_call_target="tpu_custom_call" | custom-call | flops 20000000000 | bytes 4194304 | tf_op jit(solution)/shard_map/pallas_call | solution.py:293
  67.6 24.1 %all_to_all.30.parts = bf16[8,528,128]{2,1,0:T(8,128)(2,1)S(1)} all-to-all(bf16[8,528,128]{2,1,0:T(8,128)(2,1)S(1)} %shard_map.96), channel_id=1, replica_groups=mesh['zh'=4,'zl'=4,'yl'=2,'yh'=2,'xh'=2,'xl'=2,'c'=2] {'yl','xl','c'}, dimensions={0} | all-to-all | bytes 2162688 | tf_op jit(solution)/shard_map/all_to_all | solution.py:364
  91.6 0.9 shard_map.97
  92.5 15.4 %all_to_all.31.att = bf16[4,512,128]{2,1,0:T(8,128)(2,1)S(1)} all-to-all(bf16[4,512,128]{2,1,0:T(8,128)(2,1)S(1)} %get-tuple-element.17), channel_id=1, replica_groups=mesh['zh'=4,'zl'=4,'yl'=2,'yh'=2,'xh'=2,'xl'=2,'c'=2] {'yh','xh'}, dimensions={0} | all-to-all | bytes 1048576 | tf_op jit(solution)/shard_map/all_to_all | solution.py:370
  107.9 2.1 copy-done.2
  110.1 1.5 shard_map.98
  111.6 26.0 %all_to_all.32.own = bf16[8,896,128]{2,1,0:T(8,128)(2,1)S(1)} all-to-all(bf16[8,896,128]{2,1,0:T(8,128)(2,1)S(1)} %shard_map.98), channel_id=1, replica_groups=mesh['zh'=4,'zl'=4,'yl'=2,'yh'=2,'xh'=2,'xl'=2,'c'=2] {'xl','yh','xh'}, dimensions={0} | all-to-all | bytes 3670016 | tf_op jit(solution)/shard_map/all_to_all | solution.py:378
  137.6 5.0 %collective-permute-start.5 = (bf16[8,896,128]{2,1,0:T(8,128)(2,1)S(1)}, bf16[8,896,128]{2,1,0:T(8,128)(2,1)S(1)}, u32[]{:S(2)}, u32[]{:S(2)}) collective-permute-start(bf16[8,896,128]{2,1,0:T(8,128)(2,1)S(1)} %all_to_all.32.own), channel_id=1, source_target_pairs={{0,1},{1,0},{2,3},{3,2},{4,5},{5,4},{6,7},{7,6},{8,9},{9,8},{10,11... | collective-permute-start | bytes 5505032 | tf_op jit(solution)/shard_map/ppermute | solution.py:379
  143.4 2.7 %collective-permute-done.5.other = bf16[8,896,128]{2,1,0:T(8,128)(2,1)S(1)} collective-permute-done((bf16[8,896,128]{2,1,0:T(8,128)(2,1)S(1)}, bf16[8,896,128]{2,1,0:T(8,128)(2,1)S(1)}, u32[]{:S(2)}, u32[]{:S(2)}) %collective-permute-start.5) | collective-permute-done | bytes 1835040 | tf_op jit(solution)/shard_map/ppermute | solution.py:379
  146.1 3.2 %shard_map.100 = (bf16[512,256]{1,0:T(8,128)(2,1)S(1)}, bf16[4,96,256]{2,1,0:T(8,128)(2,1)}, bf16[4,96,256]{2,1,0:T(8,128)(2,1)S(1)}, bf16[8,96,256]{2,1,0:T(8,128)(2,1)}, bf16[8,96,256]{2,1,0:T(8,128)(2,1)}) custom-call(s32[7]{0:T(128)S(1)} %stack.31.place, bf16[8,896,128]{2,1,0:T(8,128)(2,1)S(1)} %all_to_all.32.own, ...), custom_call_target="tpu_custom_call" | custom-call | flops 800000000 | bytes 4194304 | tf_op jit(solution)/shard_map/pallas_call | solution.py:293
  149.3 1.9 collective-permute-start.8
  151.2 3.4 %collective-permute-start.9 = (bf16[8,96,256]{2,1,0:T(8,128)(2,1)}, bf16[8,96,256]{2,1,0:T(8,128)(2,1)S(1)}, u32[]{:S(2)}, u32[]{:S(2)}) collective-permute-start(bf16[8,96,256]{2,1,0:T(8,128)(2,1)} %get-tuple-element.24), channel_id=1, source_target_pairs={{32,0},{64,32},{96,64},{128,96},{160,128},{192,160},{224,192},{256... | collective-permute-start | bytes 1179656 | tf_op jit(solution)/shard_map/ppermute | solution.py:327
  154.5 6.1 %collective-permute-start.6 = (bf16[4,96,256]{2,1,0:T(8,128)(2,1)}, bf16[4,96,256]{2,1,0:T(8,128)(2,1)S(1)}, u32[]{:S(2)}, u32[]{:S(2)}) collective-permute-start(bf16[4,96,256]{2,1,0:T(8,128)(2,1)} %get-tuple-element.21), channel_id=1, source_target_pairs={{448,0},{480,32},{0,64},{32,96},{64,128},{96,160},{128,192},{160,2... | collective-permute-start | bytes 589832 | tf_op jit(solution)/shard_map/ppermute | solution.py:327
  160.6 1.9 collective-permute-start.7
  162.6 5.1 %all-to-all-start.5 = ((bf16[4,128,128]{2,1,0:T(8,128)(2,1)}), bf16[4,128,128]{2,1,0:T(8,128)(2,1)}, u32[]{:S(2)}, u32[]{:S(2)}) async-start(bf16[4,128,128]{2,1,0:T(8,128)(2,1)} %bitcast.10), calls=%async_computation.5 | async-start | bytes 262144 | tf_op jit(solution)/shard_map/all_to_all | solution.py:367
  167.7 1.5 copy-done.1
  169.2 0.9 shard_map.101.kept
  170.1 5.8 %collective-permute-done.7.far_above = bf16[4,96,256]{2,1,0:T(8,128)(2,1)S(1)} collective-permute-done((bf16[4,96,256]{2,1,0:T(8,128)(2,1)S(1)}, bf16[4,96,256]{2,1,0:T(8,128)(2,1)S(1)}, u32[]{:S(2)}, u32[]{:S(2)}) %collective-permute-start.7) | collective-permute-done | bytes 196640 | tf_op jit(solution)/shard_map/ppermute | solution.py:327
  175.9 1.0 shard_map.102
  176.9 11.9 %all-to-all-start.4 = ((bf16[8,96,256]{2,1,0:T(8,128)(2,1)}), bf16[8,96,256]{2,1,0:T(8,128)(2,1)S(1)}, u32[]{:S(2)}, u32[]{:S(2)}) async-start(bf16[8,96,256]{2,1,0:T(8,128)(2,1)} %shard_map.102), calls=%async_computation.4 | async-start | bytes 786432 | tf_op jit(solution)/shard_map/all_to_all | solution.py:397
  188.8 1.7 copy.10
  190.5 23.0 %all-to-all-done.4.terms = bf16[8,96,256]{2,1,0:T(8,128)(2,1)S(1)} async-done(((bf16[8,96,256]{2,1,0:T(8,128)(2,1)}), bf16[8,96,256]{2,1,0:T(8,128)(2,1)S(1)}, u32[]{:S(2)}, u32[]{:S(2)}) %all-to-all-start.4) | async-done | bytes 393248 | tf_op jit(solution)/shard_map/all_to_all | solution.py:397
  (29 shorter events, 2.4 us)
Async XLA Ops:
  7.2 16.6 %copy-start.5 = (bf16[512,128]{1,0:T(8,128)(2,1)S(1)}, bf16[512,128]{1,0:T(8,128)(2,1)}, u32[]{:S(2)}) copy-start(bf16[512,128]{1,0:T(8,128)(2,1)} %param.8) | copy-start | bytes 393220
  7.2 100.8 %all-gather.2.cloned.1.call-start = ((), (), s32[]{:S(2)}) async-start(), calls=%async_computation.6 | async-start | bytes 4915200 | tf_op jit(solution)/shard_map/all_gather | solution.py:337
  10.8 21.0 %copy-start.6 = (bf16[16,128]{1,0:T(8,128)(2,1)S(1)}, bf16[16,128]{1,0:T(8,128)(2,1)}, u32[]{:S(2)}) copy-start(bf16[16,128]{1,0:T(8,128)(2,1)} %get-tuple-element.16) | copy-start | bytes 12292
  10.8 33.0 %all-to-all-start = ((bf16[4,272,128]{2,1,0:T(8,128)(2,1)}), bf16[4,272,128]{2,1,0:T(8,128)(2,1)S(1)}, u32[]{:S(2)}, u32[]{:S(2)}) async-start(bf16[4,272,128]{2,1,0:T(8,128)(2,1)} %get-tuple-element.15), calls=%async_computation | async-start | bytes 557056 | tf_op jit(solution)/shard_map/all_to_all | solution.py:331
  31.8 23.6 %collective-permute-start.4 = (bf16[2064,128]{1,0:T(8,128)(2,1)S(1)}, bf16[2064,128]{1,0:T(8,128)(2,1)S(1)}, u32[]{:S(2)}, u32[]{:S(2)}) collective-permute-start(bf16[2064,128]{1,0:T(8,128)(2,1)S(1)} %constant_dynamic-update-slice_fusion.q_own), channel_id=1, source_target_pairs={{0,16},{16,0},{1,17},{17,1},{2,18},{18,2},{3,19},{19,3},{4,20},{20... | collective-permute-start | bytes 1585160 | tf_op jit(solution)/shard_map/ppermute | solution.py:336
  43.8 16.6 %collective-permute-start = (bf16[4,272,128]{2,1,0:T(8,128)(2,1)S(1)}, bf16[4,272,128]{2,1,0:T(8,128)(2,1)S(1)}, u32[]{:S(2)}, u32[]{:S(2)}) collective-permute-start(bf16[4,272,128]{2,1,0:T(8,128)(2,1)S(1)} %all-to-all-done.kv0), channel_id=1, source_target_pairs={{480,0},{0,32},{32,64},{64,96},{96,128},{128,160},{160,192},{192,2... | collective-permute-start | bytes 835592 | tf_op jit(solution)/shard_map/ppermute | solution.py:327
  45.7 14.7 %collective-permute-start.1 = (bf16[4,272,128]{2,1,0:T(8,128)(2,1)S(1)}, bf16[4,272,128]{2,1,0:T(8,128)(2,1)S(1)}, u32[]{:S(2)}, u32[]{:S(2)}) collective-permute-start(bf16[4,272,128]{2,1,0:T(8,128)(2,1)S(1)} %all-to-all-done.kv0), channel_id=1, source_target_pairs={{32,0},{64,32},{96,64},{128,96},{160,128},{192,160},{224,192},{256... | collective-permute-start | bytes 835592 | tf_op jit(solution)/shard_map/ppermute | solution.py:327
  49.1 7.0 %collective-permute-start.2 = (bf16[2,272,128]{2,1,0:T(8,128)(2,1)S(1)}, bf16[2,272,128]{2,1,0:T(8,128)(2,1)S(1)}, u32[]{:S(2)}, u32[]{:S(2)}) collective-permute-start(bf16[2,272,128]{2,1,0:T(8,128)(2,1)S(1)} %get-tuple-element.27), channel_id=1, source_target_pairs={{448,0},{480,32},{0,64},{32,96},{64,128},{96,160},{128,192},{160,2... | collective-permute-start | bytes 417800 | tf_op jit(solution)/shard_map/ppermute | solution.py:327
  52.1 8.3 %collective-permute-start.3 = (bf16[2,272,128]{2,1,0:T(8,128)(2,1)S(1)}, bf16[2,272,128]{2,1,0:T(8,128)(2,1)S(1)}, u32[]{:S(2)}, u32[]{:S(2)}) collective-permute-start(bf16[2,272,128]{2,1,0:T(8,128)(2,1)S(1)} %get-tuple-element.26), channel_id=1, source_target_pairs={{64,0},{96,32},{128,64},{160,96},{192,128},{224,160},{256,192},{28... | collective-permute-start | bytes 417800 | tf_op jit(solution)/shard_map/ppermute | solution.py:327
  67.5 40.4 %copy-start.4 = (bf16[32,4096]{1,0:T(8,128)(2,1)S(1)}, bf16[32,4096]{1,0:T(8,128)(2,1)}, u32[]{:S(2)}) copy-start(bf16[32,4096]{1,0:T(8,128)(2,1)} %teacher.1) | copy-start | bytes 786436
  107.9 2.1 copy-start.2
  111.6 31.1 %copy-start.3 = (bf16[3072,256]{1,0:T(8,128)(2,1)S(1)}, bf16[3072,256]{1,0:T(8,128)(2,1)}, u32[]{:S(2)}) copy-start(bf16[3072,256]{1,0:T(8,128)(2,1)} %projector.1) | copy-start | bytes 4718596
  137.6 8.4 %collective-permute-start.5 = (bf16[8,896,128]{2,1,0:T(8,128)(2,1)S(1)}, bf16[8,896,128]{2,1,0:T(8,128)(2,1)S(1)}, u32[]{:S(2)}, u32[]{:S(2)}) collective-permute-start(bf16[8,896,128]{2,1,0:T(8,128)(2,1)S(1)} %all_to_all.32.own), channel_id=1, source_target_pairs={{0,1},{1,0},{2,3},{3,2},{4,5},{5,4},{6,7},{7,6},{8,9},{9,8},{10,11... | collective-permute-start | bytes 5505032 | tf_op jit(solution)/shard_map/ppermute | solution.py:379
  146.1 3.2 %copy-start = (bf16[8,896,128]{2,1,0:T(8,128)(2,1)}, bf16[8,896,128]{2,1,0:T(8,128)(2,1)S(1)}, u32[]{:S(2)}) copy-start(bf16[8,896,128]{2,1,0:T(8,128)(2,1)S(1)} %collective-permute-done.5.other) | copy-start | bytes 5505028
  149.3 26.6 %collective-permute-start.8 = (bf16[8,96,256]{2,1,0:T(8,128)(2,1)}, bf16[8,96,256]{2,1,0:T(8,128)(2,1)S(1)}, u32[]{:S(2)}, u32[]{:S(2)}) collective-permute-start(bf16[8,96,256]{2,1,0:T(8,128)(2,1)} %get-tuple-element.23), channel_id=1, source_target_pairs={{480,0},{0,32},{32,64},{64,96},{96,128},{128,160},{160,192},{192,2... | collective-permute-start | bytes 1179656 | tf_op jit(solution)/shard_map/ppermute | solution.py:327
  151.2 24.7 %collective-permute-start.9 = (bf16[8,96,256]{2,1,0:T(8,128)(2,1)}, bf16[8,96,256]{2,1,0:T(8,128)(2,1)S(1)}, u32[]{:S(2)}, u32[]{:S(2)}) collective-permute-start(bf16[8,96,256]{2,1,0:T(8,128)(2,1)} %get-tuple-element.24), channel_id=1, source_target_pairs={{32,0},{64,32},{96,64},{128,96},{160,128},{192,160},{224,192},{256... | collective-permute-start | bytes 1179656 | tf_op jit(solution)/shard_map/ppermute | solution.py:327
  154.5 15.6 %collective-permute-start.6 = (bf16[4,96,256]{2,1,0:T(8,128)(2,1)}, bf16[4,96,256]{2,1,0:T(8,128)(2,1)S(1)}, u32[]{:S(2)}, u32[]{:S(2)}) collective-permute-start(bf16[4,96,256]{2,1,0:T(8,128)(2,1)} %get-tuple-element.21), channel_id=1, source_target_pairs={{448,0},{480,32},{0,64},{32,96},{64,128},{96,160},{128,192},{160,2... | collective-permute-start | bytes 589832 | tf_op jit(solution)/shard_map/ppermute | solution.py:327
  160.6 15.2 %collective-permute-start.7 = (bf16[4,96,256]{2,1,0:T(8,128)(2,1)S(1)}, bf16[4,96,256]{2,1,0:T(8,128)(2,1)S(1)}, u32[]{:S(2)}, u32[]{:S(2)}) collective-permute-start(bf16[4,96,256]{2,1,0:T(8,128)(2,1)S(1)} %get-tuple-element.22), channel_id=1, source_target_pairs={{64,0},{96,32},{128,64},{160,96},{192,128},{224,160},{256,192},{28... | collective-permute-start | bytes 589832 | tf_op jit(solution)/shard_map/ppermute | solution.py:327
  162.6 14.3 %all-to-all-start.5 = ((bf16[4,128,128]{2,1,0:T(8,128)(2,1)}), bf16[4,128,128]{2,1,0:T(8,128)(2,1)}, u32[]{:S(2)}, u32[]{:S(2)}) async-start(bf16[4,128,128]{2,1,0:T(8,128)(2,1)} %bitcast.10), calls=%async_computation.5 | async-start | bytes 262144 | tf_op jit(solution)/shard_map/all_to_all | solution.py:367
  167.7 1.5 copy-start.1
  176.9 36.6 %all-to-all-start.4 = ((bf16[8,96,256]{2,1,0:T(8,128)(2,1)}), bf16[8,96,256]{2,1,0:T(8,128)(2,1)S(1)}, u32[]{:S(2)}, u32[]{:S(2)}) async-start(bf16[8,96,256]{2,1,0:T(8,128)(2,1)} %shard_map.102), calls=%async_computation.4 | async-start | bytes 786432 | tf_op jit(solution)/shard_map/all_to_all | solution.py:397
Sparse Core Ops, SparseCore 0:
  10.9 56.0 all-gather.1
